TPU v7x, 128 devices: a whole 4x4x4 slice. The times are simulated.
128 devices in a mesh: dp: 16 (over x, y_lo, core), tensor: 8 (over y_hi, z).
Axes of the slice: x: 4, y: 4 (y_hi: 2, y_lo: 2; y = y_hi * 2 + y_lo), z: 4, core: 2. Of those that a mesh axis runs over, the one named last changes fastest.
Arguments:
- hidden_in: bfloat16 [16, 1024, 1536], P('dp', 'tensor'), may hold values from -6 to 6
- grad_out: bfloat16 [16, 1024, 1536], P('dp', 'tensor'), may hold values from -6 to 6
- norm_in: float32 [2, 1536], replicated, may hold values from 0.5 to 1.5
- w_z: bfloat16 [2, 1536, 3072], P(None, None, 'tensor'), may hold values from -0.15625 to 0.15625
- w_x: bfloat16 [2, 1536, 3072], P(None, None, 'tensor'), may hold values from -1.7350552 to 1.7350552
- w_bc: bfloat16 [2, 1536, 256], P(None, None, 'tensor'), may hold values from -0.15625 to 0.15625
- w_dt: bfloat16 [2, 1536, 48], P(None, None, 'tensor'), may hold values from -0.15625 to 0.15625
- conv_x: float32 [2, 4, 3072], P(None, None, 'tensor'), may hold values from -3 to 3
- conv_x_bias: float32 [2, 3072], P(None, 'tensor'), may hold values from -3 to 3
- conv_bc: float32 [2, 4, 256], replicated, may hold values from -3 to 3
- conv_bc_bias: float32 [2, 256], replicated, may hold values from -3 to 3
- dt_bias: float32 [2, 48], P(None, 'tensor'), may hold values from -7 to -2.3
- a_log: float32 [2, 48], P(None, 'tensor'), may hold values from 0 to 2.77
- skip: float32 [2, 48], P(None, 'tensor'), may hold values from 0.5 to 2
- norm_gate: float32 [2, 3072], P(None, 'tensor'), may hold values from 0.5 to 1.5
- w_out: bfloat16 [2, 3072, 1536], P(None, 'tensor'), may hold values from -0.109375 to 0.109375
Outputs:
- hidden_out: float32 [16, 1024, 1536], P('dp', 'tensor')
- grad_in: float32 [16, 1024, 1536], P('dp', 'tensor')
- grad_norm_in: float32 [2, 1536], replicated
- grad_w_z: float32 [2, 1536, 3072], P(None, None, 'tensor')
- grad_w_x: float32 [2, 1536, 3072], P(None, None, 'tensor')
- grad_w_bc: float32 [2, 1536, 256], P(None, None, 'tensor')
- grad_w_dt: float32 [2, 1536, 48], P(None, None, 'tensor')
- grad_conv_x: float32 [2, 4, 3072], P(None, None, 'tensor')
- grad_conv_x_bias: float32 [2, 3072], P(None, 'tensor')
- grad_conv_bc: float32 [2, 4, 256], replicated
- grad_conv_bc_bias: float32 [2, 256], replicated
- grad_dt_bias: float32 [2, 48], P(None, 'tensor')
- grad_a_log: float32 [2, 48], P(None, 'tensor')
- grad_skip: float32 [2, 48], P(None, 'tensor')
- grad_norm_gate: float32 [2, 3072], P(None, 'tensor')
- grad_w_out: float32 [2, 3072, 1536], P(None, 'tensor')
All inputs are finite; a program needn't handle non-finite values.
Results may differ from a plain program's by a relative error of at most 0.025.
Values may be sent and summed in bfloat16 or wider, within the bound.
No kernel may reach another device: no remote copies, remote signals or barrier semaphores. Data moves between devices by JAX's collectives and lax.ppermute only.
A program may use at most 192 MiB of HBM per device.

v0:
```python
import functools

import jax
import jax.numpy as jnp
from jax import lax
from jax.experimental import pallas as pl
from jax.experimental.pallas import tpu as pltpu
from jax.sharding import PartitionSpec as P

SPAN = 256
EPS = 1e-05
LANES = 128
VMEM_BYTES = 56 * 1024 * 1024

f32 = jnp.float32
bf16 = jnp.bfloat16
highest = lax.Precision.HIGHEST

ROWS = ((0,), (0,))
COLS = ((1,), (1,))
PLAIN = ((1,), (0,))


def dot(left, right, dims=PLAIN, precision=None):
    return lax.dot_general(
        left, right, (dims, ((), ())), preferred_element_type=f32, precision=precision
    )


def sigmoid(v):
    return 1.0 / (1.0 + jnp.exp(-v))


def softplus(v):
    return jnp.maximum(v, 0.0) + jnp.log1p(jnp.exp(-jnp.abs(v)))


def spread_heads(per_head, channels, head_dim):
    rows = per_head.shape[0]
    per_tile = LANES // head_dim
    lane = lax.broadcasted_iota(jnp.int32, (rows, LANES), 1)
    tiles = []
    for tile in range(channels // LANES):
        out = jnp.broadcast_to(
            per_head[:, tile * per_tile : tile * per_tile + 1], (rows, LANES)
        )
        for sub in range(1, per_tile):
            head = tile * per_tile + sub
            out = jnp.where(
                lane >= sub * head_dim,
                jnp.broadcast_to(per_head[:, head : head + 1], (rows, LANES)),
                out,
            )
        tiles.append(out)
    return jnp.concatenate(tiles, axis=1)


def conv_taps(buf, taps, offset, width):
    out = offset
    for j in range(4):
        out = out + taps[j : j + 1] * buf[pl.ds(5 + j, width), :]
    return out


def decay_matrix(mask, cum_col, cum_row):
    return jnp.exp(jnp.where(mask, cum_col - cum_row, -1e30))


def span_values(dt, head_ref):
    length = dt.shape[0]
    rows = lax.broadcasted_iota(jnp.int32, (length, length), 0)
    cols = lax.broadcasted_iota(jnp.int32, (length, length), 1)
    mask = rows >= cols
    pre = dt + head_ref[0:1, :]
    step = softplus(pre)
    rate = head_ref[1:2, :] * step
    cum = dot(mask.astype(f32), rate, PLAIN, highest)
    return mask, pre, step, rate, cum


def put_half(place_ref, span, half, mine_ref, other_ref, value):
    own = span // half == place_ref[0]

    @pl.when(own)
    def _():
        mine_ref[...] = value

    @pl.when(jnp.logical_not(own))
    def _():
        other_ref[...] = value


def place_pieces(plan, place_ref, pieces, outs):
    core, z = place_ref[0], place_ref[1]
    for piece, other, dz, start, out, per, offset, rows in plan:
        member = (1 - core if other else core) * NZ + lax.rem(z + dz, NZ)
        row = pl.multiple_of(member * per + offset, 16)
        outs[out][pl.ds(row, rows), :] = pieces[piece][start : start + rows, :]


def cut_weights(w_ref, width):
    channels = w_ref.shape[1]
    parts = [w_ref.at[0:width, :], w_ref.at[width : 2 * width, :]]
    return parts + cut_out(w_ref.at[2 * width : 3 * width, :])


def cut_out(wo_ref):
    rows, channels = wo_ref.shape
    return [wo_ref.at[i * channels : (i + 1) * channels, :] for i in range(rows // channels)]


def times_out(v, wo_refs):
    return jnp.concatenate([dot(v, wo_ref[...]) for wo_ref in wo_refs], axis=1)


def times_out_t(v, wo_refs):
    channels = wo_refs[0].shape[1]
    return sum(
        dot(v[:, i * channels : (i + 1) * channels], wo_ref[...], COLS)
        for i, wo_ref in enumerate(wo_refs)
    )


def put_columns(place_ref, span, mine_ref, other_ref, columns):
    per = columns.shape[0] // (NC * NZ)
    rows = mine_ref.shape[0] // NZ

    def place_columns(core, ref):
        for z in range(NZ):
            at = (core * NZ + z) * per
            ref[pl.ds(pl.multiple_of(z * rows + span * per, 16), per), :] = columns[at : at + per, :]

    for core in range(NC):
        mine = place_ref[0] == core

        @pl.when(mine)
        def _(core=core):
            place_columns(core, mine_ref)

        @pl.when(jnp.logical_not(mine))
        def _(core=core):
            place_columns(core, other_ref)


def forward_kernel(plans, head_dim, place_ref, *refs):
    last_layer = len(plans) == 2
    refs = list(refs)

    def take(count):
        taken = refs[:count]
        del refs[:count]
        return taken

    piece_refs = [take(count) for _, count in plans]
    w_here, w_there, wdt_ref, cx_ref, cbc_ref, head_ref = take(6)
    w_ref, xn_ref, wbc_ref, z_ref, xp_ref, bc_ref, dt_ref, y_ref, hin_ref, mine_ref, other_ref = take(11)
    if last_layer:
        g_ref, sums_ref, gg_ref = take(3)
    w_sem, xn_all, xbuf, bbuf, hst = take(5)
    if last_layer:
        [g_all] = take(1)
    length = z_ref.shape[0]
    channels = w_ref.shape[1]
    state = hst.shape[0]
    span = pl.program_id(0)
    wz_ref, wx_ref, *wo_refs = cut_weights(w_ref, xn_ref.shape[1])

    @pl.when(span == 0)
    def _():
        @pl.when(place_ref[2] == 1)
        def _():
            pltpu.make_async_copy(w_here, w_ref, w_sem).start()

        @pl.when(place_ref[2] == 0)
        def _():
            pltpu.make_async_copy(w_there, w_ref, w_sem).start()

        if last_layer:
            place_pieces(plans[0][0], place_ref, piece_refs[0], [xn_all])
            place_pieces(plans[1][0], place_ref, piece_refs[1], [g_all, wbc_ref])
        else:
            place_pieces(plans[0][0], place_ref, piece_refs[0], [xn_all, wbc_ref])
        xbuf[0:8, :] = jnp.zeros((8, channels), f32)
        bbuf[0:8, :] = jnp.zeros((8, 2 * state), f32)
        hst[...] = jnp.zeros_like(hst)
        pltpu.make_async_copy(w_here, w_ref, w_sem).wait()

    here = pl.ds(pl.multiple_of(span * length, length), length)
    xn = xn_all[here, :]
    xn_ref[...] = xn
    z = dot(xn, wz_ref[...])
    z_ref[...] = z
    xp = dot(xn, wx_ref[...])
    xp_ref[...] = xp
    xbuf[8:, :] = xp
    bc = dot(xn, wbc_ref[...], COLS).astype(bf16)
    bc_ref[...] = bc
    bbuf[8:, :] = bc.astype(f32)
    dt = dot(xn, wdt_ref[...], COLS)
    dt_ref[...] = dt

    pre_x = conv_taps(xbuf, cx_ref[0:4, :], cx_ref[4:5, :], length)
    xc = pre_x * sigmoid(pre_x)
    pre_bc = conv_taps(bbuf, cbc_ref[0:4, :], cbc_ref[4:5, :], length)
    bcc = (pre_bc * sigmoid(pre_bc)).astype(bf16)
    xbuf[0:8, :] = xbuf[length : length + 8, :]
    bbuf[0:8, :] = bbuf[length : length + 8, :]
    b_mat = bcc[:, :state]
    c_mat = bcc[:, state:]

    mask, _, step, _, cum = span_values(dt, head_ref)
    cum_t = jnp.transpose(cum)
    scores = dot(c_mat, b_mat, COLS)
    xs = xc * spread_heads(step, channels, head_dim)
    xs_b = xs.astype(bf16)
    lane = lax.broadcasted_iota(jnp.int32, (length, LANES), 1)
    per_tile = LANES // head_dim
    tiles = []
    for tile in range(channels // LANES):
        xs_tile = xs_b[:, tile * LANES : (tile + 1) * LANES]
        out = None
        for sub in range(per_tile):
            head = tile * per_tile + sub
            decay = decay_matrix(mask, cum[:, head : head + 1], cum_t[head : head + 1, :])
            part = dot((scores * decay).astype(bf16), xs_tile)
            out = part if out is None else jnp.where(lane >= sub * head_dim, part, out)
        tiles.append(out)
    hin = hst[...]
    hin_ref[0] = hin
    last = cum[length - 1 : length, :]
    y = jnp.concatenate(tiles, axis=1)
    y = y + dot(c_mat, hin.astype(bf16)) * spread_heads(jnp.exp(cum), channels, head_dim)
    y = y + cx_ref[6:7, :] * xc
    y_ref[...] = y
    tail = spread_heads(jnp.exp(last - cum), channels, head_dim)
    keep = spread_heads(jnp.exp(last), channels, head_dim)
    hst[...] = keep * hin + dot(b_mat, (tail * xs).astype(bf16), ROWS)

    gated = y * (z * sigmoid(z))
    scaled = gated * cx_ref[5:6, :]
    squares = jnp.sum(gated * gated, axis=1, keepdims=True)
    high = squares.astype(bf16).astype(f32)
    extra = jnp.where(lane == 0, high, jnp.where(lane == 1, squares - high, 0.0)).astype(bf16)
    mixed = times_out(scaled.astype(bf16), wo_refs).astype(bf16)
    put_half(
        place_ref,
        span,
        pl.num_programs(0) // 2,
        mine_ref,
        other_ref,
        jnp.concatenate([mixed, extra], axis=1),
    )
    if last_layer:
        g = g_all[here, :]
        g_ref[...] = g
        gg = times_out_t(g, wo_refs)
        gg_ref[...] = gg
        products = jnp.sum(gg * scaled, axis=1, keepdims=True)
        both = jnp.where(lane == 0, squares, jnp.where(lane == 1, products, 0.0))
        sums_ref[...] = jnp.transpose(both)[0:8, :]


def gate_part(gg, rms, coef, z, y, cx_ref):
    norm_gate = cx_ref[5:6, :]
    sz = sigmoid(z)
    silu_z = z * sz
    gated = y * silu_z
    rg = rms * gg
    gate_out = (gated * rms * norm_gate).astype(bf16)
    d_gated = rg * norm_gate - gated * coef
    dz = (d_gated * y * (sz * (1.0 + z * (1.0 - sz)))).astype(bf16)
    return dz, d_gated * silu_z, gate_out, jnp.sum(rg * gated, axis=0, keepdims=True)


def gate_kernel(plan, n_pieces, width, place_ref, *refs):
    pieces = refs[:n_pieces]
    z_ref, y_ref, wo_ref, cx_ref, g_ref, dz_ref, dy_ref, go_ref, acc_ref, first_all = refs[n_pieces:]
    length = z_ref.shape[0]
    span = pl.program_id(0)

    @pl.when(span == 0)
    def _():
        place_pieces(plan, place_ref, pieces, [first_all])
        acc_ref[...] = jnp.zeros_like(acc_ref)

    first = first_all[pl.ds(pl.multiple_of(span * length, length), length), :]
    g = first[:, :width]
    g_ref[...] = g
    tok = first[:, width:].astype(f32)
    rms = tok[:, 0:1] + tok[:, 1:2]
    coef = tok[:, 2:3] + tok[:, 3:4]
    gg = times_out_t(g, cut_out(wo_ref))
    dz, dy, gate_out, acc_norm = gate_part(gg, rms, coef, z_ref[...], y_ref[...], cx_ref)
    dz_ref[...] = dz
    dy_ref[...] = dy
    go_ref[...] = gate_out
    acc_ref[5:6, :] += acc_norm


def last_gate_kernel(inner_all, place_ref, gg_ref, tok_ref, z_ref, y_ref, cx_ref, dz_ref, dy_ref, go_ref, acc_ref):
    @pl.when(pl.program_id(0) == 0)
    def _():
        acc_ref[...] = jnp.zeros_like(acc_ref)

    tok = jnp.transpose(tok_ref[...])
    rms = lax.rsqrt(tok[:, 0:1] / inner_all + EPS)
    coef = rms * rms * rms * tok[:, 1:2] / inner_all
    dz, dy, gate_out, acc_norm = gate_part(gg_ref[...], rms, coef, z_ref[...], y_ref[...], cx_ref)
    dz_ref[...] = dz
    dy_ref[...] = dy
    go_ref[...] = gate_out
    acc_ref[5:6, :] += acc_norm


def scan_kernel(head_dim, place_ref, *refs):
    (dy_ref, dz_ref, xn_ref, xp_ref, xhalo_ref, bc_ref, bchalo_ref, dt_ref, hin_ref,
     w_ref, wbc_ref, wdt_ref, cx_ref, cbc_ref, head_ref, pick_ref,
     dxt_ref, bcmine_ref, bcother_ref, mine_ref, other_ref, acc_ref, acch_ref, shared_ref,
     accbc, accn, xbuf, bbuf, dubuf, dubbuf, dhst) = refs
    length = xp_ref.shape[0]
    channels = w_ref.shape[1]
    width = xn_ref.shape[1]
    state = dhst.shape[0]
    step_id = pl.program_id(0)
    first_span = step_id == pl.num_programs(0) - 1

    @pl.when(step_id == 0)
    def _():
        dubuf[length:, :] = jnp.zeros((8, channels), f32)
        dubbuf[length:, :] = jnp.zeros((8, 2 * state), f32)
        dhst[...] = jnp.zeros_like(dhst)
        accn[...] = jnp.zeros_like(accn)
        acc_ref[...] = jnp.zeros_like(acc_ref)
        accbc[...] = jnp.zeros_like(accbc)
        acch_ref[...] = jnp.zeros_like(acch_ref)

    @pl.when(first_span)
    def _():
        xbuf[0:8, :] = jnp.zeros((8, channels), f32)
        bbuf[0:8, :] = jnp.zeros((8, 2 * state), f32)

    @pl.when(jnp.logical_not(first_span))
    def _():
        xbuf[0:8, :] = xhalo_ref[...]
        bbuf[0:8, :] = bchalo_ref[...].astype(f32)[8:16, :]

    xbuf[8:, :] = xp_ref[...]
    bbuf[8:, :] = bc_ref[...].astype(f32)
    dz_b, dy = dz_ref[...], dy_ref[...]
    skip = cx_ref[6:7, :]

    pre_x = conv_taps(xbuf, cx_ref[0:4, :], cx_ref[4:5, :], length)
    sx = sigmoid(pre_x)
    xc = pre_x * sx
    pre_bc = conv_taps(bbuf, cbc_ref[0:4, :], cbc_ref[4:5, :], length)
    sbc = sigmoid(pre_bc)
    bcc = (pre_bc * sbc).astype(bf16)
    b_mat = bcc[:, :state]
    c_mat = bcc[:, state:]
    mask, pre_dt, step, rate, cum = span_values(dt_ref[...], head_ref)
    cum_t = jnp.transpose(cum)
    last = cum[length - 1 : length, :]
    scores = dot(c_mat, b_mat, COLS)
    step_all = spread_heads(step, channels, head_dim)
    xs = xc * step_all
    xs_b = xs.astype(bf16)
    tail = spread_heads(jnp.exp(last - cum), channels, head_dim)
    keep = spread_heads(jnp.exp(last), channels, head_dim)

    hin = hin_ref[0]
    hin_b = hin.astype(bf16)
    dh = dhst[...]
    dh_b = dh.astype(bf16)
    dye = dy * spread_heads(jnp.exp(cum), channels, head_dim)
    dye_b = dye.astype(bf16)
    txs = tail * xs
    txs_b = txs.astype(bf16)
    carried = dot(c_mat, hin_b)
    pulled = dot(b_mat, dh_b)
    d_c = dot(dye_b, hin_b, COLS)
    d_b = dot(txs_b, dh_b, COLS)
    dhst[...] = keep * dh + dot(c_mat, dye_b, ROWS)
    into = txs * pulled
    across = dye * carried - into
    at_last = jnp.sum(into, axis=0, keepdims=True) + keep * jnp.sum(hin * dh, axis=0, keepdims=True)

    dy_b = dy.astype(bf16)
    dy_t = jnp.transpose(dy).astype(bf16)
    lane = lax.broadcasted_iota(jnp.int32, (length, LANES), 1)
    per_tile = LANES // head_dim
    d_scores = jnp.zeros((length, length), f32)
    row_sums = jnp.zeros((length, LANES), f32)
    col_sums = []
    dxs_parts = []
    for head in range(channels // head_dim):
        tile, sub = divmod(head, per_tile)
        dy_tile = dy_b[:, tile * LANES : (tile + 1) * LANES]
        own = (lane >= sub * head_dim) & (lane < (sub + 1) * head_dim)
        dy_head = jnp.where(own, dy_tile, jnp.zeros_like(dy_tile))
        d_m = dot(dy_head, xs_b[:, tile * LANES : (tile + 1) * LANES], COLS)
        decay = decay_matrix(mask, cum[:, head : head + 1], cum_t[head : head + 1, :])
        dxs_parts.append(
            dot(dy_t[head * head_dim : (head + 1) * head_dim, :], (scores * decay).astype(bf16))
        )
        d_m = d_m * decay
        d_scores = d_scores + d_m
        pairs = d_m * scores
        row_sums = jnp.where(lane == head, jnp.sum(pairs, axis=1, keepdims=True), row_sums)
        col_sums.append(jnp.sum(pairs, axis=0, keepdims=True))
    heads = len(col_sums)
    col_sums = jnp.concatenate(col_sums + [jnp.zeros((LANES - heads, length), f32)], axis=0)
    dxs = jnp.transpose(jnp.concatenate(dxs_parts, axis=0)) + tail * pulled
    pick = pick_ref[...]
    d_cum = row_sums - jnp.transpose(col_sums) + dot(across, pick, PLAIN, highest)
    at_last = dot(jnp.broadcast_to(at_last, (8, channels)), pick, PLAIN, highest)[0:1, :]
    d_rate = dot(mask.astype(f32), d_cum, ROWS, highest) + at_last
    d_step = d_rate * head_ref[1:2, :] + dot(dxs * xc, pick, PLAIN, highest)
    d_dt = d_step * sigmoid(pre_dt)
    acch_ref[0:1, :] += jnp.sum(d_dt, axis=0, keepdims=True)
    acch_ref[1:2, :] += jnp.sum(d_rate * rate, axis=0, keepdims=True)
    dt_b = d_dt.astype(bf16)
    ds_b = d_scores.astype(bf16)
    d_c = d_c + dot(ds_b, b_mat)
    d_b = d_b + dot(ds_b, c_mat, ROWS)
    d_xc = dxs * step_all + skip * dy
    acc_skip = jnp.sum(dy * xc, axis=0, keepdims=True)

    d_u = d_xc * (sx * (1.0 + pre_x * (1.0 - sx)))
    d_ub = jnp.concatenate([d_b, d_c], axis=1) * (sbc * (1.0 + pre_bc * (1.0 - sbc)))
    dubuf[0:length, :] = d_u
    dubbuf[0:length, :] = d_ub
    d_x = jnp.zeros_like(d_u)
    d_bc = jnp.zeros_like(d_ub)
    acc_rows = []
    accbc_rows = []
    for j in range(4):
        d_x = d_x + cx_ref[j : j + 1, :] * dubuf[pl.ds(3 - j, length), :]
        d_bc = d_bc + cbc_ref[j : j + 1, :] * dubbuf[pl.ds(3 - j, length), :]
        acc_rows.append(jnp.sum(d_u * xbuf[pl.ds(5 + j, length), :], axis=0, keepdims=True))
        accbc_rows.append(jnp.sum(d_ub * bbuf[pl.ds(5 + j, length), :], axis=0, keepdims=True))
    dubuf[length:, :] = d_u[0:8, :]
    dubbuf[length:, :] = d_ub[0:8, :]
    zero = jnp.zeros((1, channels), f32)
    acc_ref[...] += jnp.concatenate(
        acc_rows + [jnp.sum(d_u, axis=0, keepdims=True), zero, acc_skip, zero], axis=0
    )
    zero = jnp.zeros((3, d_ub.shape[1]), f32)
    accbc[...] += jnp.concatenate(
        accbc_rows + [jnp.sum(d_ub, axis=0, keepdims=True), zero], axis=0
    )
    dx_b = d_x.astype(bf16)
    dbc_b = d_bc.astype(bf16)
    dxt_ref[:, :channels] = dx_b
    dxt_ref[:, channels:] = dt_b
    put_columns(
        place_ref,
        pl.num_programs(0) - 1 - step_id,
        bcmine_ref,
        bcother_ref,
        jnp.transpose(d_bc).astype(bf16),
    )
    total = dot(dz_b, w_ref[0:width, :], COLS) + dot(dx_b, w_ref[width : 2 * width, :], COLS)
    total = total + dot(dbc_b, wbc_ref[...]) + dot(dt_b, wdt_ref[...])
    accn[0:1, :] += jnp.sum(total * xn_ref[...].astype(f32), axis=0, keepdims=True)

    @pl.when(first_span)
    def _():
        lanes = shared_ref.shape[1]
        lines = [accn[0:1, i * lanes : (i + 1) * lanes] for i in range(width // lanes)]
        shared = jnp.concatenate(lines + [accbc[0:5, :]], axis=0)
        shared_ref[0 : shared.shape[0], :] = shared.astype(bf16)
        shared_ref[shared.shape[0] :, :] = jnp.zeros(
            (shared_ref.shape[0] - shared.shape[0], lanes), bf16
        )

    put_half(
        place_ref,
        pl.num_programs(0) - 1 - step_id,
        pl.num_programs(0) // 2,
        mine_ref,
        other_ref,
        total.astype(bf16),
    )


def whole(shape):
    zeros = (0,) * len(shape)
    return pl.BlockSpec(shape, lambda i, p: zeros)


def span_rows(columns):
    return pl.BlockSpec((SPAN, columns), lambda i, p: (i, 0))


def half_rows(columns, spans, reverse):
    half = spans // 2

    def block(i, core):
        span = spans - 1 - i if reverse else i
        return jnp.clip(span - half * core, 0, half - 1), 0

    return [
        pl.BlockSpec((SPAN, columns), lambda i, p: block(i, p[0])),
        pl.BlockSpec((SPAN, columns), lambda i, p: block(i, 1 - p[0])),
    ]


def span_call(kernel, name, spans, place, operands, in_specs, shapes, out_specs, scratch, flops):
    moved = sum(v.size * v.dtype.itemsize for v in [*operands, *shapes])
    return pl.pallas_call(
        kernel,
        grid_spec=pltpu.PrefetchScalarGridSpec(
            num_scalar_prefetch=1,
            grid=(spans,),
            in_specs=in_specs,
            out_specs=out_specs,
            scratch_shapes=scratch,
        ),
        out_shape=shapes,
        compiler_params=pltpu.CompilerParams(
            dimension_semantics=("arbitrary",), vmem_limit_bytes=VMEM_BYTES
        ),
        cost_estimate=pl.CostEstimate(flops=flops, bytes_accessed=moved, transcendentals=0),
        name=name,
    )(place, *operands)


def run_forward(place, gathered, weights, small, state, head_dim):
    channels = weights[0].shape[1]
    width = gathered[0][0][0].shape[1]
    anywhere = pl.BlockSpec(memory_space=pl.ANY)
    tokens = NC * NZ * gathered[0][2][0]
    spans = tokens // SPAN
    last_layer = len(gathered) == 2
    plans = [(cut_plan(*one), len(one[0])) for one in gathered]
    operands = [p for one in gathered for p in one[0]]
    in_specs = [whole(v.shape) for v in operands] + [anywhere] * 2
    operands += [*weights, *small]
    in_specs += [whole(v.shape) for v in operands[len(in_specs) :]]
    shapes = [
        jax.ShapeDtypeStruct(weights[0].shape, bf16),
        jax.ShapeDtypeStruct((tokens, width), bf16),
        jax.ShapeDtypeStruct((2 * state, width), bf16),
        jax.ShapeDtypeStruct((tokens, channels), f32),
        jax.ShapeDtypeStruct((tokens, channels), f32),
        jax.ShapeDtypeStruct((tokens, 2 * state), bf16),
        jax.ShapeDtypeStruct((tokens, LANES), f32),
        jax.ShapeDtypeStruct((tokens, channels), f32),
        jax.ShapeDtypeStruct((spans, state, channels), f32),
        jax.ShapeDtypeStruct((tokens // 2, width + LANES), bf16),
        jax.ShapeDtypeStruct((tokens // 2, width + LANES), bf16),
    ]
    out_specs = [whole(weights[0].shape), span_rows(width), whole((2 * state, width))]
    out_specs += [span_rows(s.shape[1]) for s in shapes[3:8]]
    out_specs.append(pl.BlockSpec((1, state, channels), lambda i, p: (i, 0, 0)))
    out_specs += half_rows(width + LANES, spans, False)
    scratch = [
        pltpu.SemaphoreType.DMA,
        pltpu.VMEM((tokens, width), bf16),
        pltpu.VMEM((SPAN + 8, channels), f32),
        pltpu.VMEM((SPAN + 8, 2 * state), f32),
        pltpu.VMEM((state, channels), f32),
    ]
    if last_layer:
        shapes += [
            jax.ShapeDtypeStruct((tokens, width), bf16),
            jax.ShapeDtypeStruct((8, tokens), f32),
            jax.ShapeDtypeStruct((tokens, channels), f32),
        ]
        out_specs += [span_rows(width), pl.BlockSpec((8, SPAN), lambda i, p: (0, i)), span_rows(channels)]
        scratch.append(pltpu.VMEM((tokens, width), bf16))
    kernel = functools.partial(forward_kernel, plans, head_dim)
    return span_call(
        kernel, "layer_forward", spans, place, operands, in_specs, shapes, out_specs, scratch, 20 * 10**9
    )


def run_gate(place, gathered, z, y, w, cx):
    tokens, channels = z.shape
    width = w.shape[0] // 3
    spans = tokens // SPAN
    plan, pieces = cut_plan(*gathered), list(gathered[0])
    operands = [*pieces, z, y, w, cx]
    in_specs = [whole(p.shape) for p in pieces]
    in_specs += [span_rows(channels), span_rows(channels)]
    in_specs += [pl.BlockSpec((width, channels), lambda i, p: (2, 0)), whole(cx.shape)]
    shapes = [
        jax.ShapeDtypeStruct((tokens, width), bf16),
        jax.ShapeDtypeStruct((tokens, channels), bf16),
        jax.ShapeDtypeStruct((tokens, channels), f32),
        jax.ShapeDtypeStruct((tokens, channels), bf16),
        jax.ShapeDtypeStruct((8, channels), f32),
    ]
    out_specs = [span_rows(s.shape[1]) for s in shapes[:4]] + [whole(shapes[4].shape)]
    scratch = [pltpu.VMEM((tokens, pieces[0].shape[1]), bf16)]
    kernel = functools.partial(gate_kernel, plan, len(pieces), width)
    return span_call(
        kernel, "gate_backward", spans, place, operands, in_specs, shapes, out_specs, scratch, 6 * 10**9
    )


def run_last_gate(place, gg, sums, z, y, cx, inner_all):
    tokens, channels = z.shape
    spans = tokens // SPAN
    rows = span_rows(channels)
    shapes = [
        jax.ShapeDtypeStruct((tokens, channels), bf16),
        jax.ShapeDtypeStruct((tokens, channels), f32),
        jax.ShapeDtypeStruct((tokens, channels), bf16),
        jax.ShapeDtypeStruct((8, channels), f32),
    ]
    return span_call(
        functools.partial(last_gate_kernel, inner_all),
        "last_gate_backward",
        spans,
        place,
        [gg, sums, z, y, cx],
        [rows, pl.BlockSpec((8, SPAN), lambda i, p: (0, i)), rows, rows, whole(cx.shape)],
        shapes,
        [rows, rows, rows, whole(shapes[3].shape)],
        [],
        10**9,
    )


def run_scan(place, dy, dz, xn, xp, bc, dt, hin, weights, small, pick, head_dim):
    tokens, channels = xp.shape
    state = hin.shape[1]
    width = xn.shape[1]
    spans = tokens // SPAN

    def rev(columns):
        return pl.BlockSpec((SPAN, columns), lambda i, p: (spans - 1 - i, 0))

    def halo(columns, rows):
        per = SPAN // rows
        return pl.BlockSpec(
            (rows, columns), lambda i, p: (jnp.maximum((spans - 1 - i) * per - 1, 0), 0)
        )

    operands = [dy, dz, xn, xp, xp, bc, bc, dt, hin, *weights, *small, pick]
    in_specs = [
        rev(channels),
        rev(channels),
        rev(width),
        rev(channels),
        halo(channels, 8),
        rev(2 * state),
        halo(2 * state, 16),
        rev(LANES),
        pl.BlockSpec((1, state, channels), lambda i, p: (spans - 1 - i, 0, 0)),
    ]
    in_specs.append(whole((2 * width, channels)))
    in_specs += [whole(v.shape) for v in operands[len(in_specs) :]]
    shapes = [
        jax.ShapeDtypeStruct((tokens, channels + LANES), bf16),
        jax.ShapeDtypeStruct((state * spans, SPAN), bf16),
        jax.ShapeDtypeStruct((state * spans, SPAN), bf16),
        jax.ShapeDtypeStruct((tokens // 2, width), bf16),
        jax.ShapeDtypeStruct((tokens // 2, width), bf16),
        jax.ShapeDtypeStruct((8, channels), f32),
        jax.ShapeDtypeStruct((8, LANES), f32),
        jax.ShapeDtypeStruct((16, 2 * state), bf16),
    ]
    out_specs = [rev(channels + LANES), whole(shapes[1].shape), whole(shapes[2].shape)]
    out_specs += half_rows(width, spans, True)
    out_specs += [whole(s.shape) for s in shapes[5:]]
    scratch = [
        pltpu.VMEM((8, 2 * state), f32),
        pltpu.VMEM((8, width), f32),
        pltpu.VMEM((SPAN + 8, channels), f32),
        pltpu.VMEM((SPAN + 8, 2 * state), f32),
        pltpu.VMEM((SPAN + 8, channels), f32),
        pltpu.VMEM((SPAN + 8, 2 * state), f32),
        pltpu.VMEM((state, channels), f32),
    ]
    kernel = functools.partial(scan_kernel, head_dim)
    return span_call(
        kernel, "scan_backward", spans, place, operands, in_specs, shapes, out_specs, scratch, 28 * 10**9
    )


def weight_kernel(pairs, *refs):
    lefts, rights, out_ref = refs[: len(pairs)], refs[len(pairs) : -1], refs[-1]
    at = 0
    for left_ref, right_ref in zip(lefts, rights):
        columns = right_ref.shape[1]
        out_ref[:, at : at + columns] = dot(left_ref[...], right_ref[...], ROWS).astype(bf16)
        at += columns


def weight_products(pairs):
    tokens = pairs[0][0].shape[0]
    rows = max(left.shape[1] for left, _ in pairs)
    block = rows // 4
    lefts, rights, columns = [], [], []
    for left, right in pairs:
        quarter = left.shape[1] == block
        lefts.append(pl.BlockSpec((tokens, block), (lambda i: (0, 0)) if quarter else (lambda i: (0, i))))
        wide = block if quarter else right.shape[1]
        rights.append(pl.BlockSpec((tokens, wide), (lambda i: (0, i)) if quarter else (lambda i: (0, 0))))
        columns.append(wide)
    return pl.pallas_call(
        functools.partial(weight_kernel, pairs_of(columns)),
        grid=(4,),
        in_specs=lefts + rights,
        out_specs=pl.BlockSpec((block, sum(columns)), lambda i: (i, 0)),
        out_shape=jax.ShapeDtypeStruct((rows, sum(columns)), bf16),
        compiler_params=pltpu.CompilerParams(vmem_limit_bytes=VMEM_BYTES),
        cost_estimate=pl.CostEstimate(
            flops=2 * tokens * rows * sum(columns), bytes_accessed=8 * 10**6, transcendentals=0
        ),
        name="weight_products",
    )(*[left for left, _ in pairs], *[right for _, right in pairs])


def pairs_of(columns):
    return tuple(columns)


SIZES = (4, 2, 2, 2, 4)
NX, NYL, NC, NYH, NZ = SIZES
EVERY = [
    (x, yl, c, yh, z)
    for x in range(NX)
    for yl in range(NYL)
    for c in range(NC)
    for yh in range(NYH)
    for z in range(NZ)
]


def linear(x, yl, c, yh, z):
    return ((((x % NX) * NYL + yl % NYL) * NC + c % NC) * NYH + yh % NYH) * NZ + z % NZ


def send(v, step, only=None):
    pairs = [(linear(*d), linear(*step(*d))) for d in EVERY if only is None or only(*d)]
    return lax.ppermute(v, ("dp", "tensor"), pairs)


def send_z(v, k):
    return send(v, lambda x, yl, c, yh, z: (x, yl, c, yh, z + k))


def send_core(v):
    return send(v, lambda x, yl, c, yh, z: (x, yl, c + 1, yh, z))


def trade(v, k):
    return send(v, lambda x, yl, c, yh, z: (x, yl, yh, c, z + k))


def traded(v):
    return send(v, lambda x, yl, c, yh, z: (x, yl, yh, c, z), lambda x, yl, c, yh, z: c != yh)


def trade_places(v):
    _, _, core, yh, _ = position()
    return jnp.where(core == yh, v, traded(v))


def position():
    dp, tensor = lax.axis_index("dp"), lax.axis_index("tensor")
    return dp // (NYL * NC), dp // NC % NYL, dp % NC, tensor // NZ, tensor % NZ


def gather(v, parts, away=False):
    arrays, sources = [], []
    for k in (0, 1, 3, 2):
        if away:
            piece = trade(v, k) if k else trade_places(v)
        else:
            piece = send_z(v, k) if k else v
        arrays += [piece, send_core(piece)]
        sources += [(False, -k % NZ, 0), (True, -k % NZ, 0)]
    return arrays, sources, parts


def cut_plan(arrays, sources, parts):
    plan = []
    for number, (piece, (other, dz, first)) in enumerate(zip(arrays, sources)):
        base = 0
        for out, per in enumerate(parts):
            begin, end = max(first, base), min(first + piece.shape[0], base + per)
            if begin < end:
                plan.append((number, other, dz, begin - first, out, per, begin - base, end - begin))
            base += per
    return plan


def fold(mine, other):
    _, _, _, _, z = position()
    rows = mine.shape[0] // NZ
    blocks = []
    for k in range(NZ):
        at = (z + k) % NZ * rows
        a = lax.dynamic_slice_in_dim(mine, at, rows, 0).astype(f32)
        blocks.append(a + lax.dynamic_slice_in_dim(other, at, rows, 0).astype(f32))
    return blocks


def fold_beside(pairs):
    folded = [fold(mine, send_core(other)) for mine, other in pairs]
    return [jnp.concatenate([blocks[k] for blocks in folded], axis=1) for k in range(NZ)]


def scatter(*pairs):
    own, one, two, three = fold_beside(pairs)
    return [own] + [send_z(b.astype(bf16), k) for k, b in ((1, one), (2, two), (3, three))]


def scatter_with_sum(mine, other, shared, meanwhile):
    half = mine.shape[0]
    rows = half // NZ
    got = after(send_core(jnp.concatenate([other, shared], axis=0)), *meanwhile)
    blocks = fold(mine, got[:half])
    total_shared = shared.astype(f32) + got[half:].astype(f32)
    packed = total_shared.astype(bf16)
    total = blocks[0]
    for k in range(1, NZ):
        got = send_z(jnp.concatenate([blocks[k].astype(bf16), packed], axis=0), k)
        total = total + got[:rows].astype(f32)
        total_shared = total_shared + got[rows:].astype(f32)
    return total, total_shared


def sum_members(v):
    both = v + send_core(v)
    total = both
    for k in range(1, NZ):
        total = total + send_z(both, k)
    return total


def sum_far(v):
    far = send(v, lambda x, yl, c, yh, z: (x, yl, c, yh + 1, z), lambda x, yl, c, yh, z: c != yh)
    return (v.astype(f32) + far.astype(f32)).astype(bf16)


def halve(v):
    _, _, core, yh, _ = position()
    half = v.shape[0] // 2
    near = send(
        v[half:], lambda x, yl, c, yh, z: (x, yl, c + 1, yh, z), lambda x, yl, c, yh, z: c == yh
    )
    return jnp.where(core == yh, v[:half], near)


def sum_beside(part):
    beside = send(part, lambda x, yl, c, yh, z: (x, yl + 1, c, yh, z))
    return (part.astype(f32) + beside.astype(f32)).astype(bf16)


def sum_x(v):
    x = position()[0]
    rows = v.shape[0] // NX
    total = lax.dynamic_slice_in_dim(v, x * rows, rows, 0).astype(f32)
    for k in range(1, NX):
        block = lax.dynamic_slice_in_dim(v, (x + k) % NX * rows, rows, 0)
        total = total + send(block, lambda x, yl, c, yh, z, k=k: (x + k, yl, c, yh, z)).astype(f32)
    return total.astype(bf16)


def collect_x(part):
    x = position()[0]
    out = jnp.zeros((NX,) + part.shape, bf16)
    out = lax.dynamic_update_index_in_dim(out, part, x, 0)
    for k in range(1, NX):
        block = send(part, lambda x, yl, c, yh, z, k=k: (x + k, yl, c, yh, z))
        out = lax.dynamic_update_index_in_dim(out, block, (x - k) % NX, 0)
    return out


def collect(part):
    out = collect_x(part)
    return out, send_core(out)


def write_kernel(columns, by_half, n_kept, place_ref, here_ref, there_ref, *refs):
    low = pl.program_id(1) if not by_half else pl.program_id(0)
    here = (low == 0) == (place_ref[2] == 1)
    for column, out_ref in zip(columns, refs[n_kept:]):
        at = slice(column, column + out_ref.shape[-1])

        @pl.when(here)
        def _(out_ref=out_ref, at=at):
            out_ref[...] = here_ref[0, :, at].astype(f32).reshape(out_ref.shape)

        @pl.when(jnp.logical_not(here))
        def _(out_ref=out_ref, at=at):
            out_ref[...] = there_ref[0, :, at].astype(f32).reshape(out_ref.shape)


def write_sums(place, halves, by_half, outputs):
    rows = halves[0].shape[1]
    total = 2 * NX * rows
    grid = (2, NX) if by_half else (NX, 2)

    def block(i, j):
        return i * grid[1] + j

    columns, shapes, specs, kept, alias = [], [], [], [], {}
    for column, kind, layer, array in outputs:
        columns.append(column)
        if kind == "flat":
            shapes.append(jax.ShapeDtypeStruct((total, LANES), f32))
            specs.append(pl.BlockSpec((rows, LANES), lambda i, j, p: (block(i, j), 0)))
        else:
            wide = total // 4
            if kind == "rows":
                shapes.append(jax.ShapeDtypeStruct((2, total, wide), f32))
                specs.append(
                    pl.BlockSpec((1, rows, wide), lambda i, j, p, layer=layer: (layer, block(i, j), 0))
                )
            else:
                per = wide // rows
                shapes.append(jax.ShapeDtypeStruct((2, wide, total), f32))
                specs.append(
                    pl.BlockSpec(
                        (1, rows, wide),
                        lambda i, j, p, layer=layer: (layer, block(i, j) % per, block(i, j) // per),
                    )
                )
        if array is not None:
            alias[3 + len(kept)] = len(shapes) - 1
            kept.append(array)
    piece = pl.BlockSpec((1, rows, halves[0].shape[2]), lambda i, j, p: (j if by_half else i, 0, 0))
    return pl.pallas_call(
        functools.partial(write_kernel, columns, by_half, len(kept)),
        grid_spec=pltpu.PrefetchScalarGridSpec(
            num_scalar_prefetch=1,
            grid=grid,
            in_specs=[piece, piece] + [pl.BlockSpec(memory_space=pl.ANY)] * len(kept),
            out_specs=specs,
        ),
        out_shape=shapes,
        input_output_aliases=alias,
        compiler_params=pltpu.CompilerParams(vmem_limit_bytes=VMEM_BYTES),
        name="write_sums",
    )(place, *halves, *kept)


def row_call(kernel, name, operands, shapes):
    return pl.pallas_call(
        kernel,
        grid=(1,),
        in_specs=[pl.BlockSpec((rows, v.shape[1]), lambda i: (0, 0)) for v, rows in operands],
        out_specs=[pl.BlockSpec(s.shape, lambda i: (0, 0)) for s in shapes],
        out_shape=shapes,
        compiler_params=pltpu.CompilerParams(vmem_limit_bytes=VMEM_BYTES),
        name=name,
    )(*[v for v, _ in operands])


def inverse_rms(v):
    return lax.rsqrt(jnp.mean(v * v, axis=-1, keepdims=True) + EPS)


def first_kernel(packed_ref, gain_ref, out_ref):
    rows = 128
    v = packed_ref[0:rows, :].astype(f32)
    out_ref[0:rows, :] = (v * inverse_rms(v) * gain_ref[...]).astype(bf16)
    out_ref[rows:, :] = packed_ref[rows : out_ref.shape[0], :]


def add_terms(own_ref, a_ref, b_ref, c_ref):
    total = own_ref[...].astype(f32) + a_ref[...].astype(f32)
    return total + (b_ref[...].astype(f32) + c_ref[...].astype(f32))


def unscaled_output(inner_all, terms, width):
    total = add_terms(*terms)
    squares = total[:, width : width + 1] + total[:, width + 1 : width + 2]
    gate_rms = lax.rsqrt(squares / inner_all + EPS)
    return gate_rms, total[:, :width] * gate_rms


def middle_kernel(inner_all, own_ref, a_ref, b_ref, c_ref, res_ref, gain_ref, res1_ref, mixed_ref, rms_ref, normed_ref):
    width = res_ref.shape[1]
    gate_rms, mixed = unscaled_output(inner_all, (own_ref, a_ref, b_ref, c_ref), width)
    res = res_ref[...].astype(f32) + mixed
    res1_ref[...] = res
    mixed_ref[...] = mixed
    rms_ref[...] = jnp.broadcast_to(gate_rms, rms_ref.shape)
    normed_ref[...] = (res * inverse_rms(res) * gain_ref[...]).astype(bf16)


def input_gradient(grad_normed, res, d_res, gain):
    inv = inverse_rms(res)
    scaled = grad_normed * gain
    dots = jnp.sum(scaled * res, axis=-1, keepdims=True) / res.shape[1]
    return d_res + inv * scaled - res * (inv * inv * inv) * dots


def between_kernel(inner_all, own_ref, a_ref, b_ref, c_ref, res_ref, dres_ref, gain_ref, mixed_ref, rms_ref, out_ref, sent_ref):
    width = res_ref.shape[1]
    grad_normed = add_terms(*(ref.at[:, 0:width] for ref in (own_ref, a_ref, b_ref, c_ref)))
    d_res = input_gradient(grad_normed, res_ref[...], dres_ref[...].astype(f32), gain_ref[...])
    out_ref[...] = d_res
    g_mixed = d_res.astype(bf16)
    sent_ref[:, :width] = g_mixed
    gate_rms = rms_ref[:, 0:1]
    products = jnp.sum(g_mixed.astype(f32) * mixed_ref[...], axis=-1, keepdims=True)
    coef = gate_rms * gate_rms * products / inner_all
    lane = lax.broadcasted_iota(jnp.int32, rms_ref.shape, 1)
    rms_high = gate_rms.astype(bf16).astype(f32)
    coef_high = coef.astype(bf16).astype(f32)
    extra = jnp.where(lane == 0, rms_high, jnp.where(lane == 1, gate_rms - rms_high, 0.0))
    extra = jnp.where(lane == 2, coef_high, jnp.where(lane == 3, coef - coef_high, extra))
    sent_ref[:, width:] = extra.astype(bf16)


def end_kernel(own_ref, a_ref, b_ref, c_ref, res_ref, dres_ref, gain_ref, hidden_ref, out_ref):
    width = res_ref.shape[1]
    grad_normed = add_terms(own_ref, a_ref, b_ref, c_ref)
    grad = input_gradient(grad_normed, res_ref[...].astype(f32), dres_ref[...], gain_ref[...])
    out_ref[:, :width] = hidden_ref[...]
    out_ref[:, width:] = grad.astype(bf16)


def last_kernel(inner_all, own_ref, a_ref, b_ref, c_ref, res_ref, out_ref):
    _, mixed = unscaled_output(inner_all, (own_ref, a_ref, b_ref, c_ref), res_ref.shape[1])
    out_ref[...] = (res_ref[...] + mixed).astype(bf16)


def after(v, *others):
    return lax.optimization_barrier((v, *others))[0]


def pad_to(v, rows, lanes):
    return jnp.pad(v, ((0, rows - v.shape[0]), (0, lanes - v.shape[1])))


def local(
    hidden_in,
    grad_out,
    norm_in,
    w_z,
    w_x,
    w_bc,
    w_dt,
    conv_x,
    conv_x_bias,
    conv_bc,
    conv_bc_bias,
    dt_bias,
    a_log,
    skip,
    norm_gate,
    w_out,
):
    layers, width, channels = w_z.shape
    heads = w_dt.shape[2]
    head_dim = channels // heads
    both = conv_bc.shape[2]
    state = both // 2
    members = NC * NZ
    inner_all = channels * members
    rows = hidden_in.shape[1]
    bc_rows = both // members
    _, _, core, yh, z = position()
    stays = core == yh
    place = jnp.stack([core, z, stays]).astype(jnp.int32)
    full = jax.ShapeDtypeStruct((rows, width), f32)

    bc_t = jnp.swapaxes(w_bc, 1, 2)
    dt_t = jnp.pad(jnp.swapaxes(w_dt, 1, 2), ((0, 0), (0, 8 - heads), (0, 0)))
    packed = jnp.concatenate([hidden_in[0], bc_t[0], dt_t.reshape(layers * 8, width)], axis=0)
    packed = trade_places(packed)
    per_channel = jnp.concatenate(
        [conv_x, conv_x_bias[:, None], norm_gate[:, None], jnp.repeat(skip, head_dim, axis=1)[:, None]],
        axis=1,
    )
    per_channel = jnp.pad(per_channel, ((0, 0), (0, 1), (0, 0)))
    per_head = jnp.stack([dt_bias, -jnp.exp(a_log)], axis=1)
    per_head = jnp.pad(per_head, ((0, 0), (0, 6), (0, LANES - heads)))
    little = jnp.concatenate([per_channel, per_head], axis=2).reshape(layers * 8, channels + LANES)
    little = trade_places(after(little, packed)).reshape(layers, 8, channels + LANES)

    def pack_weights(layer):
        quarters = [w_out[layer, :, i * channels : (i + 1) * channels] for i in range(width // channels)]
        return jnp.concatenate([w_z[layer], w_x[layer], *quarters], axis=0)

    w0 = pack_weights(0)
    w0 = w0, traded(after(w0, packed))

    [sent] = row_call(
        first_kernel,
        "first_norm",
        [(packed, packed.shape[0]), (norm_in[0:1], 1)],
        [jax.ShapeDtypeStruct((rows + bc_rows, width), bf16)],
    )
    gathered0 = gather(sent, (rows, bc_rows))
    wdt = [pad_to(packed[rows + bc_rows + 8 * l : rows + bc_rows + 8 * (l + 1)], LANES, width) for l in range(layers)]
    smalls = []
    for layer in range(layers):
        cbc = jnp.concatenate([conv_bc[layer], conv_bc_bias[layer][None], jnp.zeros((3, both), f32)], axis=0)
        smalls.append((little[layer, :, :channels], cbc, little[layer, :, channels:]))
    channel_head = jnp.arange(channels) // head_dim
    pick = (channel_head[:, None] == jnp.arange(LANES)[None, :]).astype(f32)

    out0 = run_forward(place, [gathered0], (*w0, wdt[0]), smalls[0], state, head_dim)
    w0, xn0, wbc0, z0, xp0, bc0, dt0, y0, hin0, mine, other = out0
    grads = jnp.concatenate([grad_out[0], bc_t[1]], axis=0)
    gathered_grad = gather(after(grads, *gathered0[0]), (rows, bc_rows), away=True)
    grad_held = gathered_grad[0][0]
    terms = scatter((mine, after(other, *gathered_grad[0][::2])))
    w1 = pack_weights(1)
    w1 = w1, traded(after(w1, mine))
    res1, mixed0, rms0, normed1 = row_call(
        functools.partial(middle_kernel, inner_all),
        "middle_norm",
        [(v, rows) for v in terms] + [(packed, rows), (norm_in[1:2], 1)],
        [full, full, jax.ShapeDtypeStruct((rows, LANES), f32), jax.ShapeDtypeStruct((rows, width), bf16)],
    )
    gathered1 = gather(normed1, (rows,))
    out1 = run_forward(
        place, [gathered1, gathered_grad], (*w1, wdt[1]), smalls[1], state, head_dim
    )
    w1, xn1, wbc1, z1, xp1, bc1, dt1, y1, hin1, mine, other, grad_rows1, sums, gg1 = out1
    sums = sum_members(sums)

    home = fold(mine, send_core(other))
    dz1, dy1, go1, acc_gate1 = run_last_gate(place, gg1, sums, z1, y1, smalls[1][0], inner_all)
    early1 = sum_far(weight_products([(xn1, dz1), (go1, grad_rows1)]))
    dy1 = after(dy1, *home)
    home = home[:1] + [send_z(home[k].astype(bf16), k) for k in range(1, NZ)]
    back1 = run_scan(
        place, dy1, dz1, xn1, xp1, bc1, dt1, hin1, (w1, wbc1, wdt[1]), smalls[1], pick, head_dim
    )
    dxt1, *bc_halves, mine, other, acc1, acch1, shared1 = back1
    terms = scatter((mine, after(other, early1, *home)), bc_halves)
    [hidden_out] = row_call(
        functools.partial(last_kernel, inner_all),
        "last_output",
        [(after(home[0], terms[1]), rows)] + [(v, rows) for v in home[1:]] + [(res1, rows)],
        [jax.ShapeDtypeStruct((rows, width), bf16)],
    )
    d_res1, sent = row_call(
        functools.partial(between_kernel, inner_all),
        "between_layers",
        [(v, rows) for v in terms]
        + [(res1, rows), (grad_held, rows), (norm_in[1:2], 1), (mixed0, rows), (rms0, rows)],
        [full, jax.ShapeDtypeStruct((rows, width + LANES), bf16)],
    )
    gathered_back = gather(sent, (rows,))
    early1 = sum_x(halve(after(early1, sent)))

    bc_at = channels + bc_rows

    def with_bc(dxt, bc_sum):
        by_token = bc_sum.reshape(-1, bc_rows, SPAN).swapaxes(1, 2).reshape(-1, bc_rows)
        spread = jnp.pad(by_token, ((0, 0), (bc_at, dxt.shape[1] - bc_at - bc_rows)))
        return dxt + spread.astype(bf16)

    dxt1 = with_bc(dxt1, sum(v[:, width:].astype(f32) for v in terms))

    z0 = after(z0, early1)
    grad_rows0, dz0, dy0, go0, acc_gate0 = run_gate(place, gathered_back, z0, y0, w0, smalls[0][0])
    early = weight_products([(xn0, dz0), (go0, grad_rows0), (xn1, dxt1)])
    dy0 = after(dy0, early)
    early = sum_x(early)
    early1 = sum_beside(after(early1, dz0))
    back0 = run_scan(
        place, dy0, dz0, xn0, xp0, bc0, dt0, hin0, (w0, wbc0, wdt[0]), smalls[0], pick, head_dim
    )
    dxt0, *bc_halves, mine, other, acc0, acch0, shared0 = back0
    halves = collect(after(early1, dxt0))
    g_wz, g_wo = write_sums(place, halves, True, [(0, "rows", 1, None), (channels, "blocks", 1, None)])

    terms = scatter((mine, other))
    [outputs] = row_call(
        end_kernel,
        "outputs",
        [(v, rows) for v in terms] + [(packed, rows), (d_res1, rows), (norm_in[0:1], 1), (hidden_out, rows)],
        [jax.ShapeDtypeStruct((rows, 2 * width), bf16)],
    )
    outputs = trade_places(outputs).astype(f32)

    shared = jnp.concatenate([shared0, shared1], axis=0)
    bc_sum, shared = scatter_with_sum(*bc_halves, shared, (early, early1))
    tiny = jnp.concatenate(
        [(acc0 + acc_gate0).reshape(-1), (acc1 + acc_gate1).reshape(-1), acch0[0:2].reshape(-1), acch1[0:2].reshape(-1)]
        + [shared.reshape(-1)]
    )
    tiny_at = bc_at + bc_rows
    tiny_lanes = channels + LANES - tiny_at
    tiny_size = tiny.shape[0]
    tiny = jnp.pad(tiny, (0, width * tiny_lanes - tiny_size)).reshape(width, tiny_lanes)
    late = weight_products([(xn0, with_bc(dxt0, bc_sum))])
    late = late + jnp.pad(tiny, ((0, 0), (tiny_at, 0))).astype(bf16)
    late = sum_beside(halve(sum_far(sum_x(late))))
    early = sum_beside(halve(sum_far(after(early, dxt0))))
    g_wz, g_wo, g_wx, narrow1 = write_sums(
        place,
        collect(early),
        False,
        [
            (0, "rows", 0, g_wz),
            (channels, "blocks", 0, g_wo),
            (2 * channels, "rows", 1, None),
            (3 * channels, "flat", 1, None),
        ],
    )
    g_wx, narrow0 = write_sums(
        place, collect(late), False, [(0, "rows", 0, g_wx), (channels, "flat", 0, None)]
    )

    tiny = narrow0[:, tiny_at - channels :].reshape(-1)[:tiny_size]
    sizes = [8 * channels, 8 * channels, 2 * LANES, 2 * LANES]
    cut = [sum(sizes[:i]) for i in range(len(sizes) + 1)]
    g_x = tiny[: cut[2]].reshape(layers, 8, channels)
    g_head = tiny[cut[2] : cut[4]].reshape(layers, 2, LANES)[:, :, :heads]
    shared = tiny[cut[4] :].reshape(layers, -1, both)
    lines = width // both
    g_norm_in = shared[:, :lines].reshape(layers, width) / norm_in
    g_bc = shared[:, lines : lines + 5]
    return (
        outputs[None, :, :width],
        outputs[None, :, width:],
        g_norm_in,
        g_wz,
        g_wx,
        jnp.stack([v[:, bc_at - channels : tiny_at - channels] for v in (narrow0, narrow1)]),
        jnp.stack([v[:, :heads] for v in (narrow0, narrow1)]),
        g_x[:, 0:4],
        g_x[:, 4],
        g_bc[:, 0:4],
        g_bc[:, 4],
        g_head[:, 0],
        g_head[:, 1],
        jnp.sum(g_x[:, 6].reshape(layers, heads, head_dim), axis=2),
        g_x[:, 5],
        g_wo,
    )


def solution(mesh):
    specs_in = (
        P("dp", "tensor", None),
        P("dp", "tensor", None),
        P(),
        P(None, None, "tensor"),
        P(None, None, "tensor"),
        P(None, None, "tensor"),
        P(None, None, "tensor"),
        P(None, None, "tensor"),
        P(None, "tensor"),
        P(),
        P(),
        P(None, "tensor"),
        P(None, "tensor"),
        P(None, "tensor"),
        P(None, "tensor"),
        P(None, "tensor", None),
    )
    specs_out = (
        P("dp", "tensor", None),
        P("dp", "tensor", None),
        P(),
        P(None, None, "tensor"),
        P(None, None, "tensor"),
        P(None, None, "tensor"),
        P(None, None, "tensor"),
        P(None, None, "tensor"),
        P(None, "tensor"),
        P(),
        P(),
        P(None, "tensor"),
        P(None, "tensor"),
        P(None, "tensor"),
        P(None, "tensor"),
        P(None, "tensor", None),
    )
    return jax.shard_map(
        local, mesh=mesh, in_specs=specs_in, out_specs=specs_out, check_vma=False
    )
```

profile of v0, /device:TPU:1, one launch (start us, length us, event | category | flops | bytes accessed | tf_op | source)
XLA Modules:
  0.0 551.6 jit_solution(15738079272037825791)
XLA Ops:
  4.2 6.3 %collective-permute-start = (bf16[176,1536]{1,0:T(8,128)(2,1)}, bf16[176,1536]{1,0:T(8,128)(2,1)S(1)}, u32[]{:S(2)}, u32[]{:S(2)}) collective-permute-start(bf16[176,1536]{1,0:T(8,128)(2,1)} %pad_maximum_fusion.1), channel_id=1, source_target_pairs={{4,8},{5,9},{6,10},{7,11},{8,4},{9,5},{10,6},{11,7},{20,24},{21,25... | collective-permute-start | bytes 1622024 | tf_op jit(solution)/shard_map/ppermute | solution.py:739
  10.6 3.3 bitcast_dynamic-update-slice_fusion.1
  20.8 3.1 collective-permute-start.8
  34.9 8.8 %collective-permute-done.2.refs_2_ = bf16[160,1536]{1,0:T(8,128)(2,1)S(1)} collective-permute-done((bf16[160,1536]{1,0:T(8,128)(2,1)}, bf16[160,1536]{1,0:T(8,128)(2,1)S(1)}, u32[]{:S(2)}, u32[]{:S(2)}) %collective-permute-start.2) | collective-permute-done | bytes 491552 | tf_op jit(solution)/shard_map/ppermute | solution.py:739
  43.7 7.4 %collective-permute-done.4.refs_4_ = bf16[160,1536]{1,0:T(8,128)(2,1)S(1)} collective-permute-done((bf16[160,1536]{1,0:T(8,128)(2,1)}, bf16[160,1536]{1,0:T(8,128)(2,1)S(1)}, u32[]{:S(2)}, u32[]{:S(2)}) %collective-permute-start.4) | collective-permute-done | bytes 491552 | tf_op jit(solution)/shard_map/ppermute | solution.py:739
  54.1 4.2 collective-permute-start.9
  62.7 2.9 collective-permute-done.9
  69.4 2.8 collective-permute-start.12
  72.2 3.3 collective-permute-start.13
  75.7 24.7 %layer_forward.2 = (bf16[4608,384]{1,0:T(8,128)(2,1)}, bf16[1024,1536]{1,0:T(8,128)(2,1)}, bf16[256,1536]{1,0:T(8,128)(2,1)}, f32[1024,384]{1,0:T(8,128)}, f32[1...) custom-call(s32[3]{0:T(128)} %pad_add_fusion.3.place_ref, ...), custom_call_target="tpu_custom_call" | custom-call | flops 20000000000 | bytes 28860416 | tf_op jit(solution)/shard_map/layer_forward/pallas_call | solution.py:510
  102.0 4.0 collective-permute-start.29
  112.3 18.5 %collective-permute-done.15.a_ref = bf16[128,1664]{1,0:T(8,128)(2,1)S(1)} collective-permute-done((bf16[128,1664]{1,0:T(8,128)(2,1)S(1)}, bf16[128,1664]{1,0:T(8,128)(2,1)S(1)}, u32[]{:S(2)}, u32[]{:S(2)}) %collective-permute-start.15) | collective-permute-done | bytes 426016 | tf_op jit(solution)/shard_map/ppermute | solution.py:739
  132.6 3.3 middle_norm.1
  140.4 7.3 %collective-permute-done.19.refs_2_ = bf16[128,1536]{1,0:T(8,128)(2,1)S(1)} collective-permute-done((bf16[128,1536]{1,0:T(8,128)(2,1)}, bf16[128,1536]{1,0:T(8,128)(2,1)S(1)}, u32[]{:S(2)}, u32[]{:S(2)}) %collective-permute-start.19) | collective-permute-done | bytes 393248 | tf_op jit(solution)/shard_map/ppermute | solution.py:739
  149.2 7.6 %collective-permute-start.22 = (bf16[128,1536]{1,0:T(8,128)(2,1)S(1)}, bf16[128,1536]{1,0:T(8,128)(2,1)S(1)}, u32[]{:S(2)}, u32[]{:S(2)}) collective-permute-start(bf16[128,1536]{1,0:T(8,128)(2,1)S(1)} %collective-permute-done.21.refs_4_), channel_id=1, source_target_pairs={{0,8},{1,9},{2,10},{3,11},{4,12},{5,13},{6,14},{7,15},{8,0},{9,1},... | collective-permute-start | bytes 1179656 | tf_op jit(solution)/shard_map/ppermute | solution.py:739
  160.1 29.0 %layer_forward.3 = (bf16[4608,384]{1,0:T(8,128)(2,1)}, bf16[1024,1536]{1,0:T(8,128)(2,1)}, bf16[256,1536]{1,0:T(8,128)(2,1)}, f32[1024,384]{1,0:T(8,128)}, f32[1...) custom-call(s32[3]{0:T(128)} %pad_add_fusion.3.place_ref, ...), custom_call_target="tpu_custom_call" | custom-call | flops 20000000000 | bytes 36757504 | tf_op jit(solution)/shard_map/layer_forward/pallas_call | solution.py:510
  189.7 3.3 collective-permute-done.30
  194.7 2.9 collective-permute-start.32
  201.0 6.2 %last_gate_backward.1 = (bf16[1024,384]{1,0:T(8,128)(2,1)}, f32[1024,384]{1,0:T(8,128)}, bf16[1024,384]{1,0:T(8,128)(2,1)}, f32[8,384]{1,0:T(8,128)}) custom-call(s32[3]{0:T(128)} %pad_add_fusion.3.place_ref, f32[1024,384]{1,0:T(8,128)} %get-tuple-element.103.gg_ref, f32[8,1024]{1,0:T(8,128)} %add_add_fusion.tok_ref, f32[1024,384]{1,0:T(8,128)} %get-tuple-element.105.z_ref, ...), custom_call_target="tpu_custom_call" | custom-call | flops 1000000000 | bytes 7921664 | tf_op jit(solution)/shard_map/last_gate_backward/pallas_call | solution.py:510
  207.2 7.6 %weight_products.3 = bf16[1536,768]{1,0:T(8,128)(2,1)} custom-call(bf16[1024,1536]{1,0:T(8,128)(2,1)} %get-tuple-element.112.refs_2_.refs_0_, bf16[1024,384]{1,0:T(8,128)(2,1)} %get-tuple-element.121.refs_1_, bf16[1024,384]{1,0:T(8,128)(2,1)} %get-tuple-element.111.refs_1_.refs_2_, bf16[1024,1536]{1,0:T(8,128)(2,1)} %get-tuple-element.122.refs_3_), custom_call_target="tpu_custom_call" | custom-call | flops 2415919104 | bytes 8000000 | tf_op jit(solution)/shard_map/weight_products/pallas_call | solution.py:703
  214.8 3.9 collective-permute-start.35
  220.0 2.9 collective-permute-start.37
  224.5 29.4 %scan_backward.2 = (bf16[1024,512]{1,0:T(8,128)(2,1)}, bf16[512,256]{1,0:T(8,128)(2,1)}, bf16[512,256]{1,0:T(8,128)(2,1)}, bf16[512,1536]{1,0:T(8,128)(2,1)}, bf...) custom-call(s32[3]{0:T(128)} %pad_add_fusion.3.place_ref, ...), custom_call_target="tpu_custom_call" | custom-call | flops 28000000000 | bytes 20692992 | tf_op jit(solution)/shard_map/scan_backward/pallas_call | solution.py:510
  255.9 3.3 collective-permute-done.40
  263.8 18.8 %collective-permute-done.41.a_ref = bf16[128,1792]{1,0:T(8,128)(2,1)S(1)} collective-permute-done((bf16[128,1792]{1,0:T(8,128)(2,1)S(1)}, bf16[128,1792]{1,0:T(8,128)(2,1)S(1)}, u32[]{:S(2)}, u32[]{:S(2)}) %collective-permute-start.41) | collective-permute-done | bytes 458784 | tf_op jit(solution)/shard_map/ppermute | solution.py:739
  284.7 3.9 between_layers.1
  306.7 4.1 collective-permute-start.44
  312.2 2.8 collective-permute-start.46
  319.2 8.8 %gate_backward.1 = (bf16[1024,1536]{1,0:T(8,128)(2,1)}, bf16[1024,384]{1,0:T(8,128)(2,1)}, f32[1024,384]{1,0:T(8,128)}, bf16[1024,384]{1,0:T(8,128)(2,1)}, f32[8,384]{1,0:T(8,128)}) custom-call(s32[3]{0:T(128)} %pad_add_fusion.3.place_ref, bf16[128,1664]{1,0:T(8,128)(2,1)} %get-tuple-element.129.refs_0_, bf16[128,1664]{1,0:T(8,128)(2,1)} %copy-done.67, ...), custom_call_target="tpu_custom_call" | custom-call | flops 6000000000 | bytes 16408576 | tf_op jit(solution)/shard_map/gate_backward/pallas_call | solution.py:510
  328.5 10.0 %weight_products.4 = bf16[1536,1280]{1,0:T(8,128)(2,1)} custom-call(bf16[1024,1536]{1,0:T(8,128)(2,1)} %get-tuple-element.136.refs_0_.refs_2_, bf16[1024,384]{1,0:T(8,128)(2,1)} %get-tuple-element.137.refs_1_, bf16[1024,1536]{1,0:T(8,128)(2,1)} %get-tuple-element.112.refs_2_.refs_0_, bf16[1024,384]{1,0:T(8,128)(2,1)} %get-tuple-element.138.refs_3_.refs_1_, ...), custom_call_target="tpu_custom_call" | custom-call | flops 4026531840 | bytes 8000000 | tf_op jit(solution)/shard_map/weight_products/pallas_call | solution.py:703
  338.5 3.5 constant_dynamic-slice_fusion.5
  347.1 29.5 %scan_backward.3 = (bf16[1024,512]{1,0:T(8,128)(2,1)}, bf16[512,256]{1,0:T(8,128)(2,1)}, bf16[512,256]{1,0:T(8,128)(2,1)}, bf16[512,1536]{1,0:T(8,128)(2,1)}, bf...) custom-call(s32[3]{0:T(128)} %pad_add_fusion.3.place_ref, ...), custom_call_target="tpu_custom_call" | custom-call | flops 28000000000 | bytes 20692992 | tf_op jit(solution)/shard_map/scan_backward/pallas_call | solution.py:510
  382.0 13.6 %collective-permute-done.85 = bf16[192,768]{1,0:T(8,128)(2,1)S(1)} collective-permute-done((bf16[192,768]{1,0:T(8,128)(2,1)S(1)}, bf16[192,768]{1,0:T(8,128)(2,1)S(1)}, u32[]{:S(2)}, u32[]{:S(2)}) %collective-permute-start.85) | collective-permute-done | bytes 294944 | tf_op jit(solution)/shard_map/ppermute | solution.py:739
  408.1 8.7 %collective-permute-start.78 = (bf16[384,1280]{1,0:T(8,128)(2,1)S(1)}, bf16[384,1280]{1,0:T(8,128)(2,1)}, u32[]{:S(2)}, u32[]{:S(2)}) collective-permute-start(bf16[384,1280]{1,0:T(8,128)(2,1)S(1)} %add_convert_fusion.2), channel_id=1, source_target_pairs={{4,0},{5,1},{6,2},{7,3},{8,12},{9,13},{10,14},{11,15},{20,16},{21,... | collective-permute-start | bytes 2949128 | tf_op jit(solution)/shard_map/ppermute | solution.py:739
  421.4 5.4 weight_products.5
  434.5 10.0 %collective-permute-done.68 = bf16[384,512]{1,0:T(8,128)(2,1)S(1)} collective-permute-done((bf16[384,512]{1,0:T(8,128)(2,1)S(1)}, bf16[384,512]{1,0:T(8,128)(2,1)S(1)}, u32[]{:S(2)}, u32[]{:S(2)}) %collective-permute-start.68) | collective-permute-done | bytes 393248 | tf_op jit(solution)/shard_map/ppermute | solution.py:739
  445.5 5.1 collective-permute-start.71
  454.3 3.5 collective-permute-start.57
  458.2 3.8 collective-permute-start.58
  470.1 2.8 last_output.1.hidden_ref
  472.9 7.5 %write_sums.3 = (f32[2,1536,384]{2,1,0:T(8,128)}, f32[2,384,1536]{2,1,0:T(8,128)}) custom-call(s32[3]{0:T(128)} %pad_add_fusion.3.place_ref, bf16[4,192,768]{2,1,0:T(8,128)(2,1)} %copy-done.2, bf16[4,192,768]{2,1,0:T(8,128)(2,1)} %copy-done.16), custom_call_target="tpu_custom_call" | custom-call | tf_op jit(solution)/shard_map/write_sums/pallas_call | solution.py:929
  481.1 3.5 outputs.1
  484.6 4.3 collective-permute-start.59
  488.9 3.7 collective-permute-start.82
  495.5 9.0 %collective-permute-done.82 = bf16[192,1280]{1,0:T(8,128)(2,1)S(1)} collective-permute-done((bf16[192,1280]{1,0:T(8,128)(2,1)S(1)}, bf16[192,1280]{1,0:T(8,128)(2,1)S(1)}, u32[]{:S(2)}, u32[]{:S(2)}) %collective-permute-start.82) | collective-permute-done | bytes 491552 | tf_op jit(solution)/shard_map/ppermute | solution.py:739
  506.2 11.5 %collective-permute-done.83 = bf16[192,1280]{1,0:T(8,128)(2,1)S(1)} collective-permute-done((bf16[192,1280]{1,0:T(8,128)(2,1)S(1)}, bf16[192,1280]{1,0:T(8,128)(2,1)S(1)}, u32[]{:S(2)}, u32[]{:S(2)}) %collective-permute-start.83) | collective-permute-done | bytes 491552 | tf_op jit(solution)/shard_map/ppermute | solution.py:739
  523.1 9.2 %write_sums.4 = (f32[2,1536,384]{2,1,0:T(8,128)}, f32[2,384,1536]{2,1,0:T(8,128)}, f32[2,1536,384]{2,1,0:T(8,128)}, f32[1536,128]{1,0:T(8,128)}) custom-call(s32[3]{0:T(128)} %pad_add_fusion.3.place_ref, bf16[4,192,1280]{2,1,0:T(8,128)(2,1)} %copy-done.1, bf16[4,192,1280]{2,1,0:T(8,128)(2,1)} %copy-done.10, ...), custom_call_target="tpu_custom_call", output_to_operand_aliasing={{0}: (3, {}), {1}: (4, {})} | custom-call | tf_op jit(solution)/shard_map/write_sums/pallas_call | solution.py:929
  533.2 6.6 %write_sums.5 = (f32[2,1536,384]{2,1,0:T(8,128)}, f32[1536,128]{1,0:T(8,128)}) custom-call(s32[3]{0:T(128)} %pad_add_fusion.3.place_ref, bf16[4,192,512]{2,1,0:T(8,128)(2,1)} %copy-done.5, bf16[4,192,512]{2,1,0:T(8,128)(2,1)} %copy-done.19, f32[2,1536,384]{2,1,0:T(8,128)} %get-tuple-element.168.refs_0_), custom_call_target="tpu_custom_call", output_to_operand_aliasing={{0}: (3, {})} | custom-call | tf_op jit(solution)/shard_map/write_sums/pallas_call | solution.py:929
  (444 shorter events, 163.0 us)
Async XLA Ops:
  4.2 15.6 %collective-permute-start = (bf16[176,1536]{1,0:T(8,128)(2,1)}, bf16[176,1536]{1,0:T(8,128)(2,1)S(1)}, u32[]{:S(2)}, u32[]{:S(2)}) collective-permute-start(bf16[176,1536]{1,0:T(8,128)(2,1)} %pad_maximum_fusion.1), channel_id=1, source_target_pairs={{4,8},{5,9},{6,10},{7,11},{8,4},{9,5},{10,6},{11,7},{20,24},{21,25... | collective-permute-start | bytes 1622024 | tf_op jit(solution)/shard_map/ppermute | solution.py:739
  20.8 54.8 %collective-permute-start.8 = (bf16[4608,384]{1,0:T(8,128)(2,1)}, bf16[4608,384]{1,0:T(8,128)(2,1)}, u32[]{:S(2)}, u32[]{:S(2)}) collective-permute-start(bf16[4608,384]{1,0:T(8,128)(2,1)} %get-tuple-element.95.refs_8_), channel_id=1, source_target_pairs={{4,8},{5,9},{6,10},{7,11},{8,4},{9,5},{10,6},{11,7},{20,24},{21,25... | collective-permute-start | bytes 10616840 | tf_op jit(solution)/shard_map/ppermute | solution.py:739
  31.3 19.9 %collective-permute-start.4 = (bf16[160,1536]{1,0:T(8,128)(2,1)}, bf16[160,1536]{1,0:T(8,128)(2,1)S(1)}, u32[]{:S(2)}, u32[]{:S(2)}) collective-permute-start(bf16[160,1536]{1,0:T(8,128)(2,1)} %first_norm.1.refs_0_), channel_id=1, source_target_pairs={{0,3},{1,0},{2,1},{3,2},{4,7},{5,4},{6,5},{7,6},{8,11},{9,8},{10,9... | collective-permute-start | bytes 1474568 | tf_op jit(solution)/shard_map/ppermute | solution.py:739
  33.4 19.2 %collective-permute-start.6 = (bf16[160,1536]{1,0:T(8,128)(2,1)}, bf16[160,1536]{1,0:T(8,128)(2,1)S(1)}, u32[]{:S(2)}, u32[]{:S(2)}) collective-permute-start(bf16[160,1536]{1,0:T(8,128)(2,1)} %first_norm.1.refs_0_), channel_id=1, source_target_pairs={{0,2},{1,3},{2,0},{3,1},{4,6},{5,7},{6,4},{7,5},{8,10},{9,11},{10,... | collective-permute-start | bytes 1474568 | tf_op jit(solution)/shard_map/ppermute | solution.py:739
  34.7 18.6 %collective-permute-start.1 = (bf16[160,1536]{1,0:T(8,128)(2,1)}, bf16[160,1536]{1,0:T(8,128)(2,1)S(1)}, u32[]{:S(2)}, u32[]{:S(2)}) collective-permute-start(bf16[160,1536]{1,0:T(8,128)(2,1)} %first_norm.1.refs_0_), channel_id=1, source_target_pairs={{0,8},{1,9},{2,10},{3,11},{4,12},{5,13},{6,14},{7,15},{8,0},{9,1},... | collective-permute-start | bytes 1474568 | tf_op jit(solution)/shard_map/ppermute | solution.py:739
  43.7 16.2 %collective-permute-start.3 = (bf16[160,1536]{1,0:T(8,128)(2,1)S(1)}, bf16[160,1536]{1,0:T(8,128)(2,1)S(1)}, u32[]{:S(2)}, u32[]{:S(2)}) collective-permute-start(bf16[160,1536]{1,0:T(8,128)(2,1)S(1)} %collective-permute-done.2.refs_2_), channel_id=1, source_target_pairs={{0,8},{1,9},{2,10},{3,11},{4,12},{5,13},{6,14},{7,15},{8,0},{9,1},... | collective-permute-start | bytes 1474568 | tf_op jit(solution)/shard_map/ppermute | solution.py:739
  66.9 33.4 %collective-permute-start.11 = (bf16[160,1536]{1,0:T(8,128)(2,1)S(1)}, bf16[160,1536]{1,0:T(8,128)(2,1)S(1)}, u32[]{:S(2)}, u32[]{:S(2)}) collective-permute-start(bf16[160,1536]{1,0:T(8,128)(2,1)S(1)} %pad_maximum_fusion.2), channel_id=1, source_target_pairs={{0,1},{1,2},{2,3},{3,0},{4,9},{5,10},{6,11},{7,8},{8,5},{9,6},{10,... | collective-permute-start | bytes 1474568 | tf_op jit(solution)/shard_map/ppermute | solution.py:739
  69.4 30.9 %collective-permute-start.12 = (bf16[160,1536]{1,0:T(8,128)(2,1)S(1)}, bf16[160,1536]{1,0:T(8,128)(2,1)S(1)}, u32[]{:S(2)}, u32[]{:S(2)}) collective-permute-start(bf16[160,1536]{1,0:T(8,128)(2,1)S(1)} %pad_maximum_fusion.2), channel_id=1, source_target_pairs={{0,3},{1,0},{2,1},{3,2},{4,11},{5,8},{6,9},{7,10},{8,7},{9,4},{10,... | collective-permute-start | bytes 1474568 | tf_op jit(solution)/shard_map/ppermute | solution.py:739
  72.2 28.1 %collective-permute-start.13 = (bf16[160,1536]{1,0:T(8,128)(2,1)S(1)}, bf16[160,1536]{1,0:T(8,128)(2,1)S(1)}, u32[]{:S(2)}, u32[]{:S(2)}) collective-permute-start(bf16[160,1536]{1,0:T(8,128)(2,1)S(1)} %pad_maximum_fusion.2), channel_id=1, source_target_pairs={{0,2},{1,3},{2,0},{3,1},{4,10},{5,11},{6,8},{7,9},{8,6},{9,7},{10,... | collective-permute-start | bytes 1474568 | tf_op jit(solution)/shard_map/ppermute | solution.py:739
  102.0 57.4 %collective-permute-start.29 = (bf16[4608,384]{1,0:T(8,128)(2,1)}, bf16[4608,384]{1,0:T(8,128)(2,1)}, u32[]{:S(2)}, u32[]{:S(2)}) collective-permute-start(bf16[4608,384]{1,0:T(8,128)(2,1)} %get-tuple-element.102.refs_16_), channel_id=1, source_target_pairs={{4,8},{5,9},{6,10},{7,11},{8,4},{9,5},{10,6},{11,7},{20,24},{21,25... | collective-permute-start | bytes 10616840 | tf_op jit(solution)/shard_map/ppermute | solution.py:739
  108.9 22.0 %collective-permute-start.15 = (bf16[128,1664]{1,0:T(8,128)(2,1)S(1)}, bf16[128,1664]{1,0:T(8,128)(2,1)S(1)}, u32[]{:S(2)}, u32[]{:S(2)}) collective-permute-start(bf16[128,1664]{1,0:T(8,128)(2,1)S(1)} %get-tuple-element.220), channel_id=1, source_target_pairs={{0,1},{1,2},{2,3},{3,0},{4,5},{5,6},{6,7},{7,4},{8,9},{9,10},{10,1... | collective-permute-start | bytes 1277960 | tf_op jit(solution)/shard_map/ppermute | solution.py:739
  109.6 22.0 %collective-permute-start.16 = (bf16[128,1664]{1,0:T(8,128)(2,1)S(1)}, bf16[128,1664]{1,0:T(8,128)(2,1)S(1)}, u32[]{:S(2)}, u32[]{:S(2)}) collective-permute-start(bf16[128,1664]{1,0:T(8,128)(2,1)S(1)} %get-tuple-element.219), channel_id=1, source_target_pairs={{0,2},{1,3},{2,0},{3,1},{4,6},{5,7},{6,4},{7,5},{8,10},{9,11},{10,... | collective-permute-start | bytes 1277960 | tf_op jit(solution)/shard_map/ppermute | solution.py:739
  110.5 21.3 %collective-permute-start.17 = (bf16[128,1664]{1,0:T(8,128)(2,1)S(1)}, bf16[128,1664]{1,0:T(8,128)(2,1)S(1)}, u32[]{:S(2)}, u32[]{:S(2)}) collective-permute-start(bf16[128,1664]{1,0:T(8,128)(2,1)S(1)} %get-tuple-element.218), channel_id=1, source_target_pairs={{0,3},{1,0},{2,1},{3,2},{4,7},{5,4},{6,5},{7,6},{8,11},{9,8},{10,9... | collective-permute-start | bytes 1277960 | tf_op jit(solution)/shard_map/ppermute | solution.py:739
  112.0 23.9 %collective-permute-start.25 = (bf16[160,1536]{1,0:T(8,128)(2,1)S(1)}, bf16[160,1536]{1,0:T(8,128)(2,1)S(1)}, u32[]{:S(2)}, u32[]{:S(2)}) collective-permute-start(bf16[160,1536]{1,0:T(8,128)(2,1)S(1)} %broadcast_select_fusion.1.refs_8_.dres_ref), channel_id=1, source_target_pairs={{0,8},{1,9},{2,10},{3,11},{4,12},{5,13},{6,14},{7,15},{8,0},{9,1},... | collective-permute-start | bytes 1474568 | tf_op jit(solution)/shard_map/ppermute | solution.py:739
  138.7 18.1 %collective-permute-start.23 = (bf16[128,1536]{1,0:T(8,128)(2,1)}, bf16[128,1536]{1,0:T(8,128)(2,1)S(1)}, u32[]{:S(2)}, u32[]{:S(2)}) collective-permute-start(bf16[128,1536]{1,0:T(8,128)(2,1)} %get-tuple-element.101.refs_0_), channel_id=1, source_target_pairs={{0,2},{1,3},{2,0},{3,1},{4,6},{5,7},{6,4},{7,5},{8,10},{9,11},{10,... | collective-permute-start | bytes 1179656 | tf_op jit(solution)/shard_map/ppermute | solution.py:739
  139.4 19.3 %collective-permute-start.18 = (bf16[128,1536]{1,0:T(8,128)(2,1)}, bf16[128,1536]{1,0:T(8,128)(2,1)S(1)}, u32[]{:S(2)}, u32[]{:S(2)}) collective-permute-start(bf16[128,1536]{1,0:T(8,128)(2,1)} %get-tuple-element.101.refs_0_), channel_id=1, source_target_pairs={{0,8},{1,9},{2,10},{3,11},{4,12},{5,13},{6,14},{7,15},{8,0},{9,1},... | collective-permute-start | bytes 1179656 | tf_op jit(solution)/shard_map/ppermute | solution.py:739
  189.1 29.6 %collective-permute-start.34 = (bf16[512,1664]{1,0:T(8,128)(2,1)}, bf16[512,1664]{1,0:T(8,128)(2,1)S(1)}, u32[]{:S(2)}, u32[]{:S(2)}) collective-permute-start(bf16[512,1664]{1,0:T(8,128)(2,1)} %get-tuple-element.109), channel_id=1, source_target_pairs={{0,8},{1,9},{2,10},{3,11},{4,12},{5,13},{6,14},{7,15},{8,0},{9,1},... | collective-permute-start | bytes 5111816 | tf_op jit(solution)/shard_map/ppermute | solution.py:739
  214.8 39.3 %collective-permute-start.35 = (bf16[1536,768]{1,0:T(8,128)(2,1)}, bf16[1536,768]{1,0:T(8,128)(2,1)S(1)}, u32[]{:S(2)}, u32[]{:S(2)}) collective-permute-start(bf16[1536,768]{1,0:T(8,128)(2,1)} %weight_products.3), channel_id=1, source_target_pairs={{4,0},{5,1},{6,2},{7,3},{8,12},{9,13},{10,14},{11,15},{20,16},{21,... | collective-permute-start | bytes 7077896 | tf_op jit(solution)/shard_map/ppermute | solution.py:739
  220.0 34.7 %collective-permute-start.36 = (bf16[128,1664]{1,0:T(8,128)(2,1)}, bf16[128,1664]{1,0:T(8,128)(2,1)S(1)}, u32[]{:S(2)}, u32[]{:S(2)}) collective-permute-start(bf16[128,1664]{1,0:T(8,128)(2,1)} %get-tuple-element.217), channel_id=1, source_target_pairs={{0,1},{1,2},{2,3},{3,0},{4,5},{5,6},{6,7},{7,4},{8,9},{9,10},{10,1... | collective-permute-start | bytes 1277960 | tf_op jit(solution)/shard_map/ppermute | solution.py:739
  220.0 34.7 %collective-permute-start.37 = (bf16[128,1664]{1,0:T(8,128)(2,1)}, bf16[128,1664]{1,0:T(8,128)(2,1)S(1)}, u32[]{:S(2)}, u32[]{:S(2)}) collective-permute-start(bf16[128,1664]{1,0:T(8,128)(2,1)} %get-tuple-element.216), channel_id=1, source_target_pairs={{0,2},{1,3},{2,0},{3,1},{4,6},{5,7},{6,4},{7,5},{8,10},{9,11},{10,... | collective-permute-start | bytes 1277960 | tf_op jit(solution)/shard_map/ppermute | solution.py:739
  222.9 31.8 %collective-permute-start.38 = (bf16[128,1664]{1,0:T(8,128)(2,1)}, bf16[128,1664]{1,0:T(8,128)(2,1)}, u32[]{:S(2)}, u32[]{:S(2)}) collective-permute-start(bf16[128,1664]{1,0:T(8,128)(2,1)} %get-tuple-element.215), channel_id=1, source_target_pairs={{0,3},{1,0},{2,1},{3,2},{4,7},{5,4},{6,5},{7,6},{8,11},{9,8},{10,9... | collective-permute-start | bytes 1277960 | tf_op jit(solution)/shard_map/ppermute | solution.py:739
  259.7 22.9 %collective-permute-start.41 = (bf16[128,1792]{1,0:T(8,128)(2,1)S(1)}, bf16[128,1792]{1,0:T(8,128)(2,1)S(1)}, u32[]{:S(2)}, u32[]{:S(2)}) collective-permute-start(bf16[128,1792]{1,0:T(8,128)(2,1)S(1)} %pad_maximum_fusion.3), channel_id=1, source_target_pairs={{0,1},{1,2},{2,3},{3,0},{4,5},{5,6},{6,7},{7,4},{8,9},{9,10},{10,1... | collective-permute-start | bytes 1376264 | tf_op jit(solution)/shard_map/ppermute | solution.py:739
  260.6 22.0 %collective-permute-start.42 = (bf16[128,1792]{1,0:T(8,128)(2,1)S(1)}, bf16[128,1792]{1,0:T(8,128)(2,1)S(1)}, u32[]{:S(2)}, u32[]{:S(2)}) collective-permute-start(bf16[128,1792]{1,0:T(8,128)(2,1)S(1)} %pad_maximum_fusion.4), channel_id=1, source_target_pairs={{0,2},{1,3},{2,0},{3,1},{4,6},{5,7},{6,4},{7,5},{8,10},{9,11},{10,... | collective-permute-start | bytes 1376264 | tf_op jit(solution)/shard_map/ppermute | solution.py:739
  261.7 21.3 %collective-permute-start.43 = (bf16[128,1792]{1,0:T(8,128)(2,1)S(1)}, bf16[128,1792]{1,0:T(8,128)(2,1)S(1)}, u32[]{:S(2)}, u32[]{:S(2)}) collective-permute-start(bf16[128,1792]{1,0:T(8,128)(2,1)S(1)} %pad_maximum_fusion.5), channel_id=1, source_target_pairs={{0,3},{1,0},{2,1},{3,2},{4,7},{5,4},{6,5},{7,6},{8,11},{9,8},{10,9... | collective-permute-start | bytes 1376264 | tf_op jit(solution)/shard_map/ppermute | solution.py:739
  293.9 18.3 %collective-permute-start.49 = (bf16[128,1664]{1,0:T(8,128)(2,1)}, bf16[128,1664]{1,0:T(8,128)(2,1)}, u32[]{:S(2)}, u32[]{:S(2)}) collective-permute-start(bf16[128,1664]{1,0:T(8,128)(2,1)} %get-tuple-element.129.refs_0_), channel_id=1, source_target_pairs={{0,2},{1,3},{2,0},{3,1},{4,6},{5,7},{6,4},{7,5},{8,10},{9,11},{10,... | collective-permute-start | bytes 1277960 | tf_op jit(solution)/shard_map/ppermute | solution.py:739
  296.5 18.5 %collective-permute-start.52 = (bf16[192,768]{1,0:T(8,128)(2,1)S(1)}, bf16[192,768]{1,0:T(8,128)(2,1)}, u32[]{:S(2)}, u32[]{:S(2)}) collective-permute-start(bf16[192,768]{1,0:T(8,128)(2,1)S(1)} %get-tuple-element.247), channel_id=1, source_target_pairs={{0,32},{1,33},{2,34},{3,35},{4,36},{5,37},{6,38},{7,39},{8,40},{9,... | collective-permute-start | bytes 884744 | tf_op jit(solution)/shard_map/ppermute | solution.py:739
  297.8 17.2 %collective-permute-start.53 = (bf16[192,768]{1,0:T(8,128)(2,1)S(1)}, bf16[192,768]{1,0:T(8,128)(2,1)}, u32[]{:S(2)}, u32[]{:S(2)}) collective-permute-start(bf16[192,768]{1,0:T(8,128)(2,1)S(1)} %get-tuple-element.249), channel_id=1, source_target_pairs={{0,64},{1,65},{2,66},{3,67},{4,68},{5,69},{6,70},{7,71},{8,72},{9,... | collective-permute-start | bytes 884744 | tf_op jit(solution)/shard_map/ppermute | solution.py:739
  328.0 52.9 %collective-permute-start.64 = (bf16[192,768]{1,0:T(8,128)(2,1)S(1)}, bf16[192,768]{1,0:T(8,128)(2,1)S(1)}, u32[]{:S(2)}, u32[]{:S(2)}) collective-permute-start(bf16[192,768]{1,0:T(8,128)(2,1)S(1)} %add_convert_fusion.16), channel_id=1, source_target_pairs={{0,16},{1,17},{2,18},{3,19},{4,20},{5,21},{6,22},{7,23},{8,24},{9,... | collective-permute-start | bytes 884744 | tf_op jit(solution)/shard_map/ppermute | solution.py:739
  342.1 54.0 %collective-permute-start.61 = (bf16[384,1280]{1,0:T(8,128)(2,1)}, bf16[384,1280]{1,0:T(8,128)(2,1)S(1)}, u32[]{:S(2)}, u32[]{:S(2)}) collective-permute-start(bf16[384,1280]{1,0:T(8,128)(2,1)} %get-tuple-element.212), channel_id=1, source_target_pairs={{0,32},{1,33},{2,34},{3,35},{4,36},{5,37},{6,38},{7,39},{8,40},{9,... | collective-permute-start | bytes 2949128 | tf_op jit(solution)/shard_map/ppermute | solution.py:739
  343.3 53.5 %collective-permute-start.62 = (bf16[384,1280]{1,0:T(8,128)(2,1)}, bf16[384,1280]{1,0:T(8,128)(2,1)}, u32[]{:S(2)}, u32[]{:S(2)}) collective-permute-start(bf16[384,1280]{1,0:T(8,128)(2,1)} %get-tuple-element.214), channel_id=1, source_target_pairs={{0,64},{1,65},{2,66},{3,67},{4,68},{5,69},{6,70},{7,71},{8,72},{9,... | collective-permute-start | bytes 2949128 | tf_op jit(solution)/shard_map/ppermute | solution.py:739
  345.7 51.9 %collective-permute-start.63 = (bf16[384,1280]{1,0:T(8,128)(2,1)}, bf16[384,1280]{1,0:T(8,128)(2,1)}, u32[]{:S(2)}, u32[]{:S(2)}) collective-permute-start(bf16[384,1280]{1,0:T(8,128)(2,1)} %get-tuple-element.213), channel_id=1, source_target_pairs={{0,96},{1,97},{2,98},{3,99},{4,100},{5,101},{6,102},{7,103},{8,104... | collective-permute-start | bytes 2949128 | tf_op jit(solution)/shard_map/ppermute | solution.py:739
  378.3 21.9 %collective-permute-start.60 = (bf16[544,256]{1,0:T(8,128)(2,1)}, bf16[544,256]{1,0:T(8,128)(2,1)S(1)}, u32[]{:S(2)}, u32[]{:S(2)}) collective-permute-start(bf16[544,256]{1,0:T(8,128)(2,1)} %pad_maximum_fusion.7), channel_id=1, source_target_pairs={{0,8},{1,9},{2,10},{3,11},{4,12},{5,13},{6,14},{7,15},{8,0},{9,1},... | collective-permute-start | bytes 835592 | tf_op jit(solution)/shard_map/ppermute | solution.py:739
  395.6 55.2 %collective-permute-start.55 = (bf16[512,1536]{1,0:T(8,128)(2,1)}, bf16[512,1536]{1,0:T(8,128)(2,1)}, u32[]{:S(2)}, u32[]{:S(2)}) collective-permute-start(bf16[512,1536]{1,0:T(8,128)(2,1)} %get-tuple-element.148), channel_id=1, source_target_pairs={{0,8},{1,9},{2,10},{3,11},{4,12},{5,13},{6,14},{7,15},{8,0},{9,1},... | collective-permute-start | bytes 4718600 | tf_op jit(solution)/shard_map/ppermute | solution.py:739
  396.7 36.3 %collective-permute-start.87 = (bf16[192,768]{1,0:T(8,128)(2,1)S(1)}, bf16[192,768]{1,0:T(8,128)(2,1)S(1)}, u32[]{:S(2)}, u32[]{:S(2)}) collective-permute-start(bf16[192,768]{1,0:T(8,128)(2,1)S(1)} %add_convert_fusion.15), channel_id=1, source_target_pairs={{0,96},{1,97},{2,98},{3,99},{4,100},{5,101},{6,102},{7,103},{8,104... | collective-permute-start | bytes 884744 | tf_op jit(solution)/shard_map/ppermute | solution.py:739
  408.1 22.3 %collective-permute-start.78 = (bf16[384,1280]{1,0:T(8,128)(2,1)S(1)}, bf16[384,1280]{1,0:T(8,128)(2,1)}, u32[]{:S(2)}, u32[]{:S(2)}) collective-permute-start(bf16[384,1280]{1,0:T(8,128)(2,1)S(1)} %add_convert_fusion.2), channel_id=1, source_target_pairs={{4,0},{5,1},{6,2},{7,3},{8,12},{9,13},{10,14},{11,15},{20,16},{21,... | collective-permute-start | bytes 2949128 | tf_op jit(solution)/shard_map/ppermute | solution.py:739
  428.5 16.0 %collective-permute-start.68 = (bf16[384,512]{1,0:T(8,128)(2,1)S(1)}, bf16[384,512]{1,0:T(8,128)(2,1)S(1)}, u32[]{:S(2)}, u32[]{:S(2)}) collective-permute-start(bf16[384,512]{1,0:T(8,128)(2,1)S(1)} %get-tuple-element.242), channel_id=1, source_target_pairs={{0,32},{1,33},{2,34},{3,35},{4,36},{5,37},{6,38},{7,39},{8,40},{9,... | collective-permute-start | bytes 1179656 | tf_op jit(solution)/shard_map/ppermute | solution.py:739
  428.8 15.7 %collective-permute-start.69 = (bf16[384,512]{1,0:T(8,128)(2,1)S(1)}, bf16[384,512]{1,0:T(8,128)(2,1)S(1)}, u32[]{:S(2)}, u32[]{:S(2)}) collective-permute-start(bf16[384,512]{1,0:T(8,128)(2,1)S(1)} %get-tuple-element.244), channel_id=1, source_target_pairs={{0,64},{1,65},{2,66},{3,67},{4,68},{5,69},{6,70},{7,71},{8,72},{9,... | collective-permute-start | bytes 1179656 | tf_op jit(solution)/shard_map/ppermute | solution.py:739
  433.0 17.7 %collective-permute-start.79 = (bf16[192,1280]{1,0:T(8,128)(2,1)S(1)}, bf16[192,1280]{1,0:T(8,128)(2,1)S(1)}, u32[]{:S(2)}, u32[]{:S(2)}) collective-permute-start(bf16[192,1280]{1,0:T(8,128)(2,1)S(1)} %slice.294), channel_id=1, source_target_pairs={{0,8},{1,9},{2,10},{3,11},{12,4},{13,5},{14,6},{15,7},{16,24},{17,... | collective-permute-start | bytes 1474568 | tf_op jit(solution)/shard_map/ppermute | solution.py:739
  444.5 23.8 %collective-permute-start.88 = (bf16[4,192,768]{2,1,0:T(8,128)(2,1)S(1)}, bf16[4,192,768]{2,1,0:T(8,128)(2,1)S(1)}, u32[]{:S(2)}, u32[]{:S(2)}) collective-permute-start(bf16[4,192,768]{2,1,0:T(8,128)(2,1)S(1)} %bitcast_dynamic-update-slice_fusion.8.here_ref), channel_id=1, source_target_pairs={{0,8},{1,9},{2,10},{3,11},{4,12},{5,13},{6,14},{7,15},{8,0},{9,1},... | collective-permute-start | bytes 3538952 | tf_op jit(solution)/shard_map/ppermute | solution.py:739
  453.6 26.7 %collective-permute-start.56 = (bf16[128,1536]{1,0:T(8,128)(2,1)}, bf16[128,1536]{1,0:T(8,128)(2,1)S(1)}, u32[]{:S(2)}, u32[]{:S(2)}) collective-permute-start(bf16[128,1536]{1,0:T(8,128)(2,1)} %get-tuple-element.224), channel_id=1, source_target_pairs={{0,1},{1,2},{2,3},{3,0},{4,5},{5,6},{6,7},{7,4},{8,9},{9,10},{10,1... | collective-permute-start | bytes 1179656 | tf_op jit(solution)/shard_map/ppermute | solution.py:739
  454.3 26.1 %collective-permute-start.57 = (bf16[128,1536]{1,0:T(8,128)(2,1)S(1)}, bf16[128,1536]{1,0:T(8,128)(2,1)}, u32[]{:S(2)}, u32[]{:S(2)}) collective-permute-start(bf16[128,1536]{1,0:T(8,128)(2,1)S(1)} %get-tuple-element.223), channel_id=1, source_target_pairs={{0,2},{1,3},{2,0},{3,1},{4,6},{5,7},{6,4},{7,5},{8,10},{9,11},{10,... | collective-permute-start | bytes 1179656 | tf_op jit(solution)/shard_map/ppermute | solution.py:739
  458.2 22.2 %collective-permute-start.58 = (bf16[128,1536]{1,0:T(8,128)(2,1)S(1)}, bf16[128,1536]{1,0:T(8,128)(2,1)}, u32[]{:S(2)}, u32[]{:S(2)}) collective-permute-start(bf16[128,1536]{1,0:T(8,128)(2,1)S(1)} %get-tuple-element.222), channel_id=1, source_target_pairs={{0,3},{1,0},{2,1},{3,2},{4,7},{5,4},{6,5},{7,6},{8,11},{9,8},{10,9... | collective-permute-start | bytes 1179656 | tf_op jit(solution)/shard_map/ppermute | solution.py:739
  468.0 25.0 %collective-permute-start.81 = (bf16[192,1280]{1,0:T(8,128)(2,1)S(1)}, bf16[192,1280]{1,0:T(8,128)(2,1)S(1)}, u32[]{:S(2)}, u32[]{:S(2)}) collective-permute-start(bf16[192,1280]{1,0:T(8,128)(2,1)S(1)} %get-tuple-element.207), channel_id=1, source_target_pairs={{0,32},{1,33},{2,34},{3,35},{4,36},{5,37},{6,38},{7,39},{8,40},{9,... | collective-permute-start | bytes 1474568 | tf_op jit(solution)/shard_map/ppermute | solution.py:739
  468.2 24.3 %collective-permute-start.73 = (bf16[192,512]{1,0:T(8,128)(2,1)S(1)}, bf16[192,512]{1,0:T(8,128)(2,1)S(1)}, u32[]{:S(2)}, u32[]{:S(2)}) collective-permute-start(bf16[192,512]{1,0:T(8,128)(2,1)S(1)} %slice_select_fusion.2), channel_id=1, source_target_pairs={{0,16},{1,17},{2,18},{3,19},{4,20},{5,21},{6,22},{7,23},{8,24},{9,... | collective-permute-start | bytes 589832 | tf_op jit(solution)/shard_map/ppermute | solution.py:739
  484.6 35.3 %collective-permute-start.59 = (bf16[128,3072]{1,0:T(8,128)(2,1)}, bf16[128,3072]{1,0:T(8,128)(2,1)S(1)}, u32[]{:S(2)}, u32[]{:S(2)}) collective-permute-start(bf16[128,3072]{1,0:T(8,128)(2,1)} %outputs.1), channel_id=1, source_target_pairs={{4,8},{5,9},{6,10},{7,11},{8,4},{9,5},{10,6},{11,7},{20,24},{21,25... | collective-permute-start | bytes 2359304 | tf_op jit(solution)/shard_map/ppermute | solution.py:739
  492.7 25.1 %collective-permute-start.74 = (bf16[192,512]{1,0:T(8,128)(2,1)S(1)}, bf16[192,512]{1,0:T(8,128)(2,1)S(1)}, u32[]{:S(2)}, u32[]{:S(2)}) collective-permute-start(bf16[192,512]{1,0:T(8,128)(2,1)S(1)} %get-tuple-element.209), channel_id=1, source_target_pairs={{0,32},{1,33},{2,34},{3,35},{4,36},{5,37},{6,38},{7,39},{8,40},{9,... | collective-permute-start | bytes 589832 | tf_op jit(solution)/shard_map/ppermute | solution.py:739
  492.8 25.1 %collective-permute-start.75 = (bf16[192,512]{1,0:T(8,128)(2,1)S(1)}, bf16[192,512]{1,0:T(8,128)(2,1)S(1)}, u32[]{:S(2)}, u32[]{:S(2)}) collective-permute-start(bf16[192,512]{1,0:T(8,128)(2,1)S(1)} %get-tuple-element.209), channel_id=1, source_target_pairs={{0,64},{1,65},{2,66},{3,67},{4,68},{5,69},{6,70},{7,71},{8,72},{9,... | collective-permute-start | bytes 589832 | tf_op jit(solution)/shard_map/ppermute | solution.py:739
  493.0 24.7 %collective-permute-start.83 = (bf16[192,1280]{1,0:T(8,128)(2,1)S(1)}, bf16[192,1280]{1,0:T(8,128)(2,1)S(1)}, u32[]{:S(2)}, u32[]{:S(2)}) collective-permute-start(bf16[192,1280]{1,0:T(8,128)(2,1)S(1)} %get-tuple-element.207), channel_id=1, source_target_pairs={{0,96},{1,97},{2,98},{3,99},{4,100},{5,101},{6,102},{7,103},{8,104... | collective-permute-start | bytes 1474568 | tf_op jit(solution)/shard_map/ppermute | solution.py:739
  (120 other events, 1175.5 us)
where the time goes:
time: 562 us; the launch traced here: 552 us
  Pallas kernels  189 us (34%)
  starting transfers between devices  146 us (26%)
  waiting for transfers between devices  133 us (24%)
  local copies, waits for them, and re-layouts  43.9 us (8%)
  other arithmetic  36.3 us (6%)
    ppermute x89, starting transfers between devices, send(): return lax.ppermute(v, ('dp', 'tensor'), pairs)  146 us
    ppermute x89, waiting for transfers between devices, send(): return lax.ppermute(v, ('dp', 'tensor'), pairs)  133 us
    pallas_call x6, Pallas kernels, span_call(): pl.pallas_call(kernel, grid_spec=pltpu.PrefetchScalarGridSpec(num_scalar_...  128 us
    pallas_call x3, Pallas kernels, write_sums(): pl.pallas_call(functools.partial(write_kernel, columns, by_half, len(kept...  23.3 us
    pallas_call x3, Pallas kernels, weight_products(): pl.pallas_call(functools.partial(weight_kernel, pairs_of(columns)), grid=...  23 us
    unnamed x174, local copies, waits for them, and re-layouts  20.1 us
    pallas_call x5, Pallas kernels, row_call(): pl.pallas_call(kernel, grid=(1,), in_specs=[pl.BlockSpec((rows, v.shape[1...  15.5 us
  transfers between devices with their start and end apart: 89, of which 26 were waited for; matrix products, arithmetic and copies ran while one was open for 10% of the time, Pallas kernels for 26%

commit v1 on v0

--- a/solution.py
+++ b/solution.py
@@ -169,11 +169,11 @@
     def _():
         @pl.when(place_ref[2] == 1)
         def _():
-            pltpu.make_async_copy(w_here, w_ref, w_sem).start()
+            pltpu.make_async_copy(w_here.at[0 : w_ref.shape[0], :], w_ref, w_sem).start()
 
         @pl.when(place_ref[2] == 0)
         def _():
-            pltpu.make_async_copy(w_there, w_ref, w_sem).start()
+            pltpu.make_async_copy(w_there.at[0 : w_ref.shape[0], :], w_ref, w_sem).start()
 
         if last_layer:
             place_pieces(plans[0][0], place_ref, piece_refs[0], [xn_all])
@@ -183,7 +183,7 @@
         xbuf[0:8, :] = jnp.zeros((8, channels), f32)
         bbuf[0:8, :] = jnp.zeros((8, 2 * state), f32)
         hst[...] = jnp.zeros_like(hst)
-        pltpu.make_async_copy(w_here, w_ref, w_sem).wait()
+        pltpu.make_async_copy(w_here.at[0 : w_ref.shape[0], :], w_ref, w_sem).wait()
 
     here = pl.ds(pl.multiple_of(span * length, length), length)
     xn = xn_all[here, :]
@@ -538,7 +538,7 @@
     operands += [*weights, *small]
     in_specs += [whole(v.shape) for v in operands[len(in_specs) :]]
     shapes = [
-        jax.ShapeDtypeStruct(weights[0].shape, bf16),
+        jax.ShapeDtypeStruct((3 * width, channels), bf16),
         jax.ShapeDtypeStruct((tokens, width), bf16),
         jax.ShapeDtypeStruct((2 * state, width), bf16),
         jax.ShapeDtypeStruct((tokens, channels), f32),
@@ -550,7 +550,7 @@
         jax.ShapeDtypeStruct((tokens // 2, width + LANES), bf16),
         jax.ShapeDtypeStruct((tokens // 2, width + LANES), bf16),
     ]
-    out_specs = [whole(weights[0].shape), span_rows(width), whole((2 * state, width))]
+    out_specs = [whole((3 * width, channels)), span_rows(width), whole((2 * state, width))]
     out_specs += [span_rows(s.shape[1]) for s in shapes[3:8]]
     out_specs.append(pl.BlockSpec((1, state, channels), lambda i, p: (i, 0, 0)))
     out_specs += half_rows(width + LANES, spans, False)
@@ -765,11 +765,11 @@
     return dp // (NYL * NC), dp // NC % NYL, dp % NC, tensor // NZ, tensor % NZ
 
 
-def gather(v, parts, away=False):
+def gather(v, parts, traded_own=None):
     arrays, sources = [], []
     for k in (0, 1, 3, 2):
-        if away:
-            piece = trade(v, k) if k else trade_places(v)
+        if traded_own is not None:
+            piece = trade(v, k) if k else traded_own
         else:
             piece = send_z(v, k) if k else v
         arrays += [piece, send_core(piece)]
@@ -813,7 +813,7 @@
 def scatter_with_sum(mine, other, shared, meanwhile):
     half = mine.shape[0]
     rows = half // NZ
-    got = after(send_core(jnp.concatenate([other, shared], axis=0)), *meanwhile)
+    got = send_core(jnp.concatenate([other, shared], axis=0))
     blocks = fold(mine, got[:half])
     total_shared = shared.astype(f32) + got[half:].astype(f32)
     packed = total_shared.astype(bf16)
@@ -822,7 +822,7 @@
         got = send_z(jnp.concatenate([blocks[k].astype(bf16), packed], axis=0), k)
         total = total + got[:rows].astype(f32)
         total_shared = total_shared + got[rows:].astype(f32)
-    return total, total_shared
+    return after(total, *meanwhile), total_shared
 
 
 def sum_members(v):
@@ -877,60 +877,67 @@
     return out, send_core(out)
 
 
-def write_kernel(columns, by_half, n_kept, place_ref, here_ref, there_ref, *refs):
-    low = pl.program_id(1) if not by_half else pl.program_id(0)
-    here = (low == 0) == (place_ref[2] == 1)
-    for column, out_ref in zip(columns, refs[n_kept:]):
-        at = slice(column, column + out_ref.shape[-1])
-
-        @pl.when(here)
-        def _(out_ref=out_ref, at=at):
-            out_ref[...] = here_ref[0, :, at].astype(f32).reshape(out_ref.shape)
-
-        @pl.when(jnp.logical_not(here))
-        def _(out_ref=out_ref, at=at):
-            out_ref[...] = there_ref[0, :, at].astype(f32).reshape(out_ref.shape)
+def write_kernel(plan, by_half, n_kept, place_ref, here_ref, there_ref, *refs):
+    rows = here_ref.shape[1]
+
+    def write(ref):
+        for (column, kind, wide), out_ref in zip(plan, refs[n_kept:]):
+            for x in range(NX):
+                value = ref[x, :, column : column + wide].astype(f32)
+                if kind != "blocks":
+                    out_ref[0, 0 if by_half else x, x if by_half else 0] = value
+                elif by_half:
+                    at = x // 2 * wide
+                    out_ref[0, x % 2 * rows : (x % 2 + 1) * rows, at : at + wide] = value
+                else:
+                    out_ref[0, :, x * wide : (x + 1) * wide] = value
+
+    here = (pl.program_id(0) == 0) == (place_ref[2] == 1)
+
+    @pl.when(here)
+    def _():
+        write(here_ref)
+
+    @pl.when(jnp.logical_not(here))
+    def _():
+        write(there_ref)
 
 
 def write_sums(place, halves, by_half, outputs):
-    rows = halves[0].shape[1]
+    rows, columns = halves[0].shape[1:]
     total = 2 * NX * rows
-    grid = (2, NX) if by_half else (NX, 2)
-
-    def block(i, j):
-        return i * grid[1] + j
-
-    columns, shapes, specs, kept, alias = [], [], [], [], {}
+    wide = total // 4
+    plan, shapes, specs, finals, kept, alias = [], [], [], [], [], {}
     for column, kind, layer, array in outputs:
-        columns.append(column)
-        if kind == "flat":
-            shapes.append(jax.ShapeDtypeStruct((total, LANES), f32))
-            specs.append(pl.BlockSpec((rows, LANES), lambda i, j, p: (block(i, j), 0)))
+        lanes = LANES if kind == "flat" else wide
+        layers = 1 if kind == "flat" else 2
+        plan.append((column, kind, lanes))
+        if kind == "blocks":
+            shape = (layers, wide, total)
+            if by_half:
+                spec = pl.BlockSpec((1, wide, total // 2), lambda h, p, layer=layer: (layer, 0, h))
+            else:
+                spec = pl.BlockSpec((1, rows, total), lambda h, p, layer=layer: (layer, h, 0))
+            finals.append(shape)
+        elif by_half:
+            shape = (layers, 2, NX, rows, lanes)
+            spec = pl.BlockSpec((1, 1, NX, rows, lanes), lambda h, p, layer=layer: (layer, h, 0, 0, 0))
+            finals.append((layers, total, lanes))
         else:
-            wide = total // 4
-            if kind == "rows":
-                shapes.append(jax.ShapeDtypeStruct((2, total, wide), f32))
-                specs.append(
-                    pl.BlockSpec((1, rows, wide), lambda i, j, p, layer=layer: (layer, block(i, j), 0))
-                )
-            else:
-                per = wide // rows
-                shapes.append(jax.ShapeDtypeStruct((2, wide, total), f32))
-                specs.append(
-                    pl.BlockSpec(
-                        (1, rows, wide),
-                        lambda i, j, p, layer=layer: (layer, block(i, j) % per, block(i, j) // per),
-                    )
-                )
+            shape = (layers, NX, 2, rows, lanes)
+            spec = pl.BlockSpec((1, NX, 1, rows, lanes), lambda h, p, layer=layer: (layer, 0, h, 0, 0))
+            finals.append((layers, total, lanes))
+        shapes.append(jax.ShapeDtypeStruct(shape, f32))
+        specs.append(spec)
         if array is not None:
             alias[3 + len(kept)] = len(shapes) - 1
-            kept.append(array)
-    piece = pl.BlockSpec((1, rows, halves[0].shape[2]), lambda i, j, p: (j if by_half else i, 0, 0))
-    return pl.pallas_call(
-        functools.partial(write_kernel, columns, by_half, len(kept)),
+            kept.append(array.reshape(shape))
+    piece = pl.BlockSpec((NX, rows, columns), lambda h, p: (0, 0, 0))
+    written = pl.pallas_call(
+        functools.partial(write_kernel, plan, by_half, len(kept)),
         grid_spec=pltpu.PrefetchScalarGridSpec(
             num_scalar_prefetch=1,
-            grid=grid,
+            grid=(2,),
             in_specs=[piece, piece] + [pl.BlockSpec(memory_space=pl.ANY)] * len(kept),
             out_specs=specs,
         ),
@@ -939,6 +946,7 @@
         compiler_params=pltpu.CompilerParams(vmem_limit_bytes=VMEM_BYTES),
         name="write_sums",
     )(place, *halves, *kept)
+    return [v.reshape(final) for v, final in zip(written, finals)]
 
 
 def row_call(kernel, name, operands, shapes):
@@ -1066,8 +1074,6 @@
 
     bc_t = jnp.swapaxes(w_bc, 1, 2)
     dt_t = jnp.pad(jnp.swapaxes(w_dt, 1, 2), ((0, 0), (0, 8 - heads), (0, 0)))
-    packed = jnp.concatenate([hidden_in[0], bc_t[0], dt_t.reshape(layers * 8, width)], axis=0)
-    packed = trade_places(packed)
     per_channel = jnp.concatenate(
         [conv_x, conv_x_bias[:, None], norm_gate[:, None], jnp.repeat(skip, head_dim, axis=1)[:, None]],
         axis=1,
@@ -1076,14 +1082,26 @@
     per_head = jnp.stack([dt_bias, -jnp.exp(a_log)], axis=1)
     per_head = jnp.pad(per_head, ((0, 0), (0, 6), (0, LANES - heads)))
     little = jnp.concatenate([per_channel, per_head], axis=2).reshape(layers * 8, channels + LANES)
-    little = trade_places(after(little, packed)).reshape(layers, 8, channels + LANES)
+    high = little.astype(bf16)
+    low = (little - high.astype(f32)).astype(bf16)
+    lines = pad_to(jnp.concatenate([high, low], axis=1), layers * 8, width)
+    packed = jnp.concatenate([hidden_in[0], bc_t[0], dt_t.reshape(layers * 8, width), lines], axis=0)
+    packed = trade_places(packed)
+    lines = packed[packed.shape[0] - layers * 8 :].astype(f32)
+    little = lines[:, : channels + LANES] + lines[:, channels + LANES : 2 * (channels + LANES)]
+    little = little.reshape(layers, 8, channels + LANES)
+
+    def blocks_below(v):
+        return [v[:, i * channels : (i + 1) * channels] for i in range(width // channels)]
 
     def pack_weights(layer):
-        quarters = [w_out[layer, :, i * channels : (i + 1) * channels] for i in range(width // channels)]
-        return jnp.concatenate([w_z[layer], w_x[layer], *quarters], axis=0)
-
-    w0 = pack_weights(0)
+        return jnp.concatenate([w_z[layer], w_x[layer], *blocks_below(w_out[layer])], axis=0)
+
+    grads = jnp.concatenate([grad_out[0], bc_t[1]], axis=0)
+    w0 = jnp.concatenate([pack_weights(0), *blocks_below(grads)], axis=0)
     w0 = w0, traded(after(w0, packed))
+    there = w0[1][3 * width :].reshape(-1, *grads.shape[:1], channels)
+    grads_here = jnp.where(stays, grads, jnp.concatenate(list(there), axis=1))
 
     [sent] = row_call(
         first_kernel,
@@ -1102,12 +1120,11 @@
 
     out0 = run_forward(place, [gathered0], (*w0, wdt[0]), smalls[0], state, head_dim)
     w0, xn0, wbc0, z0, xp0, bc0, dt0, y0, hin0, mine, other = out0
-    grads = jnp.concatenate([grad_out[0], bc_t[1]], axis=0)
-    gathered_grad = gather(after(grads, *gathered0[0]), (rows, bc_rows), away=True)
+    gathered_grad = gather(after(grads, *gathered0[0]), (rows, bc_rows), grads_here)
     grad_held = gathered_grad[0][0]
-    terms = scatter((mine, after(other, *gathered_grad[0][::2])))
+    terms = scatter((mine, after(other, *gathered_grad[0][2::2])))
     w1 = pack_weights(1)
-    w1 = w1, traded(after(w1, mine))
+    w1 = w1, traded(after(w1, terms[0]))
     res1, mixed0, rms0, normed1 = row_call(
         functools.partial(middle_kernel, inner_all),
         "middle_norm",
@@ -1166,9 +1183,6 @@
         place, dy0, dz0, xn0, xp0, bc0, dt0, hin0, (w0, wbc0, wdt[0]), smalls[0], pick, head_dim
     )
     dxt0, *bc_halves, mine, other, acc0, acch0, shared0 = back0
-    halves = collect(after(early1, dxt0))
-    g_wz, g_wo = write_sums(place, halves, True, [(0, "rows", 1, None), (channels, "blocks", 1, None)])
-
     terms = scatter((mine, other))
     [outputs] = row_call(
         end_kernel,
@@ -1190,7 +1204,10 @@
     tiny = jnp.pad(tiny, (0, width * tiny_lanes - tiny_size)).reshape(width, tiny_lanes)
     late = weight_products([(xn0, with_bc(dxt0, bc_sum))])
     late = late + jnp.pad(tiny, ((0, 0), (tiny_at, 0))).astype(bf16)
-    late = sum_beside(halve(sum_far(sum_x(late))))
+    late = sum_x(late)
+    halves = collect(after(early1, late))
+    g_wz, g_wo = write_sums(place, halves, True, [(0, "rows", 1, None), (channels, "blocks", 1, None)])
+    late = sum_beside(halve(sum_far(late)))
     early = sum_beside(halve(sum_far(after(early, dxt0))))
     g_wz, g_wo, g_wx, narrow1 = write_sums(
         place,
@@ -1200,13 +1217,14 @@
             (0, "rows", 0, g_wz),
             (channels, "blocks", 0, g_wo),
             (2 * channels, "rows", 1, None),
-            (3 * channels, "flat", 1, None),
+            (3 * channels, "flat", 0, None),
         ],
     )
     g_wx, narrow0 = write_sums(
         place, collect(late), False, [(0, "rows", 0, g_wx), (channels, "flat", 0, None)]
     )
 
+    narrow0, narrow1 = narrow0[0], narrow1[0]
     tiny = narrow0[:, tiny_at - channels :].reshape(-1)[:tiny_size]
     sizes = [8 * channels, 8 * channels, 2 * LANES, 2 * LANES]
     cut = [sum(sizes[:i]) for i in range(len(sizes) + 1)]

time: 562 us -> 595 us (1.059)
  the two profiles are of different devices: /device:TPU:1 before, /device:TPU:31 now
where the time goes in v1:
time: 595 us; the launch traced here: 584 us
  Pallas kernels  181 us (30%)
  starting transfers between devices  161 us (27%)
  waiting for transfers between devices  153 us (26%)
  local copies, waits for them, and re-layouts  47.9 us (8%)
  other arithmetic  38.5 us (6%)
    ppermute x87, starting transfers between devices, send(): return lax.ppermute(v, ('dp', 'tensor'), pairs)  161 us
    ppermute x87, waiting for transfers between devices, send(): return lax.ppermute(v, ('dp', 'tensor'), pairs)  153 us
    pallas_call x6, Pallas kernels, span_call(): pl.pallas_call(kernel, grid_spec=pltpu.PrefetchScalarGridSpec(num_scalar_...  127 us
    pallas_call x3, Pallas kernels, weight_products(): pl.pallas_call(functools.partial(weight_kernel, pairs_of(columns)), grid=...  23 us
    unnamed x165, local copies, waits for them, and re-layouts  22.6 us
    pallas_call x5, Pallas kernels, row_call(): pl.pallas_call(kernel, grid=(1,), in_specs=[pl.BlockSpec((rows, v.shape[1...  15.5 us
    pallas_call x3, Pallas kernels, write_sums(): pl.pallas_call(functools.partial(write_kernel, plan, by_half, len(kept)),...  14.8 us
  transfers between devices with their start and end apart: 87, of which 31 were waited for; matrix products, arithmetic and copies ran while one was open for 8% of the time, Pallas kernels for 16%

profile of v1, /device:TPU:31, one launch (start us, length us, event | category | flops | bytes accessed | tf_op | source)
XLA Modules:
  0.0 584.0 jit_solution(12414670578460827991)
XLA Ops:
  24.3 2.6 collective-permute-start.8
  36.0 5.6 collective-permute-start.1
  45.1 6.0 %collective-permute-start.3 = (bf16[160,1536]{1,0:T(8,128)(2,1)S(1)}, bf16[160,1536]{1,0:T(8,128)(2,1)S(1)}, u32[]{:S(2)}, u32[]{:S(2)}) collective-permute-start(bf16[160,1536]{1,0:T(8,128)(2,1)S(1)} %collective-permute-done.2.refs_2_), channel_id=1, source_target_pairs={{0,8},{1,9},{2,10},{3,11},{4,12},{5,13},{6,14},{7,15},{8,0},{9,1},... | collective-permute-start | bytes 1474568 | tf_op jit(solution)/shard_map/ppermute | solution.py:739
  51.2 5.8 %collective-permute-start.5 = (bf16[160,1536]{1,0:T(8,128)(2,1)S(1)}, bf16[160,1536]{1,0:T(8,128)(2,1)S(1)}, u32[]{:S(2)}, u32[]{:S(2)}) collective-permute-start(bf16[160,1536]{1,0:T(8,128)(2,1)S(1)} %collective-permute-done.4.refs_4_), channel_id=1, source_target_pairs={{0,8},{1,9},{2,10},{3,11},{4,12},{5,13},{6,14},{7,15},{8,0},{9,1},... | collective-permute-start | bytes 1474568 | tf_op jit(solution)/shard_map/ppermute | solution.py:739
  63.1 24.7 %layer_forward.2 = (bf16[4608,384]{1,0:T(8,128)(2,1)}, bf16[1024,1536]{1,0:T(8,128)(2,1)}, bf16[256,1536]{1,0:T(8,128)(2,1)}, f32[1024,384]{1,0:T(8,128)}, f32[1...) custom-call(s32[3]{0:T(128)} %pad_add_fusion.3.place_ref, ...), custom_call_target="tpu_custom_call" | custom-call | flops 20000000000 | bytes 29843456 | tf_op jit(solution)/shard_map/layer_forward/pallas_call | solution.py:510
  87.9 24.9 %collective-permute-start.12 = (bf16[512,1664]{1,0:T(8,128)(2,1)}, bf16[512,1664]{1,0:T(8,128)(2,1)}, u32[]{:S(2)}, u32[]{:S(2)}) collective-permute-start(bf16[512,1664]{1,0:T(8,128)(2,1)} %get-tuple-element.98), channel_id=1, source_target_pairs={{0,8},{1,9},{2,10},{3,11},{4,12},{5,13},{6,14},{7,15},{8,0},{9,1},... | collective-permute-start | bytes 5111816 | tf_op jit(solution)/shard_map/ppermute | solution.py:739
  116.3 2.8 add_convert_fusion.4
  127.4 6.4 %collective-permute-done.13.a_ref = bf16[128,1664]{1,0:T(8,128)(2,1)S(1)} collective-permute-done((bf16[128,1664]{1,0:T(8,128)(2,1)S(1)}, bf16[128,1664]{1,0:T(8,128)(2,1)S(1)}, u32[]{:S(2)}, u32[]{:S(2)}) %collective-permute-start.13) | collective-permute-done | bytes 426016 | tf_op jit(solution)/shard_map/ppermute | solution.py:739
  135.9 7.2 %collective-permute-done.14.b_ref = bf16[128,1664]{1,0:T(8,128)(2,1)S(1)} collective-permute-done((bf16[128,1664]{1,0:T(8,128)(2,1)S(1)}, bf16[128,1664]{1,0:T(8,128)(2,1)S(1)}, u32[]{:S(2)}, u32[]{:S(2)}) %collective-permute-start.14) | collective-permute-done | bytes 426016 | tf_op jit(solution)/shard_map/ppermute | solution.py:739
  145.1 3.3 middle_norm.1
  153.5 6.7 %collective-permute-done.17.refs_2_ = bf16[128,1536]{1,0:T(8,128)(2,1)S(1)} collective-permute-done((bf16[128,1536]{1,0:T(8,128)(2,1)}, bf16[128,1536]{1,0:T(8,128)(2,1)S(1)}, u32[]{:S(2)}, u32[]{:S(2)}) %collective-permute-start.17) | collective-permute-done | bytes 393248 | tf_op jit(solution)/shard_map/ppermute | solution.py:739
  163.0 6.5 %collective-permute-done.21.refs_6_ = bf16[128,1536]{1,0:T(8,128)(2,1)S(1)} collective-permute-done((bf16[128,1536]{1,0:T(8,128)(2,1)}, bf16[128,1536]{1,0:T(8,128)(2,1)S(1)}, u32[]{:S(2)}, u32[]{:S(2)}) %collective-permute-start.21) | collective-permute-done | bytes 393248 | tf_op jit(solution)/shard_map/ppermute | solution.py:739
  172.9 28.9 %layer_forward.3 = (bf16[4608,384]{1,0:T(8,128)(2,1)}, bf16[1024,1536]{1,0:T(8,128)(2,1)}, bf16[256,1536]{1,0:T(8,128)(2,1)}, f32[1024,384]{1,0:T(8,128)}, f32[1...) custom-call(s32[3]{0:T(128)} %pad_add_fusion.3.place_ref, ...), custom_call_target="tpu_custom_call" | custom-call | flops 20000000000 | bytes 36757504 | tf_op jit(solution)/shard_map/layer_forward/pallas_call | solution.py:510
  202.4 3.4 collective-permute-done.28
  213.5 6.2 %last_gate_backward.1 = (bf16[1024,384]{1,0:T(8,128)(2,1)}, f32[1024,384]{1,0:T(8,128)}, bf16[1024,384]{1,0:T(8,128)(2,1)}, f32[8,384]{1,0:T(8,128)}) custom-call(s32[3]{0:T(128)} %pad_add_fusion.3.place_ref, f32[1024,384]{1,0:T(8,128)} %get-tuple-element.101.gg_ref, f32[8,1024]{1,0:T(8,128)} %add_add_fusion.tok_ref, f32[1024,384]{1,0:T(8,128)} %get-tuple-element.103.z_ref, ...), custom_call_target="tpu_custom_call" | custom-call | flops 1000000000 | bytes 7921664 | tf_op jit(solution)/shard_map/last_gate_backward/pallas_call | solution.py:510
  219.7 7.6 %weight_products.3 = bf16[1536,768]{1,0:T(8,128)(2,1)} custom-call(bf16[1024,1536]{1,0:T(8,128)(2,1)} %get-tuple-element.110.refs_2_.refs_0_, bf16[1024,384]{1,0:T(8,128)(2,1)} %get-tuple-element.119.refs_1_, bf16[1024,384]{1,0:T(8,128)(2,1)} %get-tuple-element.109.refs_1_.refs_2_, bf16[1024,1536]{1,0:T(8,128)(2,1)} %get-tuple-element.120.refs_3_), custom_call_target="tpu_custom_call" | custom-call | flops 2415919104 | bytes 8000000 | tf_op jit(solution)/shard_map/weight_products/pallas_call | solution.py:703
  234.4 29.4 %scan_backward.2 = (bf16[1024,512]{1,0:T(8,128)(2,1)}, bf16[512,256]{1,0:T(8,128)(2,1)}, bf16[512,256]{1,0:T(8,128)(2,1)}, bf16[512,1536]{1,0:T(8,128)(2,1)}, bf...) custom-call(s32[3]{0:T(128)} %pad_add_fusion.3.place_ref, ...), custom_call_target="tpu_custom_call" | custom-call | flops 28000000000 | bytes 20692992 | tf_op jit(solution)/shard_map/scan_backward/pallas_call | solution.py:510
  265.2 4.8 collective-permute-start.37
  270.0 3.4 collective-permute-done.38
  278.1 18.7 %collective-permute-done.39.a_ref = bf16[128,1792]{1,0:T(8,128)(2,1)S(1)} collective-permute-done((bf16[128,1792]{1,0:T(8,128)(2,1)S(1)}, bf16[128,1792]{1,0:T(8,128)(2,1)S(1)}, u32[]{:S(2)}, u32[]{:S(2)}) %collective-permute-start.39) | collective-permute-done | bytes 458784 | tf_op jit(solution)/shard_map/ppermute | solution.py:739
  298.9 3.8 between_layers.1
  302.9 4.5 collective-permute-start.49
  313.8 6.0 %collective-permute-done.43.refs_2_ = bf16[128,1664]{1,0:T(8,128)(2,1)S(1)} collective-permute-done((bf16[128,1664]{1,0:T(8,128)(2,1)}, bf16[128,1664]{1,0:T(8,128)(2,1)S(1)}, u32[]{:S(2)}, u32[]{:S(2)}) %collective-permute-start.43) | collective-permute-done | bytes 426016 | tf_op jit(solution)/shard_map/ppermute | solution.py:739
  321.6 7.0 %collective-permute-done.45.refs_4_ = bf16[128,1664]{1,0:T(8,128)(2,1)} collective-permute-done((bf16[128,1664]{1,0:T(8,128)(2,1)}, bf16[128,1664]{1,0:T(8,128)(2,1)}, u32[]{:S(2)}, u32[]{:S(2)}) %collective-permute-start.45) | collective-permute-done | bytes 426016 | tf_op jit(solution)/shard_map/ppermute | solution.py:739
  333.7 8.8 %gate_backward.1 = (bf16[1024,1536]{1,0:T(8,128)(2,1)}, bf16[1024,384]{1,0:T(8,128)(2,1)}, f32[1024,384]{1,0:T(8,128)}, bf16[1024,384]{1,0:T(8,128)(2,1)}, f32[8,384]{1,0:T(8,128)}) custom-call(s32[3]{0:T(128)} %pad_add_fusion.3.place_ref, bf16[128,1664]{1,0:T(8,128)(2,1)} %get-tuple-element.127.refs_0_, bf16[128,1664]{1,0:T(8,128)(2,1)} %copy-done.58, ...), custom_call_target="tpu_custom_call" | custom-call | flops 6000000000 | bytes 16408576 | tf_op jit(solution)/shard_map/gate_backward/pallas_call | solution.py:510
  342.5 10.1 %weight_products.4 = bf16[1536,1280]{1,0:T(8,128)(2,1)} custom-call(bf16[1024,1536]{1,0:T(8,128)(2,1)} %get-tuple-element.134.refs_0_.refs_2_, bf16[1024,384]{1,0:T(8,128)(2,1)} %get-tuple-element.135.refs_1_, bf16[1024,1536]{1,0:T(8,128)(2,1)} %get-tuple-element.110.refs_2_.refs_0_, bf16[1024,384]{1,0:T(8,128)(2,1)} %get-tuple-element.136.refs_3_.refs_1_, ...), custom_call_target="tpu_custom_call" | custom-call | flops 4026531840 | bytes 8000000 | tf_op jit(solution)/shard_map/weight_products/pallas_call | solution.py:703
  352.6 29.4 %scan_backward.3 = (bf16[1024,512]{1,0:T(8,128)(2,1)}, bf16[512,256]{1,0:T(8,128)(2,1)}, bf16[512,256]{1,0:T(8,128)(2,1)}, bf16[512,1536]{1,0:T(8,128)(2,1)}, bf...) custom-call(s32[3]{0:T(128)} %pad_add_fusion.3.place_ref, ...), custom_call_target="tpu_custom_call" | custom-call | flops 28000000000 | bytes 20692992 | tf_op jit(solution)/shard_map/scan_backward/pallas_call | solution.py:510
  385.5 3.5 constant_dynamic-slice_fusion.5
  401.7 10.6 %collective-permute-done.62 = bf16[384,1280]{1,0:T(8,128)(2,1)} collective-permute-done((bf16[384,1280]{1,0:T(8,128)(2,1)}, bf16[384,1280]{1,0:T(8,128)(2,1)}, u32[]{:S(2)}, u32[]{:S(2)}) %collective-permute-start.62) | collective-permute-done | bytes 983072 | tf_op jit(solution)/shard_map/ppermute | solution.py:739
  413.7 22.0 %collective-permute-done.64 = bf16[384,1280]{1,0:T(8,128)(2,1)} collective-permute-done((bf16[384,1280]{1,0:T(8,128)(2,1)}, bf16[384,1280]{1,0:T(8,128)(2,1)}, u32[]{:S(2)}, u32[]{:S(2)}) %collective-permute-start.64) | collective-permute-done | bytes 983072 | tf_op jit(solution)/shard_map/ppermute | solution.py:739
  435.7 2.6 add_convert_fusion.2
  439.6 5.4 weight_products.5
  450.5 2.8 last_output.1.hidden_ref
  453.4 4.8 collective-permute-done.66
  458.8 11.4 %collective-permute-done.68 = bf16[384,512]{1,0:T(8,128)(2,1)} collective-permute-done((bf16[384,512]{1,0:T(8,128)(2,1)S(1)}, bf16[384,512]{1,0:T(8,128)(2,1)}, u32[]{:S(2)}, u32[]{:S(2)}) %collective-permute-start.68) | collective-permute-done | bytes 393248 | tf_op jit(solution)/shard_map/ppermute | solution.py:739
  476.6 5.5 collective-permute-start.77
  482.2 2.6 add_convert_fusion.9
  488.8 12.6 %collective-permute-done.78 = bf16[192,1280]{1,0:T(8,128)(2,1)S(1)} collective-permute-done((bf16[192,1280]{1,0:T(8,128)(2,1)S(1)}, bf16[192,1280]{1,0:T(8,128)(2,1)S(1)}, u32[]{:S(2)}, u32[]{:S(2)}) %collective-permute-start.78) | collective-permute-done | bytes 491552 | tf_op jit(solution)/shard_map/ppermute | solution.py:739
  501.4 2.6 collective-permute-start.70
  509.6 3.5 outputs.1
  519.0 6.8 %collective-permute-done.80 = bf16[192,1280]{1,0:T(8,128)(2,1)S(1)} collective-permute-done((bf16[192,1280]{1,0:T(8,128)(2,1)S(1)}, bf16[192,1280]{1,0:T(8,128)(2,1)S(1)}, u32[]{:S(2)}, u32[]{:S(2)}) %collective-permute-start.80) | collective-permute-done | bytes 491552 | tf_op jit(solution)/shard_map/ppermute | solution.py:739
  527.1 6.8 %collective-permute-done.81 = bf16[192,1280]{1,0:T(8,128)(2,1)S(1)} collective-permute-done((bf16[192,1280]{1,0:T(8,128)(2,1)S(1)}, bf16[192,1280]{1,0:T(8,128)(2,1)S(1)}, u32[]{:S(2)}, u32[]{:S(2)}) %collective-permute-start.81) | collective-permute-done | bytes 491552 | tf_op jit(solution)/shard_map/ppermute | solution.py:739
  533.9 5.8 collective-permute-start.74
  539.7 6.2 %collective-permute-start.82 = (bf16[4,192,1280]{2,1,0:T(8,128)(2,1)S(1)}, bf16[4,192,1280]{2,1,0:T(8,128)(2,1)S(1)}, u32[]{:S(2)}, u32[]{:S(2)}) collective-permute-start(bf16[4,192,1280]{2,1,0:T(8,128)(2,1)S(1)} %bitcast_dynamic-update-slice_fusion.4.here_ref), channel_id=1, source_target_pairs={{0,8},{1,9},{2,10},{3,11},{4,12},{5,13},{6,14},{7,15},{8,0},{9,1},... | collective-permute-start | bytes 5898248 | tf_op jit(solution)/shard_map/ppermute | solution.py:739
  546.1 6.7 %collective-permute-start.75 = (bf16[4,192,512]{2,1,0:T(8,128)(2,1)S(1)}, bf16[4,192,512]{2,1,0:T(8,128)(2,1)S(1)}, u32[]{:S(2)}, u32[]{:S(2)}) collective-permute-start(bf16[4,192,512]{2,1,0:T(8,128)(2,1)S(1)} %bitcast_dynamic-update-slice_fusion.12.here_ref), channel_id=1, source_target_pairs={{0,8},{1,9},{2,10},{3,11},{4,12},{5,13},{6,14},{7,15},{8,0},{9,1},... | collective-permute-start | bytes 2359304 | tf_op jit(solution)/shard_map/ppermute | solution.py:739
  555.3 4.6 write_sums.3
  561.2 6.3 %write_sums.4 = (f32[2,4,2,192,384]{4,3,2,1,0:T(8,128)}, f32[2,384,1536]{2,1,0:T(8,128)}, f32[2,4,2,192,384]{4,3,2,1,0:T(8,128)}, f32[1,4,2,192,128]{4,3,2,1,0:T(8,128)}) custom-call(s32[3]{0:T(128)} %pad_add_fusion.3.place_ref, bf16[4,192,1280]{2,1,0:T(8,128)(2,1)} %copy-done.2, ...), custom_call_target="tpu_custom_call", output_to_operand_aliasing={{0}: (3, {}), {1}: (4, {})} | custom-call | tf_op jit(solution)/shard_map/write_sums/pallas_call | solution.py:936
  568.4 3.8 write_sums.5
  (433 shorter events, 170.1 us)
Async XLA Ops:
  8.6 14.7 %collective-permute-start = (bf16[192,1536]{1,0:T(8,128)(2,1)}, bf16[192,1536]{1,0:T(8,128)(2,1)}, u32[]{:S(2)}, u32[]{:S(2)}) collective-permute-start(bf16[192,1536]{1,0:T(8,128)(2,1)} %pad_maximum_fusion.2), channel_id=1, source_target_pairs={{4,8},{5,9},{6,10},{7,11},{8,4},{9,5},{10,6},{11,7},{20,24},{21,25... | collective-permute-start | bytes 1769480 | tf_op jit(solution)/shard_map/ppermute | solution.py:739
  24.3 34.5 %collective-permute-start.8 = (bf16[5248,384]{1,0:T(8,128)(2,1)}, bf16[5248,384]{1,0:T(8,128)(2,1)}, u32[]{:S(2)}, u32[]{:S(2)}) collective-permute-start(bf16[5248,384]{1,0:T(8,128)(2,1)} %fusion.8.refs_8_), channel_id=1, source_target_pairs={{4,8},{5,9},{6,10},{7,11},{8,4},{9,5},{10,6},{11,7},{20,24},{21,25... | collective-permute-start | bytes 12091400 | tf_op jit(solution)/shard_map/ppermute | solution.py:739
  32.6 18.6 %collective-permute-start.4 = (bf16[160,1536]{1,0:T(8,128)(2,1)}, bf16[160,1536]{1,0:T(8,128)(2,1)S(1)}, u32[]{:S(2)}, u32[]{:S(2)}) collective-permute-start(bf16[160,1536]{1,0:T(8,128)(2,1)} %first_norm.1.refs_0_), channel_id=1, source_target_pairs={{0,3},{1,0},{2,1},{3,2},{4,7},{5,4},{6,5},{7,6},{8,11},{9,8},{10,9... | collective-permute-start | bytes 1474568 | tf_op jit(solution)/shard_map/ppermute | solution.py:739
  34.7 22.3 %collective-permute-start.6 = (bf16[160,1536]{1,0:T(8,128)(2,1)}, bf16[160,1536]{1,0:T(8,128)(2,1)S(1)}, u32[]{:S(2)}, u32[]{:S(2)}) collective-permute-start(bf16[160,1536]{1,0:T(8,128)(2,1)} %first_norm.1.refs_0_), channel_id=1, source_target_pairs={{0,2},{1,3},{2,0},{3,1},{4,6},{5,7},{6,4},{7,5},{8,10},{9,11},{10,... | collective-permute-start | bytes 1474568 | tf_op jit(solution)/shard_map/ppermute | solution.py:739
  36.0 24.1 %collective-permute-start.1 = (bf16[160,1536]{1,0:T(8,128)(2,1)}, bf16[160,1536]{1,0:T(8,128)(2,1)S(1)}, u32[]{:S(2)}, u32[]{:S(2)}) collective-permute-start(bf16[160,1536]{1,0:T(8,128)(2,1)} %first_norm.1.refs_0_), channel_id=1, source_target_pairs={{0,8},{1,9},{2,10},{3,11},{4,12},{5,13},{6,14},{7,15},{8,0},{9,1},... | collective-permute-start | bytes 1474568 | tf_op jit(solution)/shard_map/ppermute | solution.py:739
  45.1 15.0 %collective-permute-start.3 = (bf16[160,1536]{1,0:T(8,128)(2,1)S(1)}, bf16[160,1536]{1,0:T(8,128)(2,1)S(1)}, u32[]{:S(2)}, u32[]{:S(2)}) collective-permute-start(bf16[160,1536]{1,0:T(8,128)(2,1)S(1)} %collective-permute-done.2.refs_2_), channel_id=1, source_target_pairs={{0,8},{1,9},{2,10},{3,11},{4,12},{5,13},{6,14},{7,15},{8,0},{9,1},... | collective-permute-start | bytes 1474568 | tf_op jit(solution)/shard_map/ppermute | solution.py:739
  60.3 27.5 %collective-permute-start.10 = (bf16[160,1536]{1,0:T(8,128)(2,1)S(1)}, bf16[160,1536]{1,0:T(8,128)(2,1)S(1)}, u32[]{:S(2)}, u32[]{:S(2)}) collective-permute-start(bf16[160,1536]{1,0:T(8,128)(2,1)S(1)} %get-tuple-element.97), channel_id=1, source_target_pairs={{0,3},{1,0},{2,1},{3,2},{4,11},{5,8},{6,9},{7,10},{8,7},{9,4},{10,... | collective-permute-start | bytes 1474568 | tf_op jit(solution)/shard_map/ppermute | solution.py:739
  62.5 25.4 %collective-permute-start.11 = (bf16[160,1536]{1,0:T(8,128)(2,1)S(1)}, bf16[160,1536]{1,0:T(8,128)(2,1)S(1)}, u32[]{:S(2)}, u32[]{:S(2)}) collective-permute-start(bf16[160,1536]{1,0:T(8,128)(2,1)S(1)} %get-tuple-element.97), channel_id=1, source_target_pairs={{0,2},{1,3},{2,0},{3,1},{4,10},{5,11},{6,8},{7,9},{8,6},{9,7},{10,... | collective-permute-start | bytes 1474568 | tf_op jit(solution)/shard_map/ppermute | solution.py:739
  62.9 24.9 %collective-permute-start.9 = (bf16[160,1536]{1,0:T(8,128)(2,1)S(1)}, bf16[160,1536]{1,0:T(8,128)(2,1)}, u32[]{:S(2)}, u32[]{:S(2)}) collective-permute-start(bf16[160,1536]{1,0:T(8,128)(2,1)S(1)} %get-tuple-element.97), channel_id=1, source_target_pairs={{0,1},{1,2},{2,3},{3,0},{4,9},{5,10},{6,11},{7,8},{8,5},{9,6},{10,... | collective-permute-start | bytes 1474568 | tf_op jit(solution)/shard_map/ppermute | solution.py:739
  87.9 28.5 %collective-permute-start.12 = (bf16[512,1664]{1,0:T(8,128)(2,1)}, bf16[512,1664]{1,0:T(8,128)(2,1)}, u32[]{:S(2)}, u32[]{:S(2)}) collective-permute-start(bf16[512,1664]{1,0:T(8,128)(2,1)} %get-tuple-element.98), channel_id=1, source_target_pairs={{0,8},{1,9},{2,10},{3,11},{4,12},{5,13},{6,14},{7,15},{8,0},{9,1},... | collective-permute-start | bytes 5111816 | tf_op jit(solution)/shard_map/ppermute | solution.py:739
  119.2 52.9 %collective-permute-start.27 = (bf16[4608,384]{1,0:T(8,128)(2,1)S(1)}, bf16[4608,384]{1,0:T(8,128)(2,1)}, u32[]{:S(2)}, u32[]{:S(2)}) collective-permute-start(bf16[4608,384]{1,0:T(8,128)(2,1)S(1)} %copy-done.32), channel_id=1, source_target_pairs={{4,8},{5,9},{6,10},{7,11},{8,4},{9,5},{10,6},{11,7},{20,24},{21,25... | collective-permute-start | bytes 10616840 | tf_op jit(solution)/shard_map/ppermute | solution.py:739
  123.6 19.5 %collective-permute-start.14 = (bf16[128,1664]{1,0:T(8,128)(2,1)S(1)}, bf16[128,1664]{1,0:T(8,128)(2,1)S(1)}, u32[]{:S(2)}, u32[]{:S(2)}) collective-permute-start(bf16[128,1664]{1,0:T(8,128)(2,1)S(1)} %get-tuple-element.237), channel_id=1, source_target_pairs={{0,2},{1,3},{2,0},{3,1},{4,6},{5,7},{6,4},{7,5},{8,10},{9,11},{10,... | collective-permute-start | bytes 1277960 | tf_op jit(solution)/shard_map/ppermute | solution.py:739
  124.5 19.9 %collective-permute-start.15 = (bf16[128,1664]{1,0:T(8,128)(2,1)S(1)}, bf16[128,1664]{1,0:T(8,128)(2,1)S(1)}, u32[]{:S(2)}, u32[]{:S(2)}) collective-permute-start(bf16[128,1664]{1,0:T(8,128)(2,1)S(1)} %get-tuple-element.236), channel_id=1, source_target_pairs={{0,3},{1,0},{2,1},{3,2},{4,7},{5,4},{6,5},{7,6},{8,11},{9,8},{10,9... | collective-permute-start | bytes 1277960 | tf_op jit(solution)/shard_map/ppermute | solution.py:739
  126.2 22.2 %collective-permute-start.23 = (bf16[160,1536]{1,0:T(8,128)(2,1)S(1)}, bf16[160,1536]{1,0:T(8,128)(2,1)}, u32[]{:S(2)}, u32[]{:S(2)}) collective-permute-start(bf16[160,1536]{1,0:T(8,128)(2,1)S(1)} %get-tuple-element.270.refs_8_.dres_ref), channel_id=1, source_target_pairs={{0,8},{1,9},{2,10},{3,11},{4,12},{5,13},{6,14},{7,15},{8,0},{9,1},... | collective-permute-start | bytes 1474568 | tf_op jit(solution)/shard_map/ppermute | solution.py:739
  133.8 16.3 %collective-permute-start.24 = (bf16[160,1536]{1,0:T(8,128)(2,1)}, bf16[160,1536]{1,0:T(8,128)(2,1)}, u32[]{:S(2)}, u32[]{:S(2)}) collective-permute-start(bf16[160,1536]{1,0:T(8,128)(2,1)} %collective-permute-done.9.refs_10_), channel_id=1, source_target_pairs={{0,8},{1,9},{2,10},{3,11},{4,12},{5,13},{6,14},{7,15},{8,0},{9,1},... | collective-permute-start | bytes 1474568 | tf_op jit(solution)/shard_map/ppermute | solution.py:739
  151.1 18.4 %collective-permute-start.21 = (bf16[128,1536]{1,0:T(8,128)(2,1)}, bf16[128,1536]{1,0:T(8,128)(2,1)S(1)}, u32[]{:S(2)}, u32[]{:S(2)}) collective-permute-start(bf16[128,1536]{1,0:T(8,128)(2,1)} %get-tuple-element.99.refs_0_), channel_id=1, source_target_pairs={{0,2},{1,3},{2,0},{3,1},{4,6},{5,7},{6,4},{7,5},{8,10},{9,11},{10,... | collective-permute-start | bytes 1179656 | tf_op jit(solution)/shard_map/ppermute | solution.py:739
  152.1 19.4 %collective-permute-start.16 = (bf16[128,1536]{1,0:T(8,128)(2,1)}, bf16[128,1536]{1,0:T(8,128)(2,1)S(1)}, u32[]{:S(2)}, u32[]{:S(2)}) collective-permute-start(bf16[128,1536]{1,0:T(8,128)(2,1)} %get-tuple-element.99.refs_0_), channel_id=1, source_target_pairs={{0,8},{1,9},{2,10},{3,11},{4,12},{5,13},{6,14},{7,15},{8,0},{9,1},... | collective-permute-start | bytes 1179656 | tf_op jit(solution)/shard_map/ppermute | solution.py:739
  201.8 27.2 %collective-permute-start.32 = (bf16[512,1664]{1,0:T(8,128)(2,1)}, bf16[512,1664]{1,0:T(8,128)(2,1)S(1)}, u32[]{:S(2)}, u32[]{:S(2)}) collective-permute-start(bf16[512,1664]{1,0:T(8,128)(2,1)} %get-tuple-element.107), channel_id=1, source_target_pairs={{0,8},{1,9},{2,10},{3,11},{4,12},{5,13},{6,14},{7,15},{8,0},{9,1},... | collective-permute-start | bytes 5111816 | tf_op jit(solution)/shard_map/ppermute | solution.py:739
  227.3 36.6 %collective-permute-start.33 = (bf16[1536,768]{1,0:T(8,128)(2,1)}, bf16[1536,768]{1,0:T(8,128)(2,1)S(1)}, u32[]{:S(2)}, u32[]{:S(2)}) collective-permute-start(bf16[1536,768]{1,0:T(8,128)(2,1)} %weight_products.3), channel_id=1, source_target_pairs={{4,0},{5,1},{6,2},{7,3},{8,12},{9,13},{10,14},{11,15},{20,16},{21,... | collective-permute-start | bytes 7077896 | tf_op jit(solution)/shard_map/ppermute | solution.py:739
  230.2 34.2 %collective-permute-start.34 = (bf16[128,1664]{1,0:T(8,128)(2,1)}, bf16[128,1664]{1,0:T(8,128)(2,1)S(1)}, u32[]{:S(2)}, u32[]{:S(2)}) collective-permute-start(bf16[128,1664]{1,0:T(8,128)(2,1)} %get-tuple-element.235), channel_id=1, source_target_pairs={{0,1},{1,2},{2,3},{3,0},{4,5},{5,6},{6,7},{7,4},{8,9},{9,10},{10,1... | collective-permute-start | bytes 1277960 | tf_op jit(solution)/shard_map/ppermute | solution.py:739
  230.5 34.0 %collective-permute-start.35 = (bf16[128,1664]{1,0:T(8,128)(2,1)}, bf16[128,1664]{1,0:T(8,128)(2,1)S(1)}, u32[]{:S(2)}, u32[]{:S(2)}) collective-permute-start(bf16[128,1664]{1,0:T(8,128)(2,1)} %get-tuple-element.234), channel_id=1, source_target_pairs={{0,2},{1,3},{2,0},{3,1},{4,6},{5,7},{6,4},{7,5},{8,10},{9,11},{10,... | collective-permute-start | bytes 1277960 | tf_op jit(solution)/shard_map/ppermute | solution.py:739
  232.4 32.1 %collective-permute-start.36 = (bf16[128,1664]{1,0:T(8,128)(2,1)}, bf16[128,1664]{1,0:T(8,128)(2,1)}, u32[]{:S(2)}, u32[]{:S(2)}) collective-permute-start(bf16[128,1664]{1,0:T(8,128)(2,1)} %get-tuple-element.233), channel_id=1, source_target_pairs={{0,3},{1,0},{2,1},{3,2},{4,7},{5,4},{6,5},{7,6},{8,11},{9,8},{10,9... | collective-permute-start | bytes 1277960 | tf_op jit(solution)/shard_map/ppermute | solution.py:739
  274.0 22.8 %collective-permute-start.39 = (bf16[128,1792]{1,0:T(8,128)(2,1)S(1)}, bf16[128,1792]{1,0:T(8,128)(2,1)S(1)}, u32[]{:S(2)}, u32[]{:S(2)}) collective-permute-start(bf16[128,1792]{1,0:T(8,128)(2,1)S(1)} %pad_maximum_fusion.3), channel_id=1, source_target_pairs={{0,1},{1,2},{2,3},{3,0},{4,5},{5,6},{6,7},{7,4},{8,9},{9,10},{10,1... | collective-permute-start | bytes 1376264 | tf_op jit(solution)/shard_map/ppermute | solution.py:739
  275.0 21.8 %collective-permute-start.40 = (bf16[128,1792]{1,0:T(8,128)(2,1)S(1)}, bf16[128,1792]{1,0:T(8,128)(2,1)S(1)}, u32[]{:S(2)}, u32[]{:S(2)}) collective-permute-start(bf16[128,1792]{1,0:T(8,128)(2,1)S(1)} %pad_maximum_fusion.4), channel_id=1, source_target_pairs={{0,2},{1,3},{2,0},{3,1},{4,6},{5,7},{6,4},{7,5},{8,10},{9,11},{10,... | collective-permute-start | bytes 1376264 | tf_op jit(solution)/shard_map/ppermute | solution.py:739
  275.9 21.3 %collective-permute-start.41 = (bf16[128,1792]{1,0:T(8,128)(2,1)S(1)}, bf16[128,1792]{1,0:T(8,128)(2,1)S(1)}, u32[]{:S(2)}, u32[]{:S(2)}) collective-permute-start(bf16[128,1792]{1,0:T(8,128)(2,1)S(1)} %pad_maximum_fusion.5), channel_id=1, source_target_pairs={{0,3},{1,0},{2,1},{3,2},{4,7},{5,4},{6,5},{7,6},{8,11},{9,8},{10,9... | collective-permute-start | bytes 1376264 | tf_op jit(solution)/shard_map/ppermute | solution.py:739
  308.4 20.2 %collective-permute-start.45 = (bf16[128,1664]{1,0:T(8,128)(2,1)}, bf16[128,1664]{1,0:T(8,128)(2,1)}, u32[]{:S(2)}, u32[]{:S(2)}) collective-permute-start(bf16[128,1664]{1,0:T(8,128)(2,1)} %get-tuple-element.127.refs_0_), channel_id=1, source_target_pairs={{0,3},{1,0},{2,1},{3,2},{4,7},{5,4},{6,5},{7,6},{8,11},{9,8},{10,9... | collective-permute-start | bytes 1277960 | tf_op jit(solution)/shard_map/ppermute | solution.py:739
  310.2 19.2 %collective-permute-start.47 = (bf16[128,1664]{1,0:T(8,128)(2,1)}, bf16[128,1664]{1,0:T(8,128)(2,1)}, u32[]{:S(2)}, u32[]{:S(2)}) collective-permute-start(bf16[128,1664]{1,0:T(8,128)(2,1)} %get-tuple-element.127.refs_0_), channel_id=1, source_target_pairs={{0,2},{1,3},{2,0},{3,1},{4,6},{5,7},{6,4},{7,5},{8,10},{9,11},{10,... | collective-permute-start | bytes 1277960 | tf_op jit(solution)/shard_map/ppermute | solution.py:739
  311.4 18.0 %collective-permute-start.50 = (bf16[192,768]{1,0:T(8,128)(2,1)S(1)}, bf16[192,768]{1,0:T(8,128)(2,1)}, u32[]{:S(2)}, u32[]{:S(2)}) collective-permute-start(bf16[192,768]{1,0:T(8,128)(2,1)S(1)} %get-tuple-element.259), channel_id=1, source_target_pairs={{0,32},{1,33},{2,34},{3,35},{4,36},{5,37},{6,38},{7,39},{8,40},{9,... | collective-permute-start | bytes 884744 | tf_op jit(solution)/shard_map/ppermute | solution.py:739
  311.6 18.3 %collective-permute-start.51 = (bf16[192,768]{1,0:T(8,128)(2,1)S(1)}, bf16[192,768]{1,0:T(8,128)(2,1)}, u32[]{:S(2)}, u32[]{:S(2)}) collective-permute-start(bf16[192,768]{1,0:T(8,128)(2,1)S(1)} %get-tuple-element.261), channel_id=1, source_target_pairs={{0,64},{1,65},{2,66},{3,67},{4,68},{5,69},{6,70},{7,71},{8,72},{9,... | collective-permute-start | bytes 884744 | tf_op jit(solution)/shard_map/ppermute | solution.py:739
  389.0 23.3 %collective-permute-start.62 = (bf16[384,1280]{1,0:T(8,128)(2,1)}, bf16[384,1280]{1,0:T(8,128)(2,1)}, u32[]{:S(2)}, u32[]{:S(2)}) collective-permute-start(bf16[384,1280]{1,0:T(8,128)(2,1)} %get-tuple-element.230), channel_id=1, source_target_pairs={{0,32},{1,33},{2,34},{3,35},{4,36},{5,37},{6,38},{7,39},{8,40},{9,... | collective-permute-start | bytes 2949128 | tf_op jit(solution)/shard_map/ppermute | solution.py:739
  389.2 24.5 %collective-permute-start.63 = (bf16[384,1280]{1,0:T(8,128)(2,1)}, bf16[384,1280]{1,0:T(8,128)(2,1)}, u32[]{:S(2)}, u32[]{:S(2)}) collective-permute-start(bf16[384,1280]{1,0:T(8,128)(2,1)} %get-tuple-element.232), channel_id=1, source_target_pairs={{0,64},{1,65},{2,66},{3,67},{4,68},{5,69},{6,70},{7,71},{8,72},{9,... | collective-permute-start | bytes 2949128 | tf_op jit(solution)/shard_map/ppermute | solution.py:739
  391.3 44.4 %collective-permute-start.64 = (bf16[384,1280]{1,0:T(8,128)(2,1)}, bf16[384,1280]{1,0:T(8,128)(2,1)}, u32[]{:S(2)}, u32[]{:S(2)}) collective-permute-start(bf16[384,1280]{1,0:T(8,128)(2,1)} %get-tuple-element.231), channel_id=1, source_target_pairs={{0,96},{1,97},{2,98},{3,99},{4,100},{5,101},{6,102},{7,103},{8,104... | collective-permute-start | bytes 2949128 | tf_op jit(solution)/shard_map/ppermute | solution.py:739
  399.7 76.9 %collective-permute-start.53 = (bf16[512,1536]{1,0:T(8,128)(2,1)}, bf16[512,1536]{1,0:T(8,128)(2,1)}, u32[]{:S(2)}, u32[]{:S(2)}) collective-permute-start(bf16[512,1536]{1,0:T(8,128)(2,1)} %get-tuple-element.146), channel_id=1, source_target_pairs={{0,8},{1,9},{2,10},{3,11},{4,12},{5,13},{6,14},{7,15},{8,0},{9,1},... | collective-permute-start | bytes 4718600 | tf_op jit(solution)/shard_map/ppermute | solution.py:739
  445.0 28.7 %collective-permute-start.76 = (bf16[384,1280]{1,0:T(8,128)(2,1)S(1)}, bf16[384,1280]{1,0:T(8,128)(2,1)}, u32[]{:S(2)}, u32[]{:S(2)}) collective-permute-start(bf16[384,1280]{1,0:T(8,128)(2,1)S(1)} %add_convert_fusion.2), channel_id=1, source_target_pairs={{4,0},{5,1},{6,2},{7,3},{8,12},{9,13},{10,14},{11,15},{20,16},{21,... | collective-permute-start | bytes 2949128 | tf_op jit(solution)/shard_map/ppermute | solution.py:739
  450.4 19.8 %collective-permute-start.68 = (bf16[384,512]{1,0:T(8,128)(2,1)S(1)}, bf16[384,512]{1,0:T(8,128)(2,1)}, u32[]{:S(2)}, u32[]{:S(2)}) collective-permute-start(bf16[384,512]{1,0:T(8,128)(2,1)S(1)} %get-tuple-element.255), channel_id=1, source_target_pairs={{0,96},{1,97},{2,98},{3,99},{4,100},{5,101},{6,102},{7,103},{8,104... | collective-permute-start | bytes 1179656 | tf_op jit(solution)/shard_map/ppermute | solution.py:739
  471.7 16.6 %collective-permute-start.84 = (bf16[192,768]{1,0:T(8,128)(2,1)S(1)}, bf16[192,768]{1,0:T(8,128)(2,1)S(1)}, u32[]{:S(2)}, u32[]{:S(2)}) collective-permute-start(bf16[192,768]{1,0:T(8,128)(2,1)S(1)} %add_convert_fusion.15), channel_id=1, source_target_pairs={{0,64},{1,65},{2,66},{3,67},{4,68},{5,69},{6,70},{7,71},{8,72},{9,... | collective-permute-start | bytes 884744 | tf_op jit(solution)/shard_map/ppermute | solution.py:739
  472.8 33.8 %collective-permute-start.85 = (bf16[192,768]{1,0:T(8,128)(2,1)S(1)}, bf16[192,768]{1,0:T(8,128)(2,1)S(1)}, u32[]{:S(2)}, u32[]{:S(2)}) collective-permute-start(bf16[192,768]{1,0:T(8,128)(2,1)S(1)} %add_convert_fusion.15), channel_id=1, source_target_pairs={{0,96},{1,97},{2,98},{3,99},{4,100},{5,101},{6,102},{7,103},{8,104... | collective-permute-start | bytes 884744 | tf_op jit(solution)/shard_map/ppermute | solution.py:739
  473.7 14.7 %collective-permute-start.69 = (bf16[384,512]{1,0:T(8,128)(2,1)S(1)}, bf16[384,512]{1,0:T(8,128)(2,1)S(1)}, u32[]{:S(2)}, u32[]{:S(2)}) collective-permute-start(bf16[384,512]{1,0:T(8,128)(2,1)S(1)} %add_convert_fusion.8), channel_id=1, source_target_pairs={{4,0},{5,1},{6,2},{7,3},{8,12},{9,13},{10,14},{11,15},{20,16},{21,... | collective-permute-start | bytes 1179656 | tf_op jit(solution)/shard_map/ppermute | solution.py:739
  484.8 22.0 %collective-permute-start.54 = (bf16[128,1536]{1,0:T(8,128)(2,1)S(1)}, bf16[128,1536]{1,0:T(8,128)(2,1)}, u32[]{:S(2)}, u32[]{:S(2)}) collective-permute-start(bf16[128,1536]{1,0:T(8,128)(2,1)S(1)} %get-tuple-element.242), channel_id=1, source_target_pairs={{0,1},{1,2},{2,3},{3,0},{4,5},{5,6},{6,7},{7,4},{8,9},{9,10},{10,1... | collective-permute-start | bytes 1179656 | tf_op jit(solution)/shard_map/ppermute | solution.py:739
  485.9 22.2 %collective-permute-start.55 = (bf16[128,1536]{1,0:T(8,128)(2,1)S(1)}, bf16[128,1536]{1,0:T(8,128)(2,1)S(1)}, u32[]{:S(2)}, u32[]{:S(2)}) collective-permute-start(bf16[128,1536]{1,0:T(8,128)(2,1)S(1)} %get-tuple-element.241), channel_id=1, source_target_pairs={{0,2},{1,3},{2,0},{3,1},{4,6},{5,7},{6,4},{7,5},{8,10},{9,11},{10,... | collective-permute-start | bytes 1179656 | tf_op jit(solution)/shard_map/ppermute | solution.py:739
  488.5 19.6 %collective-permute-start.56 = (bf16[128,1536]{1,0:T(8,128)(2,1)S(1)}, bf16[128,1536]{1,0:T(8,128)(2,1)S(1)}, u32[]{:S(2)}, u32[]{:S(2)}) collective-permute-start(bf16[128,1536]{1,0:T(8,128)(2,1)S(1)} %get-tuple-element.240), channel_id=1, source_target_pairs={{0,3},{1,0},{2,1},{3,2},{4,7},{5,4},{6,5},{7,6},{8,11},{9,8},{10,9... | collective-permute-start | bytes 1179656 | tf_op jit(solution)/shard_map/ppermute | solution.py:739
  506.8 47.4 %collective-permute-start.86 = (bf16[4,192,768]{2,1,0:T(8,128)(2,1)S(1)}, bf16[4,192,768]{2,1,0:T(8,128)(2,1)S(1)}, u32[]{:S(2)}, u32[]{:S(2)}) collective-permute-start(bf16[4,192,768]{2,1,0:T(8,128)(2,1)S(1)} %bitcast_dynamic-update-slice_fusion.8.here_ref), channel_id=1, source_target_pairs={{0,8},{1,9},{2,10},{3,11},{4,12},{5,13},{6,14},{7,15},{8,0},{9,1},... | collective-permute-start | bytes 3538952 | tf_op jit(solution)/shard_map/ppermute | solution.py:739
  513.0 39.8 %collective-permute-start.57 = (bf16[128,3072]{1,0:T(8,128)(2,1)}, bf16[128,3072]{1,0:T(8,128)(2,1)S(1)}, u32[]{:S(2)}, u32[]{:S(2)}) collective-permute-start(bf16[128,3072]{1,0:T(8,128)(2,1)} %outputs.1), channel_id=1, source_target_pairs={{4,8},{5,9},{6,10},{7,11},{8,4},{9,5},{10,6},{11,7},{20,24},{21,25... | collective-permute-start | bytes 2359304 | tf_op jit(solution)/shard_map/ppermute | solution.py:739
  515.0 24.7 %collective-permute-start.72 = (bf16[192,512]{1,0:T(8,128)(2,1)S(1)}, bf16[192,512]{1,0:T(8,128)(2,1)S(1)}, u32[]{:S(2)}, u32[]{:S(2)}) collective-permute-start(bf16[192,512]{1,0:T(8,128)(2,1)S(1)} %get-tuple-element.223), channel_id=1, source_target_pairs={{0,32},{1,33},{2,34},{3,35},{4,36},{5,37},{6,38},{7,39},{8,40},{9,... | collective-permute-start | bytes 589832 | tf_op jit(solution)/shard_map/ppermute | solution.py:739
  517.4 16.4 %collective-permute-start.81 = (bf16[192,1280]{1,0:T(8,128)(2,1)S(1)}, bf16[192,1280]{1,0:T(8,128)(2,1)S(1)}, u32[]{:S(2)}, u32[]{:S(2)}) collective-permute-start(bf16[192,1280]{1,0:T(8,128)(2,1)S(1)} %get-tuple-element.221), channel_id=1, source_target_pairs={{0,96},{1,97},{2,98},{3,99},{4,100},{5,101},{6,102},{7,103},{8,104... | collective-permute-start | bytes 1474568 | tf_op jit(solution)/shard_map/ppermute | solution.py:739
  525.8 20.2 %collective-permute-start.73 = (bf16[192,512]{1,0:T(8,128)(2,1)S(1)}, bf16[192,512]{1,0:T(8,128)(2,1)S(1)}, u32[]{:S(2)}, u32[]{:S(2)}) collective-permute-start(bf16[192,512]{1,0:T(8,128)(2,1)S(1)} %get-tuple-element.223), channel_id=1, source_target_pairs={{0,64},{1,65},{2,66},{3,67},{4,68},{5,69},{6,70},{7,71},{8,72},{9,... | collective-permute-start | bytes 589832 | tf_op jit(solution)/shard_map/ppermute | solution.py:739
  539.7 20.2 %collective-permute-start.82 = (bf16[4,192,1280]{2,1,0:T(8,128)(2,1)S(1)}, bf16[4,192,1280]{2,1,0:T(8,128)(2,1)S(1)}, u32[]{:S(2)}, u32[]{:S(2)}) collective-permute-start(bf16[4,192,1280]{2,1,0:T(8,128)(2,1)S(1)} %bitcast_dynamic-update-slice_fusion.4.here_ref), channel_id=1, source_target_pairs={{0,8},{1,9},{2,10},{3,11},{4,12},{5,13},{6,14},{7,15},{8,0},{9,1},... | collective-permute-start | bytes 5898248 | tf_op jit(solution)/shard_map/ppermute | solution.py:739
  546.1 21.4 %collective-permute-start.75 = (bf16[4,192,512]{2,1,0:T(8,128)(2,1)S(1)}, bf16[4,192,512]{2,1,0:T(8,128)(2,1)S(1)}, u32[]{:S(2)}, u32[]{:S(2)}) collective-permute-start(bf16[4,192,512]{2,1,0:T(8,128)(2,1)S(1)} %bitcast_dynamic-update-slice_fusion.12.here_ref), channel_id=1, source_target_pairs={{0,8},{1,9},{2,10},{3,11},{4,12},{5,13},{6,14},{7,15},{8,0},{9,1},... | collective-permute-start | bytes 2359304 | tf_op jit(solution)/shard_map/ppermute | solution.py:739
  (109 other events, 968.3 us)

commit v2 on v1

--- a/solution.py
+++ b/solution.py
@@ -98,29 +98,6 @@
         outs[out][pl.ds(row, rows), :] = pieces[piece][start : start + rows, :]
 
 
-def cut_weights(w_ref, width):
-    channels = w_ref.shape[1]
-    parts = [w_ref.at[0:width, :], w_ref.at[width : 2 * width, :]]
-    return parts + cut_out(w_ref.at[2 * width : 3 * width, :])
-
-
-def cut_out(wo_ref):
-    rows, channels = wo_ref.shape
-    return [wo_ref.at[i * channels : (i + 1) * channels, :] for i in range(rows // channels)]
-
-
-def times_out(v, wo_refs):
-    return jnp.concatenate([dot(v, wo_ref[...]) for wo_ref in wo_refs], axis=1)
-
-
-def times_out_t(v, wo_refs):
-    channels = wo_refs[0].shape[1]
-    return sum(
-        dot(v[:, i * channels : (i + 1) * channels], wo_ref[...], COLS)
-        for i, wo_ref in enumerate(wo_refs)
-    )
-
-
 def put_columns(place_ref, span, mine_ref, other_ref, columns):
     per = columns.shape[0] // (NC * NZ)
     rows = mine_ref.shape[0] // NZ
@@ -142,7 +119,7 @@
             place_columns(core, other_ref)
 
 
-def forward_kernel(plans, head_dim, place_ref, *refs):
+def forward_kernel(plans, there_plan, head_dim, place_ref, *refs):
     last_layer = len(plans) == 2
     refs = list(refs)
 
@@ -152,7 +129,9 @@
         return taken
 
     piece_refs = [take(count) for _, count in plans]
-    w_here, w_there, wdt_ref, cx_ref, cbc_ref, head_ref = take(6)
+    [w_here] = take(1)
+    w_there = take(len(there_plan))
+    wdt_ref, cx_ref, cbc_ref, head_ref = take(4)
     w_ref, xn_ref, wbc_ref, z_ref, xp_ref, bc_ref, dt_ref, y_ref, hin_ref, mine_ref, other_ref = take(11)
     if last_layer:
         g_ref, sums_ref, gg_ref = take(3)
@@ -160,20 +139,23 @@
     if last_layer:
         [g_all] = take(1)
     length = z_ref.shape[0]
-    channels = w_ref.shape[1]
+    channels = cx_ref.shape[1]
     state = hst.shape[0]
     span = pl.program_id(0)
-    wz_ref, wx_ref, *wo_refs = cut_weights(w_ref, xn_ref.shape[1])
 
     @pl.when(span == 0)
     def _():
         @pl.when(place_ref[2] == 1)
         def _():
-            pltpu.make_async_copy(w_here.at[0 : w_ref.shape[0], :], w_ref, w_sem).start()
+            pltpu.make_async_copy(w_here, w_ref, w_sem).start()
 
         @pl.when(place_ref[2] == 0)
         def _():
-            pltpu.make_async_copy(w_there.at[0 : w_ref.shape[0], :], w_ref, w_sem).start()
+            for part, (start, k) in zip(w_there, there_plan):
+                rows = part.shape[0]
+                if k is not None:
+                    start = pl.multiple_of(lax.rem(place_ref[3] + NX - k, NX) * rows, 16)
+                pltpu.make_async_copy(part, w_ref.at[pl.ds(start, rows), :], w_sem).start()
 
         if last_layer:
             place_pieces(plans[0][0], place_ref, piece_refs[0], [xn_all])
@@ -183,15 +165,16 @@
         xbuf[0:8, :] = jnp.zeros((8, channels), f32)
         bbuf[0:8, :] = jnp.zeros((8, 2 * state), f32)
         hst[...] = jnp.zeros_like(hst)
-        pltpu.make_async_copy(w_here.at[0 : w_ref.shape[0], :], w_ref, w_sem).wait()
+        pltpu.make_async_copy(w_here, w_ref, w_sem).wait()
 
     here = pl.ds(pl.multiple_of(span * length, length), length)
     xn = xn_all[here, :]
     xn_ref[...] = xn
-    z = dot(xn, wz_ref[...])
-    z_ref[...] = z
-    xp = dot(xn, wx_ref[...])
-    xp_ref[...] = xp
+    zx = dot(xn, w_ref[:, : 2 * channels])
+    z = zx[:, :channels]
+    z_ref[...] = z.astype(bf16)
+    xp = zx[:, channels:]
+    xp_ref[...] = xp.astype(bf16)
     xbuf[8:, :] = xp
     bc = dot(xn, wbc_ref[...], COLS).astype(bf16)
     bc_ref[...] = bc
@@ -231,7 +214,7 @@
     y = jnp.concatenate(tiles, axis=1)
     y = y + dot(c_mat, hin.astype(bf16)) * spread_heads(jnp.exp(cum), channels, head_dim)
     y = y + cx_ref[6:7, :] * xc
-    y_ref[...] = y
+    y_ref[...] = y.astype(bf16)
     tail = spread_heads(jnp.exp(last - cum), channels, head_dim)
     keep = spread_heads(jnp.exp(last), channels, head_dim)
     hst[...] = keep * hin + dot(b_mat, (tail * xs).astype(bf16), ROWS)
@@ -241,7 +224,7 @@
     squares = jnp.sum(gated * gated, axis=1, keepdims=True)
     high = squares.astype(bf16).astype(f32)
     extra = jnp.where(lane == 0, high, jnp.where(lane == 1, squares - high, 0.0)).astype(bf16)
-    mixed = times_out(scaled.astype(bf16), wo_refs).astype(bf16)
+    mixed = dot(scaled.astype(bf16), w_ref[:, 2 * channels :], COLS).astype(bf16)
     put_half(
         place_ref,
         span,
@@ -253,7 +236,7 @@
     if last_layer:
         g = g_all[here, :]
         g_ref[...] = g
-        gg = times_out_t(g, wo_refs)
+        gg = dot(g, w_ref[:, 2 * channels :])
         gg_ref[...] = gg
         products = jnp.sum(gg * scaled, axis=1, keepdims=True)
         both = jnp.where(lane == 0, squares, jnp.where(lane == 1, products, 0.0))
@@ -261,6 +244,7 @@
 
 
 def gate_part(gg, rms, coef, z, y, cx_ref):
+    z, y = z.astype(f32), y.astype(f32)
     norm_gate = cx_ref[5:6, :]
     sz = sigmoid(z)
     silu_z = z * sz
@@ -289,7 +273,7 @@
     tok = first[:, width:].astype(f32)
     rms = tok[:, 0:1] + tok[:, 1:2]
     coef = tok[:, 2:3] + tok[:, 3:4]
-    gg = times_out_t(g, cut_out(wo_ref))
+    gg = dot(g, wo_ref[...])
     dz, dy, gate_out, acc_norm = gate_part(gg, rms, coef, z_ref[...], y_ref[...], cx_ref)
     dz_ref[...] = dz
     dy_ref[...] = dy
@@ -297,28 +281,19 @@
     acc_ref[5:6, :] += acc_norm
 
 
-def last_gate_kernel(inner_all, place_ref, gg_ref, tok_ref, z_ref, y_ref, cx_ref, dz_ref, dy_ref, go_ref, acc_ref):
-    @pl.when(pl.program_id(0) == 0)
-    def _():
-        acc_ref[...] = jnp.zeros_like(acc_ref)
-
-    tok = jnp.transpose(tok_ref[...])
-    rms = lax.rsqrt(tok[:, 0:1] / inner_all + EPS)
-    coef = rms * rms * rms * tok[:, 1:2] / inner_all
-    dz, dy, gate_out, acc_norm = gate_part(gg_ref[...], rms, coef, z_ref[...], y_ref[...], cx_ref)
-    dz_ref[...] = dz
-    dy_ref[...] = dy
-    go_ref[...] = gate_out
-    acc_ref[5:6, :] += acc_norm
-
-
-def scan_kernel(head_dim, place_ref, *refs):
-    (dy_ref, dz_ref, xn_ref, xp_ref, xhalo_ref, bc_ref, bchalo_ref, dt_ref, hin_ref,
-     w_ref, wbc_ref, wdt_ref, cx_ref, cbc_ref, head_ref, pick_ref,
-     dxt_ref, bcmine_ref, bcother_ref, mine_ref, other_ref, acc_ref, acch_ref, shared_ref,
+def scan_kernel(with_gate, head_dim, inner_all, place_ref, *refs):
+    if with_gate:
+        (gg_ref, tok_ref, z_ref, y_ref), refs = refs[:4], refs[4:]
+    else:
+        (dy_ref, dz_ref), refs = refs[:2], refs[2:]
+    (xn_ref, xp_ref, xhalo_ref, bc_ref, bchalo_ref, dt_ref, hin_ref,
+     w_ref, wbc_ref, wdt_ref, cx_ref, cbc_ref, head_ref, pick_ref), refs = refs[:14], refs[14:]
+    if with_gate:
+        (dz_ref, go_ref), refs = refs[:2], refs[2:]
+    (dxt_ref, bcmine_ref, bcother_ref, mine_ref, other_ref, acc_ref, acch_ref, shared_ref,
      accbc, accn, xbuf, bbuf, dubuf, dubbuf, dhst) = refs
     length = xp_ref.shape[0]
-    channels = w_ref.shape[1]
+    channels = cx_ref.shape[1]
     width = xn_ref.shape[1]
     state = dhst.shape[0]
     step_id = pl.program_id(0)
@@ -341,12 +316,23 @@
 
     @pl.when(jnp.logical_not(first_span))
     def _():
-        xbuf[0:8, :] = xhalo_ref[...]
+        xbuf[0:8, :] = xhalo_ref[...].astype(f32)[8:16, :]
         bbuf[0:8, :] = bchalo_ref[...].astype(f32)[8:16, :]
 
-    xbuf[8:, :] = xp_ref[...]
+    xbuf[8:, :] = xp_ref[...].astype(f32)
     bbuf[8:, :] = bc_ref[...].astype(f32)
-    dz_b, dy = dz_ref[...], dy_ref[...]
+    if with_gate:
+        tok = jnp.transpose(tok_ref[...])
+        rms = lax.rsqrt(tok[:, 0:1] / inner_all + EPS)
+        coef = rms * rms * rms * tok[:, 1:2] / inner_all
+        dz_b, dy, gate_out, acc_norm = gate_part(
+            gg_ref[...], rms, coef, z_ref[...], y_ref[...], cx_ref
+        )
+        dz_ref[...] = dz_b
+        go_ref[...] = gate_out
+    else:
+        dz_b, dy = dz_ref[...], dy_ref[...]
+        acc_norm = jnp.zeros((1, channels), f32)
     skip = cx_ref[6:7, :]
 
     pre_x = conv_taps(xbuf, cx_ref[0:4, :], cx_ref[4:5, :], length)
@@ -442,7 +428,7 @@
     dubbuf[length:, :] = d_ub[0:8, :]
     zero = jnp.zeros((1, channels), f32)
     acc_ref[...] += jnp.concatenate(
-        acc_rows + [jnp.sum(d_u, axis=0, keepdims=True), zero, acc_skip, zero], axis=0
+        acc_rows + [jnp.sum(d_u, axis=0, keepdims=True), acc_norm, acc_skip, zero], axis=0
     )
     zero = jnp.zeros((3, d_ub.shape[1]), f32)
     accbc[...] += jnp.concatenate(
@@ -459,7 +445,7 @@
         bcother_ref,
         jnp.transpose(d_bc).astype(bf16),
     )
-    total = dot(dz_b, w_ref[0:width, :], COLS) + dot(dx_b, w_ref[width : 2 * width, :], COLS)
+    total = dot(jnp.concatenate([dz_b, dx_b], axis=1), w_ref[...], COLS)
     total = total + dot(dbc_b, wbc_ref[...]) + dot(dt_b, wdt_ref[...])
     accn[0:1, :] += jnp.sum(total * xn_ref[...].astype(f32), axis=0, keepdims=True)
 
@@ -525,8 +511,9 @@
     )(place, *operands)
 
 
-def run_forward(place, gathered, weights, small, state, head_dim):
-    channels = weights[0].shape[1]
+def run_forward(place, gathered, w, wdt, small, state, head_dim):
+    w_here, w_there, there_plan = w
+    channels = small[0].shape[1]
     width = gathered[0][0][0].shape[1]
     anywhere = pl.BlockSpec(memory_space=pl.ANY)
     tokens = NC * NZ * gathered[0][2][0]
@@ -534,23 +521,23 @@
     last_layer = len(gathered) == 2
     plans = [(cut_plan(*one), len(one[0])) for one in gathered]
     operands = [p for one in gathered for p in one[0]]
-    in_specs = [whole(v.shape) for v in operands] + [anywhere] * 2
-    operands += [*weights, *small]
+    in_specs = [whole(v.shape) for v in operands] + [anywhere] * (1 + len(w_there))
+    operands += [w_here, *w_there, wdt, *small]
     in_specs += [whole(v.shape) for v in operands[len(in_specs) :]]
     shapes = [
-        jax.ShapeDtypeStruct((3 * width, channels), bf16),
+        jax.ShapeDtypeStruct(w_here.shape, bf16),
         jax.ShapeDtypeStruct((tokens, width), bf16),
         jax.ShapeDtypeStruct((2 * state, width), bf16),
-        jax.ShapeDtypeStruct((tokens, channels), f32),
-        jax.ShapeDtypeStruct((tokens, channels), f32),
+        jax.ShapeDtypeStruct((tokens, channels), bf16),
+        jax.ShapeDtypeStruct((tokens, channels), bf16),
         jax.ShapeDtypeStruct((tokens, 2 * state), bf16),
         jax.ShapeDtypeStruct((tokens, LANES), f32),
-        jax.ShapeDtypeStruct((tokens, channels), f32),
+        jax.ShapeDtypeStruct((tokens, channels), bf16),
         jax.ShapeDtypeStruct((spans, state, channels), f32),
         jax.ShapeDtypeStruct((tokens // 2, width + LANES), bf16),
         jax.ShapeDtypeStruct((tokens // 2, width + LANES), bf16),
     ]
-    out_specs = [whole((3 * width, channels)), span_rows(width), whole((2 * state, width))]
+    out_specs = [whole(w_here.shape), span_rows(width), whole((2 * state, width))]
     out_specs += [span_rows(s.shape[1]) for s in shapes[3:8]]
     out_specs.append(pl.BlockSpec((1, state, channels), lambda i, p: (i, 0, 0)))
     out_specs += half_rows(width + LANES, spans, False)
@@ -569,7 +556,7 @@
         ]
         out_specs += [span_rows(width), pl.BlockSpec((8, SPAN), lambda i, p: (0, i)), span_rows(channels)]
         scratch.append(pltpu.VMEM((tokens, width), bf16))
-    kernel = functools.partial(forward_kernel, plans, head_dim)
+    kernel = functools.partial(forward_kernel, plans, there_plan, head_dim)
     return span_call(
         kernel, "layer_forward", spans, place, operands, in_specs, shapes, out_specs, scratch, 20 * 10**9
     )
@@ -577,13 +564,13 @@
 
 def run_gate(place, gathered, z, y, w, cx):
     tokens, channels = z.shape
-    width = w.shape[0] // 3
+    width = w.shape[0]
     spans = tokens // SPAN
     plan, pieces = cut_plan(*gathered), list(gathered[0])
     operands = [*pieces, z, y, w, cx]
     in_specs = [whole(p.shape) for p in pieces]
     in_specs += [span_rows(channels), span_rows(channels)]
-    in_specs += [pl.BlockSpec((width, channels), lambda i, p: (2, 0)), whole(cx.shape)]
+    in_specs += [pl.BlockSpec((width, channels), lambda i, p: (0, 2)), whole(cx.shape)]
     shapes = [
         jax.ShapeDtypeStruct((tokens, width), bf16),
         jax.ShapeDtypeStruct((tokens, channels), bf16),
@@ -599,35 +586,12 @@
     )
 
 
-def run_last_gate(place, gg, sums, z, y, cx, inner_all):
-    tokens, channels = z.shape
-    spans = tokens // SPAN
-    rows = span_rows(channels)
-    shapes = [
-        jax.ShapeDtypeStruct((tokens, channels), bf16),
-        jax.ShapeDtypeStruct((tokens, channels), f32),
-        jax.ShapeDtypeStruct((tokens, channels), bf16),
-        jax.ShapeDtypeStruct((8, channels), f32),
-    ]
-    return span_call(
-        functools.partial(last_gate_kernel, inner_all),
-        "last_gate_backward",
-        spans,
-        place,
-        [gg, sums, z, y, cx],
-        [rows, pl.BlockSpec((8, SPAN), lambda i, p: (0, i)), rows, rows, whole(cx.shape)],
-        shapes,
-        [rows, rows, rows, whole(shapes[3].shape)],
-        [],
-        10**9,
-    )
-
-
-def run_scan(place, dy, dz, xn, xp, bc, dt, hin, weights, small, pick, head_dim):
+def run_scan(place, lead, xn, xp, bc, dt, hin, weights, small, pick, head_dim, inner_all):
     tokens, channels = xp.shape
     state = hin.shape[1]
     width = xn.shape[1]
     spans = tokens // SPAN
+    with_gate = len(lead) == 4
 
     def rev(columns):
         return pl.BlockSpec((SPAN, columns), lambda i, p: (spans - 1 - i, 0))
@@ -638,19 +602,21 @@
             (rows, columns), lambda i, p: (jnp.maximum((spans - 1 - i) * per - 1, 0), 0)
         )
 
-    operands = [dy, dz, xn, xp, xp, bc, bc, dt, hin, *weights, *small, pick]
-    in_specs = [
-        rev(channels),
-        rev(channels),
+    operands = [*lead, xn, xp, xp, bc, bc, dt, hin, *weights, *small, pick]
+    in_specs = [rev(channels)] * 2
+    if with_gate:
+        tok = pl.BlockSpec((8, SPAN), lambda i, p: (0, spans - 1 - i))
+        in_specs = [rev(channels), tok, rev(channels), rev(channels)]
+    in_specs += [
         rev(width),
         rev(channels),
-        halo(channels, 8),
+        halo(channels, 16),
         rev(2 * state),
         halo(2 * state, 16),
         rev(LANES),
         pl.BlockSpec((1, state, channels), lambda i, p: (spans - 1 - i, 0, 0)),
     ]
-    in_specs.append(whole((2 * width, channels)))
+    in_specs.append(whole((width, 2 * channels)))
     in_specs += [whole(v.shape) for v in operands[len(in_specs) :]]
     shapes = [
         jax.ShapeDtypeStruct((tokens, channels + LANES), bf16),
@@ -665,6 +631,9 @@
     out_specs = [rev(channels + LANES), whole(shapes[1].shape), whole(shapes[2].shape)]
     out_specs += half_rows(width, spans, True)
     out_specs += [whole(s.shape) for s in shapes[5:]]
+    if with_gate:
+        shapes = [jax.ShapeDtypeStruct((tokens, channels), bf16)] * 2 + shapes
+        out_specs = [rev(channels)] * 2 + out_specs
     scratch = [
         pltpu.VMEM((8, 2 * state), f32),
         pltpu.VMEM((8, width), f32),
@@ -674,48 +643,65 @@
         pltpu.VMEM((SPAN + 8, 2 * state), f32),
         pltpu.VMEM((state, channels), f32),
     ]
-    kernel = functools.partial(scan_kernel, head_dim)
+    kernel = functools.partial(scan_kernel, with_gate, head_dim, inner_all)
     return span_call(
         kernel, "scan_backward", spans, place, operands, in_specs, shapes, out_specs, scratch, 28 * 10**9
     )
 
 
-def weight_kernel(pairs, *refs):
-    lefts, rights, out_ref = refs[: len(pairs)], refs[len(pairs) : -1], refs[-1]
-    at = 0
-    for left_ref, right_ref in zip(lefts, rights):
-        columns = right_ref.shape[1]
-        out_ref[:, at : at + columns] = dot(left_ref[...], right_ref[...], ROWS).astype(bf16)
-        at += columns
-
-
-def weight_products(pairs):
+def weight_kernel(n_pairs, split, place_ref, *refs):
+    lefts, rights, outs = refs[:n_pairs], refs[n_pairs : 2 * n_pairs], refs[2 * n_pairs :]
+
+    def write(out_ref):
+        at = 0
+        for left_ref, right_ref in zip(lefts, rights):
+            columns = right_ref.shape[1]
+            out_ref[:, at : at + columns] = dot(left_ref[...], right_ref[...], ROWS).astype(bf16)
+            at += columns
+
+    if not split:
+        write(outs[0])
+        return
+    for k, out_ref in enumerate(outs):
+        pl.when(pl.program_id(0) == k)(functools.partial(write, out_ref))
+
+
+def weight_products(place, pairs, split=True):
     tokens = pairs[0][0].shape[0]
     rows = max(left.shape[1] for left, _ in pairs)
     block = rows // 4
+
+    def at(i, p):
+        return lax.rem(p[3] + i, NX) if split else i
+
     lefts, rights, columns = [], [], []
     for left, right in pairs:
         quarter = left.shape[1] == block
-        lefts.append(pl.BlockSpec((tokens, block), (lambda i: (0, 0)) if quarter else (lambda i: (0, i))))
+        cut, uncut = (lambda i, p: (0, at(i, p))), (lambda i, p: (0, 0))
+        lefts.append(pl.BlockSpec((tokens, block), uncut if quarter else cut))
         wide = block if quarter else right.shape[1]
-        rights.append(pl.BlockSpec((tokens, wide), (lambda i: (0, i)) if quarter else (lambda i: (0, 0))))
+        rights.append(pl.BlockSpec((tokens, wide), cut if quarter else uncut))
         columns.append(wide)
-    return pl.pallas_call(
-        functools.partial(weight_kernel, pairs_of(columns)),
-        grid=(4,),
-        in_specs=lefts + rights,
-        out_specs=pl.BlockSpec((block, sum(columns)), lambda i: (i, 0)),
-        out_shape=jax.ShapeDtypeStruct((rows, sum(columns)), bf16),
+    columns = sum(columns)
+    if split:
+        out_specs = [whole((block, columns))] * 4
+        shapes = [jax.ShapeDtypeStruct((block, columns), bf16)] * 4
+    else:
+        out_specs = [pl.BlockSpec((block, columns), lambda i, p: (i, 0))]
+        shapes = [jax.ShapeDtypeStruct((rows, columns), bf16)]
+    out = pl.pallas_call(
+        functools.partial(weight_kernel, len(pairs), split),
+        grid_spec=pltpu.PrefetchScalarGridSpec(
+            num_scalar_prefetch=1, grid=(4,), in_specs=lefts + rights, out_specs=out_specs
+        ),
+        out_shape=shapes,
         compiler_params=pltpu.CompilerParams(vmem_limit_bytes=VMEM_BYTES),
         cost_estimate=pl.CostEstimate(
-            flops=2 * tokens * rows * sum(columns), bytes_accessed=8 * 10**6, transcendentals=0
+            flops=2 * tokens * rows * columns, bytes_accessed=8 * 10**6, transcendentals=0
         ),
         name="weight_products",
-    )(*[left for left, _ in pairs], *[right for _, right in pairs])
-
-
-def pairs_of(columns):
-    return tuple(columns)
+    )(place, *[left for left, _ in pairs], *[right for _, right in pairs])
+    return out if split else out[0]
 
 
 SIZES = (4, 2, 2, 2, 4)
@@ -760,6 +746,23 @@
     return jnp.where(core == yh, v, traded(v))
 
 
+def quarter_of_half(v):
+    x = position()[0]
+    rows = v.shape[0] // 2 // NX
+    return traded(lax.dynamic_slice_in_dim(v, x * rows, rows, 0))
+
+
+def traded_by_x(v, quarter, ready):
+    half = v.shape[0] // 2
+    parts, plan = [quarter], [(None, 0)]
+    for k in range(1, NX):
+        parts.append(
+            send(quarter, lambda x, yl, c, yh, z, k=k: (x + k, yl, c, yh, z), lambda x, yl, c, yh, z: c != yh)
+        )
+        plan.append((None, k))
+    return parts + [traded(after(v[half:], ready))], plan + [(half, None)]
+
+
 def position():
     dp, tensor = lax.axis_index("dp"), lax.axis_index("tensor")
     return dp // (NYL * NC), dp // NC % NYL, dp % NC, tensor // NZ, tensor % NZ
@@ -813,7 +816,7 @@
 def scatter_with_sum(mine, other, shared, meanwhile):
     half = mine.shape[0]
     rows = half // NZ
-    got = send_core(jnp.concatenate([other, shared], axis=0))
+    got = after(send_core(jnp.concatenate([other, shared], axis=0)), *meanwhile)
     blocks = fold(mine, got[:half])
     total_shared = shared.astype(f32) + got[half:].astype(f32)
     packed = total_shared.astype(bf16)
@@ -822,7 +825,7 @@
         got = send_z(jnp.concatenate([blocks[k].astype(bf16), packed], axis=0), k)
         total = total + got[:rows].astype(f32)
         total_shared = total_shared + got[rows:].astype(f32)
-    return after(total, *meanwhile), total_shared
+    return total, total_shared
 
 
 def sum_members(v):
@@ -833,8 +836,12 @@
     return total
 
 
-def sum_far(v):
-    far = send(v, lambda x, yl, c, yh, z: (x, yl, c, yh + 1, z), lambda x, yl, c, yh, z: c != yh)
+def send_far(v):
+    return send(v, lambda x, yl, c, yh, z: (x, yl, c, yh + 1, z), lambda x, yl, c, yh, z: c != yh)
+
+
+def sum_far(v, far=None):
+    far = send_far(v) if far is None else far
     return (v.astype(f32) + far.astype(f32)).astype(bf16)
 
 
@@ -852,14 +859,18 @@
     return (part.astype(f32) + beside.astype(f32)).astype(bf16)
 
 
-def sum_x(v):
+def sum_x(blocks):
+    total = blocks[0].astype(f32)
+    for k in range(1, NX):
+        got = send(blocks[k], lambda x, yl, c, yh, z, k=k: (x + k, yl, c, yh, z))
+        total = total + got.astype(f32)
+    return total.astype(bf16)
+
+
+def cut_x(v):
     x = position()[0]
     rows = v.shape[0] // NX
-    total = lax.dynamic_slice_in_dim(v, x * rows, rows, 0).astype(f32)
-    for k in range(1, NX):
-        block = lax.dynamic_slice_in_dim(v, (x + k) % NX * rows, rows, 0)
-        total = total + send(block, lambda x, yl, c, yh, z, k=k: (x + k, yl, c, yh, z)).astype(f32)
-    return total.astype(bf16)
+    return [lax.dynamic_slice_in_dim(v, (x + k) % NX * rows, rows, 0) for k in range(NX)]
 
 
 def collect_x(part):
@@ -1067,10 +1078,13 @@
     inner_all = channels * members
     rows = hidden_in.shape[1]
     bc_rows = both // members
-    _, _, core, yh, z = position()
+    x, _, core, yh, z = position()
     stays = core == yh
-    place = jnp.stack([core, z, stays]).astype(jnp.int32)
+    place = jnp.stack([core, z, stays, x]).astype(jnp.int32)
     full = jax.ShapeDtypeStruct((rows, width), f32)
+
+    def pack_weights(layer):
+        return jnp.concatenate([w_z[layer], w_x[layer], w_out[layer].T], axis=1)
 
     bc_t = jnp.swapaxes(w_bc, 1, 2)
     dt_t = jnp.pad(jnp.swapaxes(w_dt, 1, 2), ((0, 0), (0, 8 - heads), (0, 0)))
@@ -1086,22 +1100,15 @@
     low = (little - high.astype(f32)).astype(bf16)
     lines = pad_to(jnp.concatenate([high, low], axis=1), layers * 8, width)
     packed = jnp.concatenate([hidden_in[0], bc_t[0], dt_t.reshape(layers * 8, width), lines], axis=0)
-    packed = trade_places(packed)
+    w0 = pack_weights(0)
+    quarter = quarter_of_half(w0)
+    packed = after(trade_places(packed), quarter)
     lines = packed[packed.shape[0] - layers * 8 :].astype(f32)
     little = lines[:, : channels + LANES] + lines[:, channels + LANES : 2 * (channels + LANES)]
     little = little.reshape(layers, 8, channels + LANES)
 
-    def blocks_below(v):
-        return [v[:, i * channels : (i + 1) * channels] for i in range(width // channels)]
-
-    def pack_weights(layer):
-        return jnp.concatenate([w_z[layer], w_x[layer], *blocks_below(w_out[layer])], axis=0)
-
+    w0 = w0, *traded_by_x(w0, quarter, packed)
     grads = jnp.concatenate([grad_out[0], bc_t[1]], axis=0)
-    w0 = jnp.concatenate([pack_weights(0), *blocks_below(grads)], axis=0)
-    w0 = w0, traded(after(w0, packed))
-    there = w0[1][3 * width :].reshape(-1, *grads.shape[:1], channels)
-    grads_here = jnp.where(stays, grads, jnp.concatenate(list(there), axis=1))
 
     [sent] = row_call(
         first_kernel,
@@ -1118,13 +1125,13 @@
     channel_head = jnp.arange(channels) // head_dim
     pick = (channel_head[:, None] == jnp.arange(LANES)[None, :]).astype(f32)
 
-    out0 = run_forward(place, [gathered0], (*w0, wdt[0]), smalls[0], state, head_dim)
+    out0 = run_forward(place, [gathered0], w0, wdt[0], smalls[0], state, head_dim)
     w0, xn0, wbc0, z0, xp0, bc0, dt0, y0, hin0, mine, other = out0
-    gathered_grad = gather(after(grads, *gathered0[0]), (rows, bc_rows), grads_here)
+    gathered_grad = gather(after(grads, *gathered0[0]), (rows, bc_rows), trade_places(grads))
     grad_held = gathered_grad[0][0]
     terms = scatter((mine, after(other, *gathered_grad[0][2::2])))
     w1 = pack_weights(1)
-    w1 = w1, traded(after(w1, terms[0]))
+    w1 = w1, [traded(after(w1, terms[0]))], [(0, None)]
     res1, mixed0, rms0, normed1 = row_call(
         functools.partial(middle_kernel, inner_all),
         "middle_norm",
@@ -1133,21 +1140,23 @@
     )
     gathered1 = gather(normed1, (rows,))
     out1 = run_forward(
-        place, [gathered1, gathered_grad], (*w1, wdt[1]), smalls[1], state, head_dim
+        place, [gathered1, gathered_grad], w1, wdt[1], smalls[1], state, head_dim
     )
     w1, xn1, wbc1, z1, xp1, bc1, dt1, y1, hin1, mine, other, grad_rows1, sums, gg1 = out1
     sums = sum_members(sums)
 
     home = fold(mine, send_core(other))
-    dz1, dy1, go1, acc_gate1 = run_last_gate(place, gg1, sums, z1, y1, smalls[1][0], inner_all)
-    early1 = sum_far(weight_products([(xn1, dz1), (go1, grad_rows1)]))
-    dy1 = after(dy1, *home)
+    sums = after(sums, *home)
     home = home[:1] + [send_z(home[k].astype(bf16), k) for k in range(1, NZ)]
     back1 = run_scan(
-        place, dy1, dz1, xn1, xp1, bc1, dt1, hin1, (w1, wbc1, wdt[1]), smalls[1], pick, head_dim
-    )
-    dxt1, *bc_halves, mine, other, acc1, acch1, shared1 = back1
-    terms = scatter((mine, after(other, early1, *home)), bc_halves)
+        place, (gg1, sums, z1, y1), xn1, xp1, bc1, dt1, hin1, (w1, wbc1, wdt[1]), smalls[1], pick, head_dim,
+        inner_all,
+    )
+    dz1, go1, dxt1, *bc_halves, mine, other, acc1, acch1, shared1 = back1
+    terms = scatter((mine, after(other, *home)), bc_halves)
+    early1 = weight_products(place, [(xn1, after(dz1, terms[0])), (go1, grad_rows1)], split=False)
+    terms[3] = after(terms[3], early1)
+    early1_far = send_far(early1)
     [hidden_out] = row_call(
         functools.partial(last_kernel, inner_all),
         "last_output",
@@ -1162,7 +1171,6 @@
         [full, jax.ShapeDtypeStruct((rows, width + LANES), bf16)],
     )
     gathered_back = gather(sent, (rows,))
-    early1 = sum_x(halve(after(early1, sent)))
 
     bc_at = channels + bc_rows
 
@@ -1173,14 +1181,17 @@
 
     dxt1 = with_bc(dxt1, sum(v[:, width:].astype(f32) for v in terms))
 
+    early1 = halve(sum_far(early1, after(early1_far, sent)))
     z0 = after(z0, early1)
+    early1 = sum_x(cut_x(early1))
     grad_rows0, dz0, dy0, go0, acc_gate0 = run_gate(place, gathered_back, z0, y0, w0, smalls[0][0])
-    early = weight_products([(xn0, dz0), (go0, grad_rows0), (xn1, dxt1)])
-    dy0 = after(dy0, early)
+    dz0 = after(dz0, early1)
+    early = weight_products(place, [(xn0, dz0), (go0, grad_rows0), (xn1, dxt1)])
+    dy0 = after(dy0, *early)
     early = sum_x(early)
     early1 = sum_beside(after(early1, dz0))
     back0 = run_scan(
-        place, dy0, dz0, xn0, xp0, bc0, dt0, hin0, (w0, wbc0, wdt[0]), smalls[0], pick, head_dim
+        place, (dy0, dz0), xn0, xp0, bc0, dt0, hin0, (w0, wbc0, wdt[0]), smalls[0], pick, head_dim, inner_all
     )
     dxt0, *bc_halves, mine, other, acc0, acch0, shared0 = back0
     terms = scatter((mine, other))
@@ -1193,18 +1204,18 @@
     outputs = trade_places(outputs).astype(f32)
 
     shared = jnp.concatenate([shared0, shared1], axis=0)
-    bc_sum, shared = scatter_with_sum(*bc_halves, shared, (early, early1))
+    bc_sum, shared = scatter_with_sum(*bc_halves, shared, (early,))
     tiny = jnp.concatenate(
-        [(acc0 + acc_gate0).reshape(-1), (acc1 + acc_gate1).reshape(-1), acch0[0:2].reshape(-1), acch1[0:2].reshape(-1)]
+        [(acc0 + acc_gate0).reshape(-1), acc1.reshape(-1), acch0[0:2].reshape(-1), acch1[0:2].reshape(-1)]
         + [shared.reshape(-1)]
     )
     tiny_at = bc_at + bc_rows
     tiny_lanes = channels + LANES - tiny_at
     tiny_size = tiny.shape[0]
     tiny = jnp.pad(tiny, (0, width * tiny_lanes - tiny_size)).reshape(width, tiny_lanes)
-    late = weight_products([(xn0, with_bc(dxt0, bc_sum))])
-    late = late + jnp.pad(tiny, ((0, 0), (tiny_at, 0))).astype(bf16)
-    late = sum_x(late)
+    tiny = jnp.pad(tiny, ((0, 0), (tiny_at, 0))).astype(bf16)
+    late = weight_products(place, [(xn0, with_bc(dxt0, bc_sum))])
+    late = sum_x([v + t for v, t in zip(late, cut_x(tiny))])
     halves = collect(after(early1, late))
     g_wz, g_wo = write_sums(place, halves, True, [(0, "rows", 1, None), (channels, "blocks", 1, None)])
     late = sum_beside(halve(sum_far(late)))

time: 595 us -> 597 us (level)
  the two profiles are of different devices: /device:TPU:31 before, /device:TPU:1 now
where the time goes in v2:
time: 597 us; the launch traced here: 586 us
  Pallas kernels  173 us (29%)
  waiting for transfers between devices  158 us (26%)
  starting transfers between devices  154 us (26%)
  local copies, waits for them, and re-layouts  49.2 us (8%)
  other arithmetic  48.1 us (8%)
    ppermute x92, waiting for transfers between devices, send(): return lax.ppermute(v, ('dp', 'tensor'), pairs)  158 us
    ppermute x92, starting transfers between devices, send(): return lax.ppermute(v, ('dp', 'tensor'), pairs)  154 us
    pallas_call x5, Pallas kernels, span_call(): pl.pallas_call(kernel, grid_spec=pltpu.PrefetchScalarGridSpec(num_scalar_...  117 us
    pallas_call x3, Pallas kernels, weight_products(): pl.pallas_call(functools.partial(weight_kernel, len(pairs), split), grid_...  25.8 us
    unnamed x185, local copies, waits for them, and re-layouts  21.5 us
    pallas_call x5, Pallas kernels, row_call(): pl.pallas_call(kernel, grid=(1,), in_specs=[pl.BlockSpec((rows, v.shape[1...  15.6 us
    pallas_call x3, Pallas kernels, write_sums(): pl.pallas_call(functools.partial(write_kernel, plan, by_half, len(kept)),...  14.8 us
  transfers between devices with their start and end apart: 92, of which 28 were waited for; matrix products, arithmetic and copies ran while one was open for 10% of the time, Pallas kernels for 23%

profile of v2, /device:TPU:1, one launch (start us, length us, event | category | flops | bytes accessed | tf_op | source)
XLA Modules:
  0.0 585.7 jit_solution(6737580180922324889)
XLA Ops:
  5.6 3.7 slice_bitcast_fusion
  10.5 6.2 %collective-permute-start.1 = (bf16[192,1152]{1,0:T(8,128)(2,1)}, bf16[192,1152]{1,0:T(8,128)(2,1)}, u32[]{:S(2)}, u32[]{:S(2)}) collective-permute-start(bf16[192,1152]{1,0:T(8,128)(2,1)} %constant_dynamic-slice_fusion.3), channel_id=1, source_target_pairs={{4,8},{5,9},{6,10},{7,11},{8,4},{9,5},{10,6},{11,7},{20,24},{21,25... | collective-permute-start | bytes 1327112 | tf_op jit(solution)/shard_map/ppermute | solution.py:725
  30.0 7.0 %collective-permute-done = bf16[192,1536]{1,0:T(8,128)(2,1)} collective-permute-done((bf16[192,1536]{1,0:T(8,128)(2,1)}, bf16[192,1536]{1,0:T(8,128)(2,1)}, u32[]{:S(2)}, u32[]{:S(2)}) %collective-permute-start) | collective-permute-done | bytes 589856 | tf_op jit(solution)/shard_map/ppermute | solution.py:725
  50.3 5.0 collective-permute-done.3.refs_2_
  55.3 3.8 collective-permute-done.5.refs_4_
  61.8 4.6 collective-permute-start.10
  73.0 5.7 collective-permute-start.13
  80.9 3.5 collective-permute-start.15
  85.3 23.1 %layer_forward.2 = (bf16[1536,1152]{1,0:T(8,128)(2,1)}, bf16[1024,1536]{1,0:T(8,128)(2,1)}, bf16[256,1536]{1,0:T(8,128)(2,1)}, bf16[1024,384]{1,0:T(8,128)(2,1)}...) custom-call(s32[4]{0:T(128)} %pad_add_fusion.2.place_ref, ...), custom_call_target="tpu_custom_call" | custom-call | flops 20000000000 | bytes 26501120 | tf_op jit(solution)/shard_map/layer_forward/pallas_call | solution.py:496
  116.9 2.9 collective-permute-start.32
  119.8 4.1 collective-permute-start.27
  128.5 38.0 %collective-permute-done.27 = bf16[160,1536]{1,0:T(8,128)(2,1)S(1)} collective-permute-done((bf16[160,1536]{1,0:T(8,128)(2,1)S(1)}, bf16[160,1536]{1,0:T(8,128)(2,1)S(1)}, u32[]{:S(2)}, u32[]{:S(2)}) %collective-permute-start.27) | collective-permute-done | bytes 491552 | tf_op jit(solution)/shard_map/ppermute | solution.py:725
  168.2 3.3 middle_norm.1
  176.3 7.1 %collective-permute-done.21.refs_2_ = bf16[128,1536]{1,0:T(8,128)(2,1)S(1)} collective-permute-done((bf16[128,1536]{1,0:T(8,128)(2,1)}, bf16[128,1536]{1,0:T(8,128)(2,1)S(1)}, u32[]{:S(2)}, u32[]{:S(2)}) %collective-permute-start.21) | collective-permute-done | bytes 393248 | tf_op jit(solution)/shard_map/ppermute | solution.py:725
  186.3 5.3 collective-permute-done.25.refs_6_
  195.1 27.0 %layer_forward.3 = (bf16[1536,1152]{1,0:T(8,128)(2,1)}, bf16[1024,1536]{1,0:T(8,128)(2,1)}, bf16[256,1536]{1,0:T(8,128)(2,1)}, bf16[1024,384]{1,0:T(8,128)(2,1)}...) custom-call(s32[4]{0:T(128)} %pad_add_fusion.2.place_ref, ...), custom_call_target="tpu_custom_call" | custom-call | flops 20000000000 | bytes 34398208 | tf_op jit(solution)/shard_map/layer_forward/pallas_call | solution.py:496
  222.7 3.3 collective-permute-done.33
  227.6 3.3 collective-permute-start.35
  241.8 29.5 %scan_backward.2 = (bf16[1024,384]{1,0:T(8,128)(2,1)}, bf16[1024,384]{1,0:T(8,128)(2,1)}, bf16[1024,512]{1,0:T(8,128)(2,1)}, bf16[512,256]{1,0:T(8,128)(2,1)}, b...) custom-call(s32[4]{0:T(128)} %pad_add_fusion.2.place_ref, ...), custom_call_target="tpu_custom_call" | custom-call | flops 28000000000 | bytes 21512192 | tf_op jit(solution)/shard_map/scan_backward/pallas_call | solution.py:496
  274.2 3.5 collective-permute-done.42
  281.5 8.1 %weight_products.3 = bf16[1536,768]{1,0:T(8,128)(2,1)} custom-call(s32[4]{0:T(128)} %pad_add_fusion.2.place_ref, bf16[1024,1536]{1,0:T(8,128)(2,1)} %get-tuple-element.119.refs_4_.refs_0_.refs_2_, bf16[1024,384]{1,0:T(8,128)(2,1)} %get-tuple-element.131.refs_1_, bf16[1024,384]{1,0:T(8,128)(2,1)} %get-tuple-element.133.refs_2_, ...), custom_call_target="tpu_custom_call" | custom-call | flops 2415919104 | bytes 8000000 | tf_op jit(solution)/shard_map/weight_products/pallas_call | solution.py:692
  289.7 4.1 collective-permute-start.53
  296.6 9.8 %collective-permute-done.45.c_ref = bf16[128,1792]{1,0:T(8,128)(2,1)S(1)} collective-permute-done((bf16[128,1792]{1,0:T(8,128)(2,1)S(1)}, bf16[128,1792]{1,0:T(8,128)(2,1)S(1)}, u32[]{:S(2)}, u32[]{:S(2)}) %collective-permute-start.45) | collective-permute-done | bytes 458784 | tf_op jit(solution)/shard_map/ppermute | solution.py:725
  308.2 7.8 %collective-permute-done.43.a_ref = bf16[128,1792]{1,0:T(8,128)(2,1)S(1)} collective-permute-done((bf16[128,1792]{1,0:T(8,128)(2,1)S(1)}, bf16[128,1792]{1,0:T(8,128)(2,1)S(1)}, u32[]{:S(2)}, u32[]{:S(2)}) %collective-permute-start.43) | collective-permute-done | bytes 458784 | tf_op jit(solution)/shard_map/ppermute | solution.py:725
  316.7 4.0 between_layers.1
  327.6 3.4 collective-permute-start.46
  334.5 12.0 %collective-permute-start.48 = (bf16[128,1664]{1,0:T(8,128)(2,1)S(1)}, bf16[128,1664]{1,0:T(8,128)(2,1)S(1)}, u32[]{:S(2)}, u32[]{:S(2)}) collective-permute-start(bf16[128,1664]{1,0:T(8,128)(2,1)S(1)} %collective-permute-done.47.refs_2_), channel_id=1, source_target_pairs={{0,8},{1,9},{2,10},{3,11},{4,12},{5,13},{6,14},{7,15},{8,0},{9,1},... | collective-permute-start | bytes 1277960 | tf_op jit(solution)/shard_map/ppermute | solution.py:725
  353.3 8.4 %gate_backward.1 = (bf16[1024,1536]{1,0:T(8,128)(2,1)}, bf16[1024,384]{1,0:T(8,128)(2,1)}, f32[1024,384]{1,0:T(8,128)}, bf16[1024,384]{1,0:T(8,128)(2,1)}, f32[8,384]{1,0:T(8,128)}) custom-call(s32[4]{0:T(128)} %pad_add_fusion.2.place_ref, bf16[128,1664]{1,0:T(8,128)(2,1)} %get-tuple-element.139.refs_0_, bf16[128,1664]{1,0:T(8,128)(2,1)} %collective-permute-done.46.refs_1_, ...), custom_call_target="tpu_custom_call" | custom-call | flops 6000000000 | bytes 14835712 | tf_op jit(solution)/shard_map/gate_backward/pallas_call | solution.py:496
  361.8 3.2 collective-permute-done.56
  365.6 11.2 %weight_products.4 = (bf16[384,1280]{1,0:T(8,128)(2,1)}, bf16[384,1280]{1,0:T(8,128)(2,1)}, bf16[384,1280]{1,0:T(8,128)(2,1)}, bf16[384,1280]{1,0:T(8,128)(2,1)}) custom-call(s32[4]{0:T(128)} %pad_add_fusion.2.place_ref, bf16[1024,1536]{1,0:T(8,128)(2,1)} %get-tuple-element.146.refs_0_.refs_2_, bf16[1024,384]{1,0:T(8,128)(2,1)} %get-tuple-element.147.refs_1_, ...), custom_call_target="tpu_custom_call" | custom-call | flops 4026531840 | bytes 8000000 | tf_op jit(solution)/shard_map/weight_products/pallas_call | solution.py:692
  380.8 29.2 %scan_backward.3 = (bf16[1024,512]{1,0:T(8,128)(2,1)}, bf16[512,256]{1,0:T(8,128)(2,1)}, bf16[512,256]{1,0:T(8,128)(2,1)}, bf16[512,1536]{1,0:T(8,128)(2,1)}, bf...) custom-call(s32[4]{0:T(128)} %pad_add_fusion.2.place_ref, ...), custom_call_target="tpu_custom_call" | custom-call | flops 28000000000 | bytes 19120128 | tf_op jit(solution)/shard_map/scan_backward/pallas_call | solution.py:496
  414.7 8.4 %collective-permute-done.65 = bf16[384,1280]{1,0:T(8,128)(2,1)} collective-permute-done((bf16[384,1280]{1,0:T(8,128)(2,1)}, bf16[384,1280]{1,0:T(8,128)(2,1)}, u32[]{:S(2)}, u32[]{:S(2)}) %collective-permute-start.65) | collective-permute-done | bytes 983072 | tf_op jit(solution)/shard_map/ppermute | solution.py:725
  427.0 3.8 collective-permute-start.68
  434.3 4.3 collective-permute-start.80
  442.9 6.4 %weight_products.5 = (bf16[384,512]{1,0:T(8,128)(2,1)}, bf16[384,512]{1,0:T(8,128)(2,1)}, bf16[384,512]{1,0:T(8,128)(2,1)}, bf16[384,512]{1,0:T(8,128)(2,1)}) custom-call(s32[4]{0:T(128)} %pad_add_fusion.2.place_ref, bf16[1024,1536]{1,0:T(8,128)(2,1)} %get-tuple-element.146.refs_0_.refs_2_, bf16[1024,512]{1,0:T(8,128)(2,1)} %pad_add_fusion.refs_1_), custom_call_target="tpu_custom_call" | custom-call | flops 1610612736 | bytes 8000000 | tf_op jit(solution)/shard_map/weight_products/pallas_call | solution.py:692
  462.5 4.6 collective-permute-done.70
  467.1 8.0 %collective-permute-done.71 = bf16[384,512]{1,0:T(8,128)(2,1)} collective-permute-done((bf16[384,512]{1,0:T(8,128)(2,1)}, bf16[384,512]{1,0:T(8,128)(2,1)}, u32[]{:S(2)}, u32[]{:S(2)}) %collective-permute-start.71) | collective-permute-done | bytes 393248 | tf_op jit(solution)/shard_map/ppermute | solution.py:725
  489.0 4.8 collective-permute-done.89
  494.7 10.6 %collective-permute-done.82 = bf16[192,1280]{1,0:T(8,128)(2,1)S(1)} collective-permute-done((bf16[192,1280]{1,0:T(8,128)(2,1)S(1)}, bf16[192,1280]{1,0:T(8,128)(2,1)S(1)}, u32[]{:S(2)}, u32[]{:S(2)}) %collective-permute-start.82) | collective-permute-done | bytes 491552 | tf_op jit(solution)/shard_map/ppermute | solution.py:725
  511.4 3.5 outputs.1
  514.9 5.5 collective-permute-start.62
  522.6 10.2 %collective-permute-done.83 = bf16[192,1280]{1,0:T(8,128)(2,1)S(1)} collective-permute-done((bf16[192,1280]{1,0:T(8,128)(2,1)S(1)}, bf16[192,1280]{1,0:T(8,128)(2,1)S(1)}, u32[]{:S(2)}, u32[]{:S(2)}) %collective-permute-start.83) | collective-permute-done | bytes 491552 | tf_op jit(solution)/shard_map/ppermute | solution.py:725
  535.9 6.9 %collective-permute-done.85 = bf16[192,1280]{1,0:T(8,128)(2,1)S(1)} collective-permute-done((bf16[192,1280]{1,0:T(8,128)(2,1)S(1)}, bf16[192,1280]{1,0:T(8,128)(2,1)S(1)}, u32[]{:S(2)}, u32[]{:S(2)}) %collective-permute-start.85) | collective-permute-done | bytes 491552 | tf_op jit(solution)/shard_map/ppermute | solution.py:725
  544.4 6.3 %collective-permute-start.86 = (bf16[4,192,1280]{2,1,0:T(8,128)(2,1)S(1)}, bf16[4,192,1280]{2,1,0:T(8,128)(2,1)S(1)}, u32[]{:S(2)}, u32[]{:S(2)}) collective-permute-start(bf16[4,192,1280]{2,1,0:T(8,128)(2,1)S(1)} %bitcast_dynamic-update-slice_fusion.here_ref), channel_id=1, source_target_pairs={{0,8},{1,9},{2,10},{3,11},{4,12},{5,13},{6,14},{7,15},{8,0},{9,1},... | collective-permute-start | bytes 5898248 | tf_op jit(solution)/shard_map/ppermute | solution.py:725
  551.0 4.5 collective-permute-start.79
  558.0 4.7 write_sums.3
  563.9 6.3 %write_sums.4 = (f32[2,4,2,192,384]{4,3,2,1,0:T(8,128)}, f32[2,384,1536]{2,1,0:T(8,128)}, f32[2,4,2,192,384]{4,3,2,1,0:T(8,128)}, f32[1,4,2,192,128]{4,3,2,1,0:T(8,128)}) custom-call(s32[4]{0:T(128)} %pad_add_fusion.2.place_ref, bf16[4,192,1280]{2,1,0:T(8,128)(2,1)} %copy-done.2, ...), custom_call_target="tpu_custom_call", output_to_operand_aliasing={{0}: (3, {}), {1}: (4, {})} | custom-call | tf_op jit(solution)/shard_map/write_sums/pallas_call | solution.py:947
  571.1 3.8 write_sums.5
  (460 shorter events, 189.0 us)
Async XLA Ops:
  10.5 28.7 %collective-permute-start.1 = (bf16[192,1152]{1,0:T(8,128)(2,1)}, bf16[192,1152]{1,0:T(8,128)(2,1)}, u32[]{:S(2)}, u32[]{:S(2)}) collective-permute-start(bf16[192,1152]{1,0:T(8,128)(2,1)} %constant_dynamic-slice_fusion.3), channel_id=1, source_target_pairs={{4,8},{5,9},{6,10},{7,11},{8,4},{9,5},{10,6},{11,7},{20,24},{21,25... | collective-permute-start | bytes 1327112 | tf_op jit(solution)/shard_map/ppermute | solution.py:725
  39.3 45.2 %collective-permute-start.12 = (bf16[768,1152]{1,0:T(8,128)(2,1)S(1)}, bf16[768,1152]{1,0:T(8,128)(2,1)}, u32[]{:S(2)}, u32[]{:S(2)}) collective-permute-start(bf16[768,1152]{1,0:T(8,128)(2,1)S(1)} %copy-done.15), channel_id=1, source_target_pairs={{4,8},{5,9},{6,10},{7,11},{8,4},{9,5},{10,6},{11,7},{20,24},{21,25... | collective-permute-start | bytes 5308424 | tf_op jit(solution)/shard_map/ppermute | solution.py:725
  61.8 16.9 %collective-permute-start.10 = (bf16[192,1152]{1,0:T(8,128)(2,1)}, bf16[192,1152]{1,0:T(8,128)(2,1)S(1)}, u32[]{:S(2)}, u32[]{:S(2)}) collective-permute-start(bf16[192,1152]{1,0:T(8,128)(2,1)} %collective-permute-done.1.refs_9_), channel_id=1, source_target_pairs={{4,68},{5,69},{6,70},{7,71},{8,72},{9,73},{10,74},{11,75},{20,84},... | collective-permute-start | bytes 1327112 | tf_op jit(solution)/shard_map/ppermute | solution.py:725
  66.4 14.5 %collective-permute-start.11 = (bf16[192,1152]{1,0:T(8,128)(2,1)}, bf16[192,1152]{1,0:T(8,128)(2,1)}, u32[]{:S(2)}, u32[]{:S(2)}) collective-permute-start(bf16[192,1152]{1,0:T(8,128)(2,1)} %collective-permute-done.1.refs_9_), channel_id=1, source_target_pairs={{4,100},{5,101},{6,102},{7,103},{8,104},{9,105},{10,106},{11,107},... | collective-permute-start | bytes 1327112 | tf_op jit(solution)/shard_map/ppermute | solution.py:725
  69.2 15.2 %collective-permute-start.9 = (bf16[192,1152]{1,0:T(8,128)(2,1)}, bf16[192,1152]{1,0:T(8,128)(2,1)S(1)}, u32[]{:S(2)}, u32[]{:S(2)}) collective-permute-start(bf16[192,1152]{1,0:T(8,128)(2,1)} %collective-permute-done.1.refs_9_), channel_id=1, source_target_pairs={{4,36},{5,37},{6,38},{7,39},{8,40},{9,41},{10,42},{11,43},{20,52},... | collective-permute-start | bytes 1327112 | tf_op jit(solution)/shard_map/ppermute | solution.py:725
  73.0 35.5 %collective-permute-start.13 = (bf16[160,1536]{1,0:T(8,128)(2,1)S(1)}, bf16[160,1536]{1,0:T(8,128)(2,1)S(1)}, u32[]{:S(2)}, u32[]{:S(2)}) collective-permute-start(bf16[160,1536]{1,0:T(8,128)(2,1)S(1)} %pad_maximum_fusion.4), channel_id=1, source_target_pairs={{0,1},{1,2},{2,3},{3,0},{4,9},{5,10},{6,11},{7,8},{8,5},{9,6},{10,... | collective-permute-start | bytes 1474568 | tf_op jit(solution)/shard_map/ppermute | solution.py:725
  78.7 29.8 %collective-permute-start.14 = (bf16[160,1536]{1,0:T(8,128)(2,1)S(1)}, bf16[160,1536]{1,0:T(8,128)(2,1)S(1)}, u32[]{:S(2)}, u32[]{:S(2)}) collective-permute-start(bf16[160,1536]{1,0:T(8,128)(2,1)S(1)} %pad_maximum_fusion.4), channel_id=1, source_target_pairs={{0,3},{1,0},{2,1},{3,2},{4,11},{5,8},{6,9},{7,10},{8,7},{9,4},{10,... | collective-permute-start | bytes 1474568 | tf_op jit(solution)/shard_map/ppermute | solution.py:725
  80.9 27.5 %collective-permute-start.15 = (bf16[160,1536]{1,0:T(8,128)(2,1)S(1)}, bf16[160,1536]{1,0:T(8,128)(2,1)S(1)}, u32[]{:S(2)}, u32[]{:S(2)}) collective-permute-start(bf16[160,1536]{1,0:T(8,128)(2,1)S(1)} %pad_maximum_fusion.4), channel_id=1, source_target_pairs={{0,2},{1,3},{2,0},{3,1},{4,10},{5,11},{6,8},{7,9},{8,6},{9,7},{10,... | collective-permute-start | bytes 1474568 | tf_op jit(solution)/shard_map/ppermute | solution.py:725
  116.9 77.5 %collective-permute-start.32 = (bf16[1536,1152]{1,0:T(8,128)(2,1)S(1)}, bf16[1536,1152]{1,0:T(8,128)(2,1)}, u32[]{:S(2)}, u32[]{:S(2)}) collective-permute-start(bf16[1536,1152]{1,0:T(8,128)(2,1)S(1)} %pad_maximum_fusion.1.refs_16_), channel_id=1, source_target_pairs={{4,8},{5,9},{6,10},{7,11},{8,4},{9,5},{10,6},{11,7},{20,24},{21,25... | collective-permute-start | bytes 10616840 | tf_op jit(solution)/shard_map/ppermute | solution.py:725
  119.8 46.6 %collective-permute-start.27 = (bf16[160,1536]{1,0:T(8,128)(2,1)S(1)}, bf16[160,1536]{1,0:T(8,128)(2,1)S(1)}, u32[]{:S(2)}, u32[]{:S(2)}) collective-permute-start(bf16[160,1536]{1,0:T(8,128)(2,1)S(1)} %copy-done.28), channel_id=1, source_target_pairs={{4,8},{5,9},{6,10},{7,11},{8,4},{9,5},{10,6},{11,7},{20,24},{21,25... | collective-permute-start | bytes 1474568 | tf_op jit(solution)/shard_map/ppermute | solution.py:725
  124.0 42.7 %collective-permute-start.17 = (bf16[128,1664]{1,0:T(8,128)(2,1)S(1)}, bf16[128,1664]{1,0:T(8,128)(2,1)S(1)}, u32[]{:S(2)}, u32[]{:S(2)}) collective-permute-start(bf16[128,1664]{1,0:T(8,128)(2,1)S(1)} %get-tuple-element.249), channel_id=1, source_target_pairs={{0,1},{1,2},{2,3},{3,0},{4,5},{5,6},{6,7},{7,4},{8,9},{9,10},{10,1... | collective-permute-start | bytes 1277960 | tf_op jit(solution)/shard_map/ppermute | solution.py:725
  125.8 41.5 %collective-permute-start.18 = (bf16[128,1664]{1,0:T(8,128)(2,1)S(1)}, bf16[128,1664]{1,0:T(8,128)(2,1)S(1)}, u32[]{:S(2)}, u32[]{:S(2)}) collective-permute-start(bf16[128,1664]{1,0:T(8,128)(2,1)S(1)} %get-tuple-element.248), channel_id=1, source_target_pairs={{0,2},{1,3},{2,0},{3,1},{4,6},{5,7},{6,4},{7,5},{8,10},{9,11},{10,... | collective-permute-start | bytes 1277960 | tf_op jit(solution)/shard_map/ppermute | solution.py:725
  126.9 40.5 %collective-permute-start.19 = (bf16[128,1664]{1,0:T(8,128)(2,1)S(1)}, bf16[128,1664]{1,0:T(8,128)(2,1)S(1)}, u32[]{:S(2)}, u32[]{:S(2)}) collective-permute-start(bf16[128,1664]{1,0:T(8,128)(2,1)S(1)} %get-tuple-element.247), channel_id=1, source_target_pairs={{0,3},{1,0},{2,1},{3,2},{4,7},{5,4},{6,5},{7,6},{8,11},{9,8},{10,9... | collective-permute-start | bytes 1277960 | tf_op jit(solution)/shard_map/ppermute | solution.py:725
  174.3 17.4 %collective-permute-start.25 = (bf16[128,1536]{1,0:T(8,128)(2,1)}, bf16[128,1536]{1,0:T(8,128)(2,1)S(1)}, u32[]{:S(2)}, u32[]{:S(2)}) collective-permute-start(bf16[128,1536]{1,0:T(8,128)(2,1)} %get-tuple-element.110.refs_0_), channel_id=1, source_target_pairs={{0,2},{1,3},{2,0},{3,1},{4,6},{5,7},{6,4},{7,5},{8,10},{9,11},{10,... | collective-permute-start | bytes 1179656 | tf_op jit(solution)/shard_map/ppermute | solution.py:725
  175.3 18.5 %collective-permute-start.20 = (bf16[128,1536]{1,0:T(8,128)(2,1)}, bf16[128,1536]{1,0:T(8,128)(2,1)S(1)}, u32[]{:S(2)}, u32[]{:S(2)}) collective-permute-start(bf16[128,1536]{1,0:T(8,128)(2,1)} %get-tuple-element.110.refs_0_), channel_id=1, source_target_pairs={{0,8},{1,9},{2,10},{3,11},{4,12},{5,13},{6,14},{7,15},{8,0},{9,1},... | collective-permute-start | bytes 1179656 | tf_op jit(solution)/shard_map/ppermute | solution.py:725
  235.9 35.5 %collective-permute-start.38 = (bf16[128,1664]{1,0:T(8,128)(2,1)S(1)}, bf16[128,1664]{1,0:T(8,128)(2,1)S(1)}, u32[]{:S(2)}, u32[]{:S(2)}) collective-permute-start(bf16[128,1664]{1,0:T(8,128)(2,1)S(1)} %get-tuple-element.246), channel_id=1, source_target_pairs={{0,1},{1,2},{2,3},{3,0},{4,5},{5,6},{6,7},{7,4},{8,9},{9,10},{10,1... | collective-permute-start | bytes 1277960 | tf_op jit(solution)/shard_map/ppermute | solution.py:725
  236.0 35.4 %collective-permute-start.39 = (bf16[128,1664]{1,0:T(8,128)(2,1)S(1)}, bf16[128,1664]{1,0:T(8,128)(2,1)S(1)}, u32[]{:S(2)}, u32[]{:S(2)}) collective-permute-start(bf16[128,1664]{1,0:T(8,128)(2,1)S(1)} %get-tuple-element.245), channel_id=1, source_target_pairs={{0,2},{1,3},{2,0},{3,1},{4,6},{5,7},{6,4},{7,5},{8,10},{9,11},{10,... | collective-permute-start | bytes 1277960 | tf_op jit(solution)/shard_map/ppermute | solution.py:725
  238.7 32.7 %collective-permute-start.40 = (bf16[128,1664]{1,0:T(8,128)(2,1)S(1)}, bf16[128,1664]{1,0:T(8,128)(2,1)S(1)}, u32[]{:S(2)}, u32[]{:S(2)}) collective-permute-start(bf16[128,1664]{1,0:T(8,128)(2,1)S(1)} %get-tuple-element.244), channel_id=1, source_target_pairs={{0,3},{1,0},{2,1},{3,2},{4,7},{5,4},{6,5},{7,6},{8,11},{9,8},{10,9... | collective-permute-start | bytes 1277960 | tf_op jit(solution)/shard_map/ppermute | solution.py:725
  289.7 31.0 %collective-permute-start.53 = (bf16[1536,768]{1,0:T(8,128)(2,1)}, bf16[1536,768]{1,0:T(8,128)(2,1)S(1)}, u32[]{:S(2)}, u32[]{:S(2)}) collective-permute-start(bf16[1536,768]{1,0:T(8,128)(2,1)} %weight_products.3), channel_id=1, source_target_pairs={{4,0},{5,1},{6,2},{7,3},{8,12},{9,13},{10,14},{11,15},{20,16},{21,... | collective-permute-start | bytes 7077896 | tf_op jit(solution)/shard_map/ppermute | solution.py:725
  293.9 14.2 %collective-permute-start.44 = (bf16[128,1792]{1,0:T(8,128)(2,1)S(1)}, bf16[128,1792]{1,0:T(8,128)(2,1)S(1)}, u32[]{:S(2)}, u32[]{:S(2)}) collective-permute-start(bf16[128,1792]{1,0:T(8,128)(2,1)S(1)} %pad_maximum_fusion.6), channel_id=1, source_target_pairs={{0,2},{1,3},{2,0},{3,1},{4,6},{5,7},{6,4},{7,5},{8,10},{9,11},{10,... | collective-permute-start | bytes 1376264 | tf_op jit(solution)/shard_map/ppermute | solution.py:725
  296.0 19.9 %collective-permute-start.43 = (bf16[128,1792]{1,0:T(8,128)(2,1)S(1)}, bf16[128,1792]{1,0:T(8,128)(2,1)S(1)}, u32[]{:S(2)}, u32[]{:S(2)}) collective-permute-start(bf16[128,1792]{1,0:T(8,128)(2,1)S(1)} %pad_maximum_fusion.5), channel_id=1, source_target_pairs={{0,1},{1,2},{2,3},{3,0},{4,5},{5,6},{6,7},{7,4},{8,9},{9,10},{10,1... | collective-permute-start | bytes 1376264 | tf_op jit(solution)/shard_map/ppermute | solution.py:725
  322.4 24.6 %collective-permute-start.54 = (bf16[768,768]{1,0:T(8,128)(2,1)}, bf16[768,768]{1,0:T(8,128)(2,1)}, u32[]{:S(2)}, u32[]{:S(2)}) collective-permute-start(bf16[768,768]{1,0:T(8,128)(2,1)} %slice.274), channel_id=1, source_target_pairs={{0,8},{1,9},{2,10},{3,11},{12,4},{13,5},{14,6},{15,7},{16,24},{17,... | collective-permute-start | bytes 3538952 | tf_op jit(solution)/shard_map/ppermute | solution.py:725
  325.0 21.5 %collective-permute-start.49 = (bf16[128,1664]{1,0:T(8,128)(2,1)S(1)}, bf16[128,1664]{1,0:T(8,128)(2,1)}, u32[]{:S(2)}, u32[]{:S(2)}) collective-permute-start(bf16[128,1664]{1,0:T(8,128)(2,1)S(1)} %copy-done.71), channel_id=1, source_target_pairs={{0,3},{1,0},{2,1},{3,2},{4,7},{5,4},{6,5},{7,6},{8,11},{9,8},{10,9... | collective-permute-start | bytes 1277960 | tf_op jit(solution)/shard_map/ppermute | solution.py:725
  327.0 19.6 %collective-permute-start.51 = (bf16[128,1664]{1,0:T(8,128)(2,1)S(1)}, bf16[128,1664]{1,0:T(8,128)(2,1)}, u32[]{:S(2)}, u32[]{:S(2)}) collective-permute-start(bf16[128,1664]{1,0:T(8,128)(2,1)S(1)} %copy-done.71), channel_id=1, source_target_pairs={{0,2},{1,3},{2,0},{3,1},{4,6},{5,7},{6,4},{7,5},{8,10},{9,11},{10,... | collective-permute-start | bytes 1277960 | tf_op jit(solution)/shard_map/ppermute | solution.py:725
  327.6 22.0 %collective-permute-start.46 = (bf16[128,1664]{1,0:T(8,128)(2,1)S(1)}, bf16[128,1664]{1,0:T(8,128)(2,1)}, u32[]{:S(2)}, u32[]{:S(2)}) collective-permute-start(bf16[128,1664]{1,0:T(8,128)(2,1)S(1)} %copy-done.71), channel_id=1, source_target_pairs={{0,8},{1,9},{2,10},{3,11},{4,12},{5,13},{6,14},{7,15},{8,0},{9,1},... | collective-permute-start | bytes 1277960 | tf_op jit(solution)/shard_map/ppermute | solution.py:725
  334.5 17.6 %collective-permute-start.48 = (bf16[128,1664]{1,0:T(8,128)(2,1)S(1)}, bf16[128,1664]{1,0:T(8,128)(2,1)S(1)}, u32[]{:S(2)}, u32[]{:S(2)}) collective-permute-start(bf16[128,1664]{1,0:T(8,128)(2,1)S(1)} %collective-permute-done.47.refs_2_), channel_id=1, source_target_pairs={{0,8},{1,9},{2,10},{3,11},{4,12},{5,13},{6,14},{7,15},{8,0},{9,1},... | collective-permute-start | bytes 1277960 | tf_op jit(solution)/shard_map/ppermute | solution.py:725
  349.6 15.3 %collective-permute-start.56 = (bf16[192,768]{1,0:T(8,128)(2,1)S(1)}, bf16[192,768]{1,0:T(8,128)(2,1)S(1)}, u32[]{:S(2)}, u32[]{:S(2)}) collective-permute-start(bf16[192,768]{1,0:T(8,128)(2,1)S(1)} %get-tuple-element.269), channel_id=1, source_target_pairs={{0,64},{1,65},{2,66},{3,67},{4,68},{5,69},{6,70},{7,71},{8,72},{9,... | collective-permute-start | bytes 884744 | tf_op jit(solution)/shard_map/ppermute | solution.py:725
  365.2 93.1 %collective-permute-start.87 = (bf16[192,768]{1,0:T(8,128)(2,1)S(1)}, bf16[192,768]{1,0:T(8,128)(2,1)}, u32[]{:S(2)}, u32[]{:S(2)}) collective-permute-start(bf16[192,768]{1,0:T(8,128)(2,1)S(1)} %add_convert_fusion.16), channel_id=1, source_target_pairs={{0,16},{1,17},{2,18},{3,19},{4,20},{5,21},{6,22},{7,23},{8,24},{9,... | collective-permute-start | bytes 884744 | tf_op jit(solution)/shard_map/ppermute | solution.py:725
  376.9 37.7 %collective-permute-start.64 = (bf16[384,1280]{1,0:T(8,128)(2,1)}, bf16[384,1280]{1,0:T(8,128)(2,1)S(1)}, u32[]{:S(2)}, u32[]{:S(2)}) collective-permute-start(bf16[384,1280]{1,0:T(8,128)(2,1)} %get-tuple-element.153), channel_id=1, source_target_pairs={{0,32},{1,33},{2,34},{3,35},{4,36},{5,37},{6,38},{7,39},{8,40},{9,... | collective-permute-start | bytes 2949128 | tf_op jit(solution)/shard_map/ppermute | solution.py:725
  378.2 44.9 %collective-permute-start.65 = (bf16[384,1280]{1,0:T(8,128)(2,1)}, bf16[384,1280]{1,0:T(8,128)(2,1)}, u32[]{:S(2)}, u32[]{:S(2)}) collective-permute-start(bf16[384,1280]{1,0:T(8,128)(2,1)} %get-tuple-element.154), channel_id=1, source_target_pairs={{0,64},{1,65},{2,66},{3,67},{4,68},{5,69},{6,70},{7,71},{8,72},{9,... | collective-permute-start | bytes 2949128 | tf_op jit(solution)/shard_map/ppermute | solution.py:725
  380.6 42.5 %collective-permute-start.66 = (bf16[384,1280]{1,0:T(8,128)(2,1)}, bf16[384,1280]{1,0:T(8,128)(2,1)}, u32[]{:S(2)}, u32[]{:S(2)}) collective-permute-start(bf16[384,1280]{1,0:T(8,128)(2,1)} %get-tuple-element.155), channel_id=1, source_target_pairs={{0,96},{1,97},{2,98},{3,99},{4,100},{5,101},{6,102},{7,103},{8,104... | collective-permute-start | bytes 2949128 | tf_op jit(solution)/shard_map/ppermute | solution.py:725
  411.1 14.7 %collective-permute-start.63 = (bf16[544,256]{1,0:T(8,128)(2,1)S(1)}, bf16[544,256]{1,0:T(8,128)(2,1)S(1)}, u32[]{:S(2)}, u32[]{:S(2)}) collective-permute-start(bf16[544,256]{1,0:T(8,128)(2,1)S(1)} %pad_maximum_fusion.9), channel_id=1, source_target_pairs={{0,8},{1,9},{2,10},{3,11},{4,12},{5,13},{6,14},{7,15},{8,0},{9,1},... | collective-permute-start | bytes 835592 | tf_op jit(solution)/shard_map/ppermute | solution.py:725
  414.6 69.2 %collective-permute-start.58 = (bf16[512,1536]{1,0:T(8,128)(2,1)}, bf16[512,1536]{1,0:T(8,128)(2,1)S(1)}, u32[]{:S(2)}, u32[]{:S(2)}) collective-permute-start(bf16[512,1536]{1,0:T(8,128)(2,1)} %get-tuple-element.163), channel_id=1, source_target_pairs={{0,8},{1,9},{2,10},{3,11},{4,12},{5,13},{6,14},{7,15},{8,0},{9,1},... | collective-permute-start | bytes 4718600 | tf_op jit(solution)/shard_map/ppermute | solution.py:725
  434.3 46.7 %collective-permute-start.80 = (bf16[384,1280]{1,0:T(8,128)(2,1)S(1)}, bf16[384,1280]{1,0:T(8,128)(2,1)}, u32[]{:S(2)}, u32[]{:S(2)}) collective-permute-start(bf16[384,1280]{1,0:T(8,128)(2,1)S(1)} %add_convert_fusion.2), channel_id=1, source_target_pairs={{4,0},{5,1},{6,2},{7,3},{8,12},{9,13},{10,14},{11,15},{20,16},{21,... | collective-permute-start | bytes 2949128 | tf_op jit(solution)/shard_map/ppermute | solution.py:725
  455.4 19.7 %collective-permute-start.71 = (bf16[384,512]{1,0:T(8,128)(2,1)}, bf16[384,512]{1,0:T(8,128)(2,1)}, u32[]{:S(2)}, u32[]{:S(2)}) collective-permute-start(bf16[384,512]{1,0:T(8,128)(2,1)} %get-tuple-element.280), channel_id=1, source_target_pairs={{0,64},{1,65},{2,66},{3,67},{4,68},{5,69},{6,70},{7,71},{8,72},{9,... | collective-permute-start | bytes 1179656 | tf_op jit(solution)/shard_map/ppermute | solution.py:725
  458.3 17.1 %collective-permute-start.72 = (bf16[384,512]{1,0:T(8,128)(2,1)}, bf16[384,512]{1,0:T(8,128)(2,1)}, u32[]{:S(2)}, u32[]{:S(2)}) collective-permute-start(bf16[384,512]{1,0:T(8,128)(2,1)} %get-tuple-element.281), channel_id=1, source_target_pairs={{0,96},{1,97},{2,98},{3,99},{4,100},{5,101},{6,102},{7,103},{8,104... | collective-permute-start | bytes 1179656 | tf_op jit(solution)/shard_map/ppermute | solution.py:725
  478.2 15.6 %collective-permute-start.89 = (bf16[192,768]{1,0:T(8,128)(2,1)S(1)}, bf16[192,768]{1,0:T(8,128)(2,1)S(1)}, u32[]{:S(2)}, u32[]{:S(2)}) collective-permute-start(bf16[192,768]{1,0:T(8,128)(2,1)S(1)} %add_convert_fusion.15), channel_id=1, source_target_pairs={{0,64},{1,65},{2,66},{3,67},{4,68},{5,69},{6,70},{7,71},{8,72},{9,... | collective-permute-start | bytes 884744 | tf_op jit(solution)/shard_map/ppermute | solution.py:725
  480.8 28.9 %collective-permute-start.90 = (bf16[192,768]{1,0:T(8,128)(2,1)S(1)}, bf16[192,768]{1,0:T(8,128)(2,1)S(1)}, u32[]{:S(2)}, u32[]{:S(2)}) collective-permute-start(bf16[192,768]{1,0:T(8,128)(2,1)S(1)} %add_convert_fusion.15), channel_id=1, source_target_pairs={{0,96},{1,97},{2,98},{3,99},{4,100},{5,101},{6,102},{7,103},{8,104... | collective-permute-start | bytes 884744 | tf_op jit(solution)/shard_map/ppermute | solution.py:725
  486.4 23.5 %collective-permute-start.59 = (bf16[128,1536]{1,0:T(8,128)(2,1)S(1)}, bf16[128,1536]{1,0:T(8,128)(2,1)S(1)}, u32[]{:S(2)}, u32[]{:S(2)}) collective-permute-start(bf16[128,1536]{1,0:T(8,128)(2,1)S(1)} %get-tuple-element.253), channel_id=1, source_target_pairs={{0,1},{1,2},{2,3},{3,0},{4,5},{5,6},{6,7},{7,4},{8,9},{9,10},{10,1... | collective-permute-start | bytes 1179656 | tf_op jit(solution)/shard_map/ppermute | solution.py:725
  488.3 22.2 %collective-permute-start.60 = (bf16[128,1536]{1,0:T(8,128)(2,1)S(1)}, bf16[128,1536]{1,0:T(8,128)(2,1)S(1)}, u32[]{:S(2)}, u32[]{:S(2)}) collective-permute-start(bf16[128,1536]{1,0:T(8,128)(2,1)S(1)} %get-tuple-element.252), channel_id=1, source_target_pairs={{0,2},{1,3},{2,0},{3,1},{4,6},{5,7},{6,4},{7,5},{8,10},{9,11},{10,... | collective-permute-start | bytes 1179656 | tf_op jit(solution)/shard_map/ppermute | solution.py:725
  494.0 16.5 %collective-permute-start.61 = (bf16[128,1536]{1,0:T(8,128)(2,1)S(1)}, bf16[128,1536]{1,0:T(8,128)(2,1)S(1)}, u32[]{:S(2)}, u32[]{:S(2)}) collective-permute-start(bf16[128,1536]{1,0:T(8,128)(2,1)S(1)} %get-tuple-element.251), channel_id=1, source_target_pairs={{0,3},{1,0},{2,1},{3,2},{4,7},{5,4},{6,5},{7,6},{8,11},{9,8},{10,9... | collective-permute-start | bytes 1179656 | tf_op jit(solution)/shard_map/ppermute | solution.py:725
  509.7 23.2 %collective-permute-start.83 = (bf16[192,1280]{1,0:T(8,128)(2,1)S(1)}, bf16[192,1280]{1,0:T(8,128)(2,1)S(1)}, u32[]{:S(2)}, u32[]{:S(2)}) collective-permute-start(bf16[192,1280]{1,0:T(8,128)(2,1)S(1)} %get-tuple-element.241), channel_id=1, source_target_pairs={{0,32},{1,33},{2,34},{3,35},{4,36},{5,37},{6,38},{7,39},{8,40},{9,... | collective-permute-start | bytes 1474568 | tf_op jit(solution)/shard_map/ppermute | solution.py:725
  510.0 46.9 %collective-permute-start.91 = (bf16[4,192,768]{2,1,0:T(8,128)(2,1)S(1)}, bf16[4,192,768]{2,1,0:T(8,128)(2,1)S(1)}, u32[]{:S(2)}, u32[]{:S(2)}) collective-permute-start(bf16[4,192,768]{2,1,0:T(8,128)(2,1)S(1)} %bitcast_dynamic-update-slice_fusion.4.here_ref), channel_id=1, source_target_pairs={{0,8},{1,9},{2,10},{3,11},{4,12},{5,13},{6,14},{7,15},{8,0},{9,1},... | collective-permute-start | bytes 3538952 | tf_op jit(solution)/shard_map/ppermute | solution.py:725
  514.9 40.7 %collective-permute-start.62 = (bf16[128,3072]{1,0:T(8,128)(2,1)}, bf16[128,3072]{1,0:T(8,128)(2,1)S(1)}, u32[]{:S(2)}, u32[]{:S(2)}) collective-permute-start(bf16[128,3072]{1,0:T(8,128)(2,1)} %outputs.1), channel_id=1, source_target_pairs={{4,8},{5,9},{6,10},{7,11},{8,4},{9,5},{10,6},{11,7},{20,24},{21,25... | collective-permute-start | bytes 2359304 | tf_op jit(solution)/shard_map/ppermute | solution.py:725
  521.5 22.9 %collective-permute-start.76 = (bf16[192,512]{1,0:T(8,128)(2,1)S(1)}, bf16[192,512]{1,0:T(8,128)(2,1)S(1)}, u32[]{:S(2)}, u32[]{:S(2)}) collective-permute-start(bf16[192,512]{1,0:T(8,128)(2,1)S(1)} %get-tuple-element.243), channel_id=1, source_target_pairs={{0,32},{1,33},{2,34},{3,35},{4,36},{5,37},{6,38},{7,39},{8,40},{9,... | collective-permute-start | bytes 589832 | tf_op jit(solution)/shard_map/ppermute | solution.py:725
  534.3 16.5 %collective-permute-start.77 = (bf16[192,512]{1,0:T(8,128)(2,1)S(1)}, bf16[192,512]{1,0:T(8,128)(2,1)S(1)}, u32[]{:S(2)}, u32[]{:S(2)}) collective-permute-start(bf16[192,512]{1,0:T(8,128)(2,1)S(1)} %get-tuple-element.243), channel_id=1, source_target_pairs={{0,64},{1,65},{2,66},{3,67},{4,68},{5,69},{6,70},{7,71},{8,72},{9,... | collective-permute-start | bytes 589832 | tf_op jit(solution)/shard_map/ppermute | solution.py:725
  544.4 18.2 %collective-permute-start.86 = (bf16[4,192,1280]{2,1,0:T(8,128)(2,1)S(1)}, bf16[4,192,1280]{2,1,0:T(8,128)(2,1)S(1)}, u32[]{:S(2)}, u32[]{:S(2)}) collective-permute-start(bf16[4,192,1280]{2,1,0:T(8,128)(2,1)S(1)} %bitcast_dynamic-update-slice_fusion.here_ref), channel_id=1, source_target_pairs={{0,8},{1,9},{2,10},{3,11},{4,12},{5,13},{6,14},{7,15},{8,0},{9,1},... | collective-permute-start | bytes 5898248 | tf_op jit(solution)/shard_map/ppermute | solution.py:725
  551.0 19.2 %collective-permute-start.79 = (bf16[4,192,512]{2,1,0:T(8,128)(2,1)S(1)}, bf16[4,192,512]{2,1,0:T(8,128)(2,1)S(1)}, u32[]{:S(2)}, u32[]{:S(2)}) collective-permute-start(bf16[4,192,512]{2,1,0:T(8,128)(2,1)S(1)} %bitcast_dynamic-update-slice_fusion.8.here_ref), channel_id=1, source_target_pairs={{0,8},{1,9},{2,10},{3,11},{4,12},{5,13},{6,14},{7,15},{8,0},{9,1},... | collective-permute-start | bytes 2359304 | tf_op jit(solution)/shard_map/ppermute | solution.py:725
  (127 other events, 1334.4 us)

commit v3 on v2

--- a/solution.py
+++ b/solution.py
@@ -746,23 +746,6 @@
     return jnp.where(core == yh, v, traded(v))
 
 
-def quarter_of_half(v):
-    x = position()[0]
-    rows = v.shape[0] // 2 // NX
-    return traded(lax.dynamic_slice_in_dim(v, x * rows, rows, 0))
-
-
-def traded_by_x(v, quarter, ready):
-    half = v.shape[0] // 2
-    parts, plan = [quarter], [(None, 0)]
-    for k in range(1, NX):
-        parts.append(
-            send(quarter, lambda x, yl, c, yh, z, k=k: (x + k, yl, c, yh, z), lambda x, yl, c, yh, z: c != yh)
-        )
-        plan.append((None, k))
-    return parts + [traded(after(v[half:], ready))], plan + [(half, None)]
-
-
 def position():
     dp, tensor = lax.axis_index("dp"), lax.axis_index("tensor")
     return dp // (NYL * NC), dp // NC % NYL, dp % NC, tensor // NZ, tensor % NZ
@@ -1100,14 +1083,13 @@
     low = (little - high.astype(f32)).astype(bf16)
     lines = pad_to(jnp.concatenate([high, low], axis=1), layers * 8, width)
     packed = jnp.concatenate([hidden_in[0], bc_t[0], dt_t.reshape(layers * 8, width), lines], axis=0)
-    w0 = pack_weights(0)
-    quarter = quarter_of_half(w0)
-    packed = after(trade_places(packed), quarter)
+    packed = trade_places(packed)
     lines = packed[packed.shape[0] - layers * 8 :].astype(f32)
     little = lines[:, : channels + LANES] + lines[:, channels + LANES : 2 * (channels + LANES)]
     little = little.reshape(layers, 8, channels + LANES)
 
-    w0 = w0, *traded_by_x(w0, quarter, packed)
+    w0 = pack_weights(0)
+    w0 = w0, [traded(after(w0, packed))], [(0, None)]
     grads = jnp.concatenate([grad_out[0], bc_t[1]], axis=0)
 
     [sent] = row_call(
@@ -1127,9 +1109,10 @@
 
     out0 = run_forward(place, [gathered0], w0, wdt[0], smalls[0], state, head_dim)
     w0, xn0, wbc0, z0, xp0, bc0, dt0, y0, hin0, mine, other = out0
-    gathered_grad = gather(after(grads, *gathered0[0]), (rows, bc_rows), trade_places(grads))
+    grads = after(grads, sent)
+    gathered_grad = gather(grads, (rows, bc_rows), trade_places(grads))
     grad_held = gathered_grad[0][0]
-    terms = scatter((mine, after(other, *gathered_grad[0][2::2])))
+    terms = scatter((mine, after(other, *gathered_grad[0][::2])))
     w1 = pack_weights(1)
     w1 = w1, [traded(after(w1, terms[0]))], [(0, None)]
     res1, mixed0, rms0, normed1 = row_call(
@@ -1154,8 +1137,8 @@
     )
     dz1, go1, dxt1, *bc_halves, mine, other, acc1, acch1, shared1 = back1
     terms = scatter((mine, after(other, *home)), bc_halves)
-    early1 = weight_products(place, [(xn1, after(dz1, terms[0])), (go1, grad_rows1)], split=False)
-    terms[3] = after(terms[3], early1)
+    early1 = weight_products(place, [(xn1, dz1), (go1, grad_rows1)], split=False)
+    terms[1] = after(terms[1], early1)
     early1_far = send_far(early1)
     [hidden_out] = row_call(
         functools.partial(last_kernel, inner_all),
@@ -1194,6 +1177,24 @@
         place, (dy0, dz0), xn0, xp0, bc0, dt0, hin0, (w0, wbc0, wdt[0]), smalls[0], pick, head_dim, inner_all
     )
     dxt0, *bc_halves, mine, other, acc0, acch0, shared0 = back0
+    shared = jnp.concatenate([shared0, shared1], axis=0)
+    bc_sum, shared = scatter_with_sum(*bc_halves, shared, (early,))
+    tiny_at = bc_at + bc_rows
+    tiny_lanes = channels + LANES - tiny_at
+    tiny = jnp.concatenate(
+        [acc0 + acc_gate0, acc1] + [pad_to(v, v.shape[0], channels) for v in (acch0[0:2], acch1[0:2], shared)],
+        axis=0,
+    )
+    tiny_shape = tiny.shape
+    tiny = pad_to(tiny.reshape(-1, tiny_lanes), width, tiny_lanes)
+    tiny = jnp.pad(tiny, ((0, 0), (tiny_at, 0))).astype(bf16)
+    early = halve(sum_far(early))
+    late = weight_products(place, [(xn0, after(with_bc(dxt0, bc_sum), early))])
+    early = sum_beside(early)
+    late = [v + t for v, t in zip(late, cut_x(tiny))]
+    mine, other = after(mine, late[0]), after(other, late[0])
+    late = after(sum_x(late), early)
+
     terms = scatter((mine, other))
     [outputs] = row_call(
         end_kernel,
@@ -1201,28 +1202,15 @@
         [(v, rows) for v in terms] + [(packed, rows), (d_res1, rows), (norm_in[0:1], 1), (hidden_out, rows)],
         [jax.ShapeDtypeStruct((rows, 2 * width), bf16)],
     )
-    outputs = trade_places(outputs).astype(f32)
-
-    shared = jnp.concatenate([shared0, shared1], axis=0)
-    bc_sum, shared = scatter_with_sum(*bc_halves, shared, (early,))
-    tiny = jnp.concatenate(
-        [(acc0 + acc_gate0).reshape(-1), acc1.reshape(-1), acch0[0:2].reshape(-1), acch1[0:2].reshape(-1)]
-        + [shared.reshape(-1)]
-    )
-    tiny_at = bc_at + bc_rows
-    tiny_lanes = channels + LANES - tiny_at
-    tiny_size = tiny.shape[0]
-    tiny = jnp.pad(tiny, (0, width * tiny_lanes - tiny_size)).reshape(width, tiny_lanes)
-    tiny = jnp.pad(tiny, ((0, 0), (tiny_at, 0))).astype(bf16)
-    late = weight_products(place, [(xn0, with_bc(dxt0, bc_sum))])
-    late = sum_x([v + t for v, t in zip(late, cut_x(tiny))])
-    halves = collect(after(early1, late))
-    g_wz, g_wo = write_sums(place, halves, True, [(0, "rows", 1, None), (channels, "blocks", 1, None)])
-    late = sum_beside(halve(sum_far(late)))
-    early = sum_beside(halve(sum_far(after(early, dxt0))))
+    outputs_home = trade_places(outputs).astype(f32)
+
+    early = collect(early)
+    early1 = collect(after(early1, early[0], outputs))
+    late = collect(sum_beside(halve(sum_far(late))))
+    g_wz, g_wo = write_sums(place, early1, True, [(0, "rows", 1, None), (channels, "blocks", 1, None)])
     g_wz, g_wo, g_wx, narrow1 = write_sums(
         place,
-        collect(early),
+        early,
         False,
         [
             (0, "rows", 0, g_wz),
@@ -1232,22 +1220,20 @@
         ],
     )
     g_wx, narrow0 = write_sums(
-        place, collect(late), False, [(0, "rows", 0, g_wx), (channels, "flat", 0, None)]
+        place, late, False, [(0, "rows", 0, g_wx), (channels, "flat", 0, None)]
     )
 
     narrow0, narrow1 = narrow0[0], narrow1[0]
-    tiny = narrow0[:, tiny_at - channels :].reshape(-1)[:tiny_size]
-    sizes = [8 * channels, 8 * channels, 2 * LANES, 2 * LANES]
-    cut = [sum(sizes[:i]) for i in range(len(sizes) + 1)]
-    g_x = tiny[: cut[2]].reshape(layers, 8, channels)
-    g_head = tiny[cut[2] : cut[4]].reshape(layers, 2, LANES)[:, :, :heads]
-    shared = tiny[cut[4] :].reshape(layers, -1, both)
+    tiny = narrow0[: tiny_shape[0] * channels // tiny_lanes, tiny_at - channels :].reshape(tiny_shape)
+    g_x = tiny[0:16].reshape(layers, 8, channels)
+    g_head = tiny[16:20, :heads].reshape(layers, 2, heads)
+    shared = tiny[20:, :both].reshape(layers, -1, both)
     lines = width // both
     g_norm_in = shared[:, :lines].reshape(layers, width) / norm_in
     g_bc = shared[:, lines : lines + 5]
     return (
-        outputs[None, :, :width],
-        outputs[None, :, width:],
+        outputs_home[None, :, :width],
+        outputs_home[None, :, width:],
         g_norm_in,
         g_wz,
         g_wx,

time: 597 us -> 579 us (0.970)
  the two profiles are of different devices: /device:TPU:1 before, /device:TPU:25 now
where the time goes in v3:
time: 579 us; the launch traced here: 569 us
  starting transfers between devices  180 us (31%)
  Pallas kernels  174 us (30%)
  waiting for transfers between devices  137 us (24%)
  other arithmetic  39.9 us (7%)
  local copies, waits for them, and re-layouts  36.4 us (6%)
    ppermute x88, starting transfers between devices, send(): return lax.ppermute(v, ('dp', 'tensor'), pairs)  180 us
    ppermute x88, waiting for transfers between devices, send(): return lax.ppermute(v, ('dp', 'tensor'), pairs)  137 us
    pallas_call x5, Pallas kernels, span_call(): pl.pallas_call(kernel, grid_spec=pltpu.PrefetchScalarGridSpec(num_scalar_...  117 us
    pallas_call x3, Pallas kernels, weight_products(): pl.pallas_call(functools.partial(weight_kernel, len(pairs), split), grid_...  25.9 us
    pallas_call x5, Pallas kernels, row_call(): pl.pallas_call(kernel, grid=(1,), in_specs=[pl.BlockSpec((rows, v.shape[1...  15.6 us
    pallas_call x3, Pallas kernels, write_sums(): pl.pallas_call(functools.partial(write_kernel, plan, by_half, len(kept)),...  14.7 us
    unnamed x178, local copies, waits for them, and re-layouts  12.9 us
  transfers between devices with their start and end apart: 88, of which 35 were waited for; matrix products, arithmetic and copies ran while one was open for 7% of the time, Pallas kernels for 22%

profile of v3, /device:TPU:25, one launch (start us, length us, event | category | flops | bytes accessed | tf_op | source)
XLA Modules:
  0.0 568.8 jit_solution(4059137845824649506)
XLA Ops:
  10.8 2.8 fusion.16
  14.3 2.8 slice_bitcast_fusion
  36.7 11.3 %collective-permute-start.1 = (bf16[160,1536]{1,0:T(8,128)(2,1)}, bf16[160,1536]{1,0:T(8,128)(2,1)S(1)}, u32[]{:S(2)}, u32[]{:S(2)}) collective-permute-start(bf16[160,1536]{1,0:T(8,128)(2,1)} %first_norm.1.refs_0_), channel_id=1, source_target_pairs={{0,8},{1,9},{2,10},{3,11},{4,12},{5,13},{6,14},{7,15},{8,0},{9,1},... | collective-permute-start | bytes 1474568 | tf_op jit(solution)/shard_map/ppermute | solution.py:725
  48.0 4.2 collective-permute-start.3
  54.0 20.6 %collective-permute-start.7 = (bf16[160,1536]{1,0:T(8,128)(2,1)S(1)}, bf16[160,1536]{1,0:T(8,128)(2,1)S(1)}, u32[]{:S(2)}, u32[]{:S(2)}) collective-permute-start(bf16[160,1536]{1,0:T(8,128)(2,1)S(1)} %collective-permute-done.6.refs_6_), channel_id=1, source_target_pairs={{0,8},{1,9},{2,10},{3,11},{4,12},{5,13},{6,14},{7,15},{8,0},{9,1},... | collective-permute-start | bytes 1474568 | tf_op jit(solution)/shard_map/ppermute | solution.py:725
  81.4 23.0 %layer_forward.2 = (bf16[1536,1152]{1,0:T(8,128)(2,1)}, bf16[1024,1536]{1,0:T(8,128)(2,1)}, bf16[256,1536]{1,0:T(8,128)(2,1)}, bf16[1024,384]{1,0:T(8,128)(2,1)}...) custom-call(s32[4]{0:T(128)} %pad_add_fusion.2.place_ref, ...), custom_call_target="tpu_custom_call" | custom-call | flops 20000000000 | bytes 26501120 | tf_op jit(solution)/shard_map/layer_forward/pallas_call | solution.py:496
  105.2 3.1 collective-permute-start.13
  111.9 2.8 add_convert_fusion.4
  120.9 3.1 collective-permute-start.24
  124.1 4.2 collective-permute-done.14.a_ref
  128.2 11.6 %collective-permute-start.25 = (bf16[160,1536]{1,0:T(8,128)(2,1)S(1)}, bf16[160,1536]{1,0:T(8,128)(2,1)S(1)}, u32[]{:S(2)}, u32[]{:S(2)}) collective-permute-start(bf16[160,1536]{1,0:T(8,128)(2,1)S(1)} %copy-done.57), channel_id=1, source_target_pairs={{0,8},{1,9},{2,10},{3,11},{4,12},{5,13},{6,14},{7,15},{8,0},{9,1},... | collective-permute-start | bytes 1474568 | tf_op jit(solution)/shard_map/ppermute | solution.py:725
  140.8 3.3 middle_norm.1
  148.8 7.1 %collective-permute-done.18.refs_2_ = bf16[128,1536]{1,0:T(8,128)(2,1)S(1)} collective-permute-done((bf16[128,1536]{1,0:T(8,128)(2,1)}, bf16[128,1536]{1,0:T(8,128)(2,1)S(1)}, u32[]{:S(2)}, u32[]{:S(2)}) %collective-permute-start.18) | collective-permute-done | bytes 393248 | tf_op jit(solution)/shard_map/ppermute | solution.py:725
  157.1 7.8 %collective-permute-start.21 = (bf16[128,1536]{1,0:T(8,128)(2,1)S(1)}, bf16[128,1536]{1,0:T(8,128)(2,1)S(1)}, u32[]{:S(2)}, u32[]{:S(2)}) collective-permute-start(bf16[128,1536]{1,0:T(8,128)(2,1)S(1)} %collective-permute-done.20.refs_4_), channel_id=1, source_target_pairs={{0,8},{1,9},{2,10},{3,11},{4,12},{5,13},{6,14},{7,15},{8,0},{9,1},... | collective-permute-start | bytes 1179656 | tf_op jit(solution)/shard_map/ppermute | solution.py:725
  168.6 27.0 %layer_forward.3 = (bf16[1536,1152]{1,0:T(8,128)(2,1)}, bf16[1024,1536]{1,0:T(8,128)(2,1)}, bf16[256,1536]{1,0:T(8,128)(2,1)}, bf16[1024,384]{1,0:T(8,128)(2,1)}...) custom-call(s32[4]{0:T(128)} %pad_add_fusion.2.place_ref, ...), custom_call_target="tpu_custom_call" | custom-call | flops 20000000000 | bytes 34398208 | tf_op jit(solution)/shard_map/layer_forward/pallas_call | solution.py:496
  196.2 3.4 collective-permute-done.29
  214.8 29.6 %scan_backward.2 = (bf16[1024,384]{1,0:T(8,128)(2,1)}, bf16[1024,384]{1,0:T(8,128)(2,1)}, bf16[1024,512]{1,0:T(8,128)(2,1)}, bf16[512,256]{1,0:T(8,128)(2,1)}, b...) custom-call(s32[4]{0:T(128)} %pad_add_fusion.2.place_ref, ...), custom_call_target="tpu_custom_call" | custom-call | flops 28000000000 | bytes 21512192 | tf_op jit(solution)/shard_map/scan_backward/pallas_call | solution.py:496
  247.3 8.3 %weight_products.3 = bf16[1536,768]{1,0:T(8,128)(2,1)} custom-call(s32[4]{0:T(128)} %pad_add_fusion.2.place_ref, bf16[1024,1536]{1,0:T(8,128)(2,1)} %get-tuple-element.119.refs_4_.refs_0_.refs_2_, bf16[1024,384]{1,0:T(8,128)(2,1)} %get-tuple-element.131.refs_1_, bf16[1024,384]{1,0:T(8,128)(2,1)} %get-tuple-element.132.refs_2_, ...), custom_call_target="tpu_custom_call" | custom-call | flops 2415919104 | bytes 8000000 | tf_op jit(solution)/shard_map/weight_products/pallas_call | solution.py:692
  256.8 5.1 collective-permute-start.38
  267.7 18.7 %collective-permute-done.39.a_ref = bf16[128,1792]{1,0:T(8,128)(2,1)S(1)} collective-permute-done((bf16[128,1792]{1,0:T(8,128)(2,1)S(1)}, bf16[128,1792]{1,0:T(8,128)(2,1)S(1)}, u32[]{:S(2)}, u32[]{:S(2)}) %collective-permute-start.39) | collective-permute-done | bytes 458784 | tf_op jit(solution)/shard_map/ppermute | solution.py:725
  288.6 4.0 between_layers.1
  293.3 4.5 collective-permute-start.50
  305.5 4.7 collective-permute-done.43.refs_2_
  310.3 8.4 %collective-permute-done.45.refs_4_ = bf16[128,1664]{1,0:T(8,128)(2,1)} collective-permute-done((bf16[128,1664]{1,0:T(8,128)(2,1)}, bf16[128,1664]{1,0:T(8,128)(2,1)}, u32[]{:S(2)}, u32[]{:S(2)}) %collective-permute-start.45) | collective-permute-done | bytes 426016 | tf_op jit(solution)/shard_map/ppermute | solution.py:725
  325.7 8.4 %gate_backward.1 = (bf16[1024,1536]{1,0:T(8,128)(2,1)}, bf16[1024,384]{1,0:T(8,128)(2,1)}, f32[1024,384]{1,0:T(8,128)}, bf16[1024,384]{1,0:T(8,128)(2,1)}, f32[8,384]{1,0:T(8,128)}) custom-call(s32[4]{0:T(128)} %pad_add_fusion.2.place_ref, bf16[128,1664]{1,0:T(8,128)(2,1)} %get-tuple-element.138.refs_0_, bf16[128,1664]{1,0:T(8,128)(2,1)} %collective-permute-done.42.refs_1_, ...), custom_call_target="tpu_custom_call" | custom-call | flops 6000000000 | bytes 14835712 | tf_op jit(solution)/shard_map/gate_backward/pallas_call | solution.py:496
  335.7 11.3 %weight_products.4 = (bf16[384,1280]{1,0:T(8,128)(2,1)}, bf16[384,1280]{1,0:T(8,128)(2,1)}, bf16[384,1280]{1,0:T(8,128)(2,1)}, bf16[384,1280]{1,0:T(8,128)(2,1)}) custom-call(s32[4]{0:T(128)} %pad_add_fusion.2.place_ref, bf16[1024,1536]{1,0:T(8,128)(2,1)} %get-tuple-element.145.refs_0_.refs_2_, bf16[1024,384]{1,0:T(8,128)(2,1)} %get-tuple-element.146.refs_1_, ...), custom_call_target="tpu_custom_call" | custom-call | flops 4026531840 | bytes 8000000 | tf_op jit(solution)/shard_map/weight_products/pallas_call | solution.py:692
  351.8 29.2 %scan_backward.3 = (bf16[1024,512]{1,0:T(8,128)(2,1)}, bf16[512,256]{1,0:T(8,128)(2,1)}, bf16[512,256]{1,0:T(8,128)(2,1)}, bf16[512,1536]{1,0:T(8,128)(2,1)}, bf...) custom-call(s32[4]{0:T(128)} %pad_add_fusion.2.place_ref, ...), custom_call_target="tpu_custom_call" | custom-call | flops 28000000000 | bytes 19120128 | tf_op jit(solution)/shard_map/scan_backward/pallas_call | solution.py:496
  382.1 3.0 collective-permute-start.54
  385.1 8.6 %collective-permute-done.56 = bf16[384,1280]{1,0:T(8,128)(2,1)S(1)} collective-permute-done((bf16[384,1280]{1,0:T(8,128)(2,1)}, bf16[384,1280]{1,0:T(8,128)(2,1)S(1)}, u32[]{:S(2)}, u32[]{:S(2)}) %collective-permute-start.56) | collective-permute-done | bytes 983072 | tf_op jit(solution)/shard_map/ppermute | solution.py:725
  397.0 3.6 collective-permute-start.59
  404.9 5.9 %collective-permute-done.61 = bf16[384,1280]{1,0:T(8,128)(2,1)} collective-permute-done((bf16[384,1280]{1,0:T(8,128)(2,1)S(1)}, bf16[384,1280]{1,0:T(8,128)(2,1)}, u32[]{:S(2)}, u32[]{:S(2)}) %collective-permute-start.61) | collective-permute-done | bytes 983072 | tf_op jit(solution)/shard_map/ppermute | solution.py:725
  417.1 6.4 %weight_products.5 = (bf16[384,512]{1,0:T(8,128)(2,1)}, bf16[384,512]{1,0:T(8,128)(2,1)}, bf16[384,512]{1,0:T(8,128)(2,1)}, bf16[384,512]{1,0:T(8,128)(2,1)}) custom-call(s32[4]{0:T(128)} %pad_add_fusion.2.place_ref, bf16[1024,1536]{1,0:T(8,128)(2,1)} %get-tuple-element.145.refs_0_.refs_2_, bf16[1024,512]{1,0:T(8,128)(2,1)} %pad_add_fusion.refs_1_), custom_call_target="tpu_custom_call" | custom-call | flops 1610612736 | bytes 8000000 | tf_op jit(solution)/shard_map/weight_products/pallas_call | solution.py:692
  432.0 6.7 %collective-permute-done.68 = bf16[384,512]{1,0:T(8,128)(2,1)S(1)} collective-permute-done((bf16[384,512]{1,0:T(8,128)(2,1)S(1)}, bf16[384,512]{1,0:T(8,128)(2,1)S(1)}, u32[]{:S(2)}, u32[]{:S(2)}) %collective-permute-start.68) | collective-permute-done | bytes 393248 | tf_op jit(solution)/shard_map/ppermute | solution.py:725
  438.7 8.4 %collective-permute-done.69 = bf16[384,512]{1,0:T(8,128)(2,1)S(1)} collective-permute-done((bf16[384,512]{1,0:T(8,128)(2,1)S(1)}, bf16[384,512]{1,0:T(8,128)(2,1)S(1)}, u32[]{:S(2)}, u32[]{:S(2)}) %collective-permute-start.69) | collective-permute-done | bytes 393248 | tf_op jit(solution)/shard_map/ppermute | solution.py:725
  452.5 2.8 last_output.1.hidden_ref
  467.3 11.3 %collective-permute-done.80 = bf16[192,1280]{1,0:T(8,128)(2,1)S(1)} collective-permute-done((bf16[192,1280]{1,0:T(8,128)(2,1)}, bf16[192,1280]{1,0:T(8,128)(2,1)S(1)}, u32[]{:S(2)}, u32[]{:S(2)}) %collective-permute-start.80) | collective-permute-done | bytes 491552 | tf_op jit(solution)/shard_map/ppermute | solution.py:725
  479.0 5.4 collective-permute-done.81
  494.0 4.3 collective-permute-done.76
  498.4 3.3 collective-permute-done.64.a_ref
  501.7 9.4 %collective-permute-done.65.b_ref = bf16[128,1536]{1,0:T(8,128)(2,1)S(1)} collective-permute-done((bf16[128,1536]{1,0:T(8,128)(2,1)S(1)}, bf16[128,1536]{1,0:T(8,128)(2,1)S(1)}, u32[]{:S(2)}, u32[]{:S(2)}) %collective-permute-start.65) | collective-permute-done | bytes 393248 | tf_op jit(solution)/shard_map/ppermute | solution.py:725
  511.9 3.5 outputs.1
  519.9 5.5 collective-permute-done.84
  525.5 2.8 collective-permute-done.85
  528.3 3.0 collective-permute-done.86
  531.3 8.2 %collective-permute-start.87 = (bf16[4,192,768]{2,1,0:T(8,128)(2,1)S(1)}, bf16[4,192,768]{2,1,0:T(8,128)(2,1)S(1)}, u32[]{:S(2)}, u32[]{:S(2)}) collective-permute-start(bf16[4,192,768]{2,1,0:T(8,128)(2,1)S(1)} %bitcast_dynamic-update-slice_fusion.4.here_ref), channel_id=1, source_target_pairs={{0,8},{1,9},{2,10},{3,11},{4,12},{5,13},{6,14},{7,15},{8,0},{9,1},... | collective-permute-start | bytes 3538952 | tf_op jit(solution)/shard_map/ppermute | solution.py:725
  543.0 4.6 write_sums.3
  547.6 6.2 %write_sums.4 = (f32[2,4,2,192,384]{4,3,2,1,0:T(8,128)}, f32[2,384,1536]{2,1,0:T(8,128)}, f32[2,4,2,192,384]{4,3,2,1,0:T(8,128)}, f32[1,4,2,192,128]{4,3,2,1,0:T(8,128)}) custom-call(s32[4]{0:T(128)} %pad_add_fusion.2.place_ref, bf16[4,192,1280]{2,1,0:T(8,128)(2,1)} %copy-done.1, ...), custom_call_target="tpu_custom_call", output_to_operand_aliasing={{0}: (3, {}), {1}: (4, {})} | custom-call | tf_op jit(solution)/shard_map/write_sums/pallas_call | solution.py:930
  553.9 3.9 write_sums.5
  (443 shorter events, 179.1 us)
Async XLA Ops:
  19.6 60.9 %collective-permute-start.8 = (bf16[1536,1152]{1,0:T(8,128)(2,1)S(1)}, bf16[1536,1152]{1,0:T(8,128)(2,1)}, u32[]{:S(2)}, u32[]{:S(2)}) collective-permute-start(bf16[1536,1152]{1,0:T(8,128)(2,1)S(1)} %pad_maximum_fusion.refs_8_), channel_id=1, source_target_pairs={{4,8},{5,9},{6,10},{7,11},{8,4},{9,5},{10,6},{11,7},{20,24},{21,25... | collective-permute-start | bytes 10616840 | tf_op jit(solution)/shard_map/ppermute | solution.py:725
  27.7 20.2 %collective-permute-start.4 = (bf16[160,1536]{1,0:T(8,128)(2,1)}, bf16[160,1536]{1,0:T(8,128)(2,1)S(1)}, u32[]{:S(2)}, u32[]{:S(2)}) collective-permute-start(bf16[160,1536]{1,0:T(8,128)(2,1)} %first_norm.1.refs_0_), channel_id=1, source_target_pairs={{0,3},{1,0},{2,1},{3,2},{4,7},{5,4},{6,5},{7,6},{8,11},{9,8},{10,9... | collective-permute-start | bytes 1474568 | tf_op jit(solution)/shard_map/ppermute | solution.py:725
  29.9 22.3 %collective-permute-start.6 = (bf16[160,1536]{1,0:T(8,128)(2,1)}, bf16[160,1536]{1,0:T(8,128)(2,1)S(1)}, u32[]{:S(2)}, u32[]{:S(2)}) collective-permute-start(bf16[160,1536]{1,0:T(8,128)(2,1)} %first_norm.1.refs_0_), channel_id=1, source_target_pairs={{0,2},{1,3},{2,0},{3,1},{4,6},{5,7},{6,4},{7,5},{8,10},{9,11},{10,... | collective-permute-start | bytes 1474568 | tf_op jit(solution)/shard_map/ppermute | solution.py:725
  31.2 22.8 %collective-permute-start.9 = (bf16[160,1536]{1,0:T(8,128)(2,1)S(1)}, bf16[160,1536]{1,0:T(8,128)(2,1)S(1)}, u32[]{:S(2)}, u32[]{:S(2)}) collective-permute-start(bf16[160,1536]{1,0:T(8,128)(2,1)S(1)} %pad_maximum_fusion.4), channel_id=1, source_target_pairs={{4,8},{5,9},{6,10},{7,11},{8,4},{9,5},{10,6},{11,7},{20,24},{21,25... | collective-permute-start | bytes 1474568 | tf_op jit(solution)/shard_map/ppermute | solution.py:725
  36.7 38.8 %collective-permute-start.1 = (bf16[160,1536]{1,0:T(8,128)(2,1)}, bf16[160,1536]{1,0:T(8,128)(2,1)S(1)}, u32[]{:S(2)}, u32[]{:S(2)}) collective-permute-start(bf16[160,1536]{1,0:T(8,128)(2,1)} %first_norm.1.refs_0_), channel_id=1, source_target_pairs={{0,8},{1,9},{2,10},{3,11},{4,12},{5,13},{6,14},{7,15},{8,0},{9,1},... | collective-permute-start | bytes 1474568 | tf_op jit(solution)/shard_map/ppermute | solution.py:725
  48.0 29.1 %collective-permute-start.3 = (bf16[160,1536]{1,0:T(8,128)(2,1)S(1)}, bf16[160,1536]{1,0:T(8,128)(2,1)S(1)}, u32[]{:S(2)}, u32[]{:S(2)}) collective-permute-start(bf16[160,1536]{1,0:T(8,128)(2,1)S(1)} %collective-permute-done.2.refs_2_), channel_id=1, source_target_pairs={{0,8},{1,9},{2,10},{3,11},{4,12},{5,13},{6,14},{7,15},{8,0},{9,1},... | collective-permute-start | bytes 1474568 | tf_op jit(solution)/shard_map/ppermute | solution.py:725
  52.2 27.1 %collective-permute-start.5 = (bf16[160,1536]{1,0:T(8,128)(2,1)S(1)}, bf16[160,1536]{1,0:T(8,128)(2,1)S(1)}, u32[]{:S(2)}, u32[]{:S(2)}) collective-permute-start(bf16[160,1536]{1,0:T(8,128)(2,1)S(1)} %collective-permute-done.4.refs_4_), channel_id=1, source_target_pairs={{0,8},{1,9},{2,10},{3,11},{4,12},{5,13},{6,14},{7,15},{8,0},{9,1},... | collective-permute-start | bytes 1474568 | tf_op jit(solution)/shard_map/ppermute | solution.py:725
  54.0 26.6 %collective-permute-start.7 = (bf16[160,1536]{1,0:T(8,128)(2,1)S(1)}, bf16[160,1536]{1,0:T(8,128)(2,1)S(1)}, u32[]{:S(2)}, u32[]{:S(2)}) collective-permute-start(bf16[160,1536]{1,0:T(8,128)(2,1)S(1)} %collective-permute-done.6.refs_6_), channel_id=1, source_target_pairs={{0,8},{1,9},{2,10},{3,11},{4,12},{5,13},{6,14},{7,15},{8,0},{9,1},... | collective-permute-start | bytes 1474568 | tf_op jit(solution)/shard_map/ppermute | solution.py:725
  75.5 28.9 %collective-permute-start.10 = (bf16[160,1536]{1,0:T(8,128)(2,1)S(1)}, bf16[160,1536]{1,0:T(8,128)(2,1)S(1)}, u32[]{:S(2)}, u32[]{:S(2)}) collective-permute-start(bf16[160,1536]{1,0:T(8,128)(2,1)S(1)} %pad_maximum_fusion.4), channel_id=1, source_target_pairs={{0,1},{1,2},{2,3},{3,0},{4,9},{5,10},{6,11},{7,8},{8,5},{9,6},{10,... | collective-permute-start | bytes 1474568 | tf_op jit(solution)/shard_map/ppermute | solution.py:725
  77.1 27.3 %collective-permute-start.11 = (bf16[160,1536]{1,0:T(8,128)(2,1)S(1)}, bf16[160,1536]{1,0:T(8,128)(2,1)S(1)}, u32[]{:S(2)}, u32[]{:S(2)}) collective-permute-start(bf16[160,1536]{1,0:T(8,128)(2,1)S(1)} %pad_maximum_fusion.4), channel_id=1, source_target_pairs={{0,3},{1,0},{2,1},{3,2},{4,11},{5,8},{6,9},{7,10},{8,7},{9,4},{10,... | collective-permute-start | bytes 1474568 | tf_op jit(solution)/shard_map/ppermute | solution.py:725
  79.3 25.1 %collective-permute-start.12 = (bf16[160,1536]{1,0:T(8,128)(2,1)S(1)}, bf16[160,1536]{1,0:T(8,128)(2,1)S(1)}, u32[]{:S(2)}, u32[]{:S(2)}) collective-permute-start(bf16[160,1536]{1,0:T(8,128)(2,1)S(1)} %pad_maximum_fusion.4), channel_id=1, source_target_pairs={{0,2},{1,3},{2,0},{3,1},{4,10},{5,11},{6,8},{7,9},{8,6},{9,7},{10,... | collective-permute-start | bytes 1474568 | tf_op jit(solution)/shard_map/ppermute | solution.py:725
  114.7 53.1 %collective-permute-start.28 = (bf16[1536,1152]{1,0:T(8,128)(2,1)S(1)}, bf16[1536,1152]{1,0:T(8,128)(2,1)}, u32[]{:S(2)}, u32[]{:S(2)}) collective-permute-start(bf16[1536,1152]{1,0:T(8,128)(2,1)S(1)} %pad_maximum_fusion.1.refs_16_), channel_id=1, source_target_pairs={{4,8},{5,9},{6,10},{7,11},{8,4},{9,5},{10,6},{11,7},{20,24},{21,25... | collective-permute-start | bytes 10616840 | tf_op jit(solution)/shard_map/ppermute | solution.py:725
  118.0 21.8 %collective-permute-start.15 = (bf16[128,1664]{1,0:T(8,128)(2,1)S(1)}, bf16[128,1664]{1,0:T(8,128)(2,1)S(1)}, u32[]{:S(2)}, u32[]{:S(2)}) collective-permute-start(bf16[128,1664]{1,0:T(8,128)(2,1)S(1)} %get-tuple-element.254), channel_id=1, source_target_pairs={{0,2},{1,3},{2,0},{3,1},{4,6},{5,7},{6,4},{7,5},{8,10},{9,11},{10,... | collective-permute-start | bytes 1277960 | tf_op jit(solution)/shard_map/ppermute | solution.py:725
  118.9 21.1 %collective-permute-start.16 = (bf16[128,1664]{1,0:T(8,128)(2,1)S(1)}, bf16[128,1664]{1,0:T(8,128)(2,1)S(1)}, u32[]{:S(2)}, u32[]{:S(2)}) collective-permute-start(bf16[128,1664]{1,0:T(8,128)(2,1)S(1)} %get-tuple-element.253), channel_id=1, source_target_pairs={{0,3},{1,0},{2,1},{3,2},{4,7},{5,4},{6,5},{7,6},{8,11},{9,8},{10,9... | collective-permute-start | bytes 1277960 | tf_op jit(solution)/shard_map/ppermute | solution.py:725
  120.9 23.2 %collective-permute-start.24 = (bf16[160,1536]{1,0:T(8,128)(2,1)S(1)}, bf16[160,1536]{1,0:T(8,128)(2,1)S(1)}, u32[]{:S(2)}, u32[]{:S(2)}) collective-permute-start(bf16[160,1536]{1,0:T(8,128)(2,1)S(1)} %copy-done.9), channel_id=1, source_target_pairs={{0,8},{1,9},{2,10},{3,11},{4,12},{5,13},{6,14},{7,15},{8,0},{9,1},... | collective-permute-start | bytes 1474568 | tf_op jit(solution)/shard_map/ppermute | solution.py:725
  128.2 16.7 %collective-permute-start.25 = (bf16[160,1536]{1,0:T(8,128)(2,1)S(1)}, bf16[160,1536]{1,0:T(8,128)(2,1)S(1)}, u32[]{:S(2)}, u32[]{:S(2)}) collective-permute-start(bf16[160,1536]{1,0:T(8,128)(2,1)S(1)} %copy-done.57), channel_id=1, source_target_pairs={{0,8},{1,9},{2,10},{3,11},{4,12},{5,13},{6,14},{7,15},{8,0},{9,1},... | collective-permute-start | bytes 1474568 | tf_op jit(solution)/shard_map/ppermute | solution.py:725
  146.8 18.4 %collective-permute-start.22 = (bf16[128,1536]{1,0:T(8,128)(2,1)}, bf16[128,1536]{1,0:T(8,128)(2,1)S(1)}, u32[]{:S(2)}, u32[]{:S(2)}) collective-permute-start(bf16[128,1536]{1,0:T(8,128)(2,1)} %get-tuple-element.110.refs_0_), channel_id=1, source_target_pairs={{0,2},{1,3},{2,0},{3,1},{4,6},{5,7},{6,4},{7,5},{8,10},{9,11},{10,... | collective-permute-start | bytes 1179656 | tf_op jit(solution)/shard_map/ppermute | solution.py:725
  147.9 19.4 %collective-permute-start.17 = (bf16[128,1536]{1,0:T(8,128)(2,1)}, bf16[128,1536]{1,0:T(8,128)(2,1)S(1)}, u32[]{:S(2)}, u32[]{:S(2)}) collective-permute-start(bf16[128,1536]{1,0:T(8,128)(2,1)} %get-tuple-element.110.refs_0_), channel_id=1, source_target_pairs={{0,8},{1,9},{2,10},{3,11},{4,12},{5,13},{6,14},{7,15},{8,0},{9,1},... | collective-permute-start | bytes 1179656 | tf_op jit(solution)/shard_map/ppermute | solution.py:725
  209.1 35.4 %collective-permute-start.34 = (bf16[128,1664]{1,0:T(8,128)(2,1)S(1)}, bf16[128,1664]{1,0:T(8,128)(2,1)S(1)}, u32[]{:S(2)}, u32[]{:S(2)}) collective-permute-start(bf16[128,1664]{1,0:T(8,128)(2,1)S(1)} %get-tuple-element.252), channel_id=1, source_target_pairs={{0,1},{1,2},{2,3},{3,0},{4,5},{5,6},{6,7},{7,4},{8,9},{9,10},{10,1... | collective-permute-start | bytes 1277960 | tf_op jit(solution)/shard_map/ppermute | solution.py:725
  209.2 35.2 %collective-permute-start.35 = (bf16[128,1664]{1,0:T(8,128)(2,1)S(1)}, bf16[128,1664]{1,0:T(8,128)(2,1)S(1)}, u32[]{:S(2)}, u32[]{:S(2)}) collective-permute-start(bf16[128,1664]{1,0:T(8,128)(2,1)S(1)} %get-tuple-element.251), channel_id=1, source_target_pairs={{0,2},{1,3},{2,0},{3,1},{4,6},{5,7},{6,4},{7,5},{8,10},{9,11},{10,... | collective-permute-start | bytes 1277960 | tf_op jit(solution)/shard_map/ppermute | solution.py:725
  211.3 33.2 %collective-permute-start.36 = (bf16[128,1664]{1,0:T(8,128)(2,1)S(1)}, bf16[128,1664]{1,0:T(8,128)(2,1)S(1)}, u32[]{:S(2)}, u32[]{:S(2)}) collective-permute-start(bf16[128,1664]{1,0:T(8,128)(2,1)S(1)} %get-tuple-element.250), channel_id=1, source_target_pairs={{0,3},{1,0},{2,1},{3,2},{4,7},{5,4},{6,5},{7,6},{8,11},{9,8},{10,9... | collective-permute-start | bytes 1277960 | tf_op jit(solution)/shard_map/ppermute | solution.py:725
  244.5 18.6 %collective-permute-start.37 = (bf16[512,1536]{1,0:T(8,128)(2,1)}, bf16[512,1536]{1,0:T(8,128)(2,1)S(1)}, u32[]{:S(2)}, u32[]{:S(2)}) collective-permute-start(bf16[512,1536]{1,0:T(8,128)(2,1)} %get-tuple-element.128), channel_id=1, source_target_pairs={{0,8},{1,9},{2,10},{3,11},{4,12},{5,13},{6,14},{7,15},{8,0},{9,1},... | collective-permute-start | bytes 4718600 | tf_op jit(solution)/shard_map/ppermute | solution.py:725
  255.5 37.0 %collective-permute-start.49 = (bf16[1536,768]{1,0:T(8,128)(2,1)}, bf16[1536,768]{1,0:T(8,128)(2,1)S(1)}, u32[]{:S(2)}, u32[]{:S(2)}) collective-permute-start(bf16[1536,768]{1,0:T(8,128)(2,1)} %weight_products.3), channel_id=1, source_target_pairs={{4,0},{5,1},{6,2},{7,3},{8,12},{9,13},{10,14},{11,15},{20,16},{21,... | collective-permute-start | bytes 7077896 | tf_op jit(solution)/shard_map/ppermute | solution.py:725
  263.6 22.8 %collective-permute-start.39 = (bf16[128,1792]{1,0:T(8,128)(2,1)S(1)}, bf16[128,1792]{1,0:T(8,128)(2,1)S(1)}, u32[]{:S(2)}, u32[]{:S(2)}) collective-permute-start(bf16[128,1792]{1,0:T(8,128)(2,1)S(1)} %pad_maximum_fusion.5), channel_id=1, source_target_pairs={{0,1},{1,2},{2,3},{3,0},{4,5},{5,6},{6,7},{7,4},{8,9},{9,10},{10,1... | collective-permute-start | bytes 1376264 | tf_op jit(solution)/shard_map/ppermute | solution.py:725
  264.0 22.5 %collective-permute-start.40 = (bf16[128,1792]{1,0:T(8,128)(2,1)S(1)}, bf16[128,1792]{1,0:T(8,128)(2,1)S(1)}, u32[]{:S(2)}, u32[]{:S(2)}) collective-permute-start(bf16[128,1792]{1,0:T(8,128)(2,1)S(1)} %pad_maximum_fusion.6), channel_id=1, source_target_pairs={{0,2},{1,3},{2,0},{3,1},{4,6},{5,7},{6,4},{7,5},{8,10},{9,11},{10,... | collective-permute-start | bytes 1376264 | tf_op jit(solution)/shard_map/ppermute | solution.py:725
  265.6 21.3 %collective-permute-start.41 = (bf16[128,1792]{1,0:T(8,128)(2,1)S(1)}, bf16[128,1792]{1,0:T(8,128)(2,1)S(1)}, u32[]{:S(2)}, u32[]{:S(2)}) collective-permute-start(bf16[128,1792]{1,0:T(8,128)(2,1)S(1)} %pad_maximum_fusion.7), channel_id=1, source_target_pairs={{0,3},{1,0},{2,1},{3,2},{4,7},{5,4},{6,5},{7,6},{8,11},{9,8},{10,9... | collective-permute-start | bytes 1376264 | tf_op jit(solution)/shard_map/ppermute | solution.py:725
  293.3 26.4 %collective-permute-start.50 = (bf16[768,768]{1,0:T(8,128)(2,1)S(1)}, bf16[768,768]{1,0:T(8,128)(2,1)}, u32[]{:S(2)}, u32[]{:S(2)}) collective-permute-start(bf16[768,768]{1,0:T(8,128)(2,1)S(1)} %slice.265), channel_id=1, source_target_pairs={{0,8},{1,9},{2,10},{3,11},{12,4},{13,5},{14,6},{15,7},{16,24},{17,... | collective-permute-start | bytes 3538952 | tf_op jit(solution)/shard_map/ppermute | solution.py:725
  298.8 19.8 %collective-permute-start.45 = (bf16[128,1664]{1,0:T(8,128)(2,1)}, bf16[128,1664]{1,0:T(8,128)(2,1)}, u32[]{:S(2)}, u32[]{:S(2)}) collective-permute-start(bf16[128,1664]{1,0:T(8,128)(2,1)} %get-tuple-element.138.refs_0_), channel_id=1, source_target_pairs={{0,3},{1,0},{2,1},{3,2},{4,7},{5,4},{6,5},{7,6},{8,11},{9,8},{10,9... | collective-permute-start | bytes 1277960 | tf_op jit(solution)/shard_map/ppermute | solution.py:725
  300.4 19.2 %collective-permute-start.47 = (bf16[128,1664]{1,0:T(8,128)(2,1)}, bf16[128,1664]{1,0:T(8,128)(2,1)}, u32[]{:S(2)}, u32[]{:S(2)}) collective-permute-start(bf16[128,1664]{1,0:T(8,128)(2,1)} %get-tuple-element.138.refs_0_), channel_id=1, source_target_pairs={{0,2},{1,3},{2,0},{3,1},{4,6},{5,7},{6,4},{7,5},{8,10},{9,11},{10,... | collective-permute-start | bytes 1277960 | tf_op jit(solution)/shard_map/ppermute | solution.py:725
  301.4 19.7 %collective-permute-start.42 = (bf16[128,1664]{1,0:T(8,128)(2,1)}, bf16[128,1664]{1,0:T(8,128)(2,1)}, u32[]{:S(2)}, u32[]{:S(2)}) collective-permute-start(bf16[128,1664]{1,0:T(8,128)(2,1)} %get-tuple-element.138.refs_0_), channel_id=1, source_target_pairs={{0,8},{1,9},{2,10},{3,11},{4,12},{5,13},{6,14},{7,15},{8,0},{9,1},... | collective-permute-start | bytes 1277960 | tf_op jit(solution)/shard_map/ppermute | solution.py:725
  347.0 38.2 %collective-permute-start.55 = (bf16[384,1280]{1,0:T(8,128)(2,1)}, bf16[384,1280]{1,0:T(8,128)(2,1)S(1)}, u32[]{:S(2)}, u32[]{:S(2)}) collective-permute-start(bf16[384,1280]{1,0:T(8,128)(2,1)} %get-tuple-element.152), channel_id=1, source_target_pairs={{0,32},{1,33},{2,34},{3,35},{4,36},{5,37},{6,38},{7,39},{8,40},{9,... | collective-permute-start | bytes 2949128 | tf_op jit(solution)/shard_map/ppermute | solution.py:725
  349.2 44.6 %collective-permute-start.56 = (bf16[384,1280]{1,0:T(8,128)(2,1)}, bf16[384,1280]{1,0:T(8,128)(2,1)S(1)}, u32[]{:S(2)}, u32[]{:S(2)}) collective-permute-start(bf16[384,1280]{1,0:T(8,128)(2,1)} %get-tuple-element.153), channel_id=1, source_target_pairs={{0,64},{1,65},{2,66},{3,67},{4,68},{5,69},{6,70},{7,71},{8,72},{9,... | collective-permute-start | bytes 2949128 | tf_op jit(solution)/shard_map/ppermute | solution.py:725
  351.6 42.1 %collective-permute-start.57 = (bf16[384,1280]{1,0:T(8,128)(2,1)}, bf16[384,1280]{1,0:T(8,128)(2,1)S(1)}, u32[]{:S(2)}, u32[]{:S(2)}) collective-permute-start(bf16[384,1280]{1,0:T(8,128)(2,1)} %get-tuple-element.154), channel_id=1, source_target_pairs={{0,96},{1,97},{2,98},{3,99},{4,100},{5,101},{6,102},{7,103},{8,104... | collective-permute-start | bytes 2949128 | tf_op jit(solution)/shard_map/ppermute | solution.py:725
  394.3 16.5 %collective-permute-start.61 = (bf16[384,1280]{1,0:T(8,128)(2,1)S(1)}, bf16[384,1280]{1,0:T(8,128)(2,1)}, u32[]{:S(2)}, u32[]{:S(2)}) collective-permute-start(bf16[384,1280]{1,0:T(8,128)(2,1)S(1)} %add_convert_fusion.2), channel_id=1, source_target_pairs={{4,0},{5,1},{6,2},{7,3},{8,12},{9,13},{10,14},{11,15},{20,16},{21,... | collective-permute-start | bytes 2949128 | tf_op jit(solution)/shard_map/ppermute | solution.py:725
  428.0 19.1 %collective-permute-start.69 = (bf16[384,512]{1,0:T(8,128)(2,1)S(1)}, bf16[384,512]{1,0:T(8,128)(2,1)S(1)}, u32[]{:S(2)}, u32[]{:S(2)}) collective-permute-start(bf16[384,512]{1,0:T(8,128)(2,1)S(1)} %get-tuple-element.287), channel_id=1, source_target_pairs={{0,64},{1,65},{2,66},{3,67},{4,68},{5,69},{6,70},{7,71},{8,72},{9,... | collective-permute-start | bytes 1179656 | tf_op jit(solution)/shard_map/ppermute | solution.py:725
  430.4 17.2 %collective-permute-start.70 = (bf16[384,512]{1,0:T(8,128)(2,1)S(1)}, bf16[384,512]{1,0:T(8,128)(2,1)}, u32[]{:S(2)}, u32[]{:S(2)}) collective-permute-start(bf16[384,512]{1,0:T(8,128)(2,1)S(1)} %get-tuple-element.288), channel_id=1, source_target_pairs={{0,96},{1,97},{2,98},{3,99},{4,100},{5,101},{6,102},{7,103},{8,104... | collective-permute-start | bytes 1179656 | tf_op jit(solution)/shard_map/ppermute | solution.py:725
  430.5 18.6 %collective-permute-start.71 = (bf16[192,1280]{1,0:T(8,128)(2,1)S(1)}, bf16[192,1280]{1,0:T(8,128)(2,1)}, u32[]{:S(2)}, u32[]{:S(2)}) collective-permute-start(bf16[192,1280]{1,0:T(8,128)(2,1)S(1)} %slice_select_fusion.1), channel_id=1, source_target_pairs={{0,16},{1,17},{2,18},{3,19},{4,20},{5,21},{6,22},{7,23},{8,24},{9,... | collective-permute-start | bytes 1474568 | tf_op jit(solution)/shard_map/ppermute | solution.py:725
  430.7 26.2 %collective-permute-start.83 = (bf16[192,768]{1,0:T(8,128)(2,1)S(1)}, bf16[192,768]{1,0:T(8,128)(2,1)}, u32[]{:S(2)}, u32[]{:S(2)}) collective-permute-start(bf16[192,768]{1,0:T(8,128)(2,1)S(1)} %add_convert_fusion.16), channel_id=1, source_target_pairs={{0,16},{1,17},{2,18},{3,19},{4,20},{5,21},{6,22},{7,23},{8,24},{9,... | collective-permute-start | bytes 884744 | tf_op jit(solution)/shard_map/ppermute | solution.py:725
  457.9 31.2 %collective-permute-start.63 = (bf16[512,1536]{1,0:T(8,128)(2,1)}, bf16[512,1536]{1,0:T(8,128)(2,1)S(1)}, u32[]{:S(2)}, u32[]{:S(2)}) collective-permute-start(bf16[512,1536]{1,0:T(8,128)(2,1)} %get-tuple-element.177), channel_id=1, source_target_pairs={{0,8},{1,9},{2,10},{3,11},{4,12},{5,13},{6,14},{7,15},{8,0},{9,1},... | collective-permute-start | bytes 4718600 | tf_op jit(solution)/shard_map/ppermute | solution.py:725
  460.5 18.1 %collective-permute-start.80 = (bf16[192,1280]{1,0:T(8,128)(2,1)}, bf16[192,1280]{1,0:T(8,128)(2,1)S(1)}, u32[]{:S(2)}, u32[]{:S(2)}) collective-permute-start(bf16[192,1280]{1,0:T(8,128)(2,1)} %get-tuple-element.243), channel_id=1, source_target_pairs={{0,64},{1,65},{2,66},{3,67},{4,68},{5,69},{6,70},{7,71},{8,72},{9,... | collective-permute-start | bytes 1474568 | tf_op jit(solution)/shard_map/ppermute | solution.py:725
  462.6 21.8 %collective-permute-start.81 = (bf16[192,1280]{1,0:T(8,128)(2,1)}, bf16[192,1280]{1,0:T(8,128)(2,1)S(1)}, u32[]{:S(2)}, u32[]{:S(2)}) collective-permute-start(bf16[192,1280]{1,0:T(8,128)(2,1)} %get-tuple-element.243), channel_id=1, source_target_pairs={{0,96},{1,97},{2,98},{3,99},{4,100},{5,101},{6,102},{7,103},{8,104... | collective-permute-start | bytes 1474568 | tf_op jit(solution)/shard_map/ppermute | solution.py:725
  463.4 15.2 %collective-permute-start.73 = (bf16[192,512]{1,0:T(8,128)(2,1)S(1)}, bf16[192,512]{1,0:T(8,128)(2,1)S(1)}, u32[]{:S(2)}, u32[]{:S(2)}) collective-permute-start(bf16[192,512]{1,0:T(8,128)(2,1)S(1)} %slice.279), channel_id=1, source_target_pairs={{0,8},{1,9},{2,10},{3,11},{12,4},{13,5},{14,6},{15,7},{16,24},{17,... | collective-permute-start | bytes 589832 | tf_op jit(solution)/shard_map/ppermute | solution.py:725
  484.4 63.2 %collective-permute-start.82 = (bf16[4,192,1280]{2,1,0:T(8,128)(2,1)S(1)}, bf16[4,192,1280]{2,1,0:T(8,128)(2,1)}, u32[]{:S(2)}, u32[]{:S(2)}) collective-permute-start(bf16[4,192,1280]{2,1,0:T(8,128)(2,1)S(1)} %bitcast_dynamic-update-slice_fusion.here_ref), channel_id=1, source_target_pairs={{0,8},{1,9},{2,10},{3,11},{4,12},{5,13},{6,14},{7,15},{8,0},{9,1},... | collective-permute-start | bytes 5898248 | tf_op jit(solution)/shard_map/ppermute | solution.py:725
  491.3 19.8 %collective-permute-start.65 = (bf16[128,1536]{1,0:T(8,128)(2,1)S(1)}, bf16[128,1536]{1,0:T(8,128)(2,1)S(1)}, u32[]{:S(2)}, u32[]{:S(2)}) collective-permute-start(bf16[128,1536]{1,0:T(8,128)(2,1)S(1)} %get-tuple-element.258), channel_id=1, source_target_pairs={{0,2},{1,3},{2,0},{3,1},{4,6},{5,7},{6,4},{7,5},{8,10},{9,11},{10,... | collective-permute-start | bytes 1179656 | tf_op jit(solution)/shard_map/ppermute | solution.py:725
  494.0 17.0 %collective-permute-start.66 = (bf16[128,1536]{1,0:T(8,128)(2,1)S(1)}, bf16[128,1536]{1,0:T(8,128)(2,1)S(1)}, u32[]{:S(2)}, u32[]{:S(2)}) collective-permute-start(bf16[128,1536]{1,0:T(8,128)(2,1)S(1)} %get-tuple-element.257), channel_id=1, source_target_pairs={{0,3},{1,0},{2,1},{3,2},{4,7},{5,4},{6,5},{7,6},{8,11},{9,8},{10,9... | collective-permute-start | bytes 1179656 | tf_op jit(solution)/shard_map/ppermute | solution.py:725
  498.4 17.0 %collective-permute-start.77 = (bf16[192,512]{1,0:T(8,128)(2,1)S(1)}, bf16[192,512]{1,0:T(8,128)(2,1)S(1)}, u32[]{:S(2)}, u32[]{:S(2)}) collective-permute-start(bf16[192,512]{1,0:T(8,128)(2,1)S(1)} %get-tuple-element.245), channel_id=1, source_target_pairs={{0,96},{1,97},{2,98},{3,99},{4,100},{5,101},{6,102},{7,103},{8,104... | collective-permute-start | bytes 589832 | tf_op jit(solution)/shard_map/ppermute | solution.py:725
  515.5 38.4 %collective-permute-start.78 = (bf16[4,192,512]{2,1,0:T(8,128)(2,1)S(1)}, bf16[4,192,512]{2,1,0:T(8,128)(2,1)}, u32[]{:S(2)}, u32[]{:S(2)}) collective-permute-start(bf16[4,192,512]{2,1,0:T(8,128)(2,1)S(1)} %bitcast_dynamic-update-slice_fusion.8.here_ref), channel_id=1, source_target_pairs={{0,8},{1,9},{2,10},{3,11},{4,12},{5,13},{6,14},{7,15},{8,0},{9,1},... | collective-permute-start | bytes 2359304 | tf_op jit(solution)/shard_map/ppermute | solution.py:725
  519.1 20.4 %collective-permute-start.67 = (bf16[128,3072]{1,0:T(8,128)(2,1)}, bf16[128,3072]{1,0:T(8,128)(2,1)S(1)}, u32[]{:S(2)}, u32[]{:S(2)}) collective-permute-start(bf16[128,3072]{1,0:T(8,128)(2,1)} %outputs.1), channel_id=1, source_target_pairs={{4,8},{5,9},{6,10},{7,11},{8,4},{9,5},{10,6},{11,7},{20,24},{21,25... | collective-permute-start | bytes 2359304 | tf_op jit(solution)/shard_map/ppermute | solution.py:725
  (122 other events, 1095.0 us)

commit v4 on v3

--- a/solution.py
+++ b/solution.py
@@ -751,14 +751,14 @@
     return dp // (NYL * NC), dp // NC % NYL, dp % NC, tensor // NZ, tensor % NZ
 
 
-def gather(v, parts, traded_own=None):
+def gather(v, parts, traded_own=None, later=()):
     arrays, sources = [], []
     for k in (0, 1, 3, 2):
         if traded_own is not None:
             piece = trade(v, k) if k else traded_own
         else:
             piece = send_z(v, k) if k else v
-        arrays += [piece, send_core(piece)]
+        arrays += [piece, send_core(after(piece, *later) if later else piece)]
         sources += [(False, -k % NZ, 0), (True, -k % NZ, 0)]
     return arrays, sources, parts
 
@@ -866,8 +866,9 @@
     return out
 
 
-def collect(part):
+def collect(part, meanwhile=()):
     out = collect_x(part)
+    out = after(out, *meanwhile) if meanwhile else out
     return out, send_core(out)
 
 
@@ -1110,11 +1111,11 @@
     out0 = run_forward(place, [gathered0], w0, wdt[0], smalls[0], state, head_dim)
     w0, xn0, wbc0, z0, xp0, bc0, dt0, y0, hin0, mine, other = out0
     grads = after(grads, sent)
-    gathered_grad = gather(grads, (rows, bc_rows), trade_places(grads))
+    gathered_grad = gather(grads, (rows, bc_rows), trade_places(grads), (mine,))
     grad_held = gathered_grad[0][0]
-    terms = scatter((mine, after(other, *gathered_grad[0][::2])))
+    terms = scatter((mine, after(other, *gathered_grad[0][2::2])))
     w1 = pack_weights(1)
-    w1 = w1, [traded(after(w1, terms[0]))], [(0, None)]
+    w1 = w1, [traded(after(w1, terms[0], grad_held))], [(0, None)]
     res1, mixed0, rms0, normed1 = row_call(
         functools.partial(middle_kernel, inner_all),
         "middle_norm",
@@ -1188,14 +1189,15 @@
     tiny_shape = tiny.shape
     tiny = pad_to(tiny.reshape(-1, tiny_lanes), width, tiny_lanes)
     tiny = jnp.pad(tiny, ((0, 0), (tiny_at, 0))).astype(bf16)
-    early = halve(sum_far(early))
-    late = weight_products(place, [(xn0, after(with_bc(dxt0, bc_sum), early))])
+    early = halve(sum_far(after(early, dxt0)))
+    home = fold(mine, send_core(other))
+    late = weight_products(place, [(xn0, after(with_bc(dxt0, bc_sum), early, home[0]))])
     early = sum_beside(early)
+    tiny = after(tiny, early)
     late = [v + t for v, t in zip(late, cut_x(tiny))]
-    mine, other = after(mine, late[0]), after(other, late[0])
-    late = after(sum_x(late), early)
-
-    terms = scatter((mine, other))
+    late = sum_x(late)
+
+    terms = home[:1] + [send_z(home[k].astype(bf16), k) for k in range(1, NZ)]
     [outputs] = row_call(
         end_kernel,
         "outputs",
@@ -1204,24 +1206,22 @@
     )
     outputs_home = trade_places(outputs).astype(f32)
 
-    early = collect(early)
-    early1 = collect(after(early1, early[0], outputs))
+    early = collect(early, (outputs,))
+    early1 = collect(after(early1, early[0]))
     late = collect(sum_beside(halve(sum_far(late))))
-    g_wz, g_wo = write_sums(place, early1, True, [(0, "rows", 1, None), (channels, "blocks", 1, None)])
     g_wz, g_wo, g_wx, narrow1 = write_sums(
         place,
         early,
         False,
         [
-            (0, "rows", 0, g_wz),
-            (channels, "blocks", 0, g_wo),
+            (0, "rows", 0, None),
+            (channels, "blocks", 0, None),
             (2 * channels, "rows", 1, None),
             (3 * channels, "flat", 0, None),
         ],
     )
-    g_wx, narrow0 = write_sums(
-        place, late, False, [(0, "rows", 0, g_wx), (channels, "flat", 0, None)]
-    )
+    g_wx, narrow0 = write_sums(place, late, False, [(0, "rows", 0, g_wx), (channels, "flat", 0, None)])
+    g_wz, g_wo = write_sums(place, early1, True, [(0, "rows", 1, g_wz), (channels, "blocks", 1, g_wo)])
 
     narrow0, narrow1 = narrow0[0], narrow1[0]
     tiny = narrow0[: tiny_shape[0] * channels // tiny_lanes, tiny_at - channels :].reshape(tiny_shape)

time: 579 us -> 563 us (0.972)
  the two profiles are of different devices: /device:TPU:25 before, /device:TPU:1 now
where the time goes in v4:
time: 563 us; the launch traced here: 553 us
  Pallas kernels  174 us (31%)
  waiting for transfers between devices  152 us (27%)
  starting transfers between devices  146 us (26%)
  local copies, waits for them, and re-layouts  44.1 us (8%)
  other arithmetic  34.9 us (6%)
    ppermute x88, waiting for transfers between devices, send(): return lax.ppermute(v, ('dp', 'tensor'), pairs)  152 us
    ppermute x88, starting transfers between devices, send(): return lax.ppermute(v, ('dp', 'tensor'), pairs)  146 us
    pallas_call x5, Pallas kernels, span_call(): pl.pallas_call(kernel, grid_spec=pltpu.PrefetchScalarGridSpec(num_scalar_...  117 us
    pallas_call x3, Pallas kernels, weight_products(): pl.pallas_call(functools.partial(weight_kernel, len(pairs), split), grid_...  25.9 us
    pallas_call x5, Pallas kernels, row_call(): pl.pallas_call(kernel, grid=(1,), in_specs=[pl.BlockSpec((rows, v.shape[1...  15.7 us
    pallas_call x3, Pallas kernels, write_sums(): pl.pallas_call(functools.partial(write_kernel, plan, by_half, len(kept)),...  14.7 us
    unnamed x182, local copies, waits for them, and re-layouts  14.6 us
  transfers between devices with their start and end apart: 88, of which 32 were waited for; matrix products, arithmetic and copies ran while one was open for 10% of the time, Pallas kernels for 24%

profile of v4, /device:TPU:1, one launch (start us, length us, event | category | flops | bytes accessed | tf_op | source)
XLA Modules:
  0.0 552.8 jit_solution(17221607155265827873)
XLA Ops:
  9.3 6.2 %collective-permute-start = (bf16[192,1536]{1,0:T(8,128)(2,1)}, bf16[192,1536]{1,0:T(8,128)(2,1)}, u32[]{:S(2)}, u32[]{:S(2)}) collective-permute-start(bf16[192,1536]{1,0:T(8,128)(2,1)} %pad_maximum_fusion.3), channel_id=1, source_target_pairs={{4,8},{5,9},{6,10},{7,11},{8,4},{9,5},{10,6},{11,7},{20,24},{21,25... | collective-permute-start | bytes 1769480 | tf_op jit(solution)/shard_map/ppermute | solution.py:725
  26.2 4.4 collective-permute-start.8
  42.0 8.3 %collective-permute-done.2.refs_2_ = bf16[160,1536]{1,0:T(8,128)(2,1)S(1)} collective-permute-done((bf16[160,1536]{1,0:T(8,128)(2,1)}, bf16[160,1536]{1,0:T(8,128)(2,1)S(1)}, u32[]{:S(2)}, u32[]{:S(2)}) %collective-permute-start.2) | collective-permute-done | bytes 491552 | tf_op jit(solution)/shard_map/ppermute | solution.py:725
  50.3 4.2 collective-permute-done.4.refs_4_
  58.0 4.0 collective-permute-start.10
  64.4 6.4 %collective-permute-done.8.refs_9_ = bf16[1536,1152]{1,0:T(8,128)(2,1)} collective-permute-done((bf16[1536,1152]{1,0:T(8,128)(2,1)}, bf16[1536,1152]{1,0:T(8,128)(2,1)}, u32[]{:S(2)}, u32[]{:S(2)}) %collective-permute-start.8) | collective-permute-done | bytes 3538976 | tf_op jit(solution)/shard_map/ppermute | solution.py:725
  70.8 23.1 %layer_forward.2 = (bf16[1536,1152]{1,0:T(8,128)(2,1)}, bf16[1024,1536]{1,0:T(8,128)(2,1)}, bf16[256,1536]{1,0:T(8,128)(2,1)}, bf16[1024,384]{1,0:T(8,128)(2,1)}...) custom-call(s32[4]{0:T(128)} %pad_add_fusion.2.place_ref, ...), custom_call_target="tpu_custom_call" | custom-call | flops 20000000000 | bytes 26501120 | tf_op jit(solution)/shard_map/layer_forward/pallas_call | solution.py:496
  97.2 4.4 collective-permute-start.23
  102.0 7.0 %collective-permute-done.23 = bf16[160,1536]{1,0:T(8,128)(2,1)S(1)} collective-permute-done((bf16[160,1536]{1,0:T(8,128)(2,1)}, bf16[160,1536]{1,0:T(8,128)(2,1)S(1)}, u32[]{:S(2)}, u32[]{:S(2)}) %collective-permute-start.23) | collective-permute-done | bytes 491552 | tf_op jit(solution)/shard_map/ppermute | solution.py:725
  112.1 4.6 collective-permute-start.28
  118.3 3.3 collective-permute-start.14
  122.5 3.7 collective-permute-done.13.a_ref
  126.3 5.4 collective-permute-done.14.b_ref
  132.7 3.3 middle_norm.1
  139.9 8.0 %collective-permute-done.17.refs_2_ = bf16[128,1536]{1,0:T(8,128)(2,1)S(1)} collective-permute-done((bf16[128,1536]{1,0:T(8,128)(2,1)}, bf16[128,1536]{1,0:T(8,128)(2,1)S(1)}, u32[]{:S(2)}, u32[]{:S(2)}) %collective-permute-start.17) | collective-permute-done | bytes 393248 | tf_op jit(solution)/shard_map/ppermute | solution.py:725
  149.0 7.8 %collective-permute-start.20 = (bf16[128,1536]{1,0:T(8,128)(2,1)S(1)}, bf16[128,1536]{1,0:T(8,128)(2,1)S(1)}, u32[]{:S(2)}, u32[]{:S(2)}) collective-permute-start(bf16[128,1536]{1,0:T(8,128)(2,1)S(1)} %collective-permute-done.19.refs_4_), channel_id=1, source_target_pairs={{0,8},{1,9},{2,10},{3,11},{4,12},{5,13},{6,14},{7,15},{8,0},{9,1},... | collective-permute-start | bytes 1179656 | tf_op jit(solution)/shard_map/ppermute | solution.py:725
  159.8 27.0 %layer_forward.3 = (bf16[1536,1152]{1,0:T(8,128)(2,1)}, bf16[1024,1536]{1,0:T(8,128)(2,1)}, bf16[256,1536]{1,0:T(8,128)(2,1)}, bf16[1024,384]{1,0:T(8,128)(2,1)}...) custom-call(s32[4]{0:T(128)} %pad_add_fusion.2.place_ref, ...), custom_call_target="tpu_custom_call" | custom-call | flops 20000000000 | bytes 34398208 | tf_op jit(solution)/shard_map/layer_forward/pallas_call | solution.py:496
  187.4 3.3 collective-permute-done.29
  192.4 3.3 collective-permute-start.31
  206.8 29.6 %scan_backward.2 = (bf16[1024,384]{1,0:T(8,128)(2,1)}, bf16[1024,384]{1,0:T(8,128)(2,1)}, bf16[1024,512]{1,0:T(8,128)(2,1)}, bf16[512,256]{1,0:T(8,128)(2,1)}, b...) custom-call(s32[4]{0:T(128)} %pad_add_fusion.2.place_ref, ...), custom_call_target="tpu_custom_call" | custom-call | flops 28000000000 | bytes 21512192 | tf_op jit(solution)/shard_map/scan_backward/pallas_call | solution.py:496
  239.1 8.3 %weight_products.3 = bf16[1536,768]{1,0:T(8,128)(2,1)} custom-call(s32[4]{0:T(128)} %pad_add_fusion.2.place_ref, bf16[1024,1536]{1,0:T(8,128)(2,1)} %get-tuple-element.127.refs_4_.refs_0_.refs_2_, bf16[1024,384]{1,0:T(8,128)(2,1)} %get-tuple-element.139.refs_1_, bf16[1024,384]{1,0:T(8,128)(2,1)} %get-tuple-element.140.refs_2_, ...), custom_call_target="tpu_custom_call" | custom-call | flops 2415919104 | bytes 8000000 | tf_op jit(solution)/shard_map/weight_products/pallas_call | solution.py:692
  247.4 4.1 collective-permute-start.49
  257.7 19.0 %collective-permute-done.39.a_ref = bf16[128,1792]{1,0:T(8,128)(2,1)S(1)} collective-permute-done((bf16[128,1792]{1,0:T(8,128)(2,1)S(1)}, bf16[128,1792]{1,0:T(8,128)(2,1)S(1)}, u32[]{:S(2)}, u32[]{:S(2)}) %collective-permute-start.39) | collective-permute-done | bytes 458784 | tf_op jit(solution)/shard_map/ppermute | solution.py:725
  278.9 3.9 between_layers.1
  294.5 2.9 last_output.1.hidden_ref
  302.2 4.2 collective-permute-done.47.refs_6_
  306.4 3.0 collective-permute-start.48
  316.7 8.4 %gate_backward.1 = (bf16[1024,1536]{1,0:T(8,128)(2,1)}, bf16[1024,384]{1,0:T(8,128)(2,1)}, f32[1024,384]{1,0:T(8,128)}, bf16[1024,384]{1,0:T(8,128)(2,1)}, f32[8,384]{1,0:T(8,128)}) custom-call(s32[4]{0:T(128)} %pad_add_fusion.2.place_ref, bf16[128,1664]{1,0:T(8,128)(2,1)} %get-tuple-element.146.refs_0_, bf16[128,1664]{1,0:T(8,128)(2,1)} %collective-permute-done.42.refs_1_, ...), custom_call_target="tpu_custom_call" | custom-call | flops 6000000000 | bytes 14835712 | tf_op jit(solution)/shard_map/gate_backward/pallas_call | solution.py:496
  327.6 11.2 %weight_products.4 = (bf16[384,1280]{1,0:T(8,128)(2,1)}, bf16[384,1280]{1,0:T(8,128)(2,1)}, bf16[384,1280]{1,0:T(8,128)(2,1)}, bf16[384,1280]{1,0:T(8,128)(2,1)}) custom-call(s32[4]{0:T(128)} %pad_add_fusion.2.place_ref, bf16[1024,1536]{1,0:T(8,128)(2,1)} %get-tuple-element.153.refs_0_.refs_2_, bf16[1024,384]{1,0:T(8,128)(2,1)} %get-tuple-element.154.refs_1_, ...), custom_call_target="tpu_custom_call" | custom-call | flops 4026531840 | bytes 8000000 | tf_op jit(solution)/shard_map/weight_products/pallas_call | solution.py:692
  343.7 29.2 %scan_backward.3 = (bf16[1024,512]{1,0:T(8,128)(2,1)}, bf16[512,256]{1,0:T(8,128)(2,1)}, bf16[512,256]{1,0:T(8,128)(2,1)}, bf16[512,1536]{1,0:T(8,128)(2,1)}, bf...) custom-call(s32[4]{0:T(128)} %pad_add_fusion.2.place_ref, ...), custom_call_target="tpu_custom_call" | custom-call | flops 28000000000 | bytes 19120128 | tf_op jit(solution)/shard_map/scan_backward/pallas_call | solution.py:496
  374.6 10.6 %collective-permute-done.61 = bf16[384,1280]{1,0:T(8,128)(2,1)S(1)} collective-permute-done((bf16[384,1280]{1,0:T(8,128)(2,1)}, bf16[384,1280]{1,0:T(8,128)(2,1)S(1)}, u32[]{:S(2)}, u32[]{:S(2)}) %collective-permute-start.61) | collective-permute-done | bytes 983072 | tf_op jit(solution)/shard_map/ppermute | solution.py:725
  391.1 3.6 collective-permute-start.64
  394.7 4.3 collective-permute-done.66
  403.8 3.6 collective-permute-start.56
  412.4 8.5 %collective-permute-done.56.b_ref = bf16[128,1536]{1,0:T(8,128)(2,1)} collective-permute-done((bf16[128,1536]{1,0:T(8,128)(2,1)}, bf16[128,1536]{1,0:T(8,128)(2,1)}, u32[]{:S(2)}, u32[]{:S(2)}) %collective-permute-start.56) | collective-permute-done | bytes 393248 | tf_op jit(solution)/shard_map/ppermute | solution.py:725
  422.7 3.5 outputs.1
  426.2 9.4 %collective-permute-start.58 = (bf16[128,3072]{1,0:T(8,128)(2,1)}, bf16[128,3072]{1,0:T(8,128)(2,1)S(1)}, u32[]{:S(2)}, u32[]{:S(2)}) collective-permute-start(bf16[128,3072]{1,0:T(8,128)(2,1)} %outputs.1), channel_id=1, source_target_pairs={{4,8},{5,9},{6,10},{7,11},{8,4},{9,5},{10,6},{11,7},{20,24},{21,25... | collective-permute-start | bytes 2359304 | tf_op jit(solution)/shard_map/ppermute | solution.py:725
  435.6 6.4 %weight_products.5 = (bf16[384,512]{1,0:T(8,128)(2,1)}, bf16[384,512]{1,0:T(8,128)(2,1)}, bf16[384,512]{1,0:T(8,128)(2,1)}, bf16[384,512]{1,0:T(8,128)(2,1)}) custom-call(s32[4]{0:T(128)} %pad_add_fusion.2.place_ref, bf16[1024,1536]{1,0:T(8,128)(2,1)} %get-tuple-element.153.refs_0_.refs_2_, bf16[1024,512]{1,0:T(8,128)(2,1)} %pad_add_fusion.refs_1_), custom_call_target="tpu_custom_call" | custom-call | flops 1610612736 | bytes 8000000 | tf_op jit(solution)/shard_map/weight_products/pallas_call | solution.py:692
  449.3 14.2 %collective-permute-done.69 = bf16[384,512]{1,0:T(8,128)(2,1)S(1)} collective-permute-done((bf16[384,512]{1,0:T(8,128)(2,1)S(1)}, bf16[384,512]{1,0:T(8,128)(2,1)S(1)}, u32[]{:S(2)}, u32[]{:S(2)}) %collective-permute-start.69) | collective-permute-done | bytes 393248 | tf_op jit(solution)/shard_map/ppermute | solution.py:725
  466.0 8.1 %collective-permute-done.70 = bf16[384,512]{1,0:T(8,128)(2,1)S(1)} collective-permute-done((bf16[384,512]{1,0:T(8,128)(2,1)S(1)}, bf16[384,512]{1,0:T(8,128)(2,1)S(1)}, u32[]{:S(2)}, u32[]{:S(2)}) %collective-permute-start.70) | collective-permute-done | bytes 393248 | tf_op jit(solution)/shard_map/ppermute | solution.py:725
  475.8 4.8 collective-permute-done.80
  488.1 4.9 collective-permute-done.74
  493.7 6.7 %collective-permute-done.84 = bf16[192,768]{1,0:T(8,128)(2,1)S(1)} collective-permute-done((bf16[192,768]{1,0:T(8,128)(2,1)S(1)}, bf16[192,768]{1,0:T(8,128)(2,1)S(1)}, u32[]{:S(2)}, u32[]{:S(2)}) %collective-permute-start.84) | collective-permute-done | bytes 294944 | tf_op jit(solution)/shard_map/ppermute | solution.py:725
  500.5 4.1 collective-permute-done.75
  509.3 6.1 %collective-permute-start.78 = (bf16[4,192,512]{2,1,0:T(8,128)(2,1)S(1)}, bf16[4,192,512]{2,1,0:T(8,128)(2,1)S(1)}, u32[]{:S(2)}, u32[]{:S(2)}) collective-permute-start(bf16[4,192,512]{2,1,0:T(8,128)(2,1)S(1)} %bitcast_dynamic-update-slice_fusion.8.here_ref), channel_id=1, source_target_pairs={{0,8},{1,9},{2,10},{3,11},{4,12},{5,13},{6,14},{7,15},{8,0},{9,1},... | collective-permute-start | bytes 2359304 | tf_op jit(solution)/shard_map/ppermute | solution.py:725
  518.5 6.2 %write_sums.3 = (f32[2,4,2,192,384]{4,3,2,1,0:T(8,128)}, f32[2,384,1536]{2,1,0:T(8,128)}, f32[2,4,2,192,384]{4,3,2,1,0:T(8,128)}, f32[1,4,2,192,128]{4,3,2,1,0:T(8,128)}) custom-call(s32[4]{0:T(128)} %pad_add_fusion.2.place_ref, bf16[4,192,1280]{2,1,0:T(8,128)(2,1)} %copy-done.1, bf16[4,192,1280]{2,1,0:T(8,128)(2,1)} %copy-done.8), custom_call_target="tpu_custom_call" | custom-call | tf_op jit(solution)/shard_map/write_sums/pallas_call | solution.py:931
  525.7 3.8 write_sums.4
  547.6 4.7 write_sums.5
  (448 shorter events, 174.8 us)
Async XLA Ops:
  9.3 14.7 %collective-permute-start = (bf16[192,1536]{1,0:T(8,128)(2,1)}, bf16[192,1536]{1,0:T(8,128)(2,1)}, u32[]{:S(2)}, u32[]{:S(2)}) collective-permute-start(bf16[192,1536]{1,0:T(8,128)(2,1)} %pad_maximum_fusion.3), channel_id=1, source_target_pairs={{4,8},{5,9},{6,10},{7,11},{8,4},{9,5},{10,6},{11,7},{20,24},{21,25... | collective-permute-start | bytes 1769480 | tf_op jit(solution)/shard_map/ppermute | solution.py:725
  26.2 44.6 %collective-permute-start.8 = (bf16[1536,1152]{1,0:T(8,128)(2,1)}, bf16[1536,1152]{1,0:T(8,128)(2,1)}, u32[]{:S(2)}, u32[]{:S(2)}) collective-permute-start(bf16[1536,1152]{1,0:T(8,128)(2,1)} %pad_maximum_fusion.refs_8_), channel_id=1, source_target_pairs={{4,8},{5,9},{6,10},{7,11},{8,4},{9,5},{10,6},{11,7},{20,24},{21,25... | collective-permute-start | bytes 10616840 | tf_op jit(solution)/shard_map/ppermute | solution.py:725
  34.7 15.5 %collective-permute-start.2 = (bf16[160,1536]{1,0:T(8,128)(2,1)}, bf16[160,1536]{1,0:T(8,128)(2,1)S(1)}, u32[]{:S(2)}, u32[]{:S(2)}) collective-permute-start(bf16[160,1536]{1,0:T(8,128)(2,1)} %first_norm.1.refs_0_), channel_id=1, source_target_pairs={{0,1},{1,2},{2,3},{3,0},{4,5},{5,6},{6,7},{7,4},{8,9},{9,10},{10,1... | collective-permute-start | bytes 1474568 | tf_op jit(solution)/shard_map/ppermute | solution.py:725
  36.4 18.1 %collective-permute-start.4 = (bf16[160,1536]{1,0:T(8,128)(2,1)}, bf16[160,1536]{1,0:T(8,128)(2,1)S(1)}, u32[]{:S(2)}, u32[]{:S(2)}) collective-permute-start(bf16[160,1536]{1,0:T(8,128)(2,1)} %first_norm.1.refs_0_), channel_id=1, source_target_pairs={{0,3},{1,0},{2,1},{3,2},{4,7},{5,4},{6,5},{7,6},{8,11},{9,8},{10,9... | collective-permute-start | bytes 1474568 | tf_op jit(solution)/shard_map/ppermute | solution.py:725
  38.5 17.5 %collective-permute-start.6 = (bf16[160,1536]{1,0:T(8,128)(2,1)}, bf16[160,1536]{1,0:T(8,128)(2,1)S(1)}, u32[]{:S(2)}, u32[]{:S(2)}) collective-permute-start(bf16[160,1536]{1,0:T(8,128)(2,1)} %first_norm.1.refs_0_), channel_id=1, source_target_pairs={{0,2},{1,3},{2,0},{3,1},{4,6},{5,7},{6,4},{7,5},{8,10},{9,11},{10,... | collective-permute-start | bytes 1474568 | tf_op jit(solution)/shard_map/ppermute | solution.py:725
  39.8 18.2 %collective-permute-start.1 = (bf16[160,1536]{1,0:T(8,128)(2,1)}, bf16[160,1536]{1,0:T(8,128)(2,1)S(1)}, u32[]{:S(2)}, u32[]{:S(2)}) collective-permute-start(bf16[160,1536]{1,0:T(8,128)(2,1)} %first_norm.1.refs_0_), channel_id=1, source_target_pairs={{0,8},{1,9},{2,10},{3,11},{4,12},{5,13},{6,14},{7,15},{8,0},{9,1},... | collective-permute-start | bytes 1474568 | tf_op jit(solution)/shard_map/ppermute | solution.py:725
  58.0 35.9 %collective-permute-start.10 = (bf16[160,1536]{1,0:T(8,128)(2,1)S(1)}, bf16[160,1536]{1,0:T(8,128)(2,1)S(1)}, u32[]{:S(2)}, u32[]{:S(2)}) collective-permute-start(bf16[160,1536]{1,0:T(8,128)(2,1)S(1)} %pad_maximum_fusion.4), channel_id=1, source_target_pairs={{0,3},{1,0},{2,1},{3,2},{4,11},{5,8},{6,9},{7,10},{8,7},{9,4},{10,... | collective-permute-start | bytes 1474568 | tf_op jit(solution)/shard_map/ppermute | solution.py:725
  62.1 31.9 %collective-permute-start.11 = (bf16[160,1536]{1,0:T(8,128)(2,1)S(1)}, bf16[160,1536]{1,0:T(8,128)(2,1)S(1)}, u32[]{:S(2)}, u32[]{:S(2)}) collective-permute-start(bf16[160,1536]{1,0:T(8,128)(2,1)S(1)} %pad_maximum_fusion.4), channel_id=1, source_target_pairs={{0,2},{1,3},{2,0},{3,1},{4,10},{5,11},{6,8},{7,9},{8,6},{9,7},{10,... | collective-permute-start | bytes 1474568 | tf_op jit(solution)/shard_map/ppermute | solution.py:725
  63.7 30.3 %collective-permute-start.9 = (bf16[160,1536]{1,0:T(8,128)(2,1)S(1)}, bf16[160,1536]{1,0:T(8,128)(2,1)S(1)}, u32[]{:S(2)}, u32[]{:S(2)}) collective-permute-start(bf16[160,1536]{1,0:T(8,128)(2,1)S(1)} %pad_maximum_fusion.4), channel_id=1, source_target_pairs={{0,1},{1,2},{2,3},{3,0},{4,9},{5,10},{6,11},{7,8},{8,5},{9,6},{10,... | collective-permute-start | bytes 1474568 | tf_op jit(solution)/shard_map/ppermute | solution.py:725
  112.1 46.9 %collective-permute-start.28 = (bf16[1536,1152]{1,0:T(8,128)(2,1)S(1)}, bf16[1536,1152]{1,0:T(8,128)(2,1)}, u32[]{:S(2)}, u32[]{:S(2)}) collective-permute-start(bf16[1536,1152]{1,0:T(8,128)(2,1)S(1)} %pad_maximum_fusion.1.refs_16_), channel_id=1, source_target_pairs={{4,8},{5,9},{6,10},{7,11},{8,4},{9,5},{10,6},{11,7},{20,24},{21,25... | collective-permute-start | bytes 10616840 | tf_op jit(solution)/shard_map/ppermute | solution.py:725
  138.8 18.3 %collective-permute-start.21 = (bf16[128,1536]{1,0:T(8,128)(2,1)}, bf16[128,1536]{1,0:T(8,128)(2,1)S(1)}, u32[]{:S(2)}, u32[]{:S(2)}) collective-permute-start(bf16[128,1536]{1,0:T(8,128)(2,1)} %get-tuple-element.114.refs_0_), channel_id=1, source_target_pairs={{0,2},{1,3},{2,0},{3,1},{4,6},{5,7},{6,4},{7,5},{8,10},{9,11},{10,... | collective-permute-start | bytes 1179656 | tf_op jit(solution)/shard_map/ppermute | solution.py:725
  139.3 19.1 %collective-permute-start.16 = (bf16[128,1536]{1,0:T(8,128)(2,1)}, bf16[128,1536]{1,0:T(8,128)(2,1)S(1)}, u32[]{:S(2)}, u32[]{:S(2)}) collective-permute-start(bf16[128,1536]{1,0:T(8,128)(2,1)} %get-tuple-element.114.refs_0_), channel_id=1, source_target_pairs={{0,8},{1,9},{2,10},{3,11},{4,12},{5,13},{6,14},{7,15},{8,0},{9,1},... | collective-permute-start | bytes 1179656 | tf_op jit(solution)/shard_map/ppermute | solution.py:725
  200.7 35.6 %collective-permute-start.34 = (bf16[128,1664]{1,0:T(8,128)(2,1)S(1)}, bf16[128,1664]{1,0:T(8,128)(2,1)S(1)}, u32[]{:S(2)}, u32[]{:S(2)}) collective-permute-start(bf16[128,1664]{1,0:T(8,128)(2,1)S(1)} %get-tuple-element.258), channel_id=1, source_target_pairs={{0,1},{1,2},{2,3},{3,0},{4,5},{5,6},{6,7},{7,4},{8,9},{9,10},{10,1... | collective-permute-start | bytes 1277960 | tf_op jit(solution)/shard_map/ppermute | solution.py:725
  200.8 35.6 %collective-permute-start.35 = (bf16[128,1664]{1,0:T(8,128)(2,1)S(1)}, bf16[128,1664]{1,0:T(8,128)(2,1)S(1)}, u32[]{:S(2)}, u32[]{:S(2)}) collective-permute-start(bf16[128,1664]{1,0:T(8,128)(2,1)S(1)} %get-tuple-element.257), channel_id=1, source_target_pairs={{0,2},{1,3},{2,0},{3,1},{4,6},{5,7},{6,4},{7,5},{8,10},{9,11},{10,... | collective-permute-start | bytes 1277960 | tf_op jit(solution)/shard_map/ppermute | solution.py:725
  203.5 32.9 %collective-permute-start.36 = (bf16[128,1664]{1,0:T(8,128)(2,1)S(1)}, bf16[128,1664]{1,0:T(8,128)(2,1)S(1)}, u32[]{:S(2)}, u32[]{:S(2)}) collective-permute-start(bf16[128,1664]{1,0:T(8,128)(2,1)S(1)} %get-tuple-element.256), channel_id=1, source_target_pairs={{0,3},{1,0},{2,1},{3,2},{4,7},{5,4},{6,5},{7,6},{8,11},{9,8},{10,9... | collective-permute-start | bytes 1277960 | tf_op jit(solution)/shard_map/ppermute | solution.py:725
  236.4 16.8 %collective-permute-start.37 = (bf16[512,1536]{1,0:T(8,128)(2,1)}, bf16[512,1536]{1,0:T(8,128)(2,1)S(1)}, u32[]{:S(2)}, u32[]{:S(2)}) collective-permute-start(bf16[512,1536]{1,0:T(8,128)(2,1)} %get-tuple-element.136), channel_id=1, source_target_pairs={{0,8},{1,9},{2,10},{3,11},{4,12},{5,13},{6,14},{7,15},{8,0},{9,1},... | collective-permute-start | bytes 4718600 | tf_op jit(solution)/shard_map/ppermute | solution.py:725
  247.4 35.5 %collective-permute-start.49 = (bf16[1536,768]{1,0:T(8,128)(2,1)}, bf16[1536,768]{1,0:T(8,128)(2,1)S(1)}, u32[]{:S(2)}, u32[]{:S(2)}) collective-permute-start(bf16[1536,768]{1,0:T(8,128)(2,1)} %weight_products.3), channel_id=1, source_target_pairs={{4,0},{5,1},{6,2},{7,3},{8,12},{9,13},{10,14},{11,15},{20,16},{21,... | collective-permute-start | bytes 7077896 | tf_op jit(solution)/shard_map/ppermute | solution.py:725
  253.6 23.1 %collective-permute-start.39 = (bf16[128,1792]{1,0:T(8,128)(2,1)S(1)}, bf16[128,1792]{1,0:T(8,128)(2,1)S(1)}, u32[]{:S(2)}, u32[]{:S(2)}) collective-permute-start(bf16[128,1792]{1,0:T(8,128)(2,1)S(1)} %pad_maximum_fusion.5), channel_id=1, source_target_pairs={{0,1},{1,2},{2,3},{3,0},{4,5},{5,6},{6,7},{7,4},{8,9},{9,10},{10,1... | collective-permute-start | bytes 1376264 | tf_op jit(solution)/shard_map/ppermute | solution.py:725
  254.0 22.7 %collective-permute-start.40 = (bf16[128,1792]{1,0:T(8,128)(2,1)S(1)}, bf16[128,1792]{1,0:T(8,128)(2,1)S(1)}, u32[]{:S(2)}, u32[]{:S(2)}) collective-permute-start(bf16[128,1792]{1,0:T(8,128)(2,1)S(1)} %pad_maximum_fusion.6), channel_id=1, source_target_pairs={{0,2},{1,3},{2,0},{3,1},{4,6},{5,7},{6,4},{7,5},{8,10},{9,11},{10,... | collective-permute-start | bytes 1376264 | tf_op jit(solution)/shard_map/ppermute | solution.py:725
  255.6 21.5 %collective-permute-start.41 = (bf16[128,1792]{1,0:T(8,128)(2,1)S(1)}, bf16[128,1792]{1,0:T(8,128)(2,1)S(1)}, u32[]{:S(2)}, u32[]{:S(2)}) collective-permute-start(bf16[128,1792]{1,0:T(8,128)(2,1)S(1)} %pad_maximum_fusion.7), channel_id=1, source_target_pairs={{0,3},{1,0},{2,1},{3,2},{4,7},{5,4},{6,5},{7,6},{8,11},{9,8},{10,9... | collective-permute-start | bytes 1376264 | tf_op jit(solution)/shard_map/ppermute | solution.py:725
  283.5 25.9 %collective-permute-start.50 = (bf16[768,768]{1,0:T(8,128)(2,1)S(1)}, bf16[768,768]{1,0:T(8,128)(2,1)}, u32[]{:S(2)}, u32[]{:S(2)}) collective-permute-start(bf16[768,768]{1,0:T(8,128)(2,1)S(1)} %slice.265), channel_id=1, source_target_pairs={{0,8},{1,9},{2,10},{3,11},{12,4},{13,5},{14,6},{15,7},{16,24},{17,... | collective-permute-start | bytes 3538952 | tf_op jit(solution)/shard_map/ppermute | solution.py:725
  288.1 18.3 %collective-permute-start.47 = (bf16[128,1664]{1,0:T(8,128)(2,1)}, bf16[128,1664]{1,0:T(8,128)(2,1)}, u32[]{:S(2)}, u32[]{:S(2)}) collective-permute-start(bf16[128,1664]{1,0:T(8,128)(2,1)} %get-tuple-element.146.refs_0_), channel_id=1, source_target_pairs={{0,2},{1,3},{2,0},{3,1},{4,6},{5,7},{6,4},{7,5},{8,10},{9,11},{10,... | collective-permute-start | bytes 1277960 | tf_op jit(solution)/shard_map/ppermute | solution.py:725
  290.1 22.1 %collective-permute-start.42 = (bf16[128,1664]{1,0:T(8,128)(2,1)}, bf16[128,1664]{1,0:T(8,128)(2,1)}, u32[]{:S(2)}, u32[]{:S(2)}) collective-permute-start(bf16[128,1664]{1,0:T(8,128)(2,1)} %get-tuple-element.146.refs_0_), channel_id=1, source_target_pairs={{0,8},{1,9},{2,10},{3,11},{4,12},{5,13},{6,14},{7,15},{8,0},{9,1},... | collective-permute-start | bytes 1277960 | tf_op jit(solution)/shard_map/ppermute | solution.py:725
  298.6 16.1 %collective-permute-start.44 = (bf16[128,1664]{1,0:T(8,128)(2,1)}, bf16[128,1664]{1,0:T(8,128)(2,1)S(1)}, u32[]{:S(2)}, u32[]{:S(2)}) collective-permute-start(bf16[128,1664]{1,0:T(8,128)(2,1)} %collective-permute-done.43.refs_2_), channel_id=1, source_target_pairs={{0,8},{1,9},{2,10},{3,11},{4,12},{5,13},{6,14},{7,15},{8,0},{9,1},... | collective-permute-start | bytes 1277960 | tf_op jit(solution)/shard_map/ppermute | solution.py:725
  300.5 15.2 %collective-permute-start.46 = (bf16[128,1664]{1,0:T(8,128)(2,1)}, bf16[128,1664]{1,0:T(8,128)(2,1)S(1)}, u32[]{:S(2)}, u32[]{:S(2)}) collective-permute-start(bf16[128,1664]{1,0:T(8,128)(2,1)} %collective-permute-done.45.refs_4_), channel_id=1, source_target_pairs={{0,8},{1,9},{2,10},{3,11},{4,12},{5,13},{6,14},{7,15},{8,0},{9,1},... | collective-permute-start | bytes 1277960 | tf_op jit(solution)/shard_map/ppermute | solution.py:725
  310.9 14.3 %collective-permute-start.51 = (bf16[192,768]{1,0:T(8,128)(2,1)S(1)}, bf16[192,768]{1,0:T(8,128)(2,1)S(1)}, u32[]{:S(2)}, u32[]{:S(2)}) collective-permute-start(bf16[192,768]{1,0:T(8,128)(2,1)S(1)} %get-tuple-element.282), channel_id=1, source_target_pairs={{0,32},{1,33},{2,34},{3,35},{4,36},{5,37},{6,38},{7,39},{8,40},{9,... | collective-permute-start | bytes 884744 | tf_op jit(solution)/shard_map/ppermute | solution.py:725
  312.2 15.2 %collective-permute-start.52 = (bf16[192,768]{1,0:T(8,128)(2,1)S(1)}, bf16[192,768]{1,0:T(8,128)(2,1)S(1)}, u32[]{:S(2)}, u32[]{:S(2)}) collective-permute-start(bf16[192,768]{1,0:T(8,128)(2,1)S(1)} %get-tuple-element.284), channel_id=1, source_target_pairs={{0,64},{1,65},{2,66},{3,67},{4,68},{5,69},{6,70},{7,71},{8,72},{9,... | collective-permute-start | bytes 884744 | tf_op jit(solution)/shard_map/ppermute | solution.py:725
  338.8 35.8 %collective-permute-start.60 = (bf16[384,1280]{1,0:T(8,128)(2,1)}, bf16[384,1280]{1,0:T(8,128)(2,1)S(1)}, u32[]{:S(2)}, u32[]{:S(2)}) collective-permute-start(bf16[384,1280]{1,0:T(8,128)(2,1)} %get-tuple-element.160), channel_id=1, source_target_pairs={{0,32},{1,33},{2,34},{3,35},{4,36},{5,37},{6,38},{7,39},{8,40},{9,... | collective-permute-start | bytes 2949128 | tf_op jit(solution)/shard_map/ppermute | solution.py:725
  340.5 44.8 %collective-permute-start.61 = (bf16[384,1280]{1,0:T(8,128)(2,1)}, bf16[384,1280]{1,0:T(8,128)(2,1)S(1)}, u32[]{:S(2)}, u32[]{:S(2)}) collective-permute-start(bf16[384,1280]{1,0:T(8,128)(2,1)} %get-tuple-element.161), channel_id=1, source_target_pairs={{0,64},{1,65},{2,66},{3,67},{4,68},{5,69},{6,70},{7,71},{8,72},{9,... | collective-permute-start | bytes 2949128 | tf_op jit(solution)/shard_map/ppermute | solution.py:725
  342.5 42.7 %collective-permute-start.62 = (bf16[384,1280]{1,0:T(8,128)(2,1)}, bf16[384,1280]{1,0:T(8,128)(2,1)S(1)}, u32[]{:S(2)}, u32[]{:S(2)}) collective-permute-start(bf16[384,1280]{1,0:T(8,128)(2,1)} %get-tuple-element.162), channel_id=1, source_target_pairs={{0,96},{1,97},{2,98},{3,99},{4,100},{5,101},{6,102},{7,103},{8,104... | collective-permute-start | bytes 2949128 | tf_op jit(solution)/shard_map/ppermute | solution.py:725
  373.0 28.3 %collective-permute-start.54 = (bf16[512,1536]{1,0:T(8,128)(2,1)}, bf16[512,1536]{1,0:T(8,128)(2,1)S(1)}, u32[]{:S(2)}, u32[]{:S(2)}) collective-permute-start(bf16[512,1536]{1,0:T(8,128)(2,1)} %get-tuple-element.170), channel_id=1, source_target_pairs={{0,8},{1,9},{2,10},{3,11},{4,12},{5,13},{6,14},{7,15},{8,0},{9,1},... | collective-permute-start | bytes 4718600 | tf_op jit(solution)/shard_map/ppermute | solution.py:725
  374.1 14.5 %collective-permute-start.83 = (bf16[192,768]{1,0:T(8,128)(2,1)S(1)}, bf16[192,768]{1,0:T(8,128)(2,1)S(1)}, u32[]{:S(2)}, u32[]{:S(2)}) collective-permute-start(bf16[192,768]{1,0:T(8,128)(2,1)S(1)} %add_convert_fusion.16), channel_id=1, source_target_pairs={{0,16},{1,17},{2,18},{3,19},{4,20},{5,21},{6,22},{7,23},{8,24},{9,... | collective-permute-start | bytes 884744 | tf_op jit(solution)/shard_map/ppermute | solution.py:725
  403.8 17.0 %collective-permute-start.56 = (bf16[128,1536]{1,0:T(8,128)(2,1)}, bf16[128,1536]{1,0:T(8,128)(2,1)}, u32[]{:S(2)}, u32[]{:S(2)}) collective-permute-start(bf16[128,1536]{1,0:T(8,128)(2,1)} %get-tuple-element.264), channel_id=1, source_target_pairs={{0,2},{1,3},{2,0},{3,1},{4,6},{5,7},{6,4},{7,5},{8,10},{9,11},{10,... | collective-permute-start | bytes 1179656 | tf_op jit(solution)/shard_map/ppermute | solution.py:725
  407.4 15.2 %collective-permute-start.57 = (bf16[128,1536]{1,0:T(8,128)(2,1)S(1)}, bf16[128,1536]{1,0:T(8,128)(2,1)}, u32[]{:S(2)}, u32[]{:S(2)}) collective-permute-start(bf16[128,1536]{1,0:T(8,128)(2,1)S(1)} %get-tuple-element.263), channel_id=1, source_target_pairs={{0,3},{1,0},{2,1},{3,2},{4,7},{5,4},{6,5},{7,6},{8,11},{9,8},{10,9... | collective-permute-start | bytes 1179656 | tf_op jit(solution)/shard_map/ppermute | solution.py:725
  407.6 34.4 %collective-permute-start.68 = (bf16[192,1280]{1,0:T(8,128)(2,1)S(1)}, bf16[192,1280]{1,0:T(8,128)(2,1)S(1)}, u32[]{:S(2)}, u32[]{:S(2)}) collective-permute-start(bf16[192,1280]{1,0:T(8,128)(2,1)S(1)} %slice_select_fusion.1), channel_id=1, source_target_pairs={{0,16},{1,17},{2,18},{3,19},{4,20},{5,21},{6,22},{7,23},{8,24},{9,... | collective-permute-start | bytes 1474568 | tf_op jit(solution)/shard_map/ppermute | solution.py:725
  426.2 21.8 %collective-permute-start.58 = (bf16[128,3072]{1,0:T(8,128)(2,1)}, bf16[128,3072]{1,0:T(8,128)(2,1)S(1)}, u32[]{:S(2)}, u32[]{:S(2)}) collective-permute-start(bf16[128,3072]{1,0:T(8,128)(2,1)} %outputs.1), channel_id=1, source_target_pairs={{4,8},{5,9},{6,10},{7,11},{8,4},{9,5},{10,6},{11,7},{20,24},{21,25... | collective-permute-start | bytes 2359304 | tf_op jit(solution)/shard_map/ppermute | solution.py:725
  442.3 33.5 %collective-permute-start.79 = (bf16[192,1280]{1,0:T(8,128)(2,1)S(1)}, bf16[192,1280]{1,0:T(8,128)(2,1)S(1)}, u32[]{:S(2)}, u32[]{:S(2)}) collective-permute-start(bf16[192,1280]{1,0:T(8,128)(2,1)S(1)} %get-tuple-element.251), channel_id=1, source_target_pairs={{0,32},{1,33},{2,34},{3,35},{4,36},{5,37},{6,38},{7,39},{8,40},{9,... | collective-permute-start | bytes 1474568 | tf_op jit(solution)/shard_map/ppermute | solution.py:725
  443.9 19.6 %collective-permute-start.69 = (bf16[384,512]{1,0:T(8,128)(2,1)S(1)}, bf16[384,512]{1,0:T(8,128)(2,1)S(1)}, u32[]{:S(2)}, u32[]{:S(2)}) collective-permute-start(bf16[384,512]{1,0:T(8,128)(2,1)S(1)} %get-tuple-element.277), channel_id=1, source_target_pairs={{0,32},{1,33},{2,34},{3,35},{4,36},{5,37},{6,38},{7,39},{8,40},{9,... | collective-permute-start | bytes 1179656 | tf_op jit(solution)/shard_map/ppermute | solution.py:725
  444.8 29.3 %collective-permute-start.70 = (bf16[384,512]{1,0:T(8,128)(2,1)S(1)}, bf16[384,512]{1,0:T(8,128)(2,1)S(1)}, u32[]{:S(2)}, u32[]{:S(2)}) collective-permute-start(bf16[384,512]{1,0:T(8,128)(2,1)S(1)} %get-tuple-element.279), channel_id=1, source_target_pairs={{0,64},{1,65},{2,66},{3,67},{4,68},{5,69},{6,70},{7,71},{8,72},{9,... | collective-permute-start | bytes 1179656 | tf_op jit(solution)/shard_map/ppermute | solution.py:725
  446.7 27.4 %collective-permute-start.71 = (bf16[384,512]{1,0:T(8,128)(2,1)S(1)}, bf16[384,512]{1,0:T(8,128)(2,1)S(1)}, u32[]{:S(2)}, u32[]{:S(2)}) collective-permute-start(bf16[384,512]{1,0:T(8,128)(2,1)S(1)} %get-tuple-element.278), channel_id=1, source_target_pairs={{0,96},{1,97},{2,98},{3,99},{4,100},{5,101},{6,102},{7,103},{8,104... | collective-permute-start | bytes 1179656 | tf_op jit(solution)/shard_map/ppermute | solution.py:725
  448.1 32.5 %collective-permute-start.80 = (bf16[192,1280]{1,0:T(8,128)(2,1)S(1)}, bf16[192,1280]{1,0:T(8,128)(2,1)S(1)}, u32[]{:S(2)}, u32[]{:S(2)}) collective-permute-start(bf16[192,1280]{1,0:T(8,128)(2,1)S(1)} %get-tuple-element.251), channel_id=1, source_target_pairs={{0,64},{1,65},{2,66},{3,67},{4,68},{5,69},{6,70},{7,71},{8,72},{9,... | collective-permute-start | bytes 1474568 | tf_op jit(solution)/shard_map/ppermute | solution.py:725
  463.5 18.6 %collective-permute-start.81 = (bf16[192,1280]{1,0:T(8,128)(2,1)S(1)}, bf16[192,1280]{1,0:T(8,128)(2,1)S(1)}, u32[]{:S(2)}, u32[]{:S(2)}) collective-permute-start(bf16[192,1280]{1,0:T(8,128)(2,1)S(1)} %get-tuple-element.251), channel_id=1, source_target_pairs={{0,96},{1,97},{2,98},{3,99},{4,100},{5,101},{6,102},{7,103},{8,104... | collective-permute-start | bytes 1474568 | tf_op jit(solution)/shard_map/ppermute | solution.py:725
  482.1 35.1 %collective-permute-start.82 = (bf16[4,192,1280]{2,1,0:T(8,128)(2,1)S(1)}, bf16[4,192,1280]{2,1,0:T(8,128)(2,1)S(1)}, u32[]{:S(2)}, u32[]{:S(2)}) collective-permute-start(bf16[4,192,1280]{2,1,0:T(8,128)(2,1)S(1)} %bitcast_dynamic-update-slice_fusion.here_ref), channel_id=1, source_target_pairs={{0,8},{1,9},{2,10},{3,11},{4,12},{5,13},{6,14},{7,15},{8,0},{9,1},... | collective-permute-start | bytes 5898248 | tf_op jit(solution)/shard_map/ppermute | solution.py:725
  484.3 16.1 %collective-permute-start.84 = (bf16[192,768]{1,0:T(8,128)(2,1)S(1)}, bf16[192,768]{1,0:T(8,128)(2,1)S(1)}, u32[]{:S(2)}, u32[]{:S(2)}) collective-permute-start(bf16[192,768]{1,0:T(8,128)(2,1)S(1)} %add_convert_fusion.15), channel_id=1, source_target_pairs={{0,32},{1,33},{2,34},{3,35},{4,36},{5,37},{6,38},{7,39},{8,40},{9,... | collective-permute-start | bytes 884744 | tf_op jit(solution)/shard_map/ppermute | solution.py:725
  484.3 31.2 %collective-permute-start.85 = (bf16[192,768]{1,0:T(8,128)(2,1)S(1)}, bf16[192,768]{1,0:T(8,128)(2,1)S(1)}, u32[]{:S(2)}, u32[]{:S(2)}) collective-permute-start(bf16[192,768]{1,0:T(8,128)(2,1)S(1)} %add_convert_fusion.15), channel_id=1, source_target_pairs={{0,64},{1,65},{2,66},{3,67},{4,68},{5,69},{6,70},{7,71},{8,72},{9,... | collective-permute-start | bytes 884744 | tf_op jit(solution)/shard_map/ppermute | solution.py:725
  485.5 30.0 %collective-permute-start.86 = (bf16[192,768]{1,0:T(8,128)(2,1)S(1)}, bf16[192,768]{1,0:T(8,128)(2,1)S(1)}, u32[]{:S(2)}, u32[]{:S(2)}) collective-permute-start(bf16[192,768]{1,0:T(8,128)(2,1)S(1)} %add_convert_fusion.15), channel_id=1, source_target_pairs={{0,96},{1,97},{2,98},{3,99},{4,100},{5,101},{6,102},{7,103},{8,104... | collective-permute-start | bytes 884744 | tf_op jit(solution)/shard_map/ppermute | solution.py:725
  509.3 15.4 %collective-permute-start.78 = (bf16[4,192,512]{2,1,0:T(8,128)(2,1)S(1)}, bf16[4,192,512]{2,1,0:T(8,128)(2,1)S(1)}, u32[]{:S(2)}, u32[]{:S(2)}) collective-permute-start(bf16[4,192,512]{2,1,0:T(8,128)(2,1)S(1)} %bitcast_dynamic-update-slice_fusion.8.here_ref), channel_id=1, source_target_pairs={{0,8},{1,9},{2,10},{3,11},{4,12},{5,13},{6,14},{7,15},{8,0},{9,1},... | collective-permute-start | bytes 2359304 | tf_op jit(solution)/shard_map/ppermute | solution.py:725
  515.6 32.1 %collective-permute-start.87 = (bf16[4,192,768]{2,1,0:T(8,128)(2,1)S(1)}, bf16[4,192,768]{2,1,0:T(8,128)(2,1)}, u32[]{:S(2)}, u32[]{:S(2)}) collective-permute-start(bf16[4,192,768]{2,1,0:T(8,128)(2,1)S(1)} %bitcast_dynamic-update-slice_fusion.4.here_ref), channel_id=1, source_target_pairs={{0,8},{1,9},{2,10},{3,11},{4,12},{5,13},{6,14},{7,15},{8,0},{9,1},... | collective-permute-start | bytes 3538952 | tf_op jit(solution)/shard_map/ppermute | solution.py:725
  (124 other events, 1101.3 us)

commit v5 on v4

--- a/solution.py
+++ b/solution.py
@@ -791,8 +791,10 @@
     return [jnp.concatenate([blocks[k] for blocks in folded], axis=1) for k in range(NZ)]
 
 
-def scatter(*pairs):
+def scatter(*pairs, meanwhile=None):
     own, one, two, three = fold_beside(pairs)
+    if meanwhile is not None:
+        two = after(two, meanwhile)
     return [own] + [send_z(b.astype(bf16), k) for k, b in ((1, one), (2, two), (3, three))]
 
 
@@ -856,29 +858,21 @@
     return [lax.dynamic_slice_in_dim(v, (x + k) % NX * rows, rows, 0) for k in range(NX)]
 
 
-def collect_x(part):
-    x = position()[0]
-    out = jnp.zeros((NX,) + part.shape, bf16)
-    out = lax.dynamic_update_index_in_dim(out, part, x, 0)
+def collect_x(part, meanwhile=()):
+    parts = [part]
     for k in range(1, NX):
-        block = send(part, lambda x, yl, c, yh, z, k=k: (x + k, yl, c, yh, z))
-        out = lax.dynamic_update_index_in_dim(out, block, (x - k) % NX, 0)
-    return out
-
-
-def collect(part, meanwhile=()):
-    out = collect_x(part)
-    out = after(out, *meanwhile) if meanwhile else out
-    return out, send_core(out)
-
-
-def write_kernel(plan, by_half, n_kept, place_ref, here_ref, there_ref, *refs):
+        got = send(part, lambda x, yl, c, yh, z, k=k: (x + k, yl, c, yh, z))
+        parts.append(after(got, *meanwhile) if meanwhile else got)
+    return jnp.stack(parts)
+
+
+def write_kernel(plan, n_kept, place_ref, here_ref, there_ref, *refs):
     rows = here_ref.shape[1]
 
     def write(ref):
-        for (column, kind, wide), out_ref in zip(plan, refs[n_kept:]):
+        for (column, kind, wide, by_half), out_ref in zip(plan, refs[n_kept:]):
             for x in range(NX):
-                value = ref[x, :, column : column + wide].astype(f32)
+                value = ref[lax.rem(place_ref[3] + NX - x, NX), :, column : column + wide].astype(f32)
                 if kind != "blocks":
                     out_ref[0, 0 if by_half else x, x if by_half else 0] = value
                 elif by_half:
@@ -898,15 +892,15 @@
         write(there_ref)
 
 
-def write_sums(place, halves, by_half, outputs):
+def write_sums(place, halves, outputs):
     rows, columns = halves[0].shape[1:]
     total = 2 * NX * rows
     wide = total // 4
     plan, shapes, specs, finals, kept, alias = [], [], [], [], [], {}
-    for column, kind, layer, array in outputs:
+    for column, kind, layer, array, by_half in outputs:
         lanes = LANES if kind == "flat" else wide
         layers = 1 if kind == "flat" else 2
-        plan.append((column, kind, lanes))
+        plan.append((column, kind, lanes, by_half))
         if kind == "blocks":
             shape = (layers, wide, total)
             if by_half:
@@ -929,7 +923,7 @@
             kept.append(array.reshape(shape))
     piece = pl.BlockSpec((NX, rows, columns), lambda h, p: (0, 0, 0))
     written = pl.pallas_call(
-        functools.partial(write_kernel, plan, by_half, len(kept)),
+        functools.partial(write_kernel, plan, len(kept)),
         grid_spec=pltpu.PrefetchScalarGridSpec(
             num_scalar_prefetch=1,
             grid=(2,),
@@ -949,7 +943,7 @@
         kernel,
         grid=(1,),
         in_specs=[pl.BlockSpec((rows, v.shape[1]), lambda i: (0, 0)) for v, rows in operands],
-        out_specs=[pl.BlockSpec(s.shape, lambda i: (0, 0)) for s in shapes],
+        out_specs=[pl.BlockSpec(s.shape, lambda i, n=len(s.shape): (0,) * n) for s in shapes],
         out_shape=shapes,
         compiler_params=pltpu.CompilerParams(vmem_limit_bytes=VMEM_BYTES),
         name=name,
@@ -1025,6 +1019,39 @@
 def last_kernel(inner_all, own_ref, a_ref, b_ref, c_ref, res_ref, out_ref):
     _, mixed = unscaled_output(inner_all, (own_ref, a_ref, b_ref, c_ref), res_ref.shape[1])
     out_ref[...] = (res_ref[...] + mixed).astype(bf16)
+
+
+TINY_ROWS = 56
+
+
+def small_kernel(head_dim, ends, narrow0_ref, narrow1_ref, gain_ref, pick_ref, norm_ref, wbc_ref, wdt_ref, cx_ref,
+                 cxb_ref, cbc_ref, cbcb_ref, dtb_ref, alog_ref, skip_ref, ng_ref):
+    bc_at, tiny_at = ends
+    heads = wdt_ref.shape[2]
+    channels = cx_ref.shape[2]
+    both = cbc_ref.shape[2]
+    lanes = narrow0_ref.shape[1] - tiny_at
+    for layer, ref in enumerate((narrow0_ref, narrow1_ref)):
+        wbc_ref[layer] = ref[:, bc_at:tiny_at]
+        wdt_ref[layer] = ref[:, 0:heads]
+    tiny = jnp.concatenate(
+        [narrow0_ref[i * TINY_ROWS : (i + 1) * TINY_ROWS, tiny_at:] for i in range(channels // lanes)], axis=1
+    )
+    lines = norm_ref.shape[1] // both
+    for layer in range(2):
+        rows = tiny[8 * layer : 8 * layer + 8]
+        cx_ref[layer] = rows[0:4]
+        cxb_ref[layer : layer + 1, :] = rows[4:5]
+        ng_ref[layer : layer + 1, :] = rows[5:6]
+        skip_ref[layer : layer + 1, :] = dot(rows, pick_ref[...], PLAIN, highest)[6:7, 0:heads]
+        at = 16 + 2 * layer
+        dtb_ref[layer : layer + 1, :] = tiny[at : at + 1, 0:heads]
+        alog_ref[layer : layer + 1, :] = tiny[at + 1 : at + 2, 0:heads]
+        at = 20 + 16 * layer
+        norm = jnp.concatenate([tiny[at + i : at + i + 1, 0:both] for i in range(lines)], axis=1)
+        norm_ref[layer : layer + 1, :] = norm / gain_ref[layer : layer + 1, :]
+        cbc_ref[layer] = tiny[at + lines : at + lines + 4, 0:both]
+        cbcb_ref[layer : layer + 1, :] = tiny[at + lines + 4 : at + lines + 5, 0:both]
 
 
 def after(v, *others):
@@ -1111,11 +1138,11 @@
     out0 = run_forward(place, [gathered0], w0, wdt[0], smalls[0], state, head_dim)
     w0, xn0, wbc0, z0, xp0, bc0, dt0, y0, hin0, mine, other = out0
     grads = after(grads, sent)
-    gathered_grad = gather(grads, (rows, bc_rows), trade_places(grads), (mine,))
+    gathered_grad = gather(grads, (rows, bc_rows), jnp.where(stays, grads, after(traded(grads), mine)), (mine,))
     grad_held = gathered_grad[0][0]
-    terms = scatter((mine, after(other, *gathered_grad[0][2::2])))
+    terms = scatter((mine, after(other, *gathered_grad[0][::2])))
     w1 = pack_weights(1)
-    w1 = w1, [traded(after(w1, terms[0], grad_held))], [(0, None)]
+    w1 = w1, [traded(after(w1, terms[0]))], [(0, None)]
     res1, mixed0, rms0, normed1 = row_call(
         functools.partial(middle_kernel, inner_all),
         "middle_norm",
@@ -1137,9 +1164,8 @@
         inner_all,
     )
     dz1, go1, dxt1, *bc_halves, mine, other, acc1, acch1, shared1 = back1
-    terms = scatter((mine, after(other, *home)), bc_halves)
     early1 = weight_products(place, [(xn1, dz1), (go1, grad_rows1)], split=False)
-    terms[1] = after(terms[1], early1)
+    terms = scatter((mine, after(other, *home)), bc_halves, meanwhile=early1)
     early1_far = send_far(early1)
     [hidden_out] = row_call(
         functools.partial(last_kernel, inner_all),
@@ -1186,17 +1212,16 @@
         [acc0 + acc_gate0, acc1] + [pad_to(v, v.shape[0], channels) for v in (acch0[0:2], acch1[0:2], shared)],
         axis=0,
     )
-    tiny_shape = tiny.shape
-    tiny = pad_to(tiny.reshape(-1, tiny_lanes), width, tiny_lanes)
+    tiny = pad_to(tiny, TINY_ROWS, channels)
+    tiny = [tiny[:, i * tiny_lanes : (i + 1) * tiny_lanes] for i in range(channels // tiny_lanes)]
+    tiny = pad_to(jnp.concatenate(tiny, axis=0), width, tiny_lanes)
     tiny = jnp.pad(tiny, ((0, 0), (tiny_at, 0))).astype(bf16)
-    early = halve(sum_far(after(early, dxt0)))
+    early = sum_beside(halve(sum_far(after(early, dxt0))))
     home = fold(mine, send_core(other))
     late = weight_products(place, [(xn0, after(with_bc(dxt0, bc_sum), early, home[0]))])
-    early = sum_beside(early)
+    early = collect_x(jnp.concatenate([early, early1], axis=1), (late[0],))
     tiny = after(tiny, early)
     late = [v + t for v, t in zip(late, cut_x(tiny))]
-    late = sum_x(late)
-
     terms = home[:1] + [send_z(home[k].astype(bf16), k) for k in range(1, NZ)]
     [outputs] = row_call(
         end_kernel,
@@ -1206,47 +1231,57 @@
     )
     outputs_home = trade_places(outputs).astype(f32)
 
-    early = collect(early, (outputs,))
-    early1 = collect(after(early1, early[0]))
-    late = collect(sum_beside(halve(sum_far(late))))
+    late = sum_x(late)
+    early = early, send_core(early)
+    at1 = 3 * channels + LANES
     g_wz, g_wo, g_wx, narrow1 = write_sums(
         place,
         early,
-        False,
         [
-            (0, "rows", 0, None),
-            (channels, "blocks", 0, None),
-            (2 * channels, "rows", 1, None),
-            (3 * channels, "flat", 0, None),
+            (0, "rows", 0, None, False),
+            (channels, "blocks", 0, None, False),
+            (2 * channels, "rows", 1, None, False),
+            (3 * channels, "flat", 0, None, False),
         ],
     )
-    g_wx, narrow0 = write_sums(place, late, False, [(0, "rows", 0, g_wx), (channels, "flat", 0, None)])
-    g_wz, g_wo = write_sums(place, early1, True, [(0, "rows", 1, g_wz), (channels, "blocks", 1, g_wo)])
+    g_wz, g_wo = write_sums(
+        place, early, [(at1, "rows", 1, g_wz, True), (at1 + channels, "blocks", 1, g_wo, True)]
+    )
+    late = collect_x(sum_beside(halve(sum_far(after(late, outputs)))), (g_wz,))
+    late = late, send_core(late)
+    g_wx, narrow0 = write_sums(
+        place, late, [(0, "rows", 0, g_wx, False), (channels, "flat", 0, None, False)]
+    )
 
     narrow0, narrow1 = narrow0[0], narrow1[0]
-    tiny = narrow0[: tiny_shape[0] * channels // tiny_lanes, tiny_at - channels :].reshape(tiny_shape)
-    g_x = tiny[0:16].reshape(layers, 8, channels)
-    g_head = tiny[16:20, :heads].reshape(layers, 2, heads)
-    shared = tiny[20:, :both].reshape(layers, -1, both)
-    lines = width // both
-    g_norm_in = shared[:, :lines].reshape(layers, width) / norm_in
-    g_bc = shared[:, lines : lines + 5]
+    small = row_call(
+        functools.partial(small_kernel, head_dim, (bc_at - channels, tiny_at - channels)),
+        "small_gradients",
+        [(narrow0, width), (narrow1, width), (norm_in, layers), (pick, channels)],
+        [
+            jax.ShapeDtypeStruct(shape, f32)
+            for shape in (
+                norm_in.shape,
+                w_bc.shape,
+                w_dt.shape,
+                conv_x.shape,
+                conv_x_bias.shape,
+                conv_bc.shape,
+                conv_bc_bias.shape,
+                dt_bias.shape,
+                a_log.shape,
+                skip.shape,
+                norm_gate.shape,
+            )
+        ],
+    )
     return (
         outputs_home[None, :, :width],
         outputs_home[None, :, width:],
-        g_norm_in,
+        small[0],
         g_wz,
         g_wx,
-        jnp.stack([v[:, bc_at - channels : tiny_at - channels] for v in (narrow0, narrow1)]),
-        jnp.stack([v[:, :heads] for v in (narrow0, narrow1)]),
-        g_x[:, 0:4],
-        g_x[:, 4],
-        g_bc[:, 0:4],
-        g_bc[:, 4],
-        g_head[:, 0],
-        g_head[:, 1],
-        jnp.sum(g_x[:, 6].reshape(layers, heads, head_dim), axis=2),
-        g_x[:, 5],
+        *small[1:],
         g_wo,
     )
 

time: 563 us -> 583 us (1.036)
  waiting for transfers between devices: 152 us -> 173 us
  other arithmetic: 34.9 us -> 45.4 us
  local copies, waits for them, and re-layouts: 44.1 us -> 33.9 us
  starting transfers between devices: 146 us -> 138 us
    ppermute x88 -> x84, waiting for transfers between devices: 152 us -> 173 us  [send(): return lax.ppermute(v, ('dp', 'tensor'), pairs)]
    slice x11 -> x0, local copies, waits for them, and re-layouts: 8.01 us -> none  [the longest x2 1.78 us: local(): v[:, bc_at - channels:tiny_at - channels]]
    ppermute x88 -> x84, starting transfers between devices: 146 us -> 138 us  [send(): return lax.ppermute(v, ('dp', 'tensor'), pairs)]
    pallas_call x5 -> x6, Pallas kernels: 15.7 us -> 19.3 us  [row_call(): pl.pallas_call(kernel, grid=(1,), in_specs=[pl.BlockSpec((rows, v.shape[1...]
    unnamed x182 -> x183, local copies, waits for them, and re-layouts: 14.6 us -> 13.3 us
  transfers between devices with their start and end apart: 88 -> 84, of which waited for: 32 -> 31; matrix products, arithmetic and copies ran while one was open for 10% -> 9% of each run, Pallas kernels for 24% -> 23%
where the time goes in v5:
time: 583 us; the launch traced here: 572 us
  Pallas kernels  179 us (31%)
  waiting for transfers between devices  173 us (30%)
  starting transfers between devices  138 us (24%)
  other arithmetic  45.4 us (8%)
  local copies, waits for them, and re-layouts  33.9 us (6%)
    ppermute x84, waiting for transfers between devices, send(): return lax.ppermute(v, ('dp', 'tensor'), pairs)  173 us
    ppermute x84, starting transfers between devices, send(): return lax.ppermute(v, ('dp', 'tensor'), pairs)  138 us
    pallas_call x5, Pallas kernels, span_call(): pl.pallas_call(kernel, grid_spec=pltpu.PrefetchScalarGridSpec(num_scalar_...  117 us
    pallas_call x3, Pallas kernels, weight_products(): pl.pallas_call(functools.partial(weight_kernel, len(pairs), split), grid_...  26 us
    pallas_call x6, Pallas kernels, row_call(): pl.pallas_call(kernel, grid=(1,), in_specs=[pl.BlockSpec((rows, v.shape[1...  19.3 us
    pallas_call x3, Pallas kernels, write_sums(): pl.pallas_call(functools.partial(write_kernel, plan, len(kept)), grid_spe...  16.7 us
    unnamed x183, local copies, waits for them, and re-layouts  13.3 us
  transfers between devices with their start and end apart: 84, of which 31 were waited for; matrix products, arithmetic and copies ran while one was open for 9% of the time, Pallas kernels for 23%

profile of v5, /device:TPU:1, one launch (start us, length us, event | category | flops | bytes accessed | tf_op | source)
XLA Modules:
  0.0 572.1 jit_solution(2214665073745075712)
XLA Ops:
  9.3 6.2 %collective-permute-start = (bf16[192,1536]{1,0:T(8,128)(2,1)}, bf16[192,1536]{1,0:T(8,128)(2,1)}, u32[]{:S(2)}, u32[]{:S(2)}) collective-permute-start(bf16[192,1536]{1,0:T(8,128)(2,1)} %pad_maximum_fusion.7), channel_id=1, source_target_pairs={{4,8},{5,9},{6,10},{7,11},{8,4},{9,5},{10,6},{11,7},{20,24},{21,25... | collective-permute-start | bytes 1769480 | tf_op jit(solution)/shard_map/ppermute | solution.py:725
  15.5 2.8 fusion.12
  26.2 4.4 collective-permute-start.8
  42.0 8.3 %collective-permute-done.2.refs_2_ = bf16[160,1536]{1,0:T(8,128)(2,1)S(1)} collective-permute-done((bf16[160,1536]{1,0:T(8,128)(2,1)}, bf16[160,1536]{1,0:T(8,128)(2,1)S(1)}, u32[]{:S(2)}, u32[]{:S(2)}) %collective-permute-start.2) | collective-permute-done | bytes 491552 | tf_op jit(solution)/shard_map/ppermute | solution.py:725
  50.3 4.2 collective-permute-done.4.refs_4_
  58.0 4.3 collective-permute-start.9
  64.1 3.6 collective-permute-start.11
  71.0 23.1 %layer_forward.2 = (bf16[1536,1152]{1,0:T(8,128)(2,1)}, bf16[1024,1536]{1,0:T(8,128)(2,1)}, bf16[256,1536]{1,0:T(8,128)(2,1)}, bf16[1024,384]{1,0:T(8,128)(2,1)}...) custom-call(s32[4]{0:T(128)} %pad_add_fusion.2.place_ref, ...), custom_call_target="tpu_custom_call" | custom-call | flops 20000000000 | bytes 26501120 | tf_op jit(solution)/shard_map/layer_forward/pallas_call | solution.py:496
  100.5 2.8 add_convert_fusion.4
  103.3 4.4 collective-permute-start.28
  109.4 3.3 collective-permute-start.15
  113.6 6.8 %collective-permute-done.14.a_ref = bf16[128,1664]{1,0:T(8,128)(2,1)S(1)} collective-permute-done((bf16[128,1664]{1,0:T(8,128)(2,1)S(1)}, bf16[128,1664]{1,0:T(8,128)(2,1)S(1)}, u32[]{:S(2)}, u32[]{:S(2)}) %collective-permute-start.14) | collective-permute-done | bytes 426016 | tf_op jit(solution)/shard_map/ppermute | solution.py:725
  120.4 10.6 %collective-permute-done.15.b_ref = bf16[128,1664]{1,0:T(8,128)(2,1)S(1)} collective-permute-done((bf16[128,1664]{1,0:T(8,128)(2,1)S(1)}, bf16[128,1664]{1,0:T(8,128)(2,1)S(1)}, u32[]{:S(2)}, u32[]{:S(2)}) %collective-permute-start.15) | collective-permute-done | bytes 426016 | tf_op jit(solution)/shard_map/ppermute | solution.py:725
  131.9 3.3 middle_norm.1
  139.5 7.5 %collective-permute-done.18.refs_2_ = bf16[128,1536]{1,0:T(8,128)(2,1)S(1)} collective-permute-done((bf16[128,1536]{1,0:T(8,128)(2,1)}, bf16[128,1536]{1,0:T(8,128)(2,1)S(1)}, u32[]{:S(2)}, u32[]{:S(2)}) %collective-permute-start.18) | collective-permute-done | bytes 393248 | tf_op jit(solution)/shard_map/ppermute | solution.py:725
  149.5 6.3 %collective-permute-done.22.refs_6_ = bf16[128,1536]{1,0:T(8,128)(2,1)S(1)} collective-permute-done((bf16[128,1536]{1,0:T(8,128)(2,1)}, bf16[128,1536]{1,0:T(8,128)(2,1)S(1)}, u32[]{:S(2)}, u32[]{:S(2)}) %collective-permute-start.22) | collective-permute-done | bytes 393248 | tf_op jit(solution)/shard_map/ppermute | solution.py:725
  159.2 27.0 %layer_forward.3 = (bf16[1536,1152]{1,0:T(8,128)(2,1)}, bf16[1024,1536]{1,0:T(8,128)(2,1)}, bf16[256,1536]{1,0:T(8,128)(2,1)}, bf16[1024,384]{1,0:T(8,128)(2,1)}...) custom-call(s32[4]{0:T(128)} %pad_add_fusion.2.place_ref, ...), custom_call_target="tpu_custom_call" | custom-call | flops 20000000000 | bytes 34398208 | tf_op jit(solution)/shard_map/layer_forward/pallas_call | solution.py:496
  186.8 3.3 collective-permute-done.29
  191.8 3.2 collective-permute-start.31
  205.9 29.6 %scan_backward.2 = (bf16[1024,384]{1,0:T(8,128)(2,1)}, bf16[1024,384]{1,0:T(8,128)(2,1)}, bf16[1024,512]{1,0:T(8,128)(2,1)}, bf16[512,256]{1,0:T(8,128)(2,1)}, b...) custom-call(s32[4]{0:T(128)} %pad_add_fusion.2.place_ref, ...), custom_call_target="tpu_custom_call" | custom-call | flops 28000000000 | bytes 21512192 | tf_op jit(solution)/shard_map/scan_backward/pallas_call | solution.py:496
  238.4 8.3 %weight_products.3 = bf16[1536,768]{1,0:T(8,128)(2,1)} custom-call(s32[4]{0:T(128)} %pad_add_fusion.2.place_ref, bf16[1024,1536]{1,0:T(8,128)(2,1)} %get-tuple-element.145.refs_4_.refs_0_.refs_2_, bf16[1024,384]{1,0:T(8,128)(2,1)} %get-tuple-element.157.refs_1_, bf16[1024,384]{1,0:T(8,128)(2,1)} %get-tuple-element.158.refs_2_, ...), custom_call_target="tpu_custom_call" | custom-call | flops 2415919104 | bytes 8000000 | tf_op jit(solution)/shard_map/weight_products/pallas_call | solution.py:692
  246.6 4.2 collective-permute-start.49
  255.5 17.9 %collective-permute-done.39.a_ref = bf16[128,1792]{1,0:T(8,128)(2,1)S(1)} collective-permute-done((bf16[128,1792]{1,0:T(8,128)(2,1)S(1)}, bf16[128,1792]{1,0:T(8,128)(2,1)S(1)}, u32[]{:S(2)}, u32[]{:S(2)}) %collective-permute-start.39) | collective-permute-done | bytes 458784 | tf_op jit(solution)/shard_map/ppermute | solution.py:725
  276.2 3.9 between_layers.1
  292.9 4.8 collective-permute-start.44
  297.7 6.7 %collective-permute-start.46 = (bf16[128,1664]{1,0:T(8,128)(2,1)}, bf16[128,1664]{1,0:T(8,128)(2,1)S(1)}, u32[]{:S(2)}, u32[]{:S(2)}) collective-permute-start(bf16[128,1664]{1,0:T(8,128)(2,1)} %collective-permute-done.45.refs_4_), channel_id=1, source_target_pairs={{0,8},{1,9},{2,10},{3,11},{4,12},{5,13},{6,14},{7,15},{8,0},{9,1},... | collective-permute-start | bytes 1277960 | tf_op jit(solution)/shard_map/ppermute | solution.py:725
  313.2 8.4 %gate_backward.1 = (bf16[1024,1536]{1,0:T(8,128)(2,1)}, bf16[1024,384]{1,0:T(8,128)(2,1)}, f32[1024,384]{1,0:T(8,128)}, bf16[1024,384]{1,0:T(8,128)(2,1)}, f32[8,384]{1,0:T(8,128)}) custom-call(s32[4]{0:T(128)} %pad_add_fusion.2.place_ref, bf16[128,1664]{1,0:T(8,128)(2,1)} %get-tuple-element.164.refs_0_, bf16[128,1664]{1,0:T(8,128)(2,1)} %collective-permute-done.42.refs_1_, ...), custom_call_target="tpu_custom_call" | custom-call | flops 6000000000 | bytes 14835712 | tf_op jit(solution)/shard_map/gate_backward/pallas_call | solution.py:496
  324.8 11.2 %weight_products.4 = (bf16[384,1280]{1,0:T(8,128)(2,1)}, bf16[384,1280]{1,0:T(8,128)(2,1)}, bf16[384,1280]{1,0:T(8,128)(2,1)}, bf16[384,1280]{1,0:T(8,128)(2,1)}) custom-call(s32[4]{0:T(128)} %pad_add_fusion.2.place_ref, bf16[1024,1536]{1,0:T(8,128)(2,1)} %get-tuple-element.171.refs_0_.refs_2_, bf16[1024,384]{1,0:T(8,128)(2,1)} %get-tuple-element.172.refs_1_, ...), custom_call_target="tpu_custom_call" | custom-call | flops 4026531840 | bytes 8000000 | tf_op jit(solution)/shard_map/weight_products/pallas_call | solution.py:692
  340.9 29.2 %scan_backward.3 = (bf16[1024,512]{1,0:T(8,128)(2,1)}, bf16[512,256]{1,0:T(8,128)(2,1)}, bf16[512,256]{1,0:T(8,128)(2,1)}, bf16[512,1536]{1,0:T(8,128)(2,1)}, bf...) custom-call(s32[4]{0:T(128)} %pad_add_fusion.2.place_ref, ...), custom_call_target="tpu_custom_call" | custom-call | flops 28000000000 | bytes 19120128 | tf_op jit(solution)/shard_map/scan_backward/pallas_call | solution.py:496
  370.2 12.3 %collective-permute-done.61 = bf16[384,1280]{1,0:T(8,128)(2,1)S(1)} collective-permute-done((bf16[384,1280]{1,0:T(8,128)(2,1)}, bf16[384,1280]{1,0:T(8,128)(2,1)S(1)}, u32[]{:S(2)}, u32[]{:S(2)}) %collective-permute-start.61) | collective-permute-done | bytes 983072 | tf_op jit(solution)/shard_map/ppermute | solution.py:725
  391.7 3.4 collective-permute-start.64
  395.1 3.3 collective-permute-done.66
  398.4 3.0 collective-permute-start.65
  406.6 5.3 collective-permute-done.67
  414.6 10.6 %collective-permute-done.68 = bf16[192,1280]{1,0:T(8,128)(2,1)S(1)} collective-permute-done((bf16[192,1280]{1,0:T(8,128)(2,1)S(1)}, bf16[192,1280]{1,0:T(8,128)(2,1)S(1)}, u32[]{:S(2)}, u32[]{:S(2)}) %collective-permute-start.68) | collective-permute-done | bytes 491552 | tf_op jit(solution)/shard_map/ppermute | solution.py:725
  436.0 6.5 %weight_products.5 = (bf16[384,512]{1,0:T(8,128)(2,1)}, bf16[384,512]{1,0:T(8,128)(2,1)}, bf16[384,512]{1,0:T(8,128)(2,1)}, bf16[384,512]{1,0:T(8,128)(2,1)}) custom-call(s32[4]{0:T(128)} %pad_add_fusion.2.place_ref, bf16[1024,1536]{1,0:T(8,128)(2,1)} %get-tuple-element.171.refs_0_.refs_2_, bf16[1024,512]{1,0:T(8,128)(2,1)} %pad_add_fusion.refs_1_), custom_call_target="tpu_custom_call" | custom-call | flops 1610612736 | bytes 8000000 | tf_op jit(solution)/shard_map/weight_products/pallas_call | solution.py:692
  442.5 3.2 collective-permute-done.70
  445.7 17.4 %collective-permute-done.71 = bf16[192,2048]{1,0:T(8,128)(2,1)} collective-permute-done((bf16[192,2048]{1,0:T(8,128)(2,1)}, bf16[192,2048]{1,0:T(8,128)(2,1)}, u32[]{:S(2)}, u32[]{:S(2)}) %collective-permute-start.71) | collective-permute-done | bytes 786464 | tf_op jit(solution)/shard_map/ppermute | solution.py:725
  473.6 14.5 %collective-permute-done.55.a_ref = bf16[128,1536]{1,0:T(8,128)(2,1)S(1)} collective-permute-done((bf16[128,1536]{1,0:T(8,128)(2,1)S(1)}, bf16[128,1536]{1,0:T(8,128)(2,1)S(1)}, u32[]{:S(2)}, u32[]{:S(2)}) %collective-permute-start.55) | collective-permute-done | bytes 393248 | tf_op jit(solution)/shard_map/ppermute | solution.py:725
  495.7 3.5 outputs.1
  499.7 8.6 %collective-permute-done.75 = bf16[384,512]{1,0:T(8,128)(2,1)} collective-permute-done((bf16[384,512]{1,0:T(8,128)(2,1)}, bf16[384,512]{1,0:T(8,128)(2,1)}, u32[]{:S(2)}, u32[]{:S(2)}) %collective-permute-start.75) | collective-permute-done | bytes 393248 | tf_op jit(solution)/shard_map/ppermute | solution.py:725
  511.2 4.7 collective-permute-done.76
  517.3 7.8 %collective-permute-start.58 = (bf16[128,3072]{1,0:T(8,128)(2,1)S(1)}, bf16[128,3072]{1,0:T(8,128)(2,1)S(1)}, u32[]{:S(2)}, u32[]{:S(2)}) collective-permute-start(bf16[128,3072]{1,0:T(8,128)(2,1)S(1)} %copy-done.6), channel_id=1, source_target_pairs={{4,8},{5,9},{6,10},{7,11},{8,4},{9,5},{10,6},{11,7},{20,24},{21,25... | collective-permute-start | bytes 2359304 | tf_op jit(solution)/shard_map/ppermute | solution.py:725
  525.7 13.7 %collective-permute-done.78 = bf16[192,512]{1,0:T(8,128)(2,1)S(1)} collective-permute-done((bf16[192,512]{1,0:T(8,128)(2,1)S(1)}, bf16[192,512]{1,0:T(8,128)(2,1)S(1)}, u32[]{:S(2)}, u32[]{:S(2)}) %collective-permute-start.78) | collective-permute-done | bytes 196640 | tf_op jit(solution)/shard_map/ppermute | solution.py:725
  544.0 7.0 %write_sums.3 = (f32[2,4,2,192,384]{4,3,2,1,0:T(8,128)}, f32[2,384,1536]{2,1,0:T(8,128)}, f32[2,4,2,192,384]{4,3,2,1,0:T(8,128)}, f32[1,4,2,192,128]{4,3,2,1,0:T(8,128)}) custom-call(s32[4]{0:T(128)} %pad_add_fusion.2.place_ref, bf16[4,192,2048]{2,1,0:T(8,128)(2,1)} %copy-done, bf16[4,192,2048]{2,1,0:T(8,128)(2,1)} %collective-permute-done.80.there_ref), custom_call_target="tpu_custom_call" | custom-call | tf_op jit(solution)/shard_map/write_sums/pallas_call | solution.py:925
  550.9 5.9 %write_sums.4 = (f32[2,2,4,192,384]{4,3,2,1,0:T(8,128)}, f32[2,384,1536]{2,1,0:T(8,128)}) custom-call(s32[4]{0:T(128)} %pad_add_fusion.2.place_ref, bf16[4,192,2048]{2,1,0:T(8,128)(2,1)} %copy-done, bf16[4,192,2048]{2,1,0:T(8,128)(2,1)} %collective-permute-done.80.there_ref, ...), custom_call_target="tpu_custom_call", output_to_operand_aliasing={{0}: (3, {}), {1}: (4, {})} | custom-call | tf_op jit(solution)/shard_map/write_sums/pallas_call | solution.py:925
  560.3 3.9 write_sums.5
  564.1 3.6 small_gradients.1
  (414 shorter events, 171.8 us)
Async XLA Ops:
  9.3 14.7 %collective-permute-start = (bf16[192,1536]{1,0:T(8,128)(2,1)}, bf16[192,1536]{1,0:T(8,128)(2,1)}, u32[]{:S(2)}, u32[]{:S(2)}) collective-permute-start(bf16[192,1536]{1,0:T(8,128)(2,1)} %pad_maximum_fusion.7), channel_id=1, source_target_pairs={{4,8},{5,9},{6,10},{7,11},{8,4},{9,5},{10,6},{11,7},{20,24},{21,25... | collective-permute-start | bytes 1769480 | tf_op jit(solution)/shard_map/ppermute | solution.py:725
  26.2 44.8 %collective-permute-start.8 = (bf16[1536,1152]{1,0:T(8,128)(2,1)}, bf16[1536,1152]{1,0:T(8,128)(2,1)}, u32[]{:S(2)}, u32[]{:S(2)}) collective-permute-start(bf16[1536,1152]{1,0:T(8,128)(2,1)} %pad_maximum_fusion.refs_8_), channel_id=1, source_target_pairs={{4,8},{5,9},{6,10},{7,11},{8,4},{9,5},{10,6},{11,7},{20,24},{21,25... | collective-permute-start | bytes 10616840 | tf_op jit(solution)/shard_map/ppermute | solution.py:725
  34.7 15.5 %collective-permute-start.2 = (bf16[160,1536]{1,0:T(8,128)(2,1)}, bf16[160,1536]{1,0:T(8,128)(2,1)S(1)}, u32[]{:S(2)}, u32[]{:S(2)}) collective-permute-start(bf16[160,1536]{1,0:T(8,128)(2,1)} %first_norm.1.refs_0_), channel_id=1, source_target_pairs={{0,1},{1,2},{2,3},{3,0},{4,5},{5,6},{6,7},{7,4},{8,9},{9,10},{10,1... | collective-permute-start | bytes 1474568 | tf_op jit(solution)/shard_map/ppermute | solution.py:725
  36.4 18.1 %collective-permute-start.4 = (bf16[160,1536]{1,0:T(8,128)(2,1)}, bf16[160,1536]{1,0:T(8,128)(2,1)S(1)}, u32[]{:S(2)}, u32[]{:S(2)}) collective-permute-start(bf16[160,1536]{1,0:T(8,128)(2,1)} %first_norm.1.refs_0_), channel_id=1, source_target_pairs={{0,3},{1,0},{2,1},{3,2},{4,7},{5,4},{6,5},{7,6},{8,11},{9,8},{10,9... | collective-permute-start | bytes 1474568 | tf_op jit(solution)/shard_map/ppermute | solution.py:725
  38.5 17.5 %collective-permute-start.6 = (bf16[160,1536]{1,0:T(8,128)(2,1)}, bf16[160,1536]{1,0:T(8,128)(2,1)S(1)}, u32[]{:S(2)}, u32[]{:S(2)}) collective-permute-start(bf16[160,1536]{1,0:T(8,128)(2,1)} %first_norm.1.refs_0_), channel_id=1, source_target_pairs={{0,2},{1,3},{2,0},{3,1},{4,6},{5,7},{6,4},{7,5},{8,10},{9,11},{10,... | collective-permute-start | bytes 1474568 | tf_op jit(solution)/shard_map/ppermute | solution.py:725
  39.8 18.2 %collective-permute-start.1 = (bf16[160,1536]{1,0:T(8,128)(2,1)}, bf16[160,1536]{1,0:T(8,128)(2,1)S(1)}, u32[]{:S(2)}, u32[]{:S(2)}) collective-permute-start(bf16[160,1536]{1,0:T(8,128)(2,1)} %first_norm.1.refs_0_), channel_id=1, source_target_pairs={{0,8},{1,9},{2,10},{3,11},{4,12},{5,13},{6,14},{7,15},{8,0},{9,1},... | collective-permute-start | bytes 1474568 | tf_op jit(solution)/shard_map/ppermute | solution.py:725
  58.0 36.1 %collective-permute-start.9 = (bf16[160,1536]{1,0:T(8,128)(2,1)S(1)}, bf16[160,1536]{1,0:T(8,128)(2,1)S(1)}, u32[]{:S(2)}, u32[]{:S(2)}) collective-permute-start(bf16[160,1536]{1,0:T(8,128)(2,1)S(1)} %pad_maximum_fusion.8), channel_id=1, source_target_pairs={{4,8},{5,9},{6,10},{7,11},{8,4},{9,5},{10,6},{11,7},{20,24},{21,25... | collective-permute-start | bytes 1474568 | tf_op jit(solution)/shard_map/ppermute | solution.py:725
  62.3 32.6 %collective-permute-start.10 = (bf16[160,1536]{1,0:T(8,128)(2,1)S(1)}, bf16[160,1536]{1,0:T(8,128)(2,1)S(1)}, u32[]{:S(2)}, u32[]{:S(2)}) collective-permute-start(bf16[160,1536]{1,0:T(8,128)(2,1)S(1)} %pad_maximum_fusion.8), channel_id=1, source_target_pairs={{0,1},{1,2},{2,3},{3,0},{4,9},{5,10},{6,11},{7,8},{8,5},{9,6},{10,... | collective-permute-start | bytes 1474568 | tf_op jit(solution)/shard_map/ppermute | solution.py:725
  64.1 30.8 %collective-permute-start.11 = (bf16[160,1536]{1,0:T(8,128)(2,1)S(1)}, bf16[160,1536]{1,0:T(8,128)(2,1)S(1)}, u32[]{:S(2)}, u32[]{:S(2)}) collective-permute-start(bf16[160,1536]{1,0:T(8,128)(2,1)S(1)} %pad_maximum_fusion.8), channel_id=1, source_target_pairs={{0,3},{1,0},{2,1},{3,2},{4,11},{5,8},{6,9},{7,10},{8,7},{9,4},{10,... | collective-permute-start | bytes 1474568 | tf_op jit(solution)/shard_map/ppermute | solution.py:725
  67.7 27.3 %collective-permute-start.12 = (bf16[160,1536]{1,0:T(8,128)(2,1)S(1)}, bf16[160,1536]{1,0:T(8,128)(2,1)S(1)}, u32[]{:S(2)}, u32[]{:S(2)}) collective-permute-start(bf16[160,1536]{1,0:T(8,128)(2,1)S(1)} %pad_maximum_fusion.8), channel_id=1, source_target_pairs={{0,2},{1,3},{2,0},{3,1},{4,10},{5,11},{6,8},{7,9},{8,6},{9,7},{10,... | collective-permute-start | bytes 1474568 | tf_op jit(solution)/shard_map/ppermute | solution.py:725
  103.3 55.2 %collective-permute-start.28 = (bf16[1536,1152]{1,0:T(8,128)(2,1)S(1)}, bf16[1536,1152]{1,0:T(8,128)(2,1)}, u32[]{:S(2)}, u32[]{:S(2)}) collective-permute-start(bf16[1536,1152]{1,0:T(8,128)(2,1)S(1)} %pad_maximum_fusion.1.refs_16_), channel_id=1, source_target_pairs={{4,8},{5,9},{6,10},{7,11},{8,4},{9,5},{10,6},{11,7},{20,24},{21,25... | collective-permute-start | bytes 10616840 | tf_op jit(solution)/shard_map/ppermute | solution.py:725
  109.4 21.6 %collective-permute-start.15 = (bf16[128,1664]{1,0:T(8,128)(2,1)S(1)}, bf16[128,1664]{1,0:T(8,128)(2,1)S(1)}, u32[]{:S(2)}, u32[]{:S(2)}) collective-permute-start(bf16[128,1664]{1,0:T(8,128)(2,1)S(1)} %get-tuple-element.274), channel_id=1, source_target_pairs={{0,2},{1,3},{2,0},{3,1},{4,6},{5,7},{6,4},{7,5},{8,10},{9,11},{10,... | collective-permute-start | bytes 1277960 | tf_op jit(solution)/shard_map/ppermute | solution.py:725
  112.7 18.3 %collective-permute-start.16 = (bf16[128,1664]{1,0:T(8,128)(2,1)S(1)}, bf16[128,1664]{1,0:T(8,128)(2,1)S(1)}, u32[]{:S(2)}, u32[]{:S(2)}) collective-permute-start(bf16[128,1664]{1,0:T(8,128)(2,1)S(1)} %get-tuple-element.273), channel_id=1, source_target_pairs={{0,3},{1,0},{2,1},{3,2},{4,7},{5,4},{6,5},{7,6},{8,11},{9,8},{10,9... | collective-permute-start | bytes 1277960 | tf_op jit(solution)/shard_map/ppermute | solution.py:725
  113.6 21.6 %collective-permute-start.24 = (bf16[160,1536]{1,0:T(8,128)(2,1)S(1)}, bf16[160,1536]{1,0:T(8,128)(2,1)S(1)}, u32[]{:S(2)}, u32[]{:S(2)}) collective-permute-start(bf16[160,1536]{1,0:T(8,128)(2,1)S(1)} %copy-done.7), channel_id=1, source_target_pairs={{0,8},{1,9},{2,10},{3,11},{4,12},{5,13},{6,14},{7,15},{8,0},{9,1},... | collective-permute-start | bytes 1474568 | tf_op jit(solution)/shard_map/ppermute | solution.py:725
  120.4 16.2 %collective-permute-start.25 = (bf16[160,1536]{1,0:T(8,128)(2,1)S(1)}, bf16[160,1536]{1,0:T(8,128)(2,1)S(1)}, u32[]{:S(2)}, u32[]{:S(2)}) collective-permute-start(bf16[160,1536]{1,0:T(8,128)(2,1)S(1)} %copy-done.63), channel_id=1, source_target_pairs={{0,8},{1,9},{2,10},{3,11},{4,12},{5,13},{6,14},{7,15},{8,0},{9,1},... | collective-permute-start | bytes 1474568 | tf_op jit(solution)/shard_map/ppermute | solution.py:725
  138.0 17.9 %collective-permute-start.22 = (bf16[128,1536]{1,0:T(8,128)(2,1)}, bf16[128,1536]{1,0:T(8,128)(2,1)S(1)}, u32[]{:S(2)}, u32[]{:S(2)}) collective-permute-start(bf16[128,1536]{1,0:T(8,128)(2,1)} %get-tuple-element.132.refs_0_), channel_id=1, source_target_pairs={{0,2},{1,3},{2,0},{3,1},{4,6},{5,7},{6,4},{7,5},{8,10},{9,11},{10,... | collective-permute-start | bytes 1179656 | tf_op jit(solution)/shard_map/ppermute | solution.py:725
  138.7 19.2 %collective-permute-start.17 = (bf16[128,1536]{1,0:T(8,128)(2,1)}, bf16[128,1536]{1,0:T(8,128)(2,1)S(1)}, u32[]{:S(2)}, u32[]{:S(2)}) collective-permute-start(bf16[128,1536]{1,0:T(8,128)(2,1)} %get-tuple-element.132.refs_0_), channel_id=1, source_target_pairs={{0,8},{1,9},{2,10},{3,11},{4,12},{5,13},{6,14},{7,15},{8,0},{9,1},... | collective-permute-start | bytes 1179656 | tf_op jit(solution)/shard_map/ppermute | solution.py:725
  199.9 35.6 %collective-permute-start.34 = (bf16[128,1664]{1,0:T(8,128)(2,1)S(1)}, bf16[128,1664]{1,0:T(8,128)(2,1)S(1)}, u32[]{:S(2)}, u32[]{:S(2)}) collective-permute-start(bf16[128,1664]{1,0:T(8,128)(2,1)S(1)} %get-tuple-element.272), channel_id=1, source_target_pairs={{0,1},{1,2},{2,3},{3,0},{4,5},{5,6},{6,7},{7,4},{8,9},{9,10},{10,1... | collective-permute-start | bytes 1277960 | tf_op jit(solution)/shard_map/ppermute | solution.py:725
  200.0 35.5 %collective-permute-start.35 = (bf16[128,1664]{1,0:T(8,128)(2,1)S(1)}, bf16[128,1664]{1,0:T(8,128)(2,1)S(1)}, u32[]{:S(2)}, u32[]{:S(2)}) collective-permute-start(bf16[128,1664]{1,0:T(8,128)(2,1)S(1)} %get-tuple-element.271), channel_id=1, source_target_pairs={{0,2},{1,3},{2,0},{3,1},{4,6},{5,7},{6,4},{7,5},{8,10},{9,11},{10,... | collective-permute-start | bytes 1277960 | tf_op jit(solution)/shard_map/ppermute | solution.py:725
  202.7 32.8 %collective-permute-start.36 = (bf16[128,1664]{1,0:T(8,128)(2,1)S(1)}, bf16[128,1664]{1,0:T(8,128)(2,1)S(1)}, u32[]{:S(2)}, u32[]{:S(2)}) collective-permute-start(bf16[128,1664]{1,0:T(8,128)(2,1)S(1)} %get-tuple-element.270), channel_id=1, source_target_pairs={{0,3},{1,0},{2,1},{3,2},{4,7},{5,4},{6,5},{7,6},{8,11},{9,8},{10,9... | collective-permute-start | bytes 1277960 | tf_op jit(solution)/shard_map/ppermute | solution.py:725
  235.6 15.3 %collective-permute-start.37 = (bf16[512,1536]{1,0:T(8,128)(2,1)}, bf16[512,1536]{1,0:T(8,128)(2,1)S(1)}, u32[]{:S(2)}, u32[]{:S(2)}) collective-permute-start(bf16[512,1536]{1,0:T(8,128)(2,1)} %get-tuple-element.154), channel_id=1, source_target_pairs={{0,8},{1,9},{2,10},{3,11},{4,12},{5,13},{6,14},{7,15},{8,0},{9,1},... | collective-permute-start | bytes 4718600 | tf_op jit(solution)/shard_map/ppermute | solution.py:725
  246.6 33.5 %collective-permute-start.49 = (bf16[1536,768]{1,0:T(8,128)(2,1)}, bf16[1536,768]{1,0:T(8,128)(2,1)S(1)}, u32[]{:S(2)}, u32[]{:S(2)}) collective-permute-start(bf16[1536,768]{1,0:T(8,128)(2,1)} %weight_products.3), channel_id=1, source_target_pairs={{4,0},{5,1},{6,2},{7,3},{8,12},{9,13},{10,14},{11,15},{20,16},{21,... | collective-permute-start | bytes 7077896 | tf_op jit(solution)/shard_map/ppermute | solution.py:725
  251.3 22.1 %collective-permute-start.39 = (bf16[128,1792]{1,0:T(8,128)(2,1)S(1)}, bf16[128,1792]{1,0:T(8,128)(2,1)S(1)}, u32[]{:S(2)}, u32[]{:S(2)}) collective-permute-start(bf16[128,1792]{1,0:T(8,128)(2,1)S(1)} %pad_maximum_fusion.9), channel_id=1, source_target_pairs={{0,1},{1,2},{2,3},{3,0},{4,5},{5,6},{6,7},{7,4},{8,9},{9,10},{10,1... | collective-permute-start | bytes 1376264 | tf_op jit(solution)/shard_map/ppermute | solution.py:725
  251.8 21.6 %collective-permute-start.40 = (bf16[128,1792]{1,0:T(8,128)(2,1)S(1)}, bf16[128,1792]{1,0:T(8,128)(2,1)S(1)}, u32[]{:S(2)}, u32[]{:S(2)}) collective-permute-start(bf16[128,1792]{1,0:T(8,128)(2,1)S(1)} %pad_maximum_fusion.4), channel_id=1, source_target_pairs={{0,2},{1,3},{2,0},{3,1},{4,6},{5,7},{6,4},{7,5},{8,10},{9,11},{10,... | collective-permute-start | bytes 1376264 | tf_op jit(solution)/shard_map/ppermute | solution.py:725
  253.4 21.1 %collective-permute-start.41 = (bf16[128,1792]{1,0:T(8,128)(2,1)S(1)}, bf16[128,1792]{1,0:T(8,128)(2,1)S(1)}, u32[]{:S(2)}, u32[]{:S(2)}) collective-permute-start(bf16[128,1792]{1,0:T(8,128)(2,1)S(1)} %pad_maximum_fusion.10), channel_id=1, source_target_pairs={{0,3},{1,0},{2,1},{3,2},{4,7},{5,4},{6,5},{7,6},{8,11},{9,8},{10,9... | collective-permute-start | bytes 1376264 | tf_op jit(solution)/shard_map/ppermute | solution.py:725
  280.8 25.1 %collective-permute-start.50 = (bf16[768,768]{1,0:T(8,128)(2,1)S(1)}, bf16[768,768]{1,0:T(8,128)(2,1)}, u32[]{:S(2)}, u32[]{:S(2)}) collective-permute-start(bf16[768,768]{1,0:T(8,128)(2,1)S(1)} %slice.220), channel_id=1, source_target_pairs={{0,8},{1,9},{2,10},{3,11},{12,4},{13,5},{14,6},{15,7},{16,24},{17,... | collective-permute-start | bytes 3538952 | tf_op jit(solution)/shard_map/ppermute | solution.py:725
  284.8 19.5 %collective-permute-start.47 = (bf16[128,1664]{1,0:T(8,128)(2,1)}, bf16[128,1664]{1,0:T(8,128)(2,1)}, u32[]{:S(2)}, u32[]{:S(2)}) collective-permute-start(bf16[128,1664]{1,0:T(8,128)(2,1)} %get-tuple-element.164.refs_0_), channel_id=1, source_target_pairs={{0,2},{1,3},{2,0},{3,1},{4,6},{5,7},{6,4},{7,5},{8,10},{9,11},{10,... | collective-permute-start | bytes 1277960 | tf_op jit(solution)/shard_map/ppermute | solution.py:725
  285.8 22.8 %collective-permute-start.42 = (bf16[128,1664]{1,0:T(8,128)(2,1)}, bf16[128,1664]{1,0:T(8,128)(2,1)}, u32[]{:S(2)}, u32[]{:S(2)}) collective-permute-start(bf16[128,1664]{1,0:T(8,128)(2,1)} %get-tuple-element.164.refs_0_), channel_id=1, source_target_pairs={{0,8},{1,9},{2,10},{3,11},{4,12},{5,13},{6,14},{7,15},{8,0},{9,1},... | collective-permute-start | bytes 1277960 | tf_op jit(solution)/shard_map/ppermute | solution.py:725
  292.9 18.2 %collective-permute-start.44 = (bf16[128,1664]{1,0:T(8,128)(2,1)}, bf16[128,1664]{1,0:T(8,128)(2,1)S(1)}, u32[]{:S(2)}, u32[]{:S(2)}) collective-permute-start(bf16[128,1664]{1,0:T(8,128)(2,1)} %collective-permute-done.43.refs_2_), channel_id=1, source_target_pairs={{0,8},{1,9},{2,10},{3,11},{4,12},{5,13},{6,14},{7,15},{8,0},{9,1},... | collective-permute-start | bytes 1277960 | tf_op jit(solution)/shard_map/ppermute | solution.py:725
  308.7 15.2 %collective-permute-start.52 = (bf16[192,768]{1,0:T(8,128)(2,1)S(1)}, bf16[192,768]{1,0:T(8,128)(2,1)S(1)}, u32[]{:S(2)}, u32[]{:S(2)}) collective-permute-start(bf16[192,768]{1,0:T(8,128)(2,1)S(1)} %get-tuple-element.297), channel_id=1, source_target_pairs={{0,64},{1,65},{2,66},{3,67},{4,68},{5,69},{6,70},{7,71},{8,72},{9,... | collective-permute-start | bytes 884744 | tf_op jit(solution)/shard_map/ppermute | solution.py:725
  336.0 34.2 %collective-permute-start.60 = (bf16[384,1280]{1,0:T(8,128)(2,1)}, bf16[384,1280]{1,0:T(8,128)(2,1)S(1)}, u32[]{:S(2)}, u32[]{:S(2)}) collective-permute-start(bf16[384,1280]{1,0:T(8,128)(2,1)} %get-tuple-element.178), channel_id=1, source_target_pairs={{0,32},{1,33},{2,34},{3,35},{4,36},{5,37},{6,38},{7,39},{8,40},{9,... | collective-permute-start | bytes 2949128 | tf_op jit(solution)/shard_map/ppermute | solution.py:725
  337.7 44.8 %collective-permute-start.61 = (bf16[384,1280]{1,0:T(8,128)(2,1)}, bf16[384,1280]{1,0:T(8,128)(2,1)S(1)}, u32[]{:S(2)}, u32[]{:S(2)}) collective-permute-start(bf16[384,1280]{1,0:T(8,128)(2,1)} %get-tuple-element.179), channel_id=1, source_target_pairs={{0,64},{1,65},{2,66},{3,67},{4,68},{5,69},{6,70},{7,71},{8,72},{9,... | collective-permute-start | bytes 2949128 | tf_op jit(solution)/shard_map/ppermute | solution.py:725
  339.7 42.8 %collective-permute-start.62 = (bf16[384,1280]{1,0:T(8,128)(2,1)}, bf16[384,1280]{1,0:T(8,128)(2,1)S(1)}, u32[]{:S(2)}, u32[]{:S(2)}) collective-permute-start(bf16[384,1280]{1,0:T(8,128)(2,1)} %get-tuple-element.180), channel_id=1, source_target_pairs={{0,96},{1,97},{2,98},{3,99},{4,100},{5,101},{6,102},{7,103},{8,104... | collective-permute-start | bytes 2949128 | tf_op jit(solution)/shard_map/ppermute | solution.py:725
  383.0 15.5 %collective-permute-start.66 = (bf16[384,1280]{1,0:T(8,128)(2,1)S(1)}, bf16[384,1280]{1,0:T(8,128)(2,1)}, u32[]{:S(2)}, u32[]{:S(2)}) collective-permute-start(bf16[384,1280]{1,0:T(8,128)(2,1)S(1)} %add_convert_fusion.2), channel_id=1, source_target_pairs={{4,0},{5,1},{6,2},{7,3},{8,12},{9,13},{10,14},{11,15},{20,16},{21,... | collective-permute-start | bytes 2949128 | tf_op jit(solution)/shard_map/ppermute | solution.py:725
  386.9 16.1 %collective-permute-start.69 = (bf16[192,768]{1,0:T(8,128)(2,1)}, bf16[192,768]{1,0:T(8,128)(2,1)S(1)}, u32[]{:S(2)}, u32[]{:S(2)}) collective-permute-start(bf16[192,768]{1,0:T(8,128)(2,1)} %add_convert_fusion.15), channel_id=1, source_target_pairs={{0,16},{1,17},{2,18},{3,19},{4,20},{5,21},{6,22},{7,23},{8,24},{9,... | collective-permute-start | bytes 884744 | tf_op jit(solution)/shard_map/ppermute | solution.py:725
  387.2 47.4 %collective-permute-start.54 = (bf16[512,1536]{1,0:T(8,128)(2,1)}, bf16[512,1536]{1,0:T(8,128)(2,1)S(1)}, u32[]{:S(2)}, u32[]{:S(2)}) collective-permute-start(bf16[512,1536]{1,0:T(8,128)(2,1)} %get-tuple-element.188), channel_id=1, source_target_pairs={{0,8},{1,9},{2,10},{3,11},{4,12},{5,13},{6,14},{7,15},{8,0},{9,1},... | collective-permute-start | bytes 4718600 | tf_op jit(solution)/shard_map/ppermute | solution.py:725
  426.6 19.1 %collective-permute-start.70 = (bf16[192,2048]{1,0:T(8,128)(2,1)}, bf16[192,2048]{1,0:T(8,128)(2,1)}, u32[]{:S(2)}, u32[]{:S(2)}) collective-permute-start(bf16[192,2048]{1,0:T(8,128)(2,1)} %get-tuple-element.299), channel_id=1, source_target_pairs={{0,32},{1,33},{2,34},{3,35},{4,36},{5,37},{6,38},{7,39},{8,40},{9,... | collective-permute-start | bytes 2359304 | tf_op jit(solution)/shard_map/ppermute | solution.py:725
  428.0 35.2 %collective-permute-start.71 = (bf16[192,2048]{1,0:T(8,128)(2,1)}, bf16[192,2048]{1,0:T(8,128)(2,1)}, u32[]{:S(2)}, u32[]{:S(2)}) collective-permute-start(bf16[192,2048]{1,0:T(8,128)(2,1)} %get-tuple-element.299), channel_id=1, source_target_pairs={{0,64},{1,65},{2,66},{3,67},{4,68},{5,69},{6,70},{7,71},{8,72},{9,... | collective-permute-start | bytes 2359304 | tf_op jit(solution)/shard_map/ppermute | solution.py:725
  429.9 34.1 %collective-permute-start.72 = (bf16[192,2048]{1,0:T(8,128)(2,1)}, bf16[192,2048]{1,0:T(8,128)(2,1)}, u32[]{:S(2)}, u32[]{:S(2)}) collective-permute-start(bf16[192,2048]{1,0:T(8,128)(2,1)} %get-tuple-element.299), channel_id=1, source_target_pairs={{0,96},{1,97},{2,98},{3,99},{4,100},{5,101},{6,102},{7,103},{8,104... | collective-permute-start | bytes 2359304 | tf_op jit(solution)/shard_map/ppermute | solution.py:725
  465.9 78.0 %collective-permute-start.80 = (bf16[4,192,2048]{2,1,0:T(8,128)(2,1)S(1)}, bf16[4,192,2048]{2,1,0:T(8,128)(2,1)}, u32[]{:S(2)}, u32[]{:S(2)}) collective-permute-start(bf16[4,192,2048]{2,1,0:T(8,128)(2,1)S(1)} %pad_maximum_fusion.2.here_ref), channel_id=1, source_target_pairs={{0,8},{1,9},{2,10},{3,11},{4,12},{5,13},{6,14},{7,15},{8,0},{9,1},... | collective-permute-start | bytes 9437192 | tf_op jit(solution)/shard_map/ppermute | solution.py:725
  467.7 20.4 %collective-permute-start.55 = (bf16[128,1536]{1,0:T(8,128)(2,1)S(1)}, bf16[128,1536]{1,0:T(8,128)(2,1)S(1)}, u32[]{:S(2)}, u32[]{:S(2)}) collective-permute-start(bf16[128,1536]{1,0:T(8,128)(2,1)S(1)} %get-tuple-element.279), channel_id=1, source_target_pairs={{0,1},{1,2},{2,3},{3,0},{4,5},{5,6},{6,7},{7,4},{8,9},{9,10},{10,1... | collective-permute-start | bytes 1179656 | tf_op jit(solution)/shard_map/ppermute | solution.py:725
  467.7 22.8 %collective-permute-start.56 = (bf16[128,1536]{1,0:T(8,128)(2,1)S(1)}, bf16[128,1536]{1,0:T(8,128)(2,1)S(1)}, u32[]{:S(2)}, u32[]{:S(2)}) collective-permute-start(bf16[128,1536]{1,0:T(8,128)(2,1)S(1)} %get-tuple-element.278), channel_id=1, source_target_pairs={{0,2},{1,3},{2,0},{3,1},{4,6},{5,7},{6,4},{7,5},{8,10},{9,11},{10,... | collective-permute-start | bytes 1179656 | tf_op jit(solution)/shard_map/ppermute | solution.py:725
  468.4 27.3 %collective-permute-start.57 = (bf16[128,1536]{1,0:T(8,128)(2,1)}, bf16[128,1536]{1,0:T(8,128)(2,1)}, u32[]{:S(2)}, u32[]{:S(2)}) collective-permute-start(bf16[128,1536]{1,0:T(8,128)(2,1)} %get-tuple-element.277), channel_id=1, source_target_pairs={{0,3},{1,0},{2,1},{3,2},{4,7},{5,4},{6,5},{7,6},{8,11},{9,8},{10,9... | collective-permute-start | bytes 1179656 | tf_op jit(solution)/shard_map/ppermute | solution.py:725
  472.0 27.3 %collective-permute-start.73 = (bf16[384,512]{1,0:T(8,128)(2,1)}, bf16[384,512]{1,0:T(8,128)(2,1)}, u32[]{:S(2)}, u32[]{:S(2)}) collective-permute-start(bf16[384,512]{1,0:T(8,128)(2,1)} %get-tuple-element.290), channel_id=1, source_target_pairs={{0,32},{1,33},{2,34},{3,35},{4,36},{5,37},{6,38},{7,39},{8,40},{9,... | collective-permute-start | bytes 1179656 | tf_op jit(solution)/shard_map/ppermute | solution.py:725
  491.3 17.0 %collective-permute-start.75 = (bf16[384,512]{1,0:T(8,128)(2,1)}, bf16[384,512]{1,0:T(8,128)(2,1)}, u32[]{:S(2)}, u32[]{:S(2)}) collective-permute-start(bf16[384,512]{1,0:T(8,128)(2,1)} %get-tuple-element.291), channel_id=1, source_target_pairs={{0,96},{1,97},{2,98},{3,99},{4,100},{5,101},{6,102},{7,103},{8,104... | collective-permute-start | bytes 1179656 | tf_op jit(solution)/shard_map/ppermute | solution.py:725
  517.3 39.7 %collective-permute-start.58 = (bf16[128,3072]{1,0:T(8,128)(2,1)S(1)}, bf16[128,3072]{1,0:T(8,128)(2,1)S(1)}, u32[]{:S(2)}, u32[]{:S(2)}) collective-permute-start(bf16[128,3072]{1,0:T(8,128)(2,1)S(1)} %copy-done.6), channel_id=1, source_target_pairs={{4,8},{5,9},{6,10},{7,11},{8,4},{9,5},{10,6},{11,7},{20,24},{21,25... | collective-permute-start | bytes 2359304 | tf_op jit(solution)/shard_map/ppermute | solution.py:725
  539.5 17.3 %collective-permute-start.79 = (bf16[192,512]{1,0:T(8,128)(2,1)S(1)}, bf16[192,512]{1,0:T(8,128)(2,1)S(1)}, u32[]{:S(2)}, u32[]{:S(2)}) collective-permute-start(bf16[192,512]{1,0:T(8,128)(2,1)S(1)} %add_convert_fusion.16), channel_id=1, source_target_pairs={{0,32},{1,33},{2,34},{3,35},{4,36},{5,37},{6,38},{7,39},{8,40},{9,... | collective-permute-start | bytes 589832 | tf_op jit(solution)/shard_map/ppermute | solution.py:725
  541.2 15.6 %collective-permute-start.81 = (bf16[192,512]{1,0:T(8,128)(2,1)S(1)}, bf16[192,512]{1,0:T(8,128)(2,1)S(1)}, u32[]{:S(2)}, u32[]{:S(2)}) collective-permute-start(bf16[192,512]{1,0:T(8,128)(2,1)S(1)} %add_convert_fusion.16), channel_id=1, source_target_pairs={{0,64},{1,65},{2,66},{3,67},{4,68},{5,69},{6,70},{7,71},{8,72},{9,... | collective-permute-start | bytes 589832 | tf_op jit(solution)/shard_map/ppermute | solution.py:725
  (122 other events, 1082.6 us)

commit v6 on v5

--- a/solution.py
+++ b/solution.py
@@ -28,7 +28,23 @@
 
 
 def sigmoid(v):
-    return 1.0 / (1.0 + jnp.exp(-v))
+    return 0.5 + 0.5 * jnp.tanh(0.5 * v)
+
+
+def dot_exact(left, right, dims=PLAIN, terms=3):
+    parts = []
+    for _ in range(terms):
+        parts.append(right.astype(bf16))
+        right = right - parts[-1].astype(f32)
+    out = dot(left.astype(bf16), jnp.concatenate(parts, axis=1), dims)
+    width = out.shape[1] // terms
+    return sum(out[:, i * width : (i + 1) * width] for i in range(terms))
+
+
+def sum_heads(v, pick):
+    high = v.astype(bf16)
+    low = (v - high.astype(f32)).astype(bf16)
+    return dot(high, pick) + dot(low, pick)
 
 
 def softplus(v):
@@ -74,7 +90,7 @@
     pre = dt + head_ref[0:1, :]
     step = softplus(pre)
     rate = head_ref[1:2, :] * step
-    cum = dot(mask.astype(f32), rate, PLAIN, highest)
+    cum = dot_exact(mask, rate)
     return mask, pre, step, rate, cum
 
 
@@ -396,11 +412,11 @@
     heads = len(col_sums)
     col_sums = jnp.concatenate(col_sums + [jnp.zeros((LANES - heads, length), f32)], axis=0)
     dxs = jnp.transpose(jnp.concatenate(dxs_parts, axis=0)) + tail * pulled
-    pick = pick_ref[...]
-    d_cum = row_sums - jnp.transpose(col_sums) + dot(across, pick, PLAIN, highest)
-    at_last = dot(jnp.broadcast_to(at_last, (8, channels)), pick, PLAIN, highest)[0:1, :]
-    d_rate = dot(mask.astype(f32), d_cum, ROWS, highest) + at_last
-    d_step = d_rate * head_ref[1:2, :] + dot(dxs * xc, pick, PLAIN, highest)
+    pick = pick_ref[...].astype(bf16)
+    d_cum = row_sums - jnp.transpose(col_sums) + sum_heads(across, pick)
+    at_last = sum_heads(jnp.broadcast_to(at_last, (16, channels)), pick)[0:1, :]
+    d_rate = dot_exact(mask, d_cum, ROWS) + at_last
+    d_step = d_rate * head_ref[1:2, :] + sum_heads(dxs * xc, pick)
     d_dt = d_step * sigmoid(pre_dt)
     acch_ref[0:1, :] += jnp.sum(d_dt, axis=0, keepdims=True)
     acch_ref[1:2, :] += jnp.sum(d_rate * rate, axis=0, keepdims=True)
@@ -1216,12 +1232,14 @@
     tiny = [tiny[:, i * tiny_lanes : (i + 1) * tiny_lanes] for i in range(channels // tiny_lanes)]
     tiny = pad_to(jnp.concatenate(tiny, axis=0), width, tiny_lanes)
     tiny = jnp.pad(tiny, ((0, 0), (tiny_at, 0))).astype(bf16)
-    early = sum_beside(halve(sum_far(after(early, dxt0))))
+    early = halve(sum_far(after(early, dxt0)))
     home = fold(mine, send_core(other))
     late = weight_products(place, [(xn0, after(with_bc(dxt0, bc_sum), early, home[0]))])
-    early = collect_x(jnp.concatenate([early, early1], axis=1), (late[0],))
+    early = sum_beside(early)
     tiny = after(tiny, early)
     late = [v + t for v, t in zip(late, cut_x(tiny))]
+    late = sum_x(late)
+
     terms = home[:1] + [send_z(home[k].astype(bf16), k) for k in range(1, NZ)]
     [outputs] = row_call(
         end_kernel,
@@ -1231,9 +1249,10 @@
     )
     outputs_home = trade_places(outputs).astype(f32)
 
-    late = sum_x(late)
+    early = after(collect_x(early), outputs)
     early = early, send_core(early)
-    at1 = 3 * channels + LANES
+    early1 = collect_x(after(early1, early[0]))
+    early1 = early1, send_core(early1)
     g_wz, g_wo, g_wx, narrow1 = write_sums(
         place,
         early,
@@ -1245,9 +1264,9 @@
         ],
     )
     g_wz, g_wo = write_sums(
-        place, early, [(at1, "rows", 1, g_wz, True), (at1 + channels, "blocks", 1, g_wo, True)]
-    )
-    late = collect_x(sum_beside(halve(sum_far(after(late, outputs)))), (g_wz,))
+        place, early1, [(0, "rows", 1, g_wz, True), (channels, "blocks", 1, g_wo, True)]
+    )
+    late = collect_x(sum_beside(halve(sum_far(late))), (g_wz,))
     late = late, send_core(late)
     g_wx, narrow0 = write_sums(
         place, late, [(0, "rows", 0, g_wx, False), (channels, "flat", 0, None, False)]

time: 583 us -> 545 us (0.935)
  waiting for transfers between devices: 173 us -> 136 us
  starting transfers between devices: 138 us -> 150 us
  Pallas kernels: 179 us -> 169 us
  other arithmetic: 45.4 us -> 38.8 us
    ppermute x84 -> x88, waiting for transfers between devices: 173 us -> 136 us  [send(): return lax.ppermute(v, ('dp', 'tensor'), pairs)]
    ppermute x84 -> x88, starting transfers between devices: 138 us -> 150 us  [send(): return lax.ppermute(v, ('dp', 'tensor'), pairs)]
    pallas_call x5, Pallas kernels: 117 us -> 110 us  [span_call(): pl.pallas_call(kernel, grid_spec=pltpu.PrefetchScalarGridSpec(num_scalar_...]
    unnamed x183 -> x151, local copies, waits for them, and re-layouts: 13.3 us -> 14.1 us
  transfers between devices with their start and end apart: 84 -> 88, of which waited for: 31 -> 28; matrix products, arithmetic and copies ran while one was open for 9% -> 9% of each run, Pallas kernels for 23% -> 23%
where the time goes in v6:
time: 545 us; the launch traced here: 534 us
  Pallas kernels  169 us (31%)
  starting transfers between devices  150 us (28%)
  waiting for transfers between devices  136 us (25%)
  other arithmetic  38.8 us (7%)
  local copies, waits for them, and re-layouts  36.8 us (7%)
    ppermute x88, starting transfers between devices, send(): return lax.ppermute(v, ('dp', 'tensor'), pairs)  150 us
    ppermute x88, waiting for transfers between devices, send(): return lax.ppermute(v, ('dp', 'tensor'), pairs)  136 us
    pallas_call x5, Pallas kernels, span_call(): pl.pallas_call(kernel, grid_spec=pltpu.PrefetchScalarGridSpec(num_scalar_...  110 us
    pallas_call x3, Pallas kernels, weight_products(): pl.pallas_call(functools.partial(weight_kernel, len(pairs), split), grid_...  25.9 us
    pallas_call x6, Pallas kernels, row_call(): pl.pallas_call(kernel, grid=(1,), in_specs=[pl.BlockSpec((rows, v.shape[1...  19.2 us
    pallas_call x3, Pallas kernels, write_sums(): pl.pallas_call(functools.partial(write_kernel, plan, len(kept)), grid_spe...  14.7 us
    unnamed x151, local copies, waits for them, and re-layouts  14.1 us
  transfers between devices with their start and end apart: 88, of which 28 were waited for; matrix products, arithmetic and copies ran while one was open for 9% of the time, Pallas kernels for 23%

profile of v6, /device:TPU:1, one launch (start us, length us, event | category | flops | bytes accessed | tf_op | source)
XLA Modules:
  0.0 533.9 jit_solution(15297452430332749582)
XLA Ops:
  9.3 6.2 %collective-permute-start = (bf16[192,1536]{1,0:T(8,128)(2,1)}, bf16[192,1536]{1,0:T(8,128)(2,1)}, u32[]{:S(2)}, u32[]{:S(2)}) collective-permute-start(bf16[192,1536]{1,0:T(8,128)(2,1)} %pad_maximum_fusion.7), channel_id=1, source_target_pairs={{4,8},{5,9},{6,10},{7,11},{8,4},{9,5},{10,6},{11,7},{20,24},{21,25... | collective-permute-start | bytes 1769480 | tf_op jit(solution)/shard_map/ppermute | solution.py:741
  26.2 4.4 collective-permute-start.8
  42.0 8.3 %collective-permute-done.2.refs_2_ = bf16[160,1536]{1,0:T(8,128)(2,1)S(1)} collective-permute-done((bf16[160,1536]{1,0:T(8,128)(2,1)}, bf16[160,1536]{1,0:T(8,128)(2,1)S(1)}, u32[]{:S(2)}, u32[]{:S(2)}) %collective-permute-start.2) | collective-permute-done | bytes 491552 | tf_op jit(solution)/shard_map/ppermute | solution.py:741
  50.2 4.2 collective-permute-done.4.refs_4_
  58.0 4.3 collective-permute-start.9
  64.1 3.6 collective-permute-start.11
  71.0 22.0 %layer_forward.2 = (bf16[1536,1152]{1,0:T(8,128)(2,1)}, bf16[1024,1536]{1,0:T(8,128)(2,1)}, bf16[256,1536]{1,0:T(8,128)(2,1)}, bf16[1024,384]{1,0:T(8,128)(2,1)}...) custom-call(s32[4]{0:T(128)} %pad_add_fusion.2.place_ref, ...), custom_call_target="tpu_custom_call" | custom-call | flops 20000000000 | bytes 26501120 | tf_op jit(solution)/shard_map/layer_forward/pallas_call | solution.py:512
  99.8 2.8 add_convert_fusion.4
  102.7 4.6 collective-permute-start.28
  108.3 3.3 collective-permute-start.15
  112.6 6.8 %collective-permute-done.14.a_ref = bf16[128,1664]{1,0:T(8,128)(2,1)S(1)} collective-permute-done((bf16[128,1664]{1,0:T(8,128)(2,1)S(1)}, bf16[128,1664]{1,0:T(8,128)(2,1)S(1)}, u32[]{:S(2)}, u32[]{:S(2)}) %collective-permute-start.14) | collective-permute-done | bytes 426016 | tf_op jit(solution)/shard_map/ppermute | solution.py:741
  119.4 10.6 %collective-permute-done.15.b_ref = bf16[128,1664]{1,0:T(8,128)(2,1)S(1)} collective-permute-done((bf16[128,1664]{1,0:T(8,128)(2,1)S(1)}, bf16[128,1664]{1,0:T(8,128)(2,1)S(1)}, u32[]{:S(2)}, u32[]{:S(2)}) %collective-permute-start.15) | collective-permute-done | bytes 426016 | tf_op jit(solution)/shard_map/ppermute | solution.py:741
  130.9 3.3 middle_norm.1
  138.4 7.6 %collective-permute-done.18.refs_2_ = bf16[128,1536]{1,0:T(8,128)(2,1)S(1)} collective-permute-done((bf16[128,1536]{1,0:T(8,128)(2,1)}, bf16[128,1536]{1,0:T(8,128)(2,1)S(1)}, u32[]{:S(2)}, u32[]{:S(2)}) %collective-permute-start.18) | collective-permute-done | bytes 393248 | tf_op jit(solution)/shard_map/ppermute | solution.py:741
  147.6 7.4 %collective-permute-start.21 = (bf16[128,1536]{1,0:T(8,128)(2,1)S(1)}, bf16[128,1536]{1,0:T(8,128)(2,1)S(1)}, u32[]{:S(2)}, u32[]{:S(2)}) collective-permute-start(bf16[128,1536]{1,0:T(8,128)(2,1)S(1)} %collective-permute-done.20.refs_4_), channel_id=1, source_target_pairs={{0,8},{1,9},{2,10},{3,11},{4,12},{5,13},{6,14},{7,15},{8,0},{9,1},... | collective-permute-start | bytes 1179656 | tf_op jit(solution)/shard_map/ppermute | solution.py:741
  158.1 25.9 %layer_forward.3 = (bf16[1536,1152]{1,0:T(8,128)(2,1)}, bf16[1024,1536]{1,0:T(8,128)(2,1)}, bf16[256,1536]{1,0:T(8,128)(2,1)}, bf16[1024,384]{1,0:T(8,128)(2,1)}...) custom-call(s32[4]{0:T(128)} %pad_add_fusion.2.place_ref, ...), custom_call_target="tpu_custom_call" | custom-call | flops 20000000000 | bytes 34398208 | tf_op jit(solution)/shard_map/layer_forward/pallas_call | solution.py:512
  184.7 3.3 collective-permute-done.29
  189.6 3.2 collective-permute-start.31
  203.8 27.2 %scan_backward.2 = (bf16[1024,384]{1,0:T(8,128)(2,1)}, bf16[1024,384]{1,0:T(8,128)(2,1)}, bf16[1024,512]{1,0:T(8,128)(2,1)}, bf16[512,256]{1,0:T(8,128)(2,1)}, b...) custom-call(s32[4]{0:T(128)} %pad_add_fusion.2.place_ref, ...), custom_call_target="tpu_custom_call" | custom-call | flops 28000000000 | bytes 21512192 | tf_op jit(solution)/shard_map/scan_backward/pallas_call | solution.py:512
  233.9 8.3 %weight_products.3 = bf16[1536,768]{1,0:T(8,128)(2,1)} custom-call(s32[4]{0:T(128)} %pad_add_fusion.2.place_ref, bf16[1024,1536]{1,0:T(8,128)(2,1)} %get-tuple-element.143.refs_4_.refs_0_.refs_2_, bf16[1024,384]{1,0:T(8,128)(2,1)} %get-tuple-element.155.refs_1_, bf16[1024,384]{1,0:T(8,128)(2,1)} %get-tuple-element.156.refs_2_, ...), custom_call_target="tpu_custom_call" | custom-call | flops 2415919104 | bytes 8000000 | tf_op jit(solution)/shard_map/weight_products/pallas_call | solution.py:708
  242.2 4.2 collective-permute-start.49
  251.0 17.9 %collective-permute-done.39.a_ref = bf16[128,1792]{1,0:T(8,128)(2,1)S(1)} collective-permute-done((bf16[128,1792]{1,0:T(8,128)(2,1)S(1)}, bf16[128,1792]{1,0:T(8,128)(2,1)S(1)}, u32[]{:S(2)}, u32[]{:S(2)}) %collective-permute-start.39) | collective-permute-done | bytes 458784 | tf_op jit(solution)/shard_map/ppermute | solution.py:741
  271.7 3.9 between_layers.1
  288.5 4.9 collective-permute-start.44
  293.4 6.5 %collective-permute-start.46 = (bf16[128,1664]{1,0:T(8,128)(2,1)}, bf16[128,1664]{1,0:T(8,128)(2,1)S(1)}, u32[]{:S(2)}, u32[]{:S(2)}) collective-permute-start(bf16[128,1664]{1,0:T(8,128)(2,1)} %collective-permute-done.45.refs_4_), channel_id=1, source_target_pairs={{0,8},{1,9},{2,10},{3,11},{4,12},{5,13},{6,14},{7,15},{8,0},{9,1},... | collective-permute-start | bytes 1277960 | tf_op jit(solution)/shard_map/ppermute | solution.py:741
  308.8 8.4 %gate_backward.1 = (bf16[1024,1536]{1,0:T(8,128)(2,1)}, bf16[1024,384]{1,0:T(8,128)(2,1)}, f32[1024,384]{1,0:T(8,128)}, bf16[1024,384]{1,0:T(8,128)(2,1)}, f32[8,384]{1,0:T(8,128)}) custom-call(s32[4]{0:T(128)} %pad_add_fusion.2.place_ref, bf16[128,1664]{1,0:T(8,128)(2,1)} %get-tuple-element.162.refs_0_, bf16[128,1664]{1,0:T(8,128)(2,1)} %collective-permute-done.42.refs_1_, ...), custom_call_target="tpu_custom_call" | custom-call | flops 6000000000 | bytes 14835712 | tf_op jit(solution)/shard_map/gate_backward/pallas_call | solution.py:512
  319.6 11.2 %weight_products.4 = (bf16[384,1280]{1,0:T(8,128)(2,1)}, bf16[384,1280]{1,0:T(8,128)(2,1)}, bf16[384,1280]{1,0:T(8,128)(2,1)}, bf16[384,1280]{1,0:T(8,128)(2,1)}) custom-call(s32[4]{0:T(128)} %pad_add_fusion.2.place_ref, bf16[1024,1536]{1,0:T(8,128)(2,1)} %get-tuple-element.169.refs_0_.refs_2_, bf16[1024,384]{1,0:T(8,128)(2,1)} %get-tuple-element.170.refs_1_, ...), custom_call_target="tpu_custom_call" | custom-call | flops 4026531840 | bytes 8000000 | tf_op jit(solution)/shard_map/weight_products/pallas_call | solution.py:708
  335.8 26.1 %scan_backward.3 = (bf16[1024,512]{1,0:T(8,128)(2,1)}, bf16[512,256]{1,0:T(8,128)(2,1)}, bf16[512,256]{1,0:T(8,128)(2,1)}, bf16[512,1536]{1,0:T(8,128)(2,1)}, bf...) custom-call(s32[4]{0:T(128)} %pad_add_fusion.2.place_ref, ...), custom_call_target="tpu_custom_call" | custom-call | flops 28000000000 | bytes 19120128 | tf_op jit(solution)/shard_map/scan_backward/pallas_call | solution.py:512
  364.1 13.3 %collective-permute-done.61 = bf16[384,1280]{1,0:T(8,128)(2,1)S(1)} collective-permute-done((bf16[384,1280]{1,0:T(8,128)(2,1)}, bf16[384,1280]{1,0:T(8,128)(2,1)S(1)}, u32[]{:S(2)}, u32[]{:S(2)}) %collective-permute-start.61) | collective-permute-done | bytes 983072 | tf_op jit(solution)/shard_map/ppermute | solution.py:741
  383.4 2.8 last_output.1.hidden_ref
  390.6 3.0 collective-permute-start.66
  398.1 5.6 %collective-permute-done.66 = bf16[384,1280]{1,0:T(8,128)(2,1)} collective-permute-done((bf16[384,1280]{1,0:T(8,128)(2,1)S(1)}, bf16[384,1280]{1,0:T(8,128)(2,1)}, u32[]{:S(2)}, u32[]{:S(2)}) %collective-permute-start.66) | collective-permute-done | bytes 983072 | tf_op jit(solution)/shard_map/ppermute | solution.py:741
  407.7 4.6 collective-permute-done.67
  418.3 6.8 %collective-permute-done.68 = bf16[192,1280]{1,0:T(8,128)(2,1)S(1)} collective-permute-done((bf16[192,1280]{1,0:T(8,128)(2,1)S(1)}, bf16[192,1280]{1,0:T(8,128)(2,1)S(1)}, u32[]{:S(2)}, u32[]{:S(2)}) %collective-permute-start.68) | collective-permute-done | bytes 491552 | tf_op jit(solution)/shard_map/ppermute | solution.py:741
  430.1 3.3 collective-permute-done.56.b_ref
  435.5 3.5 outputs.1
  439.0 6.4 %weight_products.5 = (bf16[384,512]{1,0:T(8,128)(2,1)}, bf16[384,512]{1,0:T(8,128)(2,1)}, bf16[384,512]{1,0:T(8,128)(2,1)}, bf16[384,512]{1,0:T(8,128)(2,1)}) custom-call(s32[4]{0:T(128)} %pad_add_fusion.2.place_ref, bf16[1024,1536]{1,0:T(8,128)(2,1)} %get-tuple-element.169.refs_0_.refs_2_, bf16[1024,512]{1,0:T(8,128)(2,1)} %pad_add_fusion.refs_1_), custom_call_target="tpu_custom_call" | custom-call | flops 1610612736 | bytes 8000000 | tf_op jit(solution)/shard_map/weight_products/pallas_call | solution.py:708
  451.5 4.6 collective-permute-start.84
  458.3 5.8 %collective-permute-done.70 = bf16[384,512]{1,0:T(8,128)(2,1)S(1)} collective-permute-done((bf16[384,512]{1,0:T(8,128)(2,1)S(1)}, bf16[384,512]{1,0:T(8,128)(2,1)S(1)}, u32[]{:S(2)}, u32[]{:S(2)}) %collective-permute-start.70) | collective-permute-done | bytes 393248 | tf_op jit(solution)/shard_map/ppermute | solution.py:741
  464.1 4.6 collective-permute-done.71
  471.3 3.7 collective-permute-done.80
  476.6 5.3 collective-permute-start.83
  483.3 5.0 collective-permute-start.58
  488.9 13.7 %collective-permute-done.74 = bf16[192,512]{1,0:T(8,128)(2,1)S(1)} collective-permute-done((bf16[192,512]{1,0:T(8,128)(2,1)S(1)}, bf16[192,512]{1,0:T(8,128)(2,1)S(1)}, u32[]{:S(2)}, u32[]{:S(2)}) %collective-permute-start.74) | collective-permute-done | bytes 196640 | tf_op jit(solution)/shard_map/ppermute | solution.py:741
  506.8 6.2 %write_sums.3 = (f32[2,4,2,192,384]{4,3,2,1,0:T(8,128)}, f32[2,384,1536]{2,1,0:T(8,128)}, f32[2,4,2,192,384]{4,3,2,1,0:T(8,128)}, f32[1,4,2,192,128]{4,3,2,1,0:T(8,128)}) custom-call(s32[4]{0:T(128)} %pad_add_fusion.2.place_ref, bf16[4,192,1280]{2,1,0:T(8,128)(2,1)} %copy-done.1, bf16[4,192,1280]{2,1,0:T(8,128)(2,1)} %copy-done.6), custom_call_target="tpu_custom_call" | custom-call | tf_op jit(solution)/shard_map/write_sums/pallas_call | solution.py:941
  514.1 4.7 write_sums.4
  522.1 3.8 write_sums.5
  526.0 3.6 small_gradients.1
  (390 shorter events, 170.7 us)
Async XLA Ops:
  26.2 44.8 %collective-permute-start.8 = (bf16[1536,1152]{1,0:T(8,128)(2,1)}, bf16[1536,1152]{1,0:T(8,128)(2,1)}, u32[]{:S(2)}, u32[]{:S(2)}) collective-permute-start(bf16[1536,1152]{1,0:T(8,128)(2,1)} %pad_maximum_fusion.refs_8_), channel_id=1, source_target_pairs={{4,8},{5,9},{6,10},{7,11},{8,4},{9,5},{10,6},{11,7},{20,24},{21,25... | collective-permute-start | bytes 10616840 | tf_op jit(solution)/shard_map/ppermute | solution.py:741
  34.7 15.5 %collective-permute-start.2 = (bf16[160,1536]{1,0:T(8,128)(2,1)}, bf16[160,1536]{1,0:T(8,128)(2,1)S(1)}, u32[]{:S(2)}, u32[]{:S(2)}) collective-permute-start(bf16[160,1536]{1,0:T(8,128)(2,1)} %first_norm.1.refs_0_), channel_id=1, source_target_pairs={{0,1},{1,2},{2,3},{3,0},{4,5},{5,6},{6,7},{7,4},{8,9},{9,10},{10,1... | collective-permute-start | bytes 1474568 | tf_op jit(solution)/shard_map/ppermute | solution.py:741
  36.4 18.1 %collective-permute-start.4 = (bf16[160,1536]{1,0:T(8,128)(2,1)}, bf16[160,1536]{1,0:T(8,128)(2,1)S(1)}, u32[]{:S(2)}, u32[]{:S(2)}) collective-permute-start(bf16[160,1536]{1,0:T(8,128)(2,1)} %first_norm.1.refs_0_), channel_id=1, source_target_pairs={{0,3},{1,0},{2,1},{3,2},{4,7},{5,4},{6,5},{7,6},{8,11},{9,8},{10,9... | collective-permute-start | bytes 1474568 | tf_op jit(solution)/shard_map/ppermute | solution.py:741
  38.5 17.5 %collective-permute-start.6 = (bf16[160,1536]{1,0:T(8,128)(2,1)}, bf16[160,1536]{1,0:T(8,128)(2,1)S(1)}, u32[]{:S(2)}, u32[]{:S(2)}) collective-permute-start(bf16[160,1536]{1,0:T(8,128)(2,1)} %first_norm.1.refs_0_), channel_id=1, source_target_pairs={{0,2},{1,3},{2,0},{3,1},{4,6},{5,7},{6,4},{7,5},{8,10},{9,11},{10,... | collective-permute-start | bytes 1474568 | tf_op jit(solution)/shard_map/ppermute | solution.py:741
  39.8 18.2 %collective-permute-start.1 = (bf16[160,1536]{1,0:T(8,128)(2,1)}, bf16[160,1536]{1,0:T(8,128)(2,1)S(1)}, u32[]{:S(2)}, u32[]{:S(2)}) collective-permute-start(bf16[160,1536]{1,0:T(8,128)(2,1)} %first_norm.1.refs_0_), channel_id=1, source_target_pairs={{0,8},{1,9},{2,10},{3,11},{4,12},{5,13},{6,14},{7,15},{8,0},{9,1},... | collective-permute-start | bytes 1474568 | tf_op jit(solution)/shard_map/ppermute | solution.py:741
  58.0 35.0 %collective-permute-start.9 = (bf16[160,1536]{1,0:T(8,128)(2,1)S(1)}, bf16[160,1536]{1,0:T(8,128)(2,1)S(1)}, u32[]{:S(2)}, u32[]{:S(2)}) collective-permute-start(bf16[160,1536]{1,0:T(8,128)(2,1)S(1)} %pad_maximum_fusion.8), channel_id=1, source_target_pairs={{4,8},{5,9},{6,10},{7,11},{8,4},{9,5},{10,6},{11,7},{20,24},{21,25... | collective-permute-start | bytes 1474568 | tf_op jit(solution)/shard_map/ppermute | solution.py:741
  62.3 31.5 %collective-permute-start.10 = (bf16[160,1536]{1,0:T(8,128)(2,1)S(1)}, bf16[160,1536]{1,0:T(8,128)(2,1)S(1)}, u32[]{:S(2)}, u32[]{:S(2)}) collective-permute-start(bf16[160,1536]{1,0:T(8,128)(2,1)S(1)} %pad_maximum_fusion.8), channel_id=1, source_target_pairs={{0,1},{1,2},{2,3},{3,0},{4,9},{5,10},{6,11},{7,8},{8,5},{9,6},{10,... | collective-permute-start | bytes 1474568 | tf_op jit(solution)/shard_map/ppermute | solution.py:741
  64.1 29.7 %collective-permute-start.11 = (bf16[160,1536]{1,0:T(8,128)(2,1)S(1)}, bf16[160,1536]{1,0:T(8,128)(2,1)S(1)}, u32[]{:S(2)}, u32[]{:S(2)}) collective-permute-start(bf16[160,1536]{1,0:T(8,128)(2,1)S(1)} %pad_maximum_fusion.8), channel_id=1, source_target_pairs={{0,3},{1,0},{2,1},{3,2},{4,11},{5,8},{6,9},{7,10},{8,7},{9,4},{10,... | collective-permute-start | bytes 1474568 | tf_op jit(solution)/shard_map/ppermute | solution.py:741
  67.7 27.3 %collective-permute-start.12 = (bf16[160,1536]{1,0:T(8,128)(2,1)S(1)}, bf16[160,1536]{1,0:T(8,128)(2,1)S(1)}, u32[]{:S(2)}, u32[]{:S(2)}) collective-permute-start(bf16[160,1536]{1,0:T(8,128)(2,1)S(1)} %pad_maximum_fusion.8), channel_id=1, source_target_pairs={{0,2},{1,3},{2,0},{3,1},{4,10},{5,11},{6,8},{7,9},{8,6},{9,7},{10,... | collective-permute-start | bytes 1474568 | tf_op jit(solution)/shard_map/ppermute | solution.py:741
  102.7 54.7 %collective-permute-start.28 = (bf16[1536,1152]{1,0:T(8,128)(2,1)S(1)}, bf16[1536,1152]{1,0:T(8,128)(2,1)}, u32[]{:S(2)}, u32[]{:S(2)}) collective-permute-start(bf16[1536,1152]{1,0:T(8,128)(2,1)S(1)} %pad_maximum_fusion.1.refs_16_), channel_id=1, source_target_pairs={{4,8},{5,9},{6,10},{7,11},{8,4},{9,5},{10,6},{11,7},{20,24},{21,25... | collective-permute-start | bytes 10616840 | tf_op jit(solution)/shard_map/ppermute | solution.py:741
  108.3 21.6 %collective-permute-start.15 = (bf16[128,1664]{1,0:T(8,128)(2,1)S(1)}, bf16[128,1664]{1,0:T(8,128)(2,1)S(1)}, u32[]{:S(2)}, u32[]{:S(2)}) collective-permute-start(bf16[128,1664]{1,0:T(8,128)(2,1)S(1)} %get-tuple-element.270), channel_id=1, source_target_pairs={{0,2},{1,3},{2,0},{3,1},{4,6},{5,7},{6,4},{7,5},{8,10},{9,11},{10,... | collective-permute-start | bytes 1277960 | tf_op jit(solution)/shard_map/ppermute | solution.py:741
  111.6 18.3 %collective-permute-start.16 = (bf16[128,1664]{1,0:T(8,128)(2,1)S(1)}, bf16[128,1664]{1,0:T(8,128)(2,1)S(1)}, u32[]{:S(2)}, u32[]{:S(2)}) collective-permute-start(bf16[128,1664]{1,0:T(8,128)(2,1)S(1)} %get-tuple-element.269), channel_id=1, source_target_pairs={{0,3},{1,0},{2,1},{3,2},{4,7},{5,4},{6,5},{7,6},{8,11},{9,8},{10,9... | collective-permute-start | bytes 1277960 | tf_op jit(solution)/shard_map/ppermute | solution.py:741
  112.3 21.8 %collective-permute-start.24 = (bf16[160,1536]{1,0:T(8,128)(2,1)S(1)}, bf16[160,1536]{1,0:T(8,128)(2,1)S(1)}, u32[]{:S(2)}, u32[]{:S(2)}) collective-permute-start(bf16[160,1536]{1,0:T(8,128)(2,1)S(1)} %copy-done.7), channel_id=1, source_target_pairs={{0,8},{1,9},{2,10},{3,11},{4,12},{5,13},{6,14},{7,15},{8,0},{9,1},... | collective-permute-start | bytes 1474568 | tf_op jit(solution)/shard_map/ppermute | solution.py:741
  119.3 15.9 %collective-permute-start.25 = (bf16[160,1536]{1,0:T(8,128)(2,1)S(1)}, bf16[160,1536]{1,0:T(8,128)(2,1)S(1)}, u32[]{:S(2)}, u32[]{:S(2)}) collective-permute-start(bf16[160,1536]{1,0:T(8,128)(2,1)S(1)} %copy-done.47), channel_id=1, source_target_pairs={{0,8},{1,9},{2,10},{3,11},{4,12},{5,13},{6,14},{7,15},{8,0},{9,1},... | collective-permute-start | bytes 1474568 | tf_op jit(solution)/shard_map/ppermute | solution.py:741
  136.9 18.1 %collective-permute-start.22 = (bf16[128,1536]{1,0:T(8,128)(2,1)}, bf16[128,1536]{1,0:T(8,128)(2,1)S(1)}, u32[]{:S(2)}, u32[]{:S(2)}) collective-permute-start(bf16[128,1536]{1,0:T(8,128)(2,1)} %get-tuple-element.130.refs_0_), channel_id=1, source_target_pairs={{0,2},{1,3},{2,0},{3,1},{4,6},{5,7},{6,4},{7,5},{8,10},{9,11},{10,... | collective-permute-start | bytes 1179656 | tf_op jit(solution)/shard_map/ppermute | solution.py:741
  137.6 19.2 %collective-permute-start.17 = (bf16[128,1536]{1,0:T(8,128)(2,1)}, bf16[128,1536]{1,0:T(8,128)(2,1)S(1)}, u32[]{:S(2)}, u32[]{:S(2)}) collective-permute-start(bf16[128,1536]{1,0:T(8,128)(2,1)} %get-tuple-element.130.refs_0_), channel_id=1, source_target_pairs={{0,8},{1,9},{2,10},{3,11},{4,12},{5,13},{6,14},{7,15},{8,0},{9,1},... | collective-permute-start | bytes 1179656 | tf_op jit(solution)/shard_map/ppermute | solution.py:741
  197.8 33.3 %collective-permute-start.34 = (bf16[128,1664]{1,0:T(8,128)(2,1)S(1)}, bf16[128,1664]{1,0:T(8,128)(2,1)S(1)}, u32[]{:S(2)}, u32[]{:S(2)}) collective-permute-start(bf16[128,1664]{1,0:T(8,128)(2,1)S(1)} %get-tuple-element.268), channel_id=1, source_target_pairs={{0,1},{1,2},{2,3},{3,0},{4,5},{5,6},{6,7},{7,4},{8,9},{9,10},{10,1... | collective-permute-start | bytes 1277960 | tf_op jit(solution)/shard_map/ppermute | solution.py:741
  197.9 33.2 %collective-permute-start.35 = (bf16[128,1664]{1,0:T(8,128)(2,1)S(1)}, bf16[128,1664]{1,0:T(8,128)(2,1)S(1)}, u32[]{:S(2)}, u32[]{:S(2)}) collective-permute-start(bf16[128,1664]{1,0:T(8,128)(2,1)S(1)} %get-tuple-element.267), channel_id=1, source_target_pairs={{0,2},{1,3},{2,0},{3,1},{4,6},{5,7},{6,4},{7,5},{8,10},{9,11},{10,... | collective-permute-start | bytes 1277960 | tf_op jit(solution)/shard_map/ppermute | solution.py:741
  200.6 30.5 %collective-permute-start.36 = (bf16[128,1664]{1,0:T(8,128)(2,1)S(1)}, bf16[128,1664]{1,0:T(8,128)(2,1)S(1)}, u32[]{:S(2)}, u32[]{:S(2)}) collective-permute-start(bf16[128,1664]{1,0:T(8,128)(2,1)S(1)} %get-tuple-element.266), channel_id=1, source_target_pairs={{0,3},{1,0},{2,1},{3,2},{4,7},{5,4},{6,5},{7,6},{8,11},{9,8},{10,9... | collective-permute-start | bytes 1277960 | tf_op jit(solution)/shard_map/ppermute | solution.py:741
  231.1 15.3 %collective-permute-start.37 = (bf16[512,1536]{1,0:T(8,128)(2,1)}, bf16[512,1536]{1,0:T(8,128)(2,1)S(1)}, u32[]{:S(2)}, u32[]{:S(2)}) collective-permute-start(bf16[512,1536]{1,0:T(8,128)(2,1)} %get-tuple-element.152), channel_id=1, source_target_pairs={{0,8},{1,9},{2,10},{3,11},{4,12},{5,13},{6,14},{7,15},{8,0},{9,1},... | collective-permute-start | bytes 4718600 | tf_op jit(solution)/shard_map/ppermute | solution.py:741
  242.2 33.5 %collective-permute-start.49 = (bf16[1536,768]{1,0:T(8,128)(2,1)}, bf16[1536,768]{1,0:T(8,128)(2,1)S(1)}, u32[]{:S(2)}, u32[]{:S(2)}) collective-permute-start(bf16[1536,768]{1,0:T(8,128)(2,1)} %weight_products.3), channel_id=1, source_target_pairs={{4,0},{5,1},{6,2},{7,3},{8,12},{9,13},{10,14},{11,15},{20,16},{21,... | collective-permute-start | bytes 7077896 | tf_op jit(solution)/shard_map/ppermute | solution.py:741
  246.8 22.1 %collective-permute-start.39 = (bf16[128,1792]{1,0:T(8,128)(2,1)S(1)}, bf16[128,1792]{1,0:T(8,128)(2,1)S(1)}, u32[]{:S(2)}, u32[]{:S(2)}) collective-permute-start(bf16[128,1792]{1,0:T(8,128)(2,1)S(1)} %pad_maximum_fusion.9), channel_id=1, source_target_pairs={{0,1},{1,2},{2,3},{3,0},{4,5},{5,6},{6,7},{7,4},{8,9},{9,10},{10,1... | collective-permute-start | bytes 1376264 | tf_op jit(solution)/shard_map/ppermute | solution.py:741
  247.3 21.6 %collective-permute-start.40 = (bf16[128,1792]{1,0:T(8,128)(2,1)S(1)}, bf16[128,1792]{1,0:T(8,128)(2,1)S(1)}, u32[]{:S(2)}, u32[]{:S(2)}) collective-permute-start(bf16[128,1792]{1,0:T(8,128)(2,1)S(1)} %pad_maximum_fusion.5), channel_id=1, source_target_pairs={{0,2},{1,3},{2,0},{3,1},{4,6},{5,7},{6,4},{7,5},{8,10},{9,11},{10,... | collective-permute-start | bytes 1376264 | tf_op jit(solution)/shard_map/ppermute | solution.py:741
  248.9 21.1 %collective-permute-start.41 = (bf16[128,1792]{1,0:T(8,128)(2,1)S(1)}, bf16[128,1792]{1,0:T(8,128)(2,1)S(1)}, u32[]{:S(2)}, u32[]{:S(2)}) collective-permute-start(bf16[128,1792]{1,0:T(8,128)(2,1)S(1)} %pad_maximum_fusion.10), channel_id=1, source_target_pairs={{0,3},{1,0},{2,1},{3,2},{4,7},{5,4},{6,5},{7,6},{8,11},{9,8},{10,9... | collective-permute-start | bytes 1376264 | tf_op jit(solution)/shard_map/ppermute | solution.py:741
  276.4 25.1 %collective-permute-start.50 = (bf16[768,768]{1,0:T(8,128)(2,1)S(1)}, bf16[768,768]{1,0:T(8,128)(2,1)}, u32[]{:S(2)}, u32[]{:S(2)}) collective-permute-start(bf16[768,768]{1,0:T(8,128)(2,1)S(1)} %slice.220), channel_id=1, source_target_pairs={{0,8},{1,9},{2,10},{3,11},{12,4},{13,5},{14,6},{15,7},{16,24},{17,... | collective-permute-start | bytes 3538952 | tf_op jit(solution)/shard_map/ppermute | solution.py:741
  280.4 19.5 %collective-permute-start.47 = (bf16[128,1664]{1,0:T(8,128)(2,1)}, bf16[128,1664]{1,0:T(8,128)(2,1)}, u32[]{:S(2)}, u32[]{:S(2)}) collective-permute-start(bf16[128,1664]{1,0:T(8,128)(2,1)} %get-tuple-element.162.refs_0_), channel_id=1, source_target_pairs={{0,2},{1,3},{2,0},{3,1},{4,6},{5,7},{6,4},{7,5},{8,10},{9,11},{10,... | collective-permute-start | bytes 1277960 | tf_op jit(solution)/shard_map/ppermute | solution.py:741
  281.3 23.0 %collective-permute-start.42 = (bf16[128,1664]{1,0:T(8,128)(2,1)}, bf16[128,1664]{1,0:T(8,128)(2,1)}, u32[]{:S(2)}, u32[]{:S(2)}) collective-permute-start(bf16[128,1664]{1,0:T(8,128)(2,1)} %get-tuple-element.162.refs_0_), channel_id=1, source_target_pairs={{0,8},{1,9},{2,10},{3,11},{4,12},{5,13},{6,14},{7,15},{8,0},{9,1},... | collective-permute-start | bytes 1277960 | tf_op jit(solution)/shard_map/ppermute | solution.py:741
  288.5 18.2 %collective-permute-start.44 = (bf16[128,1664]{1,0:T(8,128)(2,1)}, bf16[128,1664]{1,0:T(8,128)(2,1)S(1)}, u32[]{:S(2)}, u32[]{:S(2)}) collective-permute-start(bf16[128,1664]{1,0:T(8,128)(2,1)} %collective-permute-done.43.refs_2_), channel_id=1, source_target_pairs={{0,8},{1,9},{2,10},{3,11},{4,12},{5,13},{6,14},{7,15},{8,0},{9,1},... | collective-permute-start | bytes 1277960 | tf_op jit(solution)/shard_map/ppermute | solution.py:741
  304.2 15.2 %collective-permute-start.52 = (bf16[192,768]{1,0:T(8,128)(2,1)S(1)}, bf16[192,768]{1,0:T(8,128)(2,1)S(1)}, u32[]{:S(2)}, u32[]{:S(2)}) collective-permute-start(bf16[192,768]{1,0:T(8,128)(2,1)S(1)} %get-tuple-element.293), channel_id=1, source_target_pairs={{0,64},{1,65},{2,66},{3,67},{4,68},{5,69},{6,70},{7,71},{8,72},{9,... | collective-permute-start | bytes 884744 | tf_op jit(solution)/shard_map/ppermute | solution.py:741
  330.9 33.2 %collective-permute-start.60 = (bf16[384,1280]{1,0:T(8,128)(2,1)}, bf16[384,1280]{1,0:T(8,128)(2,1)S(1)}, u32[]{:S(2)}, u32[]{:S(2)}) collective-permute-start(bf16[384,1280]{1,0:T(8,128)(2,1)} %get-tuple-element.176), channel_id=1, source_target_pairs={{0,32},{1,33},{2,34},{3,35},{4,36},{5,37},{6,38},{7,39},{8,40},{9,... | collective-permute-start | bytes 2949128 | tf_op jit(solution)/shard_map/ppermute | solution.py:741
  332.6 44.8 %collective-permute-start.61 = (bf16[384,1280]{1,0:T(8,128)(2,1)}, bf16[384,1280]{1,0:T(8,128)(2,1)S(1)}, u32[]{:S(2)}, u32[]{:S(2)}) collective-permute-start(bf16[384,1280]{1,0:T(8,128)(2,1)} %get-tuple-element.177), channel_id=1, source_target_pairs={{0,64},{1,65},{2,66},{3,67},{4,68},{5,69},{6,70},{7,71},{8,72},{9,... | collective-permute-start | bytes 2949128 | tf_op jit(solution)/shard_map/ppermute | solution.py:741
  334.6 42.8 %collective-permute-start.62 = (bf16[384,1280]{1,0:T(8,128)(2,1)}, bf16[384,1280]{1,0:T(8,128)(2,1)S(1)}, u32[]{:S(2)}, u32[]{:S(2)}) collective-permute-start(bf16[384,1280]{1,0:T(8,128)(2,1)} %get-tuple-element.178), channel_id=1, source_target_pairs={{0,96},{1,97},{2,98},{3,99},{4,100},{5,101},{6,102},{7,103},{8,104... | collective-permute-start | bytes 2949128 | tf_op jit(solution)/shard_map/ppermute | solution.py:741
  386.2 26.7 %collective-permute-start.54 = (bf16[512,1536]{1,0:T(8,128)(2,1)}, bf16[512,1536]{1,0:T(8,128)(2,1)S(1)}, u32[]{:S(2)}, u32[]{:S(2)}) collective-permute-start(bf16[512,1536]{1,0:T(8,128)(2,1)} %get-tuple-element.186), channel_id=1, source_target_pairs={{0,8},{1,9},{2,10},{3,11},{4,12},{5,13},{6,14},{7,15},{8,0},{9,1},... | collective-permute-start | bytes 4718600 | tf_op jit(solution)/shard_map/ppermute | solution.py:741
  415.9 17.5 %collective-permute-start.56 = (bf16[128,1536]{1,0:T(8,128)(2,1)S(1)}, bf16[128,1536]{1,0:T(8,128)(2,1)S(1)}, u32[]{:S(2)}, u32[]{:S(2)}) collective-permute-start(bf16[128,1536]{1,0:T(8,128)(2,1)S(1)} %get-tuple-element.274), channel_id=1, source_target_pairs={{0,2},{1,3},{2,0},{3,1},{4,6},{5,7},{6,4},{7,5},{8,10},{9,11},{10,... | collective-permute-start | bytes 1179656 | tf_op jit(solution)/shard_map/ppermute | solution.py:741
  416.1 18.6 %collective-permute-start.57 = (bf16[128,1536]{1,0:T(8,128)(2,1)S(1)}, bf16[128,1536]{1,0:T(8,128)(2,1)S(1)}, u32[]{:S(2)}, u32[]{:S(2)}) collective-permute-start(bf16[128,1536]{1,0:T(8,128)(2,1)S(1)} %get-tuple-element.273), channel_id=1, source_target_pairs={{0,3},{1,0},{2,1},{3,2},{4,7},{5,4},{6,5},{7,6},{8,11},{9,8},{10,9... | collective-permute-start | bytes 1179656 | tf_op jit(solution)/shard_map/ppermute | solution.py:741
  425.2 22.9 %collective-permute-start.77 = (bf16[192,1280]{1,0:T(8,128)(2,1)S(1)}, bf16[192,1280]{1,0:T(8,128)(2,1)S(1)}, u32[]{:S(2)}, u32[]{:S(2)}) collective-permute-start(bf16[192,1280]{1,0:T(8,128)(2,1)S(1)} %add_convert_fusion.3), channel_id=1, source_target_pairs={{0,32},{1,33},{2,34},{3,35},{4,36},{5,37},{6,38},{7,39},{8,40},{9,... | collective-permute-start | bytes 1474568 | tf_op jit(solution)/shard_map/ppermute | solution.py:741
  426.7 23.4 %collective-permute-start.78 = (bf16[192,1280]{1,0:T(8,128)(2,1)S(1)}, bf16[192,1280]{1,0:T(8,128)(2,1)S(1)}, u32[]{:S(2)}, u32[]{:S(2)}) collective-permute-start(bf16[192,1280]{1,0:T(8,128)(2,1)S(1)} %add_convert_fusion.3), channel_id=1, source_target_pairs={{0,64},{1,65},{2,66},{3,67},{4,68},{5,69},{6,70},{7,71},{8,72},{9,... | collective-permute-start | bytes 1474568 | tf_op jit(solution)/shard_map/ppermute | solution.py:741
  428.6 22.7 %collective-permute-start.79 = (bf16[192,1280]{1,0:T(8,128)(2,1)S(1)}, bf16[192,1280]{1,0:T(8,128)(2,1)S(1)}, u32[]{:S(2)}, u32[]{:S(2)}) collective-permute-start(bf16[192,1280]{1,0:T(8,128)(2,1)S(1)} %add_convert_fusion.3), channel_id=1, source_target_pairs={{0,96},{1,97},{2,98},{3,99},{4,100},{5,101},{6,102},{7,103},{8,104... | collective-permute-start | bytes 1474568 | tf_op jit(solution)/shard_map/ppermute | solution.py:741
  433.4 22.7 %collective-permute-start.76 = (bf16[192,768]{1,0:T(8,128)(2,1)S(1)}, bf16[192,768]{1,0:T(8,128)(2,1)S(1)}, u32[]{:S(2)}, u32[]{:S(2)}) collective-permute-start(bf16[192,768]{1,0:T(8,128)(2,1)S(1)} %add_convert_fusion.15), channel_id=1, source_target_pairs={{0,16},{1,17},{2,18},{3,19},{4,20},{5,21},{6,22},{7,23},{8,24},{9,... | collective-permute-start | bytes 884744 | tf_op jit(solution)/shard_map/ppermute | solution.py:741
  448.2 15.9 %collective-permute-start.70 = (bf16[384,512]{1,0:T(8,128)(2,1)S(1)}, bf16[384,512]{1,0:T(8,128)(2,1)S(1)}, u32[]{:S(2)}, u32[]{:S(2)}) collective-permute-start(bf16[384,512]{1,0:T(8,128)(2,1)S(1)} %get-tuple-element.288), channel_id=1, source_target_pairs={{0,64},{1,65},{2,66},{3,67},{4,68},{5,69},{6,70},{7,71},{8,72},{9,... | collective-permute-start | bytes 1179656 | tf_op jit(solution)/shard_map/ppermute | solution.py:741
  450.1 18.6 %collective-permute-start.71 = (bf16[384,512]{1,0:T(8,128)(2,1)S(1)}, bf16[384,512]{1,0:T(8,128)(2,1)S(1)}, u32[]{:S(2)}, u32[]{:S(2)}) collective-permute-start(bf16[384,512]{1,0:T(8,128)(2,1)S(1)} %get-tuple-element.287), channel_id=1, source_target_pairs={{0,96},{1,97},{2,98},{3,99},{4,100},{5,101},{6,102},{7,103},{8,104... | collective-permute-start | bytes 1179656 | tf_op jit(solution)/shard_map/ppermute | solution.py:741
  451.5 54.0 %collective-permute-start.84 = (bf16[4,192,1280]{2,1,0:T(8,128)(2,1)S(1)}, bf16[4,192,1280]{2,1,0:T(8,128)(2,1)S(1)}, u32[]{:S(2)}, u32[]{:S(2)}) collective-permute-start(bf16[4,192,1280]{2,1,0:T(8,128)(2,1)S(1)} %pad_maximum_fusion.2.here_ref), channel_id=1, source_target_pairs={{0,8},{1,9},{2,10},{3,11},{4,12},{5,13},{6,14},{7,15},{8,0},{9,1},... | collective-permute-start | bytes 5898248 | tf_op jit(solution)/shard_map/ppermute | solution.py:741
  456.2 18.9 %collective-permute-start.80 = (bf16[192,768]{1,0:T(8,128)(2,1)S(1)}, bf16[192,768]{1,0:T(8,128)(2,1)S(1)}, u32[]{:S(2)}, u32[]{:S(2)}) collective-permute-start(bf16[192,768]{1,0:T(8,128)(2,1)S(1)} %add_convert_fusion.14), channel_id=1, source_target_pairs={{0,32},{1,33},{2,34},{3,35},{4,36},{5,37},{6,38},{7,39},{8,40},{9,... | collective-permute-start | bytes 884744 | tf_op jit(solution)/shard_map/ppermute | solution.py:741
  456.5 19.9 %collective-permute-start.81 = (bf16[192,768]{1,0:T(8,128)(2,1)S(1)}, bf16[192,768]{1,0:T(8,128)(2,1)S(1)}, u32[]{:S(2)}, u32[]{:S(2)}) collective-permute-start(bf16[192,768]{1,0:T(8,128)(2,1)S(1)} %add_convert_fusion.14), channel_id=1, source_target_pairs={{0,64},{1,65},{2,66},{3,67},{4,68},{5,69},{6,70},{7,71},{8,72},{9,... | collective-permute-start | bytes 884744 | tf_op jit(solution)/shard_map/ppermute | solution.py:741
  476.6 36.5 %collective-permute-start.83 = (bf16[4,192,768]{2,1,0:T(8,128)(2,1)S(1)}, bf16[4,192,768]{2,1,0:T(8,128)(2,1)S(1)}, u32[]{:S(2)}, u32[]{:S(2)}) collective-permute-start(bf16[4,192,768]{2,1,0:T(8,128)(2,1)S(1)} %pad_maximum_fusion.3.here_ref), channel_id=1, source_target_pairs={{0,8},{1,9},{2,10},{3,11},{4,12},{5,13},{6,14},{7,15},{8,0},{9,1},... | collective-permute-start | bytes 3538952 | tf_op jit(solution)/shard_map/ppermute | solution.py:741
  483.3 35.7 %collective-permute-start.58 = (bf16[128,3072]{1,0:T(8,128)(2,1)S(1)}, bf16[128,3072]{1,0:T(8,128)(2,1)S(1)}, u32[]{:S(2)}, u32[]{:S(2)}) collective-permute-start(bf16[128,3072]{1,0:T(8,128)(2,1)S(1)} %copy-done.5), channel_id=1, source_target_pairs={{4,8},{5,9},{6,10},{7,11},{8,4},{9,5},{10,6},{11,7},{20,24},{21,25... | collective-permute-start | bytes 2359304 | tf_op jit(solution)/shard_map/ppermute | solution.py:741
  502.7 16.0 %collective-permute-start.75 = (bf16[192,512]{1,0:T(8,128)(2,1)S(1)}, bf16[192,512]{1,0:T(8,128)(2,1)S(1)}, u32[]{:S(2)}, u32[]{:S(2)}) collective-permute-start(bf16[192,512]{1,0:T(8,128)(2,1)S(1)} %add_convert_fusion.16), channel_id=1, source_target_pairs={{0,32},{1,33},{2,34},{3,35},{4,36},{5,37},{6,38},{7,39},{8,40},{9,... | collective-permute-start | bytes 589832 | tf_op jit(solution)/shard_map/ppermute | solution.py:741
  502.9 15.9 %collective-permute-start.85 = (bf16[192,512]{1,0:T(8,128)(2,1)S(1)}, bf16[192,512]{1,0:T(8,128)(2,1)S(1)}, u32[]{:S(2)}, u32[]{:S(2)}) collective-permute-start(bf16[192,512]{1,0:T(8,128)(2,1)S(1)} %add_convert_fusion.16), channel_id=1, source_target_pairs={{0,64},{1,65},{2,66},{3,67},{4,68},{5,69},{6,70},{7,71},{8,72},{9,... | collective-permute-start | bytes 589832 | tf_op jit(solution)/shard_map/ppermute | solution.py:741
  (110 other events, 1063.8 us)

commit v7 on v6

--- a/solution.py
+++ b/solution.py
@@ -1043,13 +1043,14 @@
 def small_kernel(head_dim, ends, narrow0_ref, narrow1_ref, gain_ref, pick_ref, norm_ref, wbc_ref, wdt_ref, cx_ref,
                  cxb_ref, cbc_ref, cbcb_ref, dtb_ref, alog_ref, skip_ref, ng_ref):
     bc_at, tiny_at = ends
-    heads = wdt_ref.shape[2]
+    heads = wdt_ref.shape[0]
     channels = cx_ref.shape[2]
     both = cbc_ref.shape[2]
     lanes = narrow0_ref.shape[1] - tiny_at
     for layer, ref in enumerate((narrow0_ref, narrow1_ref)):
-        wbc_ref[layer] = ref[:, bc_at:tiny_at]
-        wdt_ref[layer] = ref[:, 0:heads]
+        columns = jnp.transpose(ref[...])
+        wbc_ref[layer] = columns[bc_at:tiny_at]
+        wdt_ref[:, layer, :] = columns[0:heads]
     tiny = jnp.concatenate(
         [narrow0_ref[i * TINY_ROWS : (i + 1) * TINY_ROWS, tiny_at:] for i in range(channels // lanes)], axis=1
     )
@@ -1233,8 +1234,8 @@
     tiny = pad_to(jnp.concatenate(tiny, axis=0), width, tiny_lanes)
     tiny = jnp.pad(tiny, ((0, 0), (tiny_at, 0))).astype(bf16)
     early = halve(sum_far(after(early, dxt0)))
-    home = fold(mine, send_core(other))
-    late = weight_products(place, [(xn0, after(with_bc(dxt0, bc_sum), early, home[0]))])
+    late = weight_products(place, [(xn0, after(with_bc(dxt0, bc_sum), early))])
+    home = fold(mine, send_core(after(other, late[0])))
     early = sum_beside(early)
     tiny = after(tiny, early)
     late = [v + t for v, t in zip(late, cut_x(tiny))]
@@ -1247,7 +1248,8 @@
         [(v, rows) for v in terms] + [(packed, rows), (d_res1, rows), (norm_in[0:1], 1), (hidden_out, rows)],
         [jax.ShapeDtypeStruct((rows, 2 * width), bf16)],
     )
-    outputs_home = trade_places(outputs).astype(f32)
+    outputs_there = traded(outputs)
+    outputs_home = jnp.where(stays, outputs, outputs_there).astype(f32)
 
     early = after(collect_x(early), outputs)
     early = early, send_core(early)
@@ -1266,7 +1268,7 @@
     g_wz, g_wo = write_sums(
         place, early1, [(0, "rows", 1, g_wz, True), (channels, "blocks", 1, g_wo, True)]
     )
-    late = collect_x(sum_beside(halve(sum_far(late))), (g_wz,))
+    late = collect_x(sum_beside(halve(sum_far(after(late, outputs_there)))), (g_wz,))
     late = late, send_core(late)
     g_wx, narrow0 = write_sums(
         place, late, [(0, "rows", 0, g_wx, False), (channels, "flat", 0, None, False)]
@@ -1281,8 +1283,8 @@
             jax.ShapeDtypeStruct(shape, f32)
             for shape in (
                 norm_in.shape,
-                w_bc.shape,
-                w_dt.shape,
+                (layers, bc_rows, width),
+                (heads, layers, width),
                 conv_x.shape,
                 conv_x_bias.shape,
                 conv_bc.shape,
@@ -1300,7 +1302,9 @@
         small[0],
         g_wz,
         g_wx,
-        *small[1:],
+        jnp.transpose(small[1], (0, 2, 1)),
+        jnp.transpose(small[2], (1, 2, 0)),
+        *small[3:],
         g_wo,
     )
 

time: 545 us -> 536 us (0.983)
  waiting for transfers between devices: 136 us -> 143 us
  local copies, waits for them, and re-layouts: 36.8 us -> 30.5 us
    ppermute x88, waiting for transfers between devices: 136 us -> 143 us  [send(): return lax.ppermute(v, ('dp', 'tensor'), pairs)]
    ppermute x88, starting transfers between devices: 150 us -> 145 us  [send(): return lax.ppermute(v, ('dp', 'tensor'), pairs)]
    unnamed x151 -> x167, local copies, waits for them, and re-layouts: 14.1 us -> 11 us
  transfers between devices with their start and end apart: 88 -> 88, of which waited for: 28 -> 34; matrix products, arithmetic and copies ran while one was open for 9% -> 8% of each run, Pallas kernels for 23% -> 23%
where the time goes in v7:
time: 536 us; the launch traced here: 526 us
  Pallas kernels  169 us (32%)
  starting transfers between devices  145 us (27%)
  waiting for transfers between devices  143 us (27%)
  other arithmetic  36.7 us (7%)
  local copies, waits for them, and re-layouts  30.5 us (6%)
    ppermute x88, starting transfers between devices, send(): return lax.ppermute(v, ('dp', 'tensor'), pairs)  145 us
    ppermute x88, waiting for transfers between devices, send(): return lax.ppermute(v, ('dp', 'tensor'), pairs)  143 us
    pallas_call x5, Pallas kernels, span_call(): pl.pallas_call(kernel, grid_spec=pltpu.PrefetchScalarGridSpec(num_scalar_...  110 us
    pallas_call x3, Pallas kernels, weight_products(): pl.pallas_call(functools.partial(weight_kernel, len(pairs), split), grid_...  25.9 us
    pallas_call x6, Pallas kernels, row_call(): pl.pallas_call(kernel, grid=(1,), in_specs=[pl.BlockSpec((rows, v.shape[1...  18.4 us
    pallas_call x3, Pallas kernels, write_sums(): pl.pallas_call(functools.partial(write_kernel, plan, len(kept)), grid_spe...  14.8 us
    unnamed x167, local copies, waits for them, and re-layouts  11 us
  transfers between devices with their start and end apart: 88, of which 34 were waited for; matrix products, arithmetic and copies ran while one was open for 8% of the time, Pallas kernels for 23%

profile of v7, /device:TPU:1, one launch (start us, length us, event | category | flops | bytes accessed | tf_op | source)
XLA Modules:
  0.0 526.0 jit_solution(11162185039236363714)
XLA Ops:
  9.3 6.2 %collective-permute-start = (bf16[192,1536]{1,0:T(8,128)(2,1)}, bf16[192,1536]{1,0:T(8,128)(2,1)}, u32[]{:S(2)}, u32[]{:S(2)}) collective-permute-start(bf16[192,1536]{1,0:T(8,128)(2,1)} %pad_maximum_fusion.7), channel_id=1, source_target_pairs={{4,8},{5,9},{6,10},{7,11},{8,4},{9,5},{10,6},{11,7},{20,24},{21,25... | collective-permute-start | bytes 1769480 | tf_op jit(solution)/shard_map/ppermute | solution.py:741
  15.5 2.8 fusion.11
  26.1 4.4 collective-permute-start.8
  41.9 8.3 %collective-permute-done.2.refs_2_ = bf16[160,1536]{1,0:T(8,128)(2,1)S(1)} collective-permute-done((bf16[160,1536]{1,0:T(8,128)(2,1)}, bf16[160,1536]{1,0:T(8,128)(2,1)S(1)}, u32[]{:S(2)}, u32[]{:S(2)}) %collective-permute-start.2) | collective-permute-done | bytes 491552 | tf_op jit(solution)/shard_map/ppermute | solution.py:741
  50.2 4.2 collective-permute-done.4.refs_4_
  58.0 4.3 collective-permute-start.9
  64.1 3.6 collective-permute-start.11
  71.0 22.0 %layer_forward.2 = (bf16[1536,1152]{1,0:T(8,128)(2,1)}, bf16[1024,1536]{1,0:T(8,128)(2,1)}, bf16[256,1536]{1,0:T(8,128)(2,1)}, bf16[1024,384]{1,0:T(8,128)(2,1)}...) custom-call(s32[4]{0:T(128)} %pad_add_fusion.2.place_ref, ...), custom_call_target="tpu_custom_call" | custom-call | flops 20000000000 | bytes 26501120 | tf_op jit(solution)/shard_map/layer_forward/pallas_call | solution.py:512
  99.8 2.8 add_convert_fusion.4
  102.6 4.6 collective-permute-start.28
  108.3 3.3 collective-permute-start.15
  112.5 6.8 %collective-permute-done.14.a_ref = bf16[128,1664]{1,0:T(8,128)(2,1)S(1)} collective-permute-done((bf16[128,1664]{1,0:T(8,128)(2,1)S(1)}, bf16[128,1664]{1,0:T(8,128)(2,1)S(1)}, u32[]{:S(2)}, u32[]{:S(2)}) %collective-permute-start.14) | collective-permute-done | bytes 426016 | tf_op jit(solution)/shard_map/ppermute | solution.py:741
  119.3 10.6 %collective-permute-done.15.b_ref = bf16[128,1664]{1,0:T(8,128)(2,1)S(1)} collective-permute-done((bf16[128,1664]{1,0:T(8,128)(2,1)S(1)}, bf16[128,1664]{1,0:T(8,128)(2,1)S(1)}, u32[]{:S(2)}, u32[]{:S(2)}) %collective-permute-start.15) | collective-permute-done | bytes 426016 | tf_op jit(solution)/shard_map/ppermute | solution.py:741
  130.9 3.3 middle_norm.1
  138.3 7.7 %collective-permute-done.18.refs_2_ = bf16[128,1536]{1,0:T(8,128)(2,1)S(1)} collective-permute-done((bf16[128,1536]{1,0:T(8,128)(2,1)}, bf16[128,1536]{1,0:T(8,128)(2,1)S(1)}, u32[]{:S(2)}, u32[]{:S(2)}) %collective-permute-start.18) | collective-permute-done | bytes 393248 | tf_op jit(solution)/shard_map/ppermute | solution.py:741
  147.6 7.4 %collective-permute-start.21 = (bf16[128,1536]{1,0:T(8,128)(2,1)S(1)}, bf16[128,1536]{1,0:T(8,128)(2,1)S(1)}, u32[]{:S(2)}, u32[]{:S(2)}) collective-permute-start(bf16[128,1536]{1,0:T(8,128)(2,1)S(1)} %collective-permute-done.20.refs_4_), channel_id=1, source_target_pairs={{0,8},{1,9},{2,10},{3,11},{4,12},{5,13},{6,14},{7,15},{8,0},{9,1},... | collective-permute-start | bytes 1179656 | tf_op jit(solution)/shard_map/ppermute | solution.py:741
  158.1 26.0 %layer_forward.3 = (bf16[1536,1152]{1,0:T(8,128)(2,1)}, bf16[1024,1536]{1,0:T(8,128)(2,1)}, bf16[256,1536]{1,0:T(8,128)(2,1)}, bf16[1024,384]{1,0:T(8,128)(2,1)}...) custom-call(s32[4]{0:T(128)} %pad_add_fusion.2.place_ref, ...), custom_call_target="tpu_custom_call" | custom-call | flops 20000000000 | bytes 34398208 | tf_op jit(solution)/shard_map/layer_forward/pallas_call | solution.py:512
  184.6 3.3 collective-permute-done.29
  189.6 3.2 collective-permute-start.31
  203.8 27.2 %scan_backward.2 = (bf16[1024,384]{1,0:T(8,128)(2,1)}, bf16[1024,384]{1,0:T(8,128)(2,1)}, bf16[1024,512]{1,0:T(8,128)(2,1)}, bf16[512,256]{1,0:T(8,128)(2,1)}, b...) custom-call(s32[4]{0:T(128)} %pad_add_fusion.2.place_ref, ...), custom_call_target="tpu_custom_call" | custom-call | flops 28000000000 | bytes 21512192 | tf_op jit(solution)/shard_map/scan_backward/pallas_call | solution.py:512
  233.9 8.3 %weight_products.3 = bf16[1536,768]{1,0:T(8,128)(2,1)} custom-call(s32[4]{0:T(128)} %pad_add_fusion.2.place_ref, bf16[1024,1536]{1,0:T(8,128)(2,1)} %get-tuple-element.145.refs_4_.refs_0_.refs_2_, bf16[1024,384]{1,0:T(8,128)(2,1)} %get-tuple-element.157.refs_1_, bf16[1024,384]{1,0:T(8,128)(2,1)} %get-tuple-element.158.refs_2_, ...), custom_call_target="tpu_custom_call" | custom-call | flops 2415919104 | bytes 8000000 | tf_op jit(solution)/shard_map/weight_products/pallas_call | solution.py:708
  242.2 4.1 collective-permute-start.49
  250.9 17.9 %collective-permute-done.39.a_ref = bf16[128,1792]{1,0:T(8,128)(2,1)S(1)} collective-permute-done((bf16[128,1792]{1,0:T(8,128)(2,1)S(1)}, bf16[128,1792]{1,0:T(8,128)(2,1)S(1)}, u32[]{:S(2)}, u32[]{:S(2)}) %collective-permute-start.39) | collective-permute-done | bytes 458784 | tf_op jit(solution)/shard_map/ppermute | solution.py:741
  271.7 3.9 between_layers.1
  288.4 5.0 collective-permute-start.44
  293.4 6.5 %collective-permute-start.46 = (bf16[128,1664]{1,0:T(8,128)(2,1)}, bf16[128,1664]{1,0:T(8,128)(2,1)S(1)}, u32[]{:S(2)}, u32[]{:S(2)}) collective-permute-start(bf16[128,1664]{1,0:T(8,128)(2,1)} %collective-permute-done.45.refs_4_), channel_id=1, source_target_pairs={{0,8},{1,9},{2,10},{3,11},{4,12},{5,13},{6,14},{7,15},{8,0},{9,1},... | collective-permute-start | bytes 1277960 | tf_op jit(solution)/shard_map/ppermute | solution.py:741
  308.8 8.4 %gate_backward.1 = (bf16[1024,1536]{1,0:T(8,128)(2,1)}, bf16[1024,384]{1,0:T(8,128)(2,1)}, f32[1024,384]{1,0:T(8,128)}, bf16[1024,384]{1,0:T(8,128)(2,1)}, f32[8,384]{1,0:T(8,128)}) custom-call(s32[4]{0:T(128)} %pad_add_fusion.2.place_ref, bf16[128,1664]{1,0:T(8,128)(2,1)} %get-tuple-element.164.refs_0_, bf16[128,1664]{1,0:T(8,128)(2,1)} %collective-permute-done.42.refs_1_, ...), custom_call_target="tpu_custom_call" | custom-call | flops 6000000000 | bytes 14835712 | tf_op jit(solution)/shard_map/gate_backward/pallas_call | solution.py:512
  319.6 11.3 %weight_products.4 = (bf16[384,1280]{1,0:T(8,128)(2,1)}, bf16[384,1280]{1,0:T(8,128)(2,1)}, bf16[384,1280]{1,0:T(8,128)(2,1)}, bf16[384,1280]{1,0:T(8,128)(2,1)}) custom-call(s32[4]{0:T(128)} %pad_add_fusion.2.place_ref, bf16[1024,1536]{1,0:T(8,128)(2,1)} %get-tuple-element.171.refs_0_.refs_2_, bf16[1024,384]{1,0:T(8,128)(2,1)} %get-tuple-element.172.refs_1_, ...), custom_call_target="tpu_custom_call" | custom-call | flops 4026531840 | bytes 8000000 | tf_op jit(solution)/shard_map/weight_products/pallas_call | solution.py:708
  335.8 26.1 %scan_backward.3 = (bf16[1024,512]{1,0:T(8,128)(2,1)}, bf16[512,256]{1,0:T(8,128)(2,1)}, bf16[512,256]{1,0:T(8,128)(2,1)}, bf16[512,1536]{1,0:T(8,128)(2,1)}, bf...) custom-call(s32[4]{0:T(128)} %pad_add_fusion.2.place_ref, ...), custom_call_target="tpu_custom_call" | custom-call | flops 28000000000 | bytes 19120128 | tf_op jit(solution)/shard_map/scan_backward/pallas_call | solution.py:512
  362.0 15.4 %collective-permute-done.56 = bf16[384,1280]{1,0:T(8,128)(2,1)S(1)} collective-permute-done((bf16[384,1280]{1,0:T(8,128)(2,1)}, bf16[384,1280]{1,0:T(8,128)(2,1)S(1)}, u32[]{:S(2)}, u32[]{:S(2)}) %collective-permute-start.56) | collective-permute-done | bytes 983072 | tf_op jit(solution)/shard_map/ppermute | solution.py:741
  385.4 4.7 collective-permute-done.61
  393.7 5.9 %collective-permute-done.62 = bf16[192,1280]{1,0:T(8,128)(2,1)} collective-permute-done((bf16[192,1280]{1,0:T(8,128)(2,1)S(1)}, bf16[192,1280]{1,0:T(8,128)(2,1)}, u32[]{:S(2)}, u32[]{:S(2)}) %collective-permute-start.62) | collective-permute-done | bytes 491552 | tf_op jit(solution)/shard_map/ppermute | solution.py:741
  400.7 6.4 %weight_products.5 = (bf16[384,512]{1,0:T(8,128)(2,1)}, bf16[384,512]{1,0:T(8,128)(2,1)}, bf16[384,512]{1,0:T(8,128)(2,1)}, bf16[384,512]{1,0:T(8,128)(2,1)}) custom-call(s32[4]{0:T(128)} %pad_add_fusion.2.place_ref, bf16[1024,1536]{1,0:T(8,128)(2,1)} %get-tuple-element.171.refs_0_.refs_2_, bf16[1024,512]{1,0:T(8,128)(2,1)} %pad_add_fusion.refs_1_), custom_call_target="tpu_custom_call" | custom-call | flops 1610612736 | bytes 8000000 | tf_op jit(solution)/shard_map/weight_products/pallas_call | solution.py:708
  408.1 2.9 last_output.1.hidden_ref
  418.1 2.9 collective-permute-start.65
  420.9 8.9 %collective-permute-done.68 = bf16[192,1280]{1,0:T(8,128)(2,1)S(1)} collective-permute-done((bf16[192,1280]{1,0:T(8,128)(2,1)S(1)}, bf16[192,1280]{1,0:T(8,128)(2,1)S(1)}, u32[]{:S(2)}, u32[]{:S(2)}) %collective-permute-start.68) | collective-permute-done | bytes 491552 | tf_op jit(solution)/shard_map/ppermute | solution.py:741
  443.2 3.5 outputs.1
  449.2 4.8 collective-permute-done.78
  453.9 5.5 %collective-permute-start.67 = (bf16[128,3072]{1,0:T(8,128)(2,1)}, bf16[128,3072]{1,0:T(8,128)(2,1)S(1)}, u32[]{:S(2)}, u32[]{:S(2)}) collective-permute-start(bf16[128,3072]{1,0:T(8,128)(2,1)} %outputs.1), channel_id=1, source_target_pairs={{4,8},{5,9},{6,10},{7,11},{8,4},{9,5},{10,6},{11,7},{20,24},{21,25... | collective-permute-start | bytes 2359304 | tf_op jit(solution)/shard_map/ppermute | solution.py:741
  460.9 4.4 collective-permute-done.69
  465.3 5.5 %collective-permute-done.70 = bf16[384,512]{1,0:T(8,128)(2,1)S(1)} collective-permute-done((bf16[384,512]{1,0:T(8,128)(2,1)}, bf16[384,512]{1,0:T(8,128)(2,1)S(1)}, u32[]{:S(2)}, u32[]{:S(2)}) %collective-permute-start.70) | collective-permute-done | bytes 393248 | tf_op jit(solution)/shard_map/ppermute | solution.py:741
  472.7 3.8 collective-permute-start.82
  480.1 3.4 collective-permute-done.81
  487.3 3.8 collective-permute-done.73
  491.6 6.0 %collective-permute-done.74 = bf16[192,512]{1,0:T(8,128)(2,1)S(1)} collective-permute-done((bf16[192,512]{1,0:T(8,128)(2,1)S(1)}, bf16[192,512]{1,0:T(8,128)(2,1)S(1)}, u32[]{:S(2)}, u32[]{:S(2)}) %collective-permute-start.74) | collective-permute-done | bytes 196640 | tf_op jit(solution)/shard_map/ppermute | solution.py:741
  502.1 6.3 %write_sums.3 = (f32[2,4,2,192,384]{4,3,2,1,0:T(8,128)}, f32[2,384,1536]{2,1,0:T(8,128)}, f32[2,4,2,192,384]{4,3,2,1,0:T(8,128)}, f32[1,4,2,192,128]{4,3,2,1,0:T(8,128)}) custom-call(s32[4]{0:T(128)} %pad_add_fusion.2.place_ref, bf16[4,192,1280]{2,1,0:T(8,128)(2,1)} %copy-done.1, bf16[4,192,1280]{2,1,0:T(8,128)(2,1)} %copy-done.6), custom_call_target="tpu_custom_call" | custom-call | tf_op jit(solution)/shard_map/write_sums/pallas_call | solution.py:941
  509.5 4.7 write_sums.4
  519.0 3.9 write_sums.5
  (406 shorter events, 167.6 us)
Async XLA Ops:
  26.1 44.8 %collective-permute-start.8 = (bf16[1536,1152]{1,0:T(8,128)(2,1)}, bf16[1536,1152]{1,0:T(8,128)(2,1)}, u32[]{:S(2)}, u32[]{:S(2)}) collective-permute-start(bf16[1536,1152]{1,0:T(8,128)(2,1)} %pad_maximum_fusion.refs_8_), channel_id=1, source_target_pairs={{4,8},{5,9},{6,10},{7,11},{8,4},{9,5},{10,6},{11,7},{20,24},{21,25... | collective-permute-start | bytes 10616840 | tf_op jit(solution)/shard_map/ppermute | solution.py:741
  34.7 15.5 %collective-permute-start.2 = (bf16[160,1536]{1,0:T(8,128)(2,1)}, bf16[160,1536]{1,0:T(8,128)(2,1)S(1)}, u32[]{:S(2)}, u32[]{:S(2)}) collective-permute-start(bf16[160,1536]{1,0:T(8,128)(2,1)} %first_norm.1.refs_0_), channel_id=1, source_target_pairs={{0,1},{1,2},{2,3},{3,0},{4,5},{5,6},{6,7},{7,4},{8,9},{9,10},{10,1... | collective-permute-start | bytes 1474568 | tf_op jit(solution)/shard_map/ppermute | solution.py:741
  36.3 18.1 %collective-permute-start.4 = (bf16[160,1536]{1,0:T(8,128)(2,1)}, bf16[160,1536]{1,0:T(8,128)(2,1)S(1)}, u32[]{:S(2)}, u32[]{:S(2)}) collective-permute-start(bf16[160,1536]{1,0:T(8,128)(2,1)} %first_norm.1.refs_0_), channel_id=1, source_target_pairs={{0,3},{1,0},{2,1},{3,2},{4,7},{5,4},{6,5},{7,6},{8,11},{9,8},{10,9... | collective-permute-start | bytes 1474568 | tf_op jit(solution)/shard_map/ppermute | solution.py:741
  38.5 17.5 %collective-permute-start.6 = (bf16[160,1536]{1,0:T(8,128)(2,1)}, bf16[160,1536]{1,0:T(8,128)(2,1)S(1)}, u32[]{:S(2)}, u32[]{:S(2)}) collective-permute-start(bf16[160,1536]{1,0:T(8,128)(2,1)} %first_norm.1.refs_0_), channel_id=1, source_target_pairs={{0,2},{1,3},{2,0},{3,1},{4,6},{5,7},{6,4},{7,5},{8,10},{9,11},{10,... | collective-permute-start | bytes 1474568 | tf_op jit(solution)/shard_map/ppermute | solution.py:741
  39.8 18.2 %collective-permute-start.1 = (bf16[160,1536]{1,0:T(8,128)(2,1)}, bf16[160,1536]{1,0:T(8,128)(2,1)S(1)}, u32[]{:S(2)}, u32[]{:S(2)}) collective-permute-start(bf16[160,1536]{1,0:T(8,128)(2,1)} %first_norm.1.refs_0_), channel_id=1, source_target_pairs={{0,8},{1,9},{2,10},{3,11},{4,12},{5,13},{6,14},{7,15},{8,0},{9,1},... | collective-permute-start | bytes 1474568 | tf_op jit(solution)/shard_map/ppermute | solution.py:741
  58.0 35.0 %collective-permute-start.9 = (bf16[160,1536]{1,0:T(8,128)(2,1)S(1)}, bf16[160,1536]{1,0:T(8,128)(2,1)S(1)}, u32[]{:S(2)}, u32[]{:S(2)}) collective-permute-start(bf16[160,1536]{1,0:T(8,128)(2,1)S(1)} %pad_maximum_fusion.8), channel_id=1, source_target_pairs={{4,8},{5,9},{6,10},{7,11},{8,4},{9,5},{10,6},{11,7},{20,24},{21,25... | collective-permute-start | bytes 1474568 | tf_op jit(solution)/shard_map/ppermute | solution.py:741
  62.3 31.6 %collective-permute-start.10 = (bf16[160,1536]{1,0:T(8,128)(2,1)S(1)}, bf16[160,1536]{1,0:T(8,128)(2,1)S(1)}, u32[]{:S(2)}, u32[]{:S(2)}) collective-permute-start(bf16[160,1536]{1,0:T(8,128)(2,1)S(1)} %pad_maximum_fusion.8), channel_id=1, source_target_pairs={{0,1},{1,2},{2,3},{3,0},{4,9},{5,10},{6,11},{7,8},{8,5},{9,6},{10,... | collective-permute-start | bytes 1474568 | tf_op jit(solution)/shard_map/ppermute | solution.py:741
  64.1 29.7 %collective-permute-start.11 = (bf16[160,1536]{1,0:T(8,128)(2,1)S(1)}, bf16[160,1536]{1,0:T(8,128)(2,1)S(1)}, u32[]{:S(2)}, u32[]{:S(2)}) collective-permute-start(bf16[160,1536]{1,0:T(8,128)(2,1)S(1)} %pad_maximum_fusion.8), channel_id=1, source_target_pairs={{0,3},{1,0},{2,1},{3,2},{4,11},{5,8},{6,9},{7,10},{8,7},{9,4},{10,... | collective-permute-start | bytes 1474568 | tf_op jit(solution)/shard_map/ppermute | solution.py:741
  67.7 27.3 %collective-permute-start.12 = (bf16[160,1536]{1,0:T(8,128)(2,1)S(1)}, bf16[160,1536]{1,0:T(8,128)(2,1)S(1)}, u32[]{:S(2)}, u32[]{:S(2)}) collective-permute-start(bf16[160,1536]{1,0:T(8,128)(2,1)S(1)} %pad_maximum_fusion.8), channel_id=1, source_target_pairs={{0,2},{1,3},{2,0},{3,1},{4,10},{5,11},{6,8},{7,9},{8,6},{9,7},{10,... | collective-permute-start | bytes 1474568 | tf_op jit(solution)/shard_map/ppermute | solution.py:741
  102.6 54.7 %collective-permute-start.28 = (bf16[1536,1152]{1,0:T(8,128)(2,1)S(1)}, bf16[1536,1152]{1,0:T(8,128)(2,1)}, u32[]{:S(2)}, u32[]{:S(2)}) collective-permute-start(bf16[1536,1152]{1,0:T(8,128)(2,1)S(1)} %pad_maximum_fusion.1.refs_16_), channel_id=1, source_target_pairs={{4,8},{5,9},{6,10},{7,11},{8,4},{9,5},{10,6},{11,7},{20,24},{21,25... | collective-permute-start | bytes 10616840 | tf_op jit(solution)/shard_map/ppermute | solution.py:741
  108.3 21.6 %collective-permute-start.15 = (bf16[128,1664]{1,0:T(8,128)(2,1)S(1)}, bf16[128,1664]{1,0:T(8,128)(2,1)S(1)}, u32[]{:S(2)}, u32[]{:S(2)}) collective-permute-start(bf16[128,1664]{1,0:T(8,128)(2,1)S(1)} %get-tuple-element.242), channel_id=1, source_target_pairs={{0,2},{1,3},{2,0},{3,1},{4,6},{5,7},{6,4},{7,5},{8,10},{9,11},{10,... | collective-permute-start | bytes 1277960 | tf_op jit(solution)/shard_map/ppermute | solution.py:741
  111.6 18.3 %collective-permute-start.16 = (bf16[128,1664]{1,0:T(8,128)(2,1)S(1)}, bf16[128,1664]{1,0:T(8,128)(2,1)S(1)}, u32[]{:S(2)}, u32[]{:S(2)}) collective-permute-start(bf16[128,1664]{1,0:T(8,128)(2,1)S(1)} %get-tuple-element.241), channel_id=1, source_target_pairs={{0,3},{1,0},{2,1},{3,2},{4,7},{5,4},{6,5},{7,6},{8,11},{9,8},{10,9... | collective-permute-start | bytes 1277960 | tf_op jit(solution)/shard_map/ppermute | solution.py:741
  112.3 21.8 %collective-permute-start.24 = (bf16[160,1536]{1,0:T(8,128)(2,1)S(1)}, bf16[160,1536]{1,0:T(8,128)(2,1)S(1)}, u32[]{:S(2)}, u32[]{:S(2)}) collective-permute-start(bf16[160,1536]{1,0:T(8,128)(2,1)S(1)} %copy-done.7), channel_id=1, source_target_pairs={{0,8},{1,9},{2,10},{3,11},{4,12},{5,13},{6,14},{7,15},{8,0},{9,1},... | collective-permute-start | bytes 1474568 | tf_op jit(solution)/shard_map/ppermute | solution.py:741
  119.3 15.9 %collective-permute-start.25 = (bf16[160,1536]{1,0:T(8,128)(2,1)S(1)}, bf16[160,1536]{1,0:T(8,128)(2,1)S(1)}, u32[]{:S(2)}, u32[]{:S(2)}) collective-permute-start(bf16[160,1536]{1,0:T(8,128)(2,1)S(1)} %copy-done.56), channel_id=1, source_target_pairs={{0,8},{1,9},{2,10},{3,11},{4,12},{5,13},{6,14},{7,15},{8,0},{9,1},... | collective-permute-start | bytes 1474568 | tf_op jit(solution)/shard_map/ppermute | solution.py:741
  136.9 18.1 %collective-permute-start.22 = (bf16[128,1536]{1,0:T(8,128)(2,1)}, bf16[128,1536]{1,0:T(8,128)(2,1)S(1)}, u32[]{:S(2)}, u32[]{:S(2)}) collective-permute-start(bf16[128,1536]{1,0:T(8,128)(2,1)} %get-tuple-element.132.refs_0_), channel_id=1, source_target_pairs={{0,2},{1,3},{2,0},{3,1},{4,6},{5,7},{6,4},{7,5},{8,10},{9,11},{10,... | collective-permute-start | bytes 1179656 | tf_op jit(solution)/shard_map/ppermute | solution.py:741
  137.6 19.2 %collective-permute-start.17 = (bf16[128,1536]{1,0:T(8,128)(2,1)}, bf16[128,1536]{1,0:T(8,128)(2,1)S(1)}, u32[]{:S(2)}, u32[]{:S(2)}) collective-permute-start(bf16[128,1536]{1,0:T(8,128)(2,1)} %get-tuple-element.132.refs_0_), channel_id=1, source_target_pairs={{0,8},{1,9},{2,10},{3,11},{4,12},{5,13},{6,14},{7,15},{8,0},{9,1},... | collective-permute-start | bytes 1179656 | tf_op jit(solution)/shard_map/ppermute | solution.py:741
  197.8 33.3 %collective-permute-start.34 = (bf16[128,1664]{1,0:T(8,128)(2,1)S(1)}, bf16[128,1664]{1,0:T(8,128)(2,1)S(1)}, u32[]{:S(2)}, u32[]{:S(2)}) collective-permute-start(bf16[128,1664]{1,0:T(8,128)(2,1)S(1)} %get-tuple-element.240), channel_id=1, source_target_pairs={{0,1},{1,2},{2,3},{3,0},{4,5},{5,6},{6,7},{7,4},{8,9},{9,10},{10,1... | collective-permute-start | bytes 1277960 | tf_op jit(solution)/shard_map/ppermute | solution.py:741
  197.9 33.2 %collective-permute-start.35 = (bf16[128,1664]{1,0:T(8,128)(2,1)S(1)}, bf16[128,1664]{1,0:T(8,128)(2,1)S(1)}, u32[]{:S(2)}, u32[]{:S(2)}) collective-permute-start(bf16[128,1664]{1,0:T(8,128)(2,1)S(1)} %get-tuple-element.239), channel_id=1, source_target_pairs={{0,2},{1,3},{2,0},{3,1},{4,6},{5,7},{6,4},{7,5},{8,10},{9,11},{10,... | collective-permute-start | bytes 1277960 | tf_op jit(solution)/shard_map/ppermute | solution.py:741
  200.6 30.5 %collective-permute-start.36 = (bf16[128,1664]{1,0:T(8,128)(2,1)S(1)}, bf16[128,1664]{1,0:T(8,128)(2,1)S(1)}, u32[]{:S(2)}, u32[]{:S(2)}) collective-permute-start(bf16[128,1664]{1,0:T(8,128)(2,1)S(1)} %get-tuple-element.238), channel_id=1, source_target_pairs={{0,3},{1,0},{2,1},{3,2},{4,7},{5,4},{6,5},{7,6},{8,11},{9,8},{10,9... | collective-permute-start | bytes 1277960 | tf_op jit(solution)/shard_map/ppermute | solution.py:741
  231.1 15.3 %collective-permute-start.37 = (bf16[512,1536]{1,0:T(8,128)(2,1)}, bf16[512,1536]{1,0:T(8,128)(2,1)S(1)}, u32[]{:S(2)}, u32[]{:S(2)}) collective-permute-start(bf16[512,1536]{1,0:T(8,128)(2,1)} %get-tuple-element.154), channel_id=1, source_target_pairs={{0,8},{1,9},{2,10},{3,11},{4,12},{5,13},{6,14},{7,15},{8,0},{9,1},... | collective-permute-start | bytes 4718600 | tf_op jit(solution)/shard_map/ppermute | solution.py:741
  242.2 33.5 %collective-permute-start.49 = (bf16[1536,768]{1,0:T(8,128)(2,1)}, bf16[1536,768]{1,0:T(8,128)(2,1)S(1)}, u32[]{:S(2)}, u32[]{:S(2)}) collective-permute-start(bf16[1536,768]{1,0:T(8,128)(2,1)} %weight_products.3), channel_id=1, source_target_pairs={{4,0},{5,1},{6,2},{7,3},{8,12},{9,13},{10,14},{11,15},{20,16},{21,... | collective-permute-start | bytes 7077896 | tf_op jit(solution)/shard_map/ppermute | solution.py:741
  246.7 22.1 %collective-permute-start.39 = (bf16[128,1792]{1,0:T(8,128)(2,1)S(1)}, bf16[128,1792]{1,0:T(8,128)(2,1)S(1)}, u32[]{:S(2)}, u32[]{:S(2)}) collective-permute-start(bf16[128,1792]{1,0:T(8,128)(2,1)S(1)} %pad_maximum_fusion.9), channel_id=1, source_target_pairs={{0,1},{1,2},{2,3},{3,0},{4,5},{5,6},{6,7},{7,4},{8,9},{9,10},{10,1... | collective-permute-start | bytes 1376264 | tf_op jit(solution)/shard_map/ppermute | solution.py:741
  247.3 21.6 %collective-permute-start.40 = (bf16[128,1792]{1,0:T(8,128)(2,1)S(1)}, bf16[128,1792]{1,0:T(8,128)(2,1)S(1)}, u32[]{:S(2)}, u32[]{:S(2)}) collective-permute-start(bf16[128,1792]{1,0:T(8,128)(2,1)S(1)} %pad_maximum_fusion.5), channel_id=1, source_target_pairs={{0,2},{1,3},{2,0},{3,1},{4,6},{5,7},{6,4},{7,5},{8,10},{9,11},{10,... | collective-permute-start | bytes 1376264 | tf_op jit(solution)/shard_map/ppermute | solution.py:741
  248.8 21.1 %collective-permute-start.41 = (bf16[128,1792]{1,0:T(8,128)(2,1)S(1)}, bf16[128,1792]{1,0:T(8,128)(2,1)S(1)}, u32[]{:S(2)}, u32[]{:S(2)}) collective-permute-start(bf16[128,1792]{1,0:T(8,128)(2,1)S(1)} %pad_maximum_fusion.10), channel_id=1, source_target_pairs={{0,3},{1,0},{2,1},{3,2},{4,7},{5,4},{6,5},{7,6},{8,11},{9,8},{10,9... | collective-permute-start | bytes 1376264 | tf_op jit(solution)/shard_map/ppermute | solution.py:741
  276.4 25.1 %collective-permute-start.50 = (bf16[768,768]{1,0:T(8,128)(2,1)S(1)}, bf16[768,768]{1,0:T(8,128)(2,1)}, u32[]{:S(2)}, u32[]{:S(2)}) collective-permute-start(bf16[768,768]{1,0:T(8,128)(2,1)S(1)} %slice.220), channel_id=1, source_target_pairs={{0,8},{1,9},{2,10},{3,11},{12,4},{13,5},{14,6},{15,7},{16,24},{17,... | collective-permute-start | bytes 3538952 | tf_op jit(solution)/shard_map/ppermute | solution.py:741
  280.4 19.5 %collective-permute-start.47 = (bf16[128,1664]{1,0:T(8,128)(2,1)}, bf16[128,1664]{1,0:T(8,128)(2,1)}, u32[]{:S(2)}, u32[]{:S(2)}) collective-permute-start(bf16[128,1664]{1,0:T(8,128)(2,1)} %get-tuple-element.164.refs_0_), channel_id=1, source_target_pairs={{0,2},{1,3},{2,0},{3,1},{4,6},{5,7},{6,4},{7,5},{8,10},{9,11},{10,... | collective-permute-start | bytes 1277960 | tf_op jit(solution)/shard_map/ppermute | solution.py:741
  281.3 23.0 %collective-permute-start.42 = (bf16[128,1664]{1,0:T(8,128)(2,1)}, bf16[128,1664]{1,0:T(8,128)(2,1)}, u32[]{:S(2)}, u32[]{:S(2)}) collective-permute-start(bf16[128,1664]{1,0:T(8,128)(2,1)} %get-tuple-element.164.refs_0_), channel_id=1, source_target_pairs={{0,8},{1,9},{2,10},{3,11},{4,12},{5,13},{6,14},{7,15},{8,0},{9,1},... | collective-permute-start | bytes 1277960 | tf_op jit(solution)/shard_map/ppermute | solution.py:741
  288.4 18.2 %collective-permute-start.44 = (bf16[128,1664]{1,0:T(8,128)(2,1)}, bf16[128,1664]{1,0:T(8,128)(2,1)S(1)}, u32[]{:S(2)}, u32[]{:S(2)}) collective-permute-start(bf16[128,1664]{1,0:T(8,128)(2,1)} %collective-permute-done.43.refs_2_), channel_id=1, source_target_pairs={{0,8},{1,9},{2,10},{3,11},{4,12},{5,13},{6,14},{7,15},{8,0},{9,1},... | collective-permute-start | bytes 1277960 | tf_op jit(solution)/shard_map/ppermute | solution.py:741
  304.2 15.2 %collective-permute-start.52 = (bf16[192,768]{1,0:T(8,128)(2,1)S(1)}, bf16[192,768]{1,0:T(8,128)(2,1)S(1)}, u32[]{:S(2)}, u32[]{:S(2)}) collective-permute-start(bf16[192,768]{1,0:T(8,128)(2,1)S(1)} %get-tuple-element.265), channel_id=1, source_target_pairs={{0,64},{1,65},{2,66},{3,67},{4,68},{5,69},{6,70},{7,71},{8,72},{9,... | collective-permute-start | bytes 884744 | tf_op jit(solution)/shard_map/ppermute | solution.py:741
  330.9 31.1 %collective-permute-start.55 = (bf16[384,1280]{1,0:T(8,128)(2,1)}, bf16[384,1280]{1,0:T(8,128)(2,1)S(1)}, u32[]{:S(2)}, u32[]{:S(2)}) collective-permute-start(bf16[384,1280]{1,0:T(8,128)(2,1)} %get-tuple-element.178), channel_id=1, source_target_pairs={{0,32},{1,33},{2,34},{3,35},{4,36},{5,37},{6,38},{7,39},{8,40},{9,... | collective-permute-start | bytes 2949128 | tf_op jit(solution)/shard_map/ppermute | solution.py:741
  332.6 44.8 %collective-permute-start.56 = (bf16[384,1280]{1,0:T(8,128)(2,1)}, bf16[384,1280]{1,0:T(8,128)(2,1)S(1)}, u32[]{:S(2)}, u32[]{:S(2)}) collective-permute-start(bf16[384,1280]{1,0:T(8,128)(2,1)} %get-tuple-element.179), channel_id=1, source_target_pairs={{0,64},{1,65},{2,66},{3,67},{4,68},{5,69},{6,70},{7,71},{8,72},{9,... | collective-permute-start | bytes 2949128 | tf_op jit(solution)/shard_map/ppermute | solution.py:741
  334.6 42.7 %collective-permute-start.57 = (bf16[384,1280]{1,0:T(8,128)(2,1)}, bf16[384,1280]{1,0:T(8,128)(2,1)S(1)}, u32[]{:S(2)}, u32[]{:S(2)}) collective-permute-start(bf16[384,1280]{1,0:T(8,128)(2,1)} %get-tuple-element.180), channel_id=1, source_target_pairs={{0,96},{1,97},{2,98},{3,99},{4,100},{5,101},{6,102},{7,103},{8,104... | collective-permute-start | bytes 2949128 | tf_op jit(solution)/shard_map/ppermute | solution.py:741
  411.0 35.7 %collective-permute-start.76 = (bf16[192,768]{1,0:T(8,128)(2,1)S(1)}, bf16[192,768]{1,0:T(8,128)(2,1)S(1)}, u32[]{:S(2)}, u32[]{:S(2)}) collective-permute-start(bf16[192,768]{1,0:T(8,128)(2,1)S(1)} %add_convert_fusion.15), channel_id=1, source_target_pairs={{0,16},{1,17},{2,18},{3,19},{4,20},{5,21},{6,22},{7,23},{8,24},{9,... | collective-permute-start | bytes 884744 | tf_op jit(solution)/shard_map/ppermute | solution.py:741
  413.4 16.5 %collective-permute-start.68 = (bf16[192,1280]{1,0:T(8,128)(2,1)S(1)}, bf16[192,1280]{1,0:T(8,128)(2,1)S(1)}, u32[]{:S(2)}, u32[]{:S(2)}) collective-permute-start(bf16[192,1280]{1,0:T(8,128)(2,1)S(1)} %slice_select_fusion.1), channel_id=1, source_target_pairs={{0,16},{1,17},{2,18},{3,19},{4,20},{5,21},{6,22},{7,23},{8,24},{9,... | collective-permute-start | bytes 1474568 | tf_op jit(solution)/shard_map/ppermute | solution.py:741
  417.1 16.0 %collective-permute-start.64 = (bf16[128,1536]{1,0:T(8,128)(2,1)S(1)}, bf16[128,1536]{1,0:T(8,128)(2,1)S(1)}, u32[]{:S(2)}, u32[]{:S(2)}) collective-permute-start(bf16[128,1536]{1,0:T(8,128)(2,1)S(1)} %get-tuple-element.247), channel_id=1, source_target_pairs={{0,1},{1,2},{2,3},{3,0},{4,5},{5,6},{6,7},{7,4},{8,9},{9,10},{10,1... | collective-permute-start | bytes 1179656 | tf_op jit(solution)/shard_map/ppermute | solution.py:741
  418.1 19.4 %collective-permute-start.65 = (bf16[128,1536]{1,0:T(8,128)(2,1)S(1)}, bf16[128,1536]{1,0:T(8,128)(2,1)S(1)}, u32[]{:S(2)}, u32[]{:S(2)}) collective-permute-start(bf16[128,1536]{1,0:T(8,128)(2,1)S(1)} %get-tuple-element.246), channel_id=1, source_target_pairs={{0,2},{1,3},{2,0},{3,1},{4,6},{5,7},{6,4},{7,5},{8,10},{9,11},{10,... | collective-permute-start | bytes 1179656 | tf_op jit(solution)/shard_map/ppermute | solution.py:741
  430.0 18.5 %collective-permute-start.77 = (bf16[192,1280]{1,0:T(8,128)(2,1)S(1)}, bf16[192,1280]{1,0:T(8,128)(2,1)S(1)}, u32[]{:S(2)}, u32[]{:S(2)}) collective-permute-start(bf16[192,1280]{1,0:T(8,128)(2,1)S(1)} %add_convert_fusion.3), channel_id=1, source_target_pairs={{0,32},{1,33},{2,34},{3,35},{4,36},{5,37},{6,38},{7,39},{8,40},{9,... | collective-permute-start | bytes 1474568 | tf_op jit(solution)/shard_map/ppermute | solution.py:741
  431.3 22.7 %collective-permute-start.78 = (bf16[192,1280]{1,0:T(8,128)(2,1)S(1)}, bf16[192,1280]{1,0:T(8,128)(2,1)S(1)}, u32[]{:S(2)}, u32[]{:S(2)}) collective-permute-start(bf16[192,1280]{1,0:T(8,128)(2,1)S(1)} %add_convert_fusion.3), channel_id=1, source_target_pairs={{0,64},{1,65},{2,66},{3,67},{4,68},{5,69},{6,70},{7,71},{8,72},{9,... | collective-permute-start | bytes 1474568 | tf_op jit(solution)/shard_map/ppermute | solution.py:741
  437.5 23.0 %collective-permute-start.79 = (bf16[192,1280]{1,0:T(8,128)(2,1)S(1)}, bf16[192,1280]{1,0:T(8,128)(2,1)S(1)}, u32[]{:S(2)}, u32[]{:S(2)}) collective-permute-start(bf16[192,1280]{1,0:T(8,128)(2,1)S(1)} %add_convert_fusion.3), channel_id=1, source_target_pairs={{0,96},{1,97},{2,98},{3,99},{4,100},{5,101},{6,102},{7,103},{8,104... | collective-permute-start | bytes 1474568 | tf_op jit(solution)/shard_map/ppermute | solution.py:741
  442.5 22.8 %collective-permute-start.69 = (bf16[384,512]{1,0:T(8,128)(2,1)}, bf16[384,512]{1,0:T(8,128)(2,1)S(1)}, u32[]{:S(2)}, u32[]{:S(2)}) collective-permute-start(bf16[384,512]{1,0:T(8,128)(2,1)} %get-tuple-element.258), channel_id=1, source_target_pairs={{0,32},{1,33},{2,34},{3,35},{4,36},{5,37},{6,38},{7,39},{8,40},{9,... | collective-permute-start | bytes 1179656 | tf_op jit(solution)/shard_map/ppermute | solution.py:741
  446.7 24.1 %collective-permute-start.70 = (bf16[384,512]{1,0:T(8,128)(2,1)}, bf16[384,512]{1,0:T(8,128)(2,1)S(1)}, u32[]{:S(2)}, u32[]{:S(2)}) collective-permute-start(bf16[384,512]{1,0:T(8,128)(2,1)} %get-tuple-element.260), channel_id=1, source_target_pairs={{0,64},{1,65},{2,66},{3,67},{4,68},{5,69},{6,70},{7,71},{8,72},{9,... | collective-permute-start | bytes 1179656 | tf_op jit(solution)/shard_map/ppermute | solution.py:741
  448.5 24.2 %collective-permute-start.71 = (bf16[384,512]{1,0:T(8,128)(2,1)}, bf16[384,512]{1,0:T(8,128)(2,1)S(1)}, u32[]{:S(2)}, u32[]{:S(2)}) collective-permute-start(bf16[384,512]{1,0:T(8,128)(2,1)} %get-tuple-element.259), channel_id=1, source_target_pairs={{0,96},{1,97},{2,98},{3,99},{4,100},{5,101},{6,102},{7,103},{8,104... | collective-permute-start | bytes 1179656 | tf_op jit(solution)/shard_map/ppermute | solution.py:741
  453.9 22.8 %collective-permute-start.67 = (bf16[128,3072]{1,0:T(8,128)(2,1)}, bf16[128,3072]{1,0:T(8,128)(2,1)S(1)}, u32[]{:S(2)}, u32[]{:S(2)}) collective-permute-start(bf16[128,3072]{1,0:T(8,128)(2,1)} %outputs.1), channel_id=1, source_target_pairs={{4,8},{5,9},{6,10},{7,11},{8,4},{9,5},{10,6},{11,7},{20,24},{21,25... | collective-permute-start | bytes 2359304 | tf_op jit(solution)/shard_map/ppermute | solution.py:741
  460.8 40.1 %collective-permute-start.84 = (bf16[4,192,1280]{2,1,0:T(8,128)(2,1)S(1)}, bf16[4,192,1280]{2,1,0:T(8,128)(2,1)S(1)}, u32[]{:S(2)}, u32[]{:S(2)}) collective-permute-start(bf16[4,192,1280]{2,1,0:T(8,128)(2,1)S(1)} %pad_maximum_fusion.2.here_ref), channel_id=1, source_target_pairs={{0,8},{1,9},{2,10},{3,11},{4,12},{5,13},{6,14},{7,15},{8,0},{9,1},... | collective-permute-start | bytes 5898248 | tf_op jit(solution)/shard_map/ppermute | solution.py:741
  465.3 14.8 %collective-permute-start.80 = (bf16[192,768]{1,0:T(8,128)(2,1)S(1)}, bf16[192,768]{1,0:T(8,128)(2,1)S(1)}, u32[]{:S(2)}, u32[]{:S(2)}) collective-permute-start(bf16[192,768]{1,0:T(8,128)(2,1)S(1)} %add_convert_fusion.14), channel_id=1, source_target_pairs={{0,32},{1,33},{2,34},{3,35},{4,36},{5,37},{6,38},{7,39},{8,40},{9,... | collective-permute-start | bytes 884744 | tf_op jit(solution)/shard_map/ppermute | solution.py:741
  484.3 24.1 %collective-permute-start.83 = (bf16[4,192,768]{2,1,0:T(8,128)(2,1)S(1)}, bf16[4,192,768]{2,1,0:T(8,128)(2,1)S(1)}, u32[]{:S(2)}, u32[]{:S(2)}) collective-permute-start(bf16[4,192,768]{2,1,0:T(8,128)(2,1)S(1)} %pad_maximum_fusion.3.here_ref), channel_id=1, source_target_pairs={{0,8},{1,9},{2,10},{3,11},{4,12},{5,13},{6,14},{7,15},{8,0},{9,1},... | collective-permute-start | bytes 3538952 | tf_op jit(solution)/shard_map/ppermute | solution.py:741
  497.7 16.5 %collective-permute-start.75 = (bf16[192,512]{1,0:T(8,128)(2,1)S(1)}, bf16[192,512]{1,0:T(8,128)(2,1)S(1)}, u32[]{:S(2)}, u32[]{:S(2)}) collective-permute-start(bf16[192,512]{1,0:T(8,128)(2,1)S(1)} %add_convert_fusion.16), channel_id=1, source_target_pairs={{0,32},{1,33},{2,34},{3,35},{4,36},{5,37},{6,38},{7,39},{8,40},{9,... | collective-permute-start | bytes 589832 | tf_op jit(solution)/shard_map/ppermute | solution.py:741
  497.9 16.2 %collective-permute-start.85 = (bf16[192,512]{1,0:T(8,128)(2,1)S(1)}, bf16[192,512]{1,0:T(8,128)(2,1)S(1)}, u32[]{:S(2)}, u32[]{:S(2)}) collective-permute-start(bf16[192,512]{1,0:T(8,128)(2,1)S(1)} %add_convert_fusion.16), channel_id=1, source_target_pairs={{0,64},{1,65},{2,66},{3,67},{4,68},{5,69},{6,70},{7,71},{8,72},{9,... | collective-permute-start | bytes 589832 | tf_op jit(solution)/shard_map/ppermute | solution.py:741
  (119 other events, 1103.3 us)

commit v8 on v7

--- a/solution.py
+++ b/solution.py
@@ -861,9 +861,19 @@
 
 
 def sum_x(blocks):
-    total = blocks[0].astype(f32)
-    for k in range(1, NX):
-        got = send(blocks[k], lambda x, yl, c, yh, z, k=k: (x + k, yl, c, yh, z))
+    return add_x(blocks[0], send_x(blocks))
+
+
+def send_x(blocks):
+    return [
+        send(blocks[k], lambda x, yl, c, yh, z, k=k: (x + k, yl, c, yh, z)) for k in range(1, NX)
+    ]
+
+
+def add_x(own, received, meanwhile=()):
+    total = own.astype(f32)
+    for got in received:
+        got = after(got, *meanwhile) if meanwhile else got
         total = total + got.astype(f32)
     return total.astype(bf16)
 
@@ -1209,7 +1219,7 @@
     dxt1 = with_bc(dxt1, sum(v[:, width:].astype(f32) for v in terms))
 
     early1 = halve(sum_far(early1, after(early1_far, sent)))
-    z0 = after(z0, early1)
+    z0 = after(z0, early1, hidden_out)
     early1 = sum_x(cut_x(early1))
     grad_rows0, dz0, dy0, go0, acc_gate0 = run_gate(place, gathered_back, z0, y0, w0, smalls[0][0])
     dz0 = after(dz0, early1)
@@ -1239,7 +1249,7 @@
     early = sum_beside(early)
     tiny = after(tiny, early)
     late = [v + t for v, t in zip(late, cut_x(tiny))]
-    late = sum_x(late)
+    late_own, late = late[0], send_x(late)
 
     terms = home[:1] + [send_z(home[k].astype(bf16), k) for k in range(1, NZ)]
     [outputs] = row_call(
@@ -1265,6 +1275,7 @@
             (3 * channels, "flat", 0, None, False),
         ],
     )
+    late = add_x(late_own, late, (g_wz,))
     g_wz, g_wo = write_sums(
         place, early1, [(0, "rows", 1, g_wz, True), (channels, "blocks", 1, g_wo, True)]
     )

time: 536 us -> 540 us (level)
  waiting for transfers between devices: 143 us -> 151 us
  starting transfers between devices: 145 us -> 138 us
    ppermute x88, waiting for transfers between devices: 143 us -> 151 us  [send(): return lax.ppermute(v, ('dp', 'tensor'), pairs)]
    ppermute x88, starting transfers between devices: 145 us -> 138 us  [send(): return lax.ppermute(v, ('dp', 'tensor'), pairs)]
  transfers between devices with their start and end apart: 88 -> 88, of which waited for: 34 -> 31; matrix products, arithmetic and copies ran while one was open for 8% -> 8% of each run, Pallas kernels for 23% -> 22%
where the time goes in v8:
time: 540 us; the launch traced here: 530 us
  Pallas kernels  169 us (31%)
  waiting for transfers between devices  151 us (28%)
  starting transfers between devices  138 us (26%)
  other arithmetic  39.1 us (7%)
  local copies, waits for them, and re-layouts  30.1 us (6%)
    ppermute x88, waiting for transfers between devices, send(): return lax.ppermute(v, ('dp', 'tensor'), pairs)  151 us
    ppermute x88, starting transfers between devices, send(): return lax.ppermute(v, ('dp', 'tensor'), pairs)  138 us
    pallas_call x5, Pallas kernels, span_call(): pl.pallas_call(kernel, grid_spec=pltpu.PrefetchScalarGridSpec(num_scalar_...  110 us
    pallas_call x3, Pallas kernels, weight_products(): pl.pallas_call(functools.partial(weight_kernel, len(pairs), split), grid_...  26.1 us
    pallas_call x6, Pallas kernels, row_call(): pl.pallas_call(kernel, grid=(1,), in_specs=[pl.BlockSpec((rows, v.shape[1...  18.4 us
    pallas_call x3, Pallas kernels, write_sums(): pl.pallas_call(functools.partial(write_kernel, plan, len(kept)), grid_spe...  14.8 us
  transfers between devices with their start and end apart: 88, of which 31 were waited for; matrix products, arithmetic and copies ran while one was open for 8% of the time, Pallas kernels for 22%

profile of v8, /device:TPU:1, one launch (start us, length us, event | category | flops | bytes accessed | tf_op | source)
XLA Modules:
  0.0 529.9 jit_solution(4913812536375595240)
XLA Ops:
  9.3 6.2 %collective-permute-start = (bf16[192,1536]{1,0:T(8,128)(2,1)}, bf16[192,1536]{1,0:T(8,128)(2,1)}, u32[]{:S(2)}, u32[]{:S(2)}) collective-permute-start(bf16[192,1536]{1,0:T(8,128)(2,1)} %pad_maximum_fusion.7), channel_id=1, source_target_pairs={{4,8},{5,9},{6,10},{7,11},{8,4},{9,5},{10,6},{11,7},{20,24},{21,25... | collective-permute-start | bytes 1769480 | tf_op jit(solution)/shard_map/ppermute | solution.py:741
  15.5 2.8 fusion.11
  19.1 2.8 slice_bitcast_fusion
  26.1 4.4 collective-permute-start.8
  41.9 8.3 %collective-permute-done.2.refs_2_ = bf16[160,1536]{1,0:T(8,128)(2,1)S(1)} collective-permute-done((bf16[160,1536]{1,0:T(8,128)(2,1)}, bf16[160,1536]{1,0:T(8,128)(2,1)S(1)}, u32[]{:S(2)}, u32[]{:S(2)}) %collective-permute-start.2) | collective-permute-done | bytes 491552 | tf_op jit(solution)/shard_map/ppermute | solution.py:741
  50.2 4.2 collective-permute-done.4.refs_4_
  58.0 4.3 collective-permute-start.9
  64.1 3.6 collective-permute-start.11
  71.0 22.0 %layer_forward.2 = (bf16[1536,1152]{1,0:T(8,128)(2,1)}, bf16[1024,1536]{1,0:T(8,128)(2,1)}, bf16[256,1536]{1,0:T(8,128)(2,1)}, bf16[1024,384]{1,0:T(8,128)(2,1)}...) custom-call(s32[4]{0:T(128)} %pad_add_fusion.2.place_ref, ...), custom_call_target="tpu_custom_call" | custom-call | flops 20000000000 | bytes 26501120 | tf_op jit(solution)/shard_map/layer_forward/pallas_call | solution.py:512
  99.8 2.8 add_convert_fusion.4
  102.6 4.6 collective-permute-start.28
  108.3 3.3 collective-permute-start.15
  112.5 6.8 %collective-permute-done.14.a_ref = bf16[128,1664]{1,0:T(8,128)(2,1)S(1)} collective-permute-done((bf16[128,1664]{1,0:T(8,128)(2,1)S(1)}, bf16[128,1664]{1,0:T(8,128)(2,1)S(1)}, u32[]{:S(2)}, u32[]{:S(2)}) %collective-permute-start.14) | collective-permute-done | bytes 426016 | tf_op jit(solution)/shard_map/ppermute | solution.py:741
  119.3 10.6 %collective-permute-done.15.b_ref = bf16[128,1664]{1,0:T(8,128)(2,1)S(1)} collective-permute-done((bf16[128,1664]{1,0:T(8,128)(2,1)S(1)}, bf16[128,1664]{1,0:T(8,128)(2,1)S(1)}, u32[]{:S(2)}, u32[]{:S(2)}) %collective-permute-start.15) | collective-permute-done | bytes 426016 | tf_op jit(solution)/shard_map/ppermute | solution.py:741
  130.9 3.3 middle_norm.1
  138.4 7.6 %collective-permute-done.18.refs_2_ = bf16[128,1536]{1,0:T(8,128)(2,1)S(1)} collective-permute-done((bf16[128,1536]{1,0:T(8,128)(2,1)}, bf16[128,1536]{1,0:T(8,128)(2,1)S(1)}, u32[]{:S(2)}, u32[]{:S(2)}) %collective-permute-start.18) | collective-permute-done | bytes 393248 | tf_op jit(solution)/shard_map/ppermute | solution.py:741
  147.6 7.4 %collective-permute-start.21 = (bf16[128,1536]{1,0:T(8,128)(2,1)S(1)}, bf16[128,1536]{1,0:T(8,128)(2,1)S(1)}, u32[]{:S(2)}, u32[]{:S(2)}) collective-permute-start(bf16[128,1536]{1,0:T(8,128)(2,1)S(1)} %collective-permute-done.20.refs_4_), channel_id=1, source_target_pairs={{0,8},{1,9},{2,10},{3,11},{4,12},{5,13},{6,14},{7,15},{8,0},{9,1},... | collective-permute-start | bytes 1179656 | tf_op jit(solution)/shard_map/ppermute | solution.py:741
  158.1 26.0 %layer_forward.3 = (bf16[1536,1152]{1,0:T(8,128)(2,1)}, bf16[1024,1536]{1,0:T(8,128)(2,1)}, bf16[256,1536]{1,0:T(8,128)(2,1)}, bf16[1024,384]{1,0:T(8,128)(2,1)}...) custom-call(s32[4]{0:T(128)} %pad_add_fusion.2.place_ref, ...), custom_call_target="tpu_custom_call" | custom-call | flops 20000000000 | bytes 34398208 | tf_op jit(solution)/shard_map/layer_forward/pallas_call | solution.py:512
  184.7 3.3 collective-permute-done.29
  189.6 3.2 collective-permute-start.31
  203.9 27.2 %scan_backward.2 = (bf16[1024,384]{1,0:T(8,128)(2,1)}, bf16[1024,384]{1,0:T(8,128)(2,1)}, bf16[1024,512]{1,0:T(8,128)(2,1)}, bf16[512,256]{1,0:T(8,128)(2,1)}, b...) custom-call(s32[4]{0:T(128)} %pad_add_fusion.2.place_ref, ...), custom_call_target="tpu_custom_call" | custom-call | flops 28000000000 | bytes 21512192 | tf_op jit(solution)/shard_map/scan_backward/pallas_call | solution.py:512
  233.9 8.3 %weight_products.3 = bf16[1536,768]{1,0:T(8,128)(2,1)} custom-call(s32[4]{0:T(128)} %pad_add_fusion.2.place_ref, bf16[1024,1536]{1,0:T(8,128)(2,1)} %get-tuple-element.148.refs_4_.refs_0_.refs_2_, bf16[1024,384]{1,0:T(8,128)(2,1)} %get-tuple-element.160.refs_1_, bf16[1024,384]{1,0:T(8,128)(2,1)} %get-tuple-element.161.refs_2_, ...), custom_call_target="tpu_custom_call" | custom-call | flops 2415919104 | bytes 8000000 | tf_op jit(solution)/shard_map/weight_products/pallas_call | solution.py:708
  242.2 4.1 collective-permute-start.49
  251.0 17.9 %collective-permute-done.39.a_ref = bf16[128,1792]{1,0:T(8,128)(2,1)S(1)} collective-permute-done((bf16[128,1792]{1,0:T(8,128)(2,1)S(1)}, bf16[128,1792]{1,0:T(8,128)(2,1)S(1)}, u32[]{:S(2)}, u32[]{:S(2)}) %collective-permute-start.39) | collective-permute-done | bytes 458784 | tf_op jit(solution)/shard_map/ppermute | solution.py:741
  271.8 3.9 between_layers.1
  281.3 2.8 collective-permute-start.42
  285.8 2.9 last_output.1.hidden_ref
  289.9 3.4 collective-permute-start.44
  293.3 6.6 %collective-permute-start.46 = (bf16[128,1664]{1,0:T(8,128)(2,1)}, bf16[128,1664]{1,0:T(8,128)(2,1)S(1)}, u32[]{:S(2)}, u32[]{:S(2)}) collective-permute-start(bf16[128,1664]{1,0:T(8,128)(2,1)} %collective-permute-done.45.refs_4_), channel_id=1, source_target_pairs={{0,8},{1,9},{2,10},{3,11},{4,12},{5,13},{6,14},{7,15},{8,0},{9,1},... | collective-permute-start | bytes 1277960 | tf_op jit(solution)/shard_map/ppermute | solution.py:741
  308.8 8.4 %gate_backward.1 = (bf16[1024,1536]{1,0:T(8,128)(2,1)}, bf16[1024,384]{1,0:T(8,128)(2,1)}, f32[1024,384]{1,0:T(8,128)}, bf16[1024,384]{1,0:T(8,128)(2,1)}, f32[8,384]{1,0:T(8,128)}) custom-call(s32[4]{0:T(128)} %pad_add_fusion.2.place_ref, bf16[128,1664]{1,0:T(8,128)(2,1)} %get-tuple-element.167.refs_0_, bf16[128,1664]{1,0:T(8,128)(2,1)} %collective-permute-done.42.refs_1_, ...), custom_call_target="tpu_custom_call" | custom-call | flops 6000000000 | bytes 14835712 | tf_op jit(solution)/shard_map/gate_backward/pallas_call | solution.py:512
  320.4 11.2 %weight_products.4 = (bf16[384,1280]{1,0:T(8,128)(2,1)}, bf16[384,1280]{1,0:T(8,128)(2,1)}, bf16[384,1280]{1,0:T(8,128)(2,1)}, bf16[384,1280]{1,0:T(8,128)(2,1)}) custom-call(s32[4]{0:T(128)} %pad_add_fusion.2.place_ref, bf16[1024,1536]{1,0:T(8,128)(2,1)} %get-tuple-element.175.refs_0_.refs_2_, bf16[1024,384]{1,0:T(8,128)(2,1)} %get-tuple-element.176.refs_1_, ...), custom_call_target="tpu_custom_call" | custom-call | flops 4026531840 | bytes 8000000 | tf_op jit(solution)/shard_map/weight_products/pallas_call | solution.py:708
  336.5 26.1 %scan_backward.3 = (bf16[1024,512]{1,0:T(8,128)(2,1)}, bf16[512,256]{1,0:T(8,128)(2,1)}, bf16[512,256]{1,0:T(8,128)(2,1)}, bf16[512,1536]{1,0:T(8,128)(2,1)}, bf...) custom-call(s32[4]{0:T(128)} %pad_add_fusion.2.place_ref, ...), custom_call_target="tpu_custom_call" | custom-call | flops 28000000000 | bytes 19120128 | tf_op jit(solution)/shard_map/scan_backward/pallas_call | solution.py:512
  362.7 15.4 %collective-permute-done.56 = bf16[384,1280]{1,0:T(8,128)(2,1)S(1)} collective-permute-done((bf16[384,1280]{1,0:T(8,128)(2,1)}, bf16[384,1280]{1,0:T(8,128)(2,1)S(1)}, u32[]{:S(2)}, u32[]{:S(2)}) %collective-permute-start.56) | collective-permute-done | bytes 983072 | tf_op jit(solution)/shard_map/ppermute | solution.py:741
  386.2 4.7 collective-permute-done.61
  394.5 5.7 %collective-permute-done.62 = bf16[192,1280]{1,0:T(8,128)(2,1)S(1)} collective-permute-done((bf16[192,1280]{1,0:T(8,128)(2,1)S(1)}, bf16[192,1280]{1,0:T(8,128)(2,1)S(1)}, u32[]{:S(2)}, u32[]{:S(2)}) %collective-permute-start.62) | collective-permute-done | bytes 491552 | tf_op jit(solution)/shard_map/ppermute | solution.py:741
  400.4 6.5 %weight_products.5 = (bf16[384,512]{1,0:T(8,128)(2,1)}, bf16[384,512]{1,0:T(8,128)(2,1)}, bf16[384,512]{1,0:T(8,128)(2,1)}, bf16[384,512]{1,0:T(8,128)(2,1)}) custom-call(s32[4]{0:T(128)} %pad_add_fusion.2.place_ref, bf16[1024,1536]{1,0:T(8,128)(2,1)} %get-tuple-element.175.refs_0_.refs_2_, bf16[1024,512]{1,0:T(8,128)(2,1)} %pad_add_fusion.refs_1_), custom_call_target="tpu_custom_call" | custom-call | flops 1610612736 | bytes 8000000 | tf_op jit(solution)/shard_map/weight_products/pallas_call | solution.py:708
  409.4 11.1 %collective-permute-done.68 = bf16[192,1280]{1,0:T(8,128)(2,1)S(1)} collective-permute-done((bf16[192,1280]{1,0:T(8,128)(2,1)S(1)}, bf16[192,1280]{1,0:T(8,128)(2,1)S(1)}, u32[]{:S(2)}, u32[]{:S(2)}) %collective-permute-start.68) | collective-permute-done | bytes 491552 | tf_op jit(solution)/shard_map/ppermute | solution.py:741
  426.1 3.1 add_convert_fusion.9
  430.3 3.0 collective-permute-start.65
  436.2 8.6 %collective-permute-done.71 = bf16[192,1280]{1,0:T(8,128)(2,1)S(1)} collective-permute-done((bf16[192,1280]{1,0:T(8,128)(2,1)S(1)}, bf16[192,1280]{1,0:T(8,128)(2,1)S(1)}, u32[]{:S(2)}, u32[]{:S(2)}) %collective-permute-start.71) | collective-permute-done | bytes 491552 | tf_op jit(solution)/shard_map/ppermute | solution.py:741
  450.3 3.5 outputs.1
  464.2 6.3 %write_sums.3 = (f32[2,4,2,192,384]{4,3,2,1,0:T(8,128)}, f32[2,384,1536]{2,1,0:T(8,128)}, f32[2,4,2,192,384]{4,3,2,1,0:T(8,128)}, f32[1,4,2,192,128]{4,3,2,1,0:T(8,128)}) custom-call(s32[4]{0:T(128)} %pad_add_fusion.2.place_ref, bf16[4,192,1280]{2,1,0:T(8,128)(2,1)} %copy-done.1, bf16[4,192,1280]{2,1,0:T(8,128)(2,1)} %collective-permute-done.73.there_ref), custom_call_target="tpu_custom_call" | custom-call | tf_op jit(solution)/shard_map/write_sums/pallas_call | solution.py:951
  470.5 10.3 %collective-permute-done.69 = bf16[384,512]{1,0:T(8,128)(2,1)} collective-permute-done((bf16[384,512]{1,0:T(8,128)(2,1)}, bf16[384,512]{1,0:T(8,128)(2,1)}, u32[]{:S(2)}, u32[]{:S(2)}) %collective-permute-start.69) | collective-permute-done | bytes 393248 | tf_op jit(solution)/shard_map/ppermute | solution.py:741
  484.2 9.1 %collective-permute-done.81 = bf16[192,768]{1,0:T(8,128)(2,1)S(1)} collective-permute-done((bf16[192,768]{1,0:T(8,128)(2,1)S(1)}, bf16[192,768]{1,0:T(8,128)(2,1)S(1)}, u32[]{:S(2)}, u32[]{:S(2)}) %collective-permute-start.81) | collective-permute-done | bytes 294944 | tf_op jit(solution)/shard_map/ppermute | solution.py:741
  499.0 5.9 %collective-permute-done.78 = bf16[192,512]{1,0:T(8,128)(2,1)S(1)} collective-permute-done((bf16[192,512]{1,0:T(8,128)(2,1)S(1)}, bf16[192,512]{1,0:T(8,128)(2,1)S(1)}, u32[]{:S(2)}, u32[]{:S(2)}) %collective-permute-start.78) | collective-permute-done | bytes 196640 | tf_op jit(solution)/shard_map/ppermute | solution.py:741
  505.9 3.2 collective-permute-start.85
  510.5 4.7 write_sums.4
  522.8 3.9 write_sums.5
  (406 shorter events, 162.0 us)
Async XLA Ops:
  9.3 14.7 %collective-permute-start = (bf16[192,1536]{1,0:T(8,128)(2,1)}, bf16[192,1536]{1,0:T(8,128)(2,1)}, u32[]{:S(2)}, u32[]{:S(2)}) collective-permute-start(bf16[192,1536]{1,0:T(8,128)(2,1)} %pad_maximum_fusion.7), channel_id=1, source_target_pairs={{4,8},{5,9},{6,10},{7,11},{8,4},{9,5},{10,6},{11,7},{20,24},{21,25... | collective-permute-start | bytes 1769480 | tf_op jit(solution)/shard_map/ppermute | solution.py:741
  26.1 44.8 %collective-permute-start.8 = (bf16[1536,1152]{1,0:T(8,128)(2,1)}, bf16[1536,1152]{1,0:T(8,128)(2,1)}, u32[]{:S(2)}, u32[]{:S(2)}) collective-permute-start(bf16[1536,1152]{1,0:T(8,128)(2,1)} %pad_maximum_fusion.refs_8_), channel_id=1, source_target_pairs={{4,8},{5,9},{6,10},{7,11},{8,4},{9,5},{10,6},{11,7},{20,24},{21,25... | collective-permute-start | bytes 10616840 | tf_op jit(solution)/shard_map/ppermute | solution.py:741
  34.7 15.5 %collective-permute-start.2 = (bf16[160,1536]{1,0:T(8,128)(2,1)}, bf16[160,1536]{1,0:T(8,128)(2,1)S(1)}, u32[]{:S(2)}, u32[]{:S(2)}) collective-permute-start(bf16[160,1536]{1,0:T(8,128)(2,1)} %first_norm.1.refs_0_), channel_id=1, source_target_pairs={{0,1},{1,2},{2,3},{3,0},{4,5},{5,6},{6,7},{7,4},{8,9},{9,10},{10,1... | collective-permute-start | bytes 1474568 | tf_op jit(solution)/shard_map/ppermute | solution.py:741
  36.3 18.1 %collective-permute-start.4 = (bf16[160,1536]{1,0:T(8,128)(2,1)}, bf16[160,1536]{1,0:T(8,128)(2,1)S(1)}, u32[]{:S(2)}, u32[]{:S(2)}) collective-permute-start(bf16[160,1536]{1,0:T(8,128)(2,1)} %first_norm.1.refs_0_), channel_id=1, source_target_pairs={{0,3},{1,0},{2,1},{3,2},{4,7},{5,4},{6,5},{7,6},{8,11},{9,8},{10,9... | collective-permute-start | bytes 1474568 | tf_op jit(solution)/shard_map/ppermute | solution.py:741
  38.5 17.5 %collective-permute-start.6 = (bf16[160,1536]{1,0:T(8,128)(2,1)}, bf16[160,1536]{1,0:T(8,128)(2,1)S(1)}, u32[]{:S(2)}, u32[]{:S(2)}) collective-permute-start(bf16[160,1536]{1,0:T(8,128)(2,1)} %first_norm.1.refs_0_), channel_id=1, source_target_pairs={{0,2},{1,3},{2,0},{3,1},{4,6},{5,7},{6,4},{7,5},{8,10},{9,11},{10,... | collective-permute-start | bytes 1474568 | tf_op jit(solution)/shard_map/ppermute | solution.py:741
  39.8 18.3 %collective-permute-start.1 = (bf16[160,1536]{1,0:T(8,128)(2,1)}, bf16[160,1536]{1,0:T(8,128)(2,1)S(1)}, u32[]{:S(2)}, u32[]{:S(2)}) collective-permute-start(bf16[160,1536]{1,0:T(8,128)(2,1)} %first_norm.1.refs_0_), channel_id=1, source_target_pairs={{0,8},{1,9},{2,10},{3,11},{4,12},{5,13},{6,14},{7,15},{8,0},{9,1},... | collective-permute-start | bytes 1474568 | tf_op jit(solution)/shard_map/ppermute | solution.py:741
  58.0 34.9 %collective-permute-start.9 = (bf16[160,1536]{1,0:T(8,128)(2,1)S(1)}, bf16[160,1536]{1,0:T(8,128)(2,1)S(1)}, u32[]{:S(2)}, u32[]{:S(2)}) collective-permute-start(bf16[160,1536]{1,0:T(8,128)(2,1)S(1)} %pad_maximum_fusion.8), channel_id=1, source_target_pairs={{4,8},{5,9},{6,10},{7,11},{8,4},{9,5},{10,6},{11,7},{20,24},{21,25... | collective-permute-start | bytes 1474568 | tf_op jit(solution)/shard_map/ppermute | solution.py:741
  62.3 31.5 %collective-permute-start.10 = (bf16[160,1536]{1,0:T(8,128)(2,1)S(1)}, bf16[160,1536]{1,0:T(8,128)(2,1)S(1)}, u32[]{:S(2)}, u32[]{:S(2)}) collective-permute-start(bf16[160,1536]{1,0:T(8,128)(2,1)S(1)} %pad_maximum_fusion.8), channel_id=1, source_target_pairs={{0,1},{1,2},{2,3},{3,0},{4,9},{5,10},{6,11},{7,8},{8,5},{9,6},{10,... | collective-permute-start | bytes 1474568 | tf_op jit(solution)/shard_map/ppermute | solution.py:741
  64.1 29.7 %collective-permute-start.11 = (bf16[160,1536]{1,0:T(8,128)(2,1)S(1)}, bf16[160,1536]{1,0:T(8,128)(2,1)S(1)}, u32[]{:S(2)}, u32[]{:S(2)}) collective-permute-start(bf16[160,1536]{1,0:T(8,128)(2,1)S(1)} %pad_maximum_fusion.8), channel_id=1, source_target_pairs={{0,3},{1,0},{2,1},{3,2},{4,11},{5,8},{6,9},{7,10},{8,7},{9,4},{10,... | collective-permute-start | bytes 1474568 | tf_op jit(solution)/shard_map/ppermute | solution.py:741
  67.7 27.3 %collective-permute-start.12 = (bf16[160,1536]{1,0:T(8,128)(2,1)S(1)}, bf16[160,1536]{1,0:T(8,128)(2,1)S(1)}, u32[]{:S(2)}, u32[]{:S(2)}) collective-permute-start(bf16[160,1536]{1,0:T(8,128)(2,1)S(1)} %pad_maximum_fusion.8), channel_id=1, source_target_pairs={{0,2},{1,3},{2,0},{3,1},{4,10},{5,11},{6,8},{7,9},{8,6},{9,7},{10,... | collective-permute-start | bytes 1474568 | tf_op jit(solution)/shard_map/ppermute | solution.py:741
  102.6 54.7 %collective-permute-start.28 = (bf16[1536,1152]{1,0:T(8,128)(2,1)S(1)}, bf16[1536,1152]{1,0:T(8,128)(2,1)}, u32[]{:S(2)}, u32[]{:S(2)}) collective-permute-start(bf16[1536,1152]{1,0:T(8,128)(2,1)S(1)} %pad_maximum_fusion.1.refs_16_), channel_id=1, source_target_pairs={{4,8},{5,9},{6,10},{7,11},{8,4},{9,5},{10,6},{11,7},{20,24},{21,25... | collective-permute-start | bytes 10616840 | tf_op jit(solution)/shard_map/ppermute | solution.py:741
  108.3 21.6 %collective-permute-start.15 = (bf16[128,1664]{1,0:T(8,128)(2,1)S(1)}, bf16[128,1664]{1,0:T(8,128)(2,1)S(1)}, u32[]{:S(2)}, u32[]{:S(2)}) collective-permute-start(bf16[128,1664]{1,0:T(8,128)(2,1)S(1)} %get-tuple-element.248), channel_id=1, source_target_pairs={{0,2},{1,3},{2,0},{3,1},{4,6},{5,7},{6,4},{7,5},{8,10},{9,11},{10,... | collective-permute-start | bytes 1277960 | tf_op jit(solution)/shard_map/ppermute | solution.py:741
  111.6 18.3 %collective-permute-start.16 = (bf16[128,1664]{1,0:T(8,128)(2,1)S(1)}, bf16[128,1664]{1,0:T(8,128)(2,1)S(1)}, u32[]{:S(2)}, u32[]{:S(2)}) collective-permute-start(bf16[128,1664]{1,0:T(8,128)(2,1)S(1)} %get-tuple-element.247), channel_id=1, source_target_pairs={{0,3},{1,0},{2,1},{3,2},{4,7},{5,4},{6,5},{7,6},{8,11},{9,8},{10,9... | collective-permute-start | bytes 1277960 | tf_op jit(solution)/shard_map/ppermute | solution.py:741
  112.3 21.9 %collective-permute-start.24 = (bf16[160,1536]{1,0:T(8,128)(2,1)S(1)}, bf16[160,1536]{1,0:T(8,128)(2,1)S(1)}, u32[]{:S(2)}, u32[]{:S(2)}) collective-permute-start(bf16[160,1536]{1,0:T(8,128)(2,1)S(1)} %copy-done.5), channel_id=1, source_target_pairs={{0,8},{1,9},{2,10},{3,11},{4,12},{5,13},{6,14},{7,15},{8,0},{9,1},... | collective-permute-start | bytes 1474568 | tf_op jit(solution)/shard_map/ppermute | solution.py:741
  119.3 15.9 %collective-permute-start.25 = (bf16[160,1536]{1,0:T(8,128)(2,1)S(1)}, bf16[160,1536]{1,0:T(8,128)(2,1)S(1)}, u32[]{:S(2)}, u32[]{:S(2)}) collective-permute-start(bf16[160,1536]{1,0:T(8,128)(2,1)S(1)} %copy-done.56), channel_id=1, source_target_pairs={{0,8},{1,9},{2,10},{3,11},{4,12},{5,13},{6,14},{7,15},{8,0},{9,1},... | collective-permute-start | bytes 1474568 | tf_op jit(solution)/shard_map/ppermute | solution.py:741
  136.9 18.1 %collective-permute-start.22 = (bf16[128,1536]{1,0:T(8,128)(2,1)}, bf16[128,1536]{1,0:T(8,128)(2,1)S(1)}, u32[]{:S(2)}, u32[]{:S(2)}) collective-permute-start(bf16[128,1536]{1,0:T(8,128)(2,1)} %get-tuple-element.135.refs_0_), channel_id=1, source_target_pairs={{0,2},{1,3},{2,0},{3,1},{4,6},{5,7},{6,4},{7,5},{8,10},{9,11},{10,... | collective-permute-start | bytes 1179656 | tf_op jit(solution)/shard_map/ppermute | solution.py:741
  137.6 19.2 %collective-permute-start.17 = (bf16[128,1536]{1,0:T(8,128)(2,1)}, bf16[128,1536]{1,0:T(8,128)(2,1)S(1)}, u32[]{:S(2)}, u32[]{:S(2)}) collective-permute-start(bf16[128,1536]{1,0:T(8,128)(2,1)} %get-tuple-element.135.refs_0_), channel_id=1, source_target_pairs={{0,8},{1,9},{2,10},{3,11},{4,12},{5,13},{6,14},{7,15},{8,0},{9,1},... | collective-permute-start | bytes 1179656 | tf_op jit(solution)/shard_map/ppermute | solution.py:741
  197.8 33.3 %collective-permute-start.34 = (bf16[128,1664]{1,0:T(8,128)(2,1)S(1)}, bf16[128,1664]{1,0:T(8,128)(2,1)S(1)}, u32[]{:S(2)}, u32[]{:S(2)}) collective-permute-start(bf16[128,1664]{1,0:T(8,128)(2,1)S(1)} %get-tuple-element.246), channel_id=1, source_target_pairs={{0,1},{1,2},{2,3},{3,0},{4,5},{5,6},{6,7},{7,4},{8,9},{9,10},{10,1... | collective-permute-start | bytes 1277960 | tf_op jit(solution)/shard_map/ppermute | solution.py:741
  197.9 33.3 %collective-permute-start.35 = (bf16[128,1664]{1,0:T(8,128)(2,1)S(1)}, bf16[128,1664]{1,0:T(8,128)(2,1)S(1)}, u32[]{:S(2)}, u32[]{:S(2)}) collective-permute-start(bf16[128,1664]{1,0:T(8,128)(2,1)S(1)} %get-tuple-element.245), channel_id=1, source_target_pairs={{0,2},{1,3},{2,0},{3,1},{4,6},{5,7},{6,4},{7,5},{8,10},{9,11},{10,... | collective-permute-start | bytes 1277960 | tf_op jit(solution)/shard_map/ppermute | solution.py:741
  200.6 30.6 %collective-permute-start.36 = (bf16[128,1664]{1,0:T(8,128)(2,1)S(1)}, bf16[128,1664]{1,0:T(8,128)(2,1)S(1)}, u32[]{:S(2)}, u32[]{:S(2)}) collective-permute-start(bf16[128,1664]{1,0:T(8,128)(2,1)S(1)} %get-tuple-element.244), channel_id=1, source_target_pairs={{0,3},{1,0},{2,1},{3,2},{4,7},{5,4},{6,5},{7,6},{8,11},{9,8},{10,9... | collective-permute-start | bytes 1277960 | tf_op jit(solution)/shard_map/ppermute | solution.py:741
  231.2 15.3 %collective-permute-start.37 = (bf16[512,1536]{1,0:T(8,128)(2,1)}, bf16[512,1536]{1,0:T(8,128)(2,1)S(1)}, u32[]{:S(2)}, u32[]{:S(2)}) collective-permute-start(bf16[512,1536]{1,0:T(8,128)(2,1)} %get-tuple-element.157), channel_id=1, source_target_pairs={{0,8},{1,9},{2,10},{3,11},{4,12},{5,13},{6,14},{7,15},{8,0},{9,1},... | collective-permute-start | bytes 4718600 | tf_op jit(solution)/shard_map/ppermute | solution.py:741
  242.2 33.5 %collective-permute-start.49 = (bf16[1536,768]{1,0:T(8,128)(2,1)}, bf16[1536,768]{1,0:T(8,128)(2,1)S(1)}, u32[]{:S(2)}, u32[]{:S(2)}) collective-permute-start(bf16[1536,768]{1,0:T(8,128)(2,1)} %weight_products.3), channel_id=1, source_target_pairs={{4,0},{5,1},{6,2},{7,3},{8,12},{9,13},{10,14},{11,15},{20,16},{21,... | collective-permute-start | bytes 7077896 | tf_op jit(solution)/shard_map/ppermute | solution.py:741
  246.8 22.1 %collective-permute-start.39 = (bf16[128,1792]{1,0:T(8,128)(2,1)S(1)}, bf16[128,1792]{1,0:T(8,128)(2,1)S(1)}, u32[]{:S(2)}, u32[]{:S(2)}) collective-permute-start(bf16[128,1792]{1,0:T(8,128)(2,1)S(1)} %pad_maximum_fusion.9), channel_id=1, source_target_pairs={{0,1},{1,2},{2,3},{3,0},{4,5},{5,6},{6,7},{7,4},{8,9},{9,10},{10,1... | collective-permute-start | bytes 1376264 | tf_op jit(solution)/shard_map/ppermute | solution.py:741
  247.3 21.6 %collective-permute-start.40 = (bf16[128,1792]{1,0:T(8,128)(2,1)S(1)}, bf16[128,1792]{1,0:T(8,128)(2,1)S(1)}, u32[]{:S(2)}, u32[]{:S(2)}) collective-permute-start(bf16[128,1792]{1,0:T(8,128)(2,1)S(1)} %pad_maximum_fusion.5), channel_id=1, source_target_pairs={{0,2},{1,3},{2,0},{3,1},{4,6},{5,7},{6,4},{7,5},{8,10},{9,11},{10,... | collective-permute-start | bytes 1376264 | tf_op jit(solution)/shard_map/ppermute | solution.py:741
  248.9 21.1 %collective-permute-start.41 = (bf16[128,1792]{1,0:T(8,128)(2,1)S(1)}, bf16[128,1792]{1,0:T(8,128)(2,1)S(1)}, u32[]{:S(2)}, u32[]{:S(2)}) collective-permute-start(bf16[128,1792]{1,0:T(8,128)(2,1)S(1)} %pad_maximum_fusion.10), channel_id=1, source_target_pairs={{0,3},{1,0},{2,1},{3,2},{4,7},{5,4},{6,5},{7,6},{8,11},{9,8},{10,9... | collective-permute-start | bytes 1376264 | tf_op jit(solution)/shard_map/ppermute | solution.py:741
  276.4 25.1 %collective-permute-start.50 = (bf16[768,768]{1,0:T(8,128)(2,1)S(1)}, bf16[768,768]{1,0:T(8,128)(2,1)}, u32[]{:S(2)}, u32[]{:S(2)}) collective-permute-start(bf16[768,768]{1,0:T(8,128)(2,1)S(1)} %slice.220), channel_id=1, source_target_pairs={{0,8},{1,9},{2,10},{3,11},{12,4},{13,5},{14,6},{15,7},{16,24},{17,... | collective-permute-start | bytes 3538952 | tf_op jit(solution)/shard_map/ppermute | solution.py:741
  278.9 14.5 %collective-permute-start.45 = (bf16[128,1664]{1,0:T(8,128)(2,1)}, bf16[128,1664]{1,0:T(8,128)(2,1)}, u32[]{:S(2)}, u32[]{:S(2)}) collective-permute-start(bf16[128,1664]{1,0:T(8,128)(2,1)} %get-tuple-element.167.refs_0_), channel_id=1, source_target_pairs={{0,3},{1,0},{2,1},{3,2},{4,7},{5,4},{6,5},{7,6},{8,11},{9,8},{10,9... | collective-permute-start | bytes 1277960 | tf_op jit(solution)/shard_map/ppermute | solution.py:741
  280.5 19.5 %collective-permute-start.47 = (bf16[128,1664]{1,0:T(8,128)(2,1)}, bf16[128,1664]{1,0:T(8,128)(2,1)}, u32[]{:S(2)}, u32[]{:S(2)}) collective-permute-start(bf16[128,1664]{1,0:T(8,128)(2,1)} %get-tuple-element.167.refs_0_), channel_id=1, source_target_pairs={{0,2},{1,3},{2,0},{3,1},{4,6},{5,7},{6,4},{7,5},{8,10},{9,11},{10,... | collective-permute-start | bytes 1277960 | tf_op jit(solution)/shard_map/ppermute | solution.py:741
  281.3 23.0 %collective-permute-start.42 = (bf16[128,1664]{1,0:T(8,128)(2,1)}, bf16[128,1664]{1,0:T(8,128)(2,1)}, u32[]{:S(2)}, u32[]{:S(2)}) collective-permute-start(bf16[128,1664]{1,0:T(8,128)(2,1)} %get-tuple-element.167.refs_0_), channel_id=1, source_target_pairs={{0,8},{1,9},{2,10},{3,11},{4,12},{5,13},{6,14},{7,15},{8,0},{9,1},... | collective-permute-start | bytes 1277960 | tf_op jit(solution)/shard_map/ppermute | solution.py:741
  289.9 16.8 %collective-permute-start.44 = (bf16[128,1664]{1,0:T(8,128)(2,1)}, bf16[128,1664]{1,0:T(8,128)(2,1)S(1)}, u32[]{:S(2)}, u32[]{:S(2)}) collective-permute-start(bf16[128,1664]{1,0:T(8,128)(2,1)} %collective-permute-done.43.refs_2_), channel_id=1, source_target_pairs={{0,8},{1,9},{2,10},{3,11},{4,12},{5,13},{6,14},{7,15},{8,0},{9,1},... | collective-permute-start | bytes 1277960 | tf_op jit(solution)/shard_map/ppermute | solution.py:741
  293.3 14.6 %collective-permute-start.46 = (bf16[128,1664]{1,0:T(8,128)(2,1)}, bf16[128,1664]{1,0:T(8,128)(2,1)S(1)}, u32[]{:S(2)}, u32[]{:S(2)}) collective-permute-start(bf16[128,1664]{1,0:T(8,128)(2,1)} %collective-permute-done.45.refs_4_), channel_id=1, source_target_pairs={{0,8},{1,9},{2,10},{3,11},{4,12},{5,13},{6,14},{7,15},{8,0},{9,1},... | collective-permute-start | bytes 1277960 | tf_op jit(solution)/shard_map/ppermute | solution.py:741
  304.3 15.2 %collective-permute-start.52 = (bf16[192,768]{1,0:T(8,128)(2,1)S(1)}, bf16[192,768]{1,0:T(8,128)(2,1)S(1)}, u32[]{:S(2)}, u32[]{:S(2)}) collective-permute-start(bf16[192,768]{1,0:T(8,128)(2,1)S(1)} %get-tuple-element.271), channel_id=1, source_target_pairs={{0,64},{1,65},{2,66},{3,67},{4,68},{5,69},{6,70},{7,71},{8,72},{9,... | collective-permute-start | bytes 884744 | tf_op jit(solution)/shard_map/ppermute | solution.py:741
  331.6 31.1 %collective-permute-start.55 = (bf16[384,1280]{1,0:T(8,128)(2,1)}, bf16[384,1280]{1,0:T(8,128)(2,1)S(1)}, u32[]{:S(2)}, u32[]{:S(2)}) collective-permute-start(bf16[384,1280]{1,0:T(8,128)(2,1)} %get-tuple-element.182), channel_id=1, source_target_pairs={{0,32},{1,33},{2,34},{3,35},{4,36},{5,37},{6,38},{7,39},{8,40},{9,... | collective-permute-start | bytes 2949128 | tf_op jit(solution)/shard_map/ppermute | solution.py:741
  333.3 44.8 %collective-permute-start.56 = (bf16[384,1280]{1,0:T(8,128)(2,1)}, bf16[384,1280]{1,0:T(8,128)(2,1)S(1)}, u32[]{:S(2)}, u32[]{:S(2)}) collective-permute-start(bf16[384,1280]{1,0:T(8,128)(2,1)} %get-tuple-element.183), channel_id=1, source_target_pairs={{0,64},{1,65},{2,66},{3,67},{4,68},{5,69},{6,70},{7,71},{8,72},{9,... | collective-permute-start | bytes 2949128 | tf_op jit(solution)/shard_map/ppermute | solution.py:741
  335.3 42.8 %collective-permute-start.57 = (bf16[384,1280]{1,0:T(8,128)(2,1)}, bf16[384,1280]{1,0:T(8,128)(2,1)S(1)}, u32[]{:S(2)}, u32[]{:S(2)}) collective-permute-start(bf16[384,1280]{1,0:T(8,128)(2,1)} %get-tuple-element.184), channel_id=1, source_target_pairs={{0,96},{1,97},{2,98},{3,99},{4,100},{5,101},{6,102},{7,103},{8,104... | collective-permute-start | bytes 2949128 | tf_op jit(solution)/shard_map/ppermute | solution.py:741
  406.9 19.1 %collective-permute-start.63 = (bf16[512,1536]{1,0:T(8,128)(2,1)}, bf16[512,1536]{1,0:T(8,128)(2,1)}, u32[]{:S(2)}, u32[]{:S(2)}) collective-permute-start(bf16[512,1536]{1,0:T(8,128)(2,1)} %get-tuple-element.202), channel_id=1, source_target_pairs={{0,8},{1,9},{2,10},{3,11},{4,12},{5,13},{6,14},{7,15},{8,0},{9,1},... | collective-permute-start | bytes 4718600 | tf_op jit(solution)/shard_map/ppermute | solution.py:741
  421.8 22.9 %collective-permute-start.71 = (bf16[192,1280]{1,0:T(8,128)(2,1)S(1)}, bf16[192,1280]{1,0:T(8,128)(2,1)S(1)}, u32[]{:S(2)}, u32[]{:S(2)}) collective-permute-start(bf16[192,1280]{1,0:T(8,128)(2,1)S(1)} %add_convert_fusion.3), channel_id=1, source_target_pairs={{0,64},{1,65},{2,66},{3,67},{4,68},{5,69},{6,70},{7,71},{8,72},{9,... | collective-permute-start | bytes 1474568 | tf_op jit(solution)/shard_map/ppermute | solution.py:741
  423.7 21.4 %collective-permute-start.72 = (bf16[192,1280]{1,0:T(8,128)(2,1)S(1)}, bf16[192,1280]{1,0:T(8,128)(2,1)S(1)}, u32[]{:S(2)}, u32[]{:S(2)}) collective-permute-start(bf16[192,1280]{1,0:T(8,128)(2,1)S(1)} %add_convert_fusion.3), channel_id=1, source_target_pairs={{0,96},{1,97},{2,98},{3,99},{4,100},{5,101},{6,102},{7,103},{8,104... | collective-permute-start | bytes 1474568 | tf_op jit(solution)/shard_map/ppermute | solution.py:741
  429.2 18.1 %collective-permute-start.64 = (bf16[128,1536]{1,0:T(8,128)(2,1)S(1)}, bf16[128,1536]{1,0:T(8,128)(2,1)S(1)}, u32[]{:S(2)}, u32[]{:S(2)}) collective-permute-start(bf16[128,1536]{1,0:T(8,128)(2,1)S(1)} %get-tuple-element.253), channel_id=1, source_target_pairs={{0,1},{1,2},{2,3},{3,0},{4,5},{5,6},{6,7},{7,4},{8,9},{9,10},{10,1... | collective-permute-start | bytes 1179656 | tf_op jit(solution)/shard_map/ppermute | solution.py:741
  430.3 18.9 %collective-permute-start.65 = (bf16[128,1536]{1,0:T(8,128)(2,1)S(1)}, bf16[128,1536]{1,0:T(8,128)(2,1)S(1)}, u32[]{:S(2)}, u32[]{:S(2)}) collective-permute-start(bf16[128,1536]{1,0:T(8,128)(2,1)S(1)} %get-tuple-element.252), channel_id=1, source_target_pairs={{0,2},{1,3},{2,0},{3,1},{4,6},{5,7},{6,4},{7,5},{8,10},{9,11},{10,... | collective-permute-start | bytes 1179656 | tf_op jit(solution)/shard_map/ppermute | solution.py:741
  433.8 15.7 %collective-permute-start.66 = (bf16[128,1536]{1,0:T(8,128)(2,1)S(1)}, bf16[128,1536]{1,0:T(8,128)(2,1)S(1)}, u32[]{:S(2)}, u32[]{:S(2)}) collective-permute-start(bf16[128,1536]{1,0:T(8,128)(2,1)S(1)} %get-tuple-element.251), channel_id=1, source_target_pairs={{0,3},{1,0},{2,1},{3,2},{4,7},{5,4},{6,5},{7,6},{8,11},{9,8},{10,9... | collective-permute-start | bytes 1179656 | tf_op jit(solution)/shard_map/ppermute | solution.py:741
  444.8 16.2 %collective-permute-start.80 = (bf16[192,768]{1,0:T(8,128)(2,1)}, bf16[192,768]{1,0:T(8,128)(2,1)}, u32[]{:S(2)}, u32[]{:S(2)}) collective-permute-start(bf16[192,768]{1,0:T(8,128)(2,1)} %add_convert_fusion.15), channel_id=1, source_target_pairs={{0,16},{1,17},{2,18},{3,19},{4,20},{5,21},{6,22},{7,23},{8,24},{9,... | collective-permute-start | bytes 884744 | tf_op jit(solution)/shard_map/ppermute | solution.py:741
  456.6 26.1 %collective-permute-start.67 = (bf16[128,3072]{1,0:T(8,128)(2,1)}, bf16[128,3072]{1,0:T(8,128)(2,1)}, u32[]{:S(2)}, u32[]{:S(2)}) collective-permute-start(bf16[128,3072]{1,0:T(8,128)(2,1)} %outputs.1), channel_id=1, source_target_pairs={{4,8},{5,9},{6,10},{7,11},{8,4},{9,5},{10,6},{11,7},{20,24},{21,25... | collective-permute-start | bytes 2359304 | tf_op jit(solution)/shard_map/ppermute | solution.py:741
  459.7 21.0 %collective-permute-start.69 = (bf16[384,512]{1,0:T(8,128)(2,1)}, bf16[384,512]{1,0:T(8,128)(2,1)}, u32[]{:S(2)}, u32[]{:S(2)}) collective-permute-start(bf16[384,512]{1,0:T(8,128)(2,1)} %get-tuple-element.264), channel_id=1, source_target_pairs={{0,32},{1,33},{2,34},{3,35},{4,36},{5,37},{6,38},{7,39},{8,40},{9,... | collective-permute-start | bytes 1179656 | tf_op jit(solution)/shard_map/ppermute | solution.py:741
  459.9 20.8 %collective-permute-start.74 = (bf16[384,512]{1,0:T(8,128)(2,1)}, bf16[384,512]{1,0:T(8,128)(2,1)}, u32[]{:S(2)}, u32[]{:S(2)}) collective-permute-start(bf16[384,512]{1,0:T(8,128)(2,1)} %get-tuple-element.266), channel_id=1, source_target_pairs={{0,64},{1,65},{2,66},{3,67},{4,68},{5,69},{6,70},{7,71},{8,72},{9,... | collective-permute-start | bytes 1179656 | tf_op jit(solution)/shard_map/ppermute | solution.py:741
  461.0 20.1 %collective-permute-start.75 = (bf16[384,512]{1,0:T(8,128)(2,1)}, bf16[384,512]{1,0:T(8,128)(2,1)}, u32[]{:S(2)}, u32[]{:S(2)}) collective-permute-start(bf16[384,512]{1,0:T(8,128)(2,1)} %get-tuple-element.265), channel_id=1, source_target_pairs={{0,96},{1,97},{2,98},{3,99},{4,100},{5,101},{6,102},{7,103},{8,104... | collective-permute-start | bytes 1179656 | tf_op jit(solution)/shard_map/ppermute | solution.py:741
  463.6 29.7 %collective-permute-start.81 = (bf16[192,768]{1,0:T(8,128)(2,1)S(1)}, bf16[192,768]{1,0:T(8,128)(2,1)S(1)}, u32[]{:S(2)}, u32[]{:S(2)}) collective-permute-start(bf16[192,768]{1,0:T(8,128)(2,1)S(1)} %add_convert_fusion.14), channel_id=1, source_target_pairs={{0,32},{1,33},{2,34},{3,35},{4,36},{5,37},{6,38},{7,39},{8,40},{9,... | collective-permute-start | bytes 884744 | tf_op jit(solution)/shard_map/ppermute | solution.py:741
  493.4 16.1 %collective-permute-start.84 = (bf16[4,192,768]{2,1,0:T(8,128)(2,1)S(1)}, bf16[4,192,768]{2,1,0:T(8,128)(2,1)S(1)}, u32[]{:S(2)}, u32[]{:S(2)}) collective-permute-start(bf16[4,192,768]{2,1,0:T(8,128)(2,1)S(1)} %pad_maximum_fusion.3.here_ref), channel_id=1, source_target_pairs={{0,8},{1,9},{2,10},{3,11},{4,12},{5,13},{6,14},{7,15},{8,0},{9,1},... | collective-permute-start | bytes 3538952 | tf_op jit(solution)/shard_map/ppermute | solution.py:741
  (119 other events, 1051.8 us)

commit v9 on v7

--- a/solution.py
+++ b/solution.py
@@ -1181,9 +1181,7 @@
         inner_all,
     )
     dz1, go1, dxt1, *bc_halves, mine, other, acc1, acch1, shared1 = back1
-    early1 = weight_products(place, [(xn1, dz1), (go1, grad_rows1)], split=False)
-    terms = scatter((mine, after(other, *home)), bc_halves, meanwhile=early1)
-    early1_far = send_far(early1)
+    terms = scatter((mine, after(other, *home)), bc_halves)
     [hidden_out] = row_call(
         functools.partial(last_kernel, inner_all),
         "last_output",
@@ -1198,6 +1196,8 @@
         [full, jax.ShapeDtypeStruct((rows, width + LANES), bf16)],
     )
     gathered_back = gather(sent, (rows,))
+    early1 = weight_products(place, [(xn1, after(dz1, sent)), (go1, grad_rows1)], split=False)
+    early1_far = send_far(early1)
 
     bc_at = channels + bc_rows
 
@@ -1208,19 +1208,17 @@
 
     dxt1 = with_bc(dxt1, sum(v[:, width:].astype(f32) for v in terms))
 
-    early1 = halve(sum_far(early1, after(early1_far, sent)))
     z0 = after(z0, early1)
-    early1 = sum_x(cut_x(early1))
     grad_rows0, dz0, dy0, go0, acc_gate0 = run_gate(place, gathered_back, z0, y0, w0, smalls[0][0])
-    dz0 = after(dz0, early1)
     early = weight_products(place, [(xn0, dz0), (go0, grad_rows0), (xn1, dxt1)])
     dy0 = after(dy0, *early)
     early = sum_x(early)
-    early1 = sum_beside(after(early1, dz0))
     back0 = run_scan(
         place, (dy0, dz0), xn0, xp0, bc0, dt0, hin0, (w0, wbc0, wdt[0]), smalls[0], pick, head_dim, inner_all
     )
     dxt0, *bc_halves, mine, other, acc0, acch0, shared0 = back0
+    early1 = sum_x(cut_x(halve(sum_far(early1, after(early1_far, early)))))
+    early1 = sum_beside(early1)
     shared = jnp.concatenate([shared0, shared1], axis=0)
     bc_sum, shared = scatter_with_sum(*bc_halves, shared, (early,))
     tiny_at = bc_at + bc_rows

time: 536 us -> 532 us (level)
  the two profiles are of different devices: /device:TPU:1 before, /device:TPU:65 now
where the time goes in v9:
time: 532 us; the launch traced here: 522 us
  Pallas kernels  168 us (32%)
  waiting for transfers between devices  143 us (27%)
  starting transfers between devices  136 us (26%)
  other arithmetic  37.6 us (7%)
  local copies, waits for them, and re-layouts  33.8 us (6%)
    ppermute x88, waiting for transfers between devices, send(): return lax.ppermute(v, ('dp', 'tensor'), pairs)  143 us
    ppermute x88, starting transfers between devices, send(): return lax.ppermute(v, ('dp', 'tensor'), pairs)  136 us
    pallas_call x5, Pallas kernels, span_call(): pl.pallas_call(kernel, grid_spec=pltpu.PrefetchScalarGridSpec(num_scalar_...  110 us
    pallas_call x3, Pallas kernels, weight_products(): pl.pallas_call(functools.partial(weight_kernel, len(pairs), split), grid_...  26 us
    pallas_call x6, Pallas kernels, row_call(): pl.pallas_call(kernel, grid=(1,), in_specs=[pl.BlockSpec((rows, v.shape[1...  18.1 us
    pallas_call x3, Pallas kernels, write_sums(): pl.pallas_call(functools.partial(write_kernel, plan, len(kept)), grid_spe...  14.7 us
    unnamed x165, local copies, waits for them, and re-layouts  12.6 us
  transfers between devices with their start and end apart: 88, of which 28 were waited for; matrix products, arithmetic and copies ran while one was open for 8% of the time, Pallas kernels for 25%

profile of v9, /device:TPU:65, one launch (start us, length us, event | category | flops | bytes accessed | tf_op | source)
XLA Modules:
  0.0 521.9 jit_solution(8370644413910127376)
XLA Ops:
  9.3 5.4 %collective-permute-start = (bf16[192,1536]{1,0:T(8,128)(2,1)}, bf16[192,1536]{1,0:T(8,128)(2,1)}, u32[]{:S(2)}, u32[]{:S(2)}) collective-permute-start(bf16[192,1536]{1,0:T(8,128)(2,1)} %pad_maximum_fusion.6), channel_id=1, source_target_pairs={{4,8},{5,9},{6,10},{7,11},{8,4},{9,5},{10,6},{11,7},{20,24},{21,25... | collective-permute-start | bytes 1769480 | tf_op jit(solution)/shard_map/ppermute | solution.py:741
  25.3 4.4 collective-permute-start.8
  39.2 12.5 %collective-permute-done.2.refs_2_ = bf16[160,1536]{1,0:T(8,128)(2,1)S(1)} collective-permute-done((bf16[160,1536]{1,0:T(8,128)(2,1)}, bf16[160,1536]{1,0:T(8,128)(2,1)S(1)}, u32[]{:S(2)}, u32[]{:S(2)}) %collective-permute-start.2) | collective-permute-done | bytes 491552 | tf_op jit(solution)/shard_map/ppermute | solution.py:741
  54.3 4.3 collective-permute-start.9
  58.5 3.1 collective-permute-start.10
  62.8 4.1 collective-permute-start.12
  66.9 3.1 collective-permute-done.8.refs_9_
  70.0 22.0 %layer_forward.2 = (bf16[1536,1152]{1,0:T(8,128)(2,1)}, bf16[1024,1536]{1,0:T(8,128)(2,1)}, bf16[256,1536]{1,0:T(8,128)(2,1)}, bf16[1024,384]{1,0:T(8,128)(2,1)}...) custom-call(s32[4]{0:T(128)} %pad_add_fusion.2.place_ref, ...), custom_call_target="tpu_custom_call" | custom-call | flops 20000000000 | bytes 26501120 | tf_op jit(solution)/shard_map/layer_forward/pallas_call | solution.py:512
  101.2 4.6 collective-permute-start.28
  108.7 17.0 %collective-permute-done.14.a_ref = bf16[128,1664]{1,0:T(8,128)(2,1)S(1)} collective-permute-done((bf16[128,1664]{1,0:T(8,128)(2,1)S(1)}, bf16[128,1664]{1,0:T(8,128)(2,1)S(1)}, u32[]{:S(2)}, u32[]{:S(2)}) %collective-permute-start.14) | collective-permute-done | bytes 426016 | tf_op jit(solution)/shard_map/ppermute | solution.py:741
  128.3 3.3 middle_norm.1
  136.6 6.1 %collective-permute-done.18.refs_2_ = bf16[128,1536]{1,0:T(8,128)(2,1)S(1)} collective-permute-done((bf16[128,1536]{1,0:T(8,128)(2,1)}, bf16[128,1536]{1,0:T(8,128)(2,1)S(1)}, u32[]{:S(2)}, u32[]{:S(2)}) %collective-permute-start.18) | collective-permute-done | bytes 393248 | tf_op jit(solution)/shard_map/ppermute | solution.py:741
  145.7 5.5 %collective-permute-done.22.refs_6_ = bf16[128,1536]{1,0:T(8,128)(2,1)S(1)} collective-permute-done((bf16[128,1536]{1,0:T(8,128)(2,1)}, bf16[128,1536]{1,0:T(8,128)(2,1)S(1)}, u32[]{:S(2)}, u32[]{:S(2)}) %collective-permute-start.22) | collective-permute-done | bytes 393248 | tf_op jit(solution)/shard_map/ppermute | solution.py:741
  154.5 25.9 %layer_forward.3 = (bf16[1536,1152]{1,0:T(8,128)(2,1)}, bf16[1024,1536]{1,0:T(8,128)(2,1)}, bf16[256,1536]{1,0:T(8,128)(2,1)}, bf16[1024,384]{1,0:T(8,128)(2,1)}...) custom-call(s32[4]{0:T(128)} %pad_add_fusion.2.place_ref, ...), custom_call_target="tpu_custom_call" | custom-call | flops 20000000000 | bytes 34398208 | tf_op jit(solution)/shard_map/layer_forward/pallas_call | solution.py:512
  181.1 3.3 collective-permute-done.29
  185.2 3.1 collective-permute-start.30
  200.8 27.2 %scan_backward.2 = (bf16[1024,384]{1,0:T(8,128)(2,1)}, bf16[1024,384]{1,0:T(8,128)(2,1)}, bf16[1024,512]{1,0:T(8,128)(2,1)}, bf16[512,256]{1,0:T(8,128)(2,1)}, b...) custom-call(s32[4]{0:T(128)} %pad_add_fusion.2.place_ref, ...), custom_call_target="tpu_custom_call" | custom-call | flops 28000000000 | bytes 21512192 | tf_op jit(solution)/shard_map/scan_backward/pallas_call | solution.py:512
  228.0 3.0 collective-permute-start.37
  231.1 3.5 collective-permute-done.38
  240.9 8.2 %collective-permute-done.39.a_ref = bf16[128,1792]{1,0:T(8,128)(2,1)S(1)} collective-permute-done((bf16[128,1792]{1,0:T(8,128)(2,1)S(1)}, bf16[128,1792]{1,0:T(8,128)(2,1)S(1)}, u32[]{:S(2)}, u32[]{:S(2)}) %collective-permute-start.39) | collective-permute-done | bytes 458784 | tf_op jit(solution)/shard_map/ppermute | solution.py:741
  249.2 9.9 %collective-permute-done.40.b_ref = bf16[128,1792]{1,0:T(8,128)(2,1)S(1)} collective-permute-done((bf16[128,1792]{1,0:T(8,128)(2,1)S(1)}, bf16[128,1792]{1,0:T(8,128)(2,1)S(1)}, u32[]{:S(2)}, u32[]{:S(2)}) %collective-permute-start.40) | collective-permute-done | bytes 458784 | tf_op jit(solution)/shard_map/ppermute | solution.py:741
  262.5 3.8 between_layers.1
  272.8 5.4 %collective-permute-done.43.refs_2_ = bf16[128,1664]{1,0:T(8,128)(2,1)S(1)} collective-permute-done((bf16[128,1664]{1,0:T(8,128)(2,1)}, bf16[128,1664]{1,0:T(8,128)(2,1)S(1)}, u32[]{:S(2)}, u32[]{:S(2)}) %collective-permute-start.43) | collective-permute-done | bytes 426016 | tf_op jit(solution)/shard_map/ppermute | solution.py:741
  282.9 5.7 %collective-permute-done.47.refs_6_ = bf16[128,1664]{1,0:T(8,128)(2,1)} collective-permute-done((bf16[128,1664]{1,0:T(8,128)(2,1)}, bf16[128,1664]{1,0:T(8,128)(2,1)}, u32[]{:S(2)}, u32[]{:S(2)}) %collective-permute-start.47) | collective-permute-done | bytes 426016 | tf_op jit(solution)/shard_map/ppermute | solution.py:741
  289.9 8.3 %weight_products.3 = bf16[1536,768]{1,0:T(8,128)(2,1)} custom-call(s32[4]{0:T(128)} %pad_add_fusion.2.place_ref, bf16[1024,1536]{1,0:T(8,128)(2,1)} %get-tuple-element.143.refs_4_.refs_0_.refs_2_, bf16[1024,384]{1,0:T(8,128)(2,1)} %get-tuple-element.160.refs_1_, bf16[1024,384]{1,0:T(8,128)(2,1)} %get-tuple-element.162.refs_2_, ...), custom_call_target="tpu_custom_call" | custom-call | flops 2415919104 | bytes 8000000 | tf_op jit(solution)/shard_map/weight_products/pallas_call | solution.py:708
  298.2 4.3 collective-permute-start.71
  304.8 8.4 %gate_backward.1 = (bf16[1024,1536]{1,0:T(8,128)(2,1)}, bf16[1024,384]{1,0:T(8,128)(2,1)}, f32[1024,384]{1,0:T(8,128)}, bf16[1024,384]{1,0:T(8,128)(2,1)}, f32[8,384]{1,0:T(8,128)}) custom-call(s32[4]{0:T(128)} %pad_add_fusion.2.place_ref, bf16[128,1664]{1,0:T(8,128)(2,1)} %get-tuple-element.158.refs_0_, bf16[128,1664]{1,0:T(8,128)(2,1)} %collective-permute-done.42.refs_1_, ...), custom_call_target="tpu_custom_call" | custom-call | flops 6000000000 | bytes 14835712 | tf_op jit(solution)/shard_map/gate_backward/pallas_call | solution.py:512
  313.2 11.3 %weight_products.4 = (bf16[384,1280]{1,0:T(8,128)(2,1)}, bf16[384,1280]{1,0:T(8,128)(2,1)}, bf16[384,1280]{1,0:T(8,128)(2,1)}, bf16[384,1280]{1,0:T(8,128)(2,1)}) custom-call(s32[4]{0:T(128)} %pad_add_fusion.2.place_ref, bf16[1024,1536]{1,0:T(8,128)(2,1)} %get-tuple-element.168.refs_0_.refs_2_, bf16[1024,384]{1,0:T(8,128)(2,1)} %get-tuple-element.169.refs_1_, ...), custom_call_target="tpu_custom_call" | custom-call | flops 4026531840 | bytes 8000000 | tf_op jit(solution)/shard_map/weight_products/pallas_call | solution.py:708
  329.3 26.1 %scan_backward.3 = (bf16[1024,512]{1,0:T(8,128)(2,1)}, bf16[512,256]{1,0:T(8,128)(2,1)}, bf16[512,256]{1,0:T(8,128)(2,1)}, bf16[512,1536]{1,0:T(8,128)(2,1)}, bf...) custom-call(s32[4]{0:T(128)} %pad_add_fusion.2.place_ref, ...), custom_call_target="tpu_custom_call" | custom-call | flops 28000000000 | bytes 19120128 | tf_op jit(solution)/shard_map/scan_backward/pallas_call | solution.py:512
  356.7 12.3 %collective-permute-done.51 = bf16[384,1280]{1,0:T(8,128)(2,1)S(1)} collective-permute-done((bf16[384,1280]{1,0:T(8,128)(2,1)}, bf16[384,1280]{1,0:T(8,128)(2,1)S(1)}, u32[]{:S(2)}, u32[]{:S(2)}) %collective-permute-start.51) | collective-permute-done | bytes 983072 | tf_op jit(solution)/shard_map/ppermute | solution.py:741
  369.5 3.4 collective-permute-start.56
  396.5 6.5 %weight_products.5 = (bf16[384,512]{1,0:T(8,128)(2,1)}, bf16[384,512]{1,0:T(8,128)(2,1)}, bf16[384,512]{1,0:T(8,128)(2,1)}, bf16[384,512]{1,0:T(8,128)(2,1)}) custom-call(s32[4]{0:T(128)} %pad_add_fusion.2.place_ref, bf16[1024,1536]{1,0:T(8,128)(2,1)} %get-tuple-element.168.refs_0_.refs_2_, bf16[1024,512]{1,0:T(8,128)(2,1)} %pad_add_fusion.refs_1_), custom_call_target="tpu_custom_call" | custom-call | flops 1610612736 | bytes 8000000 | tf_op jit(solution)/shard_map/weight_products/pallas_call | solution.py:708
  406.4 2.9 collective-permute-start.74
  410.8 6.1 %collective-permute-done.63 = bf16[192,1280]{1,0:T(8,128)(2,1)S(1)} collective-permute-done((bf16[192,1280]{1,0:T(8,128)(2,1)S(1)}, bf16[192,1280]{1,0:T(8,128)(2,1)S(1)}, u32[]{:S(2)}, u32[]{:S(2)}) %collective-permute-start.63) | collective-permute-done | bytes 491552 | tf_op jit(solution)/shard_map/ppermute | solution.py:741
  425.4 7.8 %collective-permute-done.60.b_ref = bf16[128,1536]{1,0:T(8,128)(2,1)S(1)} collective-permute-done((bf16[128,1536]{1,0:T(8,128)(2,1)S(1)}, bf16[128,1536]{1,0:T(8,128)(2,1)S(1)}, u32[]{:S(2)}, u32[]{:S(2)}) %collective-permute-start.60) | collective-permute-done | bytes 393248 | tf_op jit(solution)/shard_map/ppermute | solution.py:741
  434.1 8.0 %collective-permute-done.61.c_ref = bf16[128,1536]{1,0:T(8,128)(2,1)S(1)} collective-permute-done((bf16[128,1536]{1,0:T(8,128)(2,1)S(1)}, bf16[128,1536]{1,0:T(8,128)(2,1)S(1)}, u32[]{:S(2)}, u32[]{:S(2)}) %collective-permute-start.61) | collective-permute-done | bytes 393248 | tf_op jit(solution)/shard_map/ppermute | solution.py:741
  442.9 3.5 outputs.1
  448.6 6.9 %collective-permute-start.62 = (bf16[128,3072]{1,0:T(8,128)(2,1)}, bf16[128,3072]{1,0:T(8,128)(2,1)S(1)}, u32[]{:S(2)}, u32[]{:S(2)}) collective-permute-start(bf16[128,3072]{1,0:T(8,128)(2,1)} %outputs.1), channel_id=1, source_target_pairs={{4,8},{5,9},{6,10},{7,11},{8,4},{9,5},{10,6},{11,7},{20,24},{21,25... | collective-permute-start | bytes 2359304 | tf_op jit(solution)/shard_map/ppermute | solution.py:741
  456.3 3.4 collective-permute-done.65
  461.6 5.3 %collective-permute-done.66 = bf16[384,512]{1,0:T(8,128)(2,1)S(1)} collective-permute-done((bf16[384,512]{1,0:T(8,128)(2,1)S(1)}, bf16[384,512]{1,0:T(8,128)(2,1)S(1)}, u32[]{:S(2)}, u32[]{:S(2)}) %collective-permute-start.66) | collective-permute-done | bytes 393248 | tf_op jit(solution)/shard_map/ppermute | solution.py:741
  466.9 3.9 collective-permute-start.82
  471.1 5.5 %collective-permute-start.67 = (bf16[384,512]{1,0:T(8,128)(2,1)S(1)}, bf16[384,512]{1,0:T(8,128)(2,1)S(1)}, u32[]{:S(2)}, u32[]{:S(2)}) collective-permute-start(bf16[384,512]{1,0:T(8,128)(2,1)S(1)} %add_convert_fusion.8), channel_id=1, source_target_pairs={{4,0},{5,1},{6,2},{7,3},{8,12},{9,13},{10,14},{11,15},{20,16},{21,... | collective-permute-start | bytes 1179656 | tf_op jit(solution)/shard_map/ppermute | solution.py:741
  482.9 3.0 collective-permute-done.68
  487.1 5.3 %collective-permute-done.69 = bf16[192,512]{1,0:T(8,128)(2,1)S(1)} collective-permute-done((bf16[192,512]{1,0:T(8,128)(2,1)S(1)}, bf16[192,512]{1,0:T(8,128)(2,1)S(1)}, u32[]{:S(2)}, u32[]{:S(2)}) %collective-permute-start.69) | collective-permute-done | bytes 196640 | tf_op jit(solution)/shard_map/ppermute | solution.py:741
  492.7 3.4 collective-permute-start.85
  498.1 6.2 %write_sums.3 = (f32[2,4,2,192,384]{4,3,2,1,0:T(8,128)}, f32[2,384,1536]{2,1,0:T(8,128)}, f32[2,4,2,192,384]{4,3,2,1,0:T(8,128)}, f32[1,4,2,192,128]{4,3,2,1,0:T(8,128)}) custom-call(s32[4]{0:T(128)} %pad_add_fusion.2.place_ref, bf16[4,192,1280]{2,1,0:T(8,128)(2,1)} %copy-done.1, bf16[4,192,1280]{2,1,0:T(8,128)(2,1)} %copy-done.6), custom_call_target="tpu_custom_call" | custom-call | tf_op jit(solution)/shard_map/write_sums/pallas_call | solution.py:941
  505.4 4.7 write_sums.4
  514.9 3.8 write_sums.5
  (402 shorter events, 164.8 us)
Async XLA Ops:
  25.3 44.6 %collective-permute-start.8 = (bf16[1536,1152]{1,0:T(8,128)(2,1)}, bf16[1536,1152]{1,0:T(8,128)(2,1)}, u32[]{:S(2)}, u32[]{:S(2)}) collective-permute-start(bf16[1536,1152]{1,0:T(8,128)(2,1)} %pad_maximum_fusion.refs_8_), channel_id=1, source_target_pairs={{4,8},{5,9},{6,10},{7,11},{8,4},{9,5},{10,6},{11,7},{20,24},{21,25... | collective-permute-start | bytes 10616840 | tf_op jit(solution)/shard_map/ppermute | solution.py:741
  33.9 17.8 %collective-permute-start.2 = (bf16[160,1536]{1,0:T(8,128)(2,1)}, bf16[160,1536]{1,0:T(8,128)(2,1)S(1)}, u32[]{:S(2)}, u32[]{:S(2)}) collective-permute-start(bf16[160,1536]{1,0:T(8,128)(2,1)} %first_norm.1.refs_0_), channel_id=1, source_target_pairs={{0,1},{1,2},{2,3},{3,0},{4,5},{5,6},{6,7},{7,4},{8,9},{9,10},{10,1... | collective-permute-start | bytes 1474568 | tf_op jit(solution)/shard_map/ppermute | solution.py:741
  35.2 16.4 %collective-permute-start.4 = (bf16[160,1536]{1,0:T(8,128)(2,1)}, bf16[160,1536]{1,0:T(8,128)(2,1)S(1)}, u32[]{:S(2)}, u32[]{:S(2)}) collective-permute-start(bf16[160,1536]{1,0:T(8,128)(2,1)} %first_norm.1.refs_0_), channel_id=1, source_target_pairs={{0,3},{1,0},{2,1},{3,2},{4,7},{5,4},{6,5},{7,6},{8,11},{9,8},{10,9... | collective-permute-start | bytes 1474568 | tf_op jit(solution)/shard_map/ppermute | solution.py:741
  35.3 16.8 %collective-permute-start.6 = (bf16[160,1536]{1,0:T(8,128)(2,1)}, bf16[160,1536]{1,0:T(8,128)(2,1)S(1)}, u32[]{:S(2)}, u32[]{:S(2)}) collective-permute-start(bf16[160,1536]{1,0:T(8,128)(2,1)} %first_norm.1.refs_0_), channel_id=1, source_target_pairs={{0,2},{1,3},{2,0},{3,1},{4,6},{5,7},{6,4},{7,5},{8,10},{9,11},{10,... | collective-permute-start | bytes 1474568 | tf_op jit(solution)/shard_map/ppermute | solution.py:741
  37.0 17.3 %collective-permute-start.1 = (bf16[160,1536]{1,0:T(8,128)(2,1)}, bf16[160,1536]{1,0:T(8,128)(2,1)S(1)}, u32[]{:S(2)}, u32[]{:S(2)}) collective-permute-start(bf16[160,1536]{1,0:T(8,128)(2,1)} %first_norm.1.refs_0_), channel_id=1, source_target_pairs={{0,8},{1,9},{2,10},{3,11},{4,12},{5,13},{6,14},{7,15},{8,0},{9,1},... | collective-permute-start | bytes 1474568 | tf_op jit(solution)/shard_map/ppermute | solution.py:741
  54.3 37.7 %collective-permute-start.9 = (bf16[160,1536]{1,0:T(8,128)(2,1)S(1)}, bf16[160,1536]{1,0:T(8,128)(2,1)S(1)}, u32[]{:S(2)}, u32[]{:S(2)}) collective-permute-start(bf16[160,1536]{1,0:T(8,128)(2,1)S(1)} %pad_maximum_fusion.7), channel_id=1, source_target_pairs={{4,8},{5,9},{6,10},{7,11},{8,4},{9,5},{10,6},{11,7},{20,24},{21,25... | collective-permute-start | bytes 1474568 | tf_op jit(solution)/shard_map/ppermute | solution.py:741
  58.5 34.2 %collective-permute-start.10 = (bf16[160,1536]{1,0:T(8,128)(2,1)S(1)}, bf16[160,1536]{1,0:T(8,128)(2,1)S(1)}, u32[]{:S(2)}, u32[]{:S(2)}) collective-permute-start(bf16[160,1536]{1,0:T(8,128)(2,1)S(1)} %pad_maximum_fusion.7), channel_id=1, source_target_pairs={{0,1},{1,2},{2,3},{3,0},{4,9},{5,10},{6,11},{7,8},{8,5},{9,6},{10,... | collective-permute-start | bytes 1474568 | tf_op jit(solution)/shard_map/ppermute | solution.py:741
  61.7 31.1 %collective-permute-start.11 = (bf16[160,1536]{1,0:T(8,128)(2,1)S(1)}, bf16[160,1536]{1,0:T(8,128)(2,1)S(1)}, u32[]{:S(2)}, u32[]{:S(2)}) collective-permute-start(bf16[160,1536]{1,0:T(8,128)(2,1)S(1)} %pad_maximum_fusion.7), channel_id=1, source_target_pairs={{0,3},{1,0},{2,1},{3,2},{4,11},{5,8},{6,9},{7,10},{8,7},{9,4},{10,... | collective-permute-start | bytes 1474568 | tf_op jit(solution)/shard_map/ppermute | solution.py:741
  62.8 30.0 %collective-permute-start.12 = (bf16[160,1536]{1,0:T(8,128)(2,1)S(1)}, bf16[160,1536]{1,0:T(8,128)(2,1)S(1)}, u32[]{:S(2)}, u32[]{:S(2)}) collective-permute-start(bf16[160,1536]{1,0:T(8,128)(2,1)S(1)} %pad_maximum_fusion.7), channel_id=1, source_target_pairs={{0,2},{1,3},{2,0},{3,1},{4,10},{5,11},{6,8},{7,9},{8,6},{9,7},{10,... | collective-permute-start | bytes 1474568 | tf_op jit(solution)/shard_map/ppermute | solution.py:741
  101.2 52.6 %collective-permute-start.28 = (bf16[1536,1152]{1,0:T(8,128)(2,1)S(1)}, bf16[1536,1152]{1,0:T(8,128)(2,1)}, u32[]{:S(2)}, u32[]{:S(2)}) collective-permute-start(bf16[1536,1152]{1,0:T(8,128)(2,1)S(1)} %pad_maximum_fusion.1.refs_16_), channel_id=1, source_target_pairs={{4,8},{5,9},{6,10},{7,11},{8,4},{9,5},{10,6},{11,7},{20,24},{21,25... | collective-permute-start | bytes 10616840 | tf_op jit(solution)/shard_map/ppermute | solution.py:741
  105.7 19.9 %collective-permute-start.14 = (bf16[128,1664]{1,0:T(8,128)(2,1)S(1)}, bf16[128,1664]{1,0:T(8,128)(2,1)S(1)}, u32[]{:S(2)}, u32[]{:S(2)}) collective-permute-start(bf16[128,1664]{1,0:T(8,128)(2,1)S(1)} %get-tuple-element.239), channel_id=1, source_target_pairs={{0,1},{1,2},{2,3},{3,0},{4,5},{5,6},{6,7},{7,4},{8,9},{9,10},{10,1... | collective-permute-start | bytes 1277960 | tf_op jit(solution)/shard_map/ppermute | solution.py:741
  107.2 18.5 %collective-permute-start.15 = (bf16[128,1664]{1,0:T(8,128)(2,1)S(1)}, bf16[128,1664]{1,0:T(8,128)(2,1)S(1)}, u32[]{:S(2)}, u32[]{:S(2)}) collective-permute-start(bf16[128,1664]{1,0:T(8,128)(2,1)S(1)} %get-tuple-element.238), channel_id=1, source_target_pairs={{0,2},{1,3},{2,0},{3,1},{4,6},{5,7},{6,4},{7,5},{8,10},{9,11},{10,... | collective-permute-start | bytes 1277960 | tf_op jit(solution)/shard_map/ppermute | solution.py:741
  107.2 20.3 %collective-permute-start.16 = (bf16[128,1664]{1,0:T(8,128)(2,1)S(1)}, bf16[128,1664]{1,0:T(8,128)(2,1)S(1)}, u32[]{:S(2)}, u32[]{:S(2)}) collective-permute-start(bf16[128,1664]{1,0:T(8,128)(2,1)S(1)} %get-tuple-element.237), channel_id=1, source_target_pairs={{0,3},{1,0},{2,1},{3,2},{4,7},{5,4},{6,5},{7,6},{8,11},{9,8},{10,9... | collective-permute-start | bytes 1277960 | tf_op jit(solution)/shard_map/ppermute | solution.py:741
  108.4 23.2 %collective-permute-start.24 = (bf16[160,1536]{1,0:T(8,128)(2,1)S(1)}, bf16[160,1536]{1,0:T(8,128)(2,1)S(1)}, u32[]{:S(2)}, u32[]{:S(2)}) collective-permute-start(bf16[160,1536]{1,0:T(8,128)(2,1)S(1)} %copy-done.7), channel_id=1, source_target_pairs={{0,8},{1,9},{2,10},{3,11},{4,12},{5,13},{6,14},{7,15},{8,0},{9,1},... | collective-permute-start | bytes 1474568 | tf_op jit(solution)/shard_map/ppermute | solution.py:741
  133.1 18.1 %collective-permute-start.22 = (bf16[128,1536]{1,0:T(8,128)(2,1)}, bf16[128,1536]{1,0:T(8,128)(2,1)S(1)}, u32[]{:S(2)}, u32[]{:S(2)}) collective-permute-start(bf16[128,1536]{1,0:T(8,128)(2,1)} %get-tuple-element.130.refs_0_), channel_id=1, source_target_pairs={{0,2},{1,3},{2,0},{3,1},{4,6},{5,7},{6,4},{7,5},{8,10},{9,11},{10,... | collective-permute-start | bytes 1179656 | tf_op jit(solution)/shard_map/ppermute | solution.py:741
  135.4 17.8 %collective-permute-start.17 = (bf16[128,1536]{1,0:T(8,128)(2,1)}, bf16[128,1536]{1,0:T(8,128)(2,1)S(1)}, u32[]{:S(2)}, u32[]{:S(2)}) collective-permute-start(bf16[128,1536]{1,0:T(8,128)(2,1)} %get-tuple-element.130.refs_0_), channel_id=1, source_target_pairs={{0,8},{1,9},{2,10},{3,11},{4,12},{5,13},{6,14},{7,15},{8,0},{9,1},... | collective-permute-start | bytes 1179656 | tf_op jit(solution)/shard_map/ppermute | solution.py:741
  194.8 33.2 %collective-permute-start.34 = (bf16[128,1664]{1,0:T(8,128)(2,1)S(1)}, bf16[128,1664]{1,0:T(8,128)(2,1)S(1)}, u32[]{:S(2)}, u32[]{:S(2)}) collective-permute-start(bf16[128,1664]{1,0:T(8,128)(2,1)S(1)} %get-tuple-element.236), channel_id=1, source_target_pairs={{0,1},{1,2},{2,3},{3,0},{4,5},{5,6},{6,7},{7,4},{8,9},{9,10},{10,1... | collective-permute-start | bytes 1277960 | tf_op jit(solution)/shard_map/ppermute | solution.py:741
  196.1 31.9 %collective-permute-start.35 = (bf16[128,1664]{1,0:T(8,128)(2,1)S(1)}, bf16[128,1664]{1,0:T(8,128)(2,1)S(1)}, u32[]{:S(2)}, u32[]{:S(2)}) collective-permute-start(bf16[128,1664]{1,0:T(8,128)(2,1)S(1)} %get-tuple-element.235), channel_id=1, source_target_pairs={{0,2},{1,3},{2,0},{3,1},{4,6},{5,7},{6,4},{7,5},{8,10},{9,11},{10,... | collective-permute-start | bytes 1277960 | tf_op jit(solution)/shard_map/ppermute | solution.py:741
  196.4 31.6 %collective-permute-start.36 = (bf16[128,1664]{1,0:T(8,128)(2,1)S(1)}, bf16[128,1664]{1,0:T(8,128)(2,1)S(1)}, u32[]{:S(2)}, u32[]{:S(2)}) collective-permute-start(bf16[128,1664]{1,0:T(8,128)(2,1)S(1)} %get-tuple-element.234), channel_id=1, source_target_pairs={{0,3},{1,0},{2,1},{3,2},{4,7},{5,4},{6,5},{7,6},{8,11},{9,8},{10,9... | collective-permute-start | bytes 1277960 | tf_op jit(solution)/shard_map/ppermute | solution.py:741
  237.5 21.6 %collective-permute-start.40 = (bf16[128,1792]{1,0:T(8,128)(2,1)S(1)}, bf16[128,1792]{1,0:T(8,128)(2,1)S(1)}, u32[]{:S(2)}, u32[]{:S(2)}) collective-permute-start(bf16[128,1792]{1,0:T(8,128)(2,1)S(1)} %pad_maximum_fusion.9), channel_id=1, source_target_pairs={{0,2},{1,3},{2,0},{3,1},{4,6},{5,7},{6,4},{7,5},{8,10},{9,11},{10,... | collective-permute-start | bytes 1376264 | tf_op jit(solution)/shard_map/ppermute | solution.py:741
  239.1 21.5 %collective-permute-start.41 = (bf16[128,1792]{1,0:T(8,128)(2,1)S(1)}, bf16[128,1792]{1,0:T(8,128)(2,1)S(1)}, u32[]{:S(2)}, u32[]{:S(2)}) collective-permute-start(bf16[128,1792]{1,0:T(8,128)(2,1)S(1)} %pad_maximum_fusion.10), channel_id=1, source_target_pairs={{0,3},{1,0},{2,1},{3,2},{4,7},{5,4},{6,5},{7,6},{8,11},{9,8},{10,9... | collective-permute-start | bytes 1376264 | tf_op jit(solution)/shard_map/ppermute | solution.py:741
  269.2 19.4 %collective-permute-start.47 = (bf16[128,1664]{1,0:T(8,128)(2,1)}, bf16[128,1664]{1,0:T(8,128)(2,1)}, u32[]{:S(2)}, u32[]{:S(2)}) collective-permute-start(bf16[128,1664]{1,0:T(8,128)(2,1)} %get-tuple-element.158.refs_0_), channel_id=1, source_target_pairs={{0,2},{1,3},{2,0},{3,1},{4,6},{5,7},{6,4},{7,5},{8,10},{9,11},{10,... | collective-permute-start | bytes 1277960 | tf_op jit(solution)/shard_map/ppermute | solution.py:741
  271.0 32.8 %collective-permute-start.42 = (bf16[128,1664]{1,0:T(8,128)(2,1)}, bf16[128,1664]{1,0:T(8,128)(2,1)}, u32[]{:S(2)}, u32[]{:S(2)}) collective-permute-start(bf16[128,1664]{1,0:T(8,128)(2,1)} %get-tuple-element.158.refs_0_), channel_id=1, source_target_pairs={{0,8},{1,9},{2,10},{3,11},{4,12},{5,13},{6,14},{7,15},{8,0},{9,1},... | collective-permute-start | bytes 1277960 | tf_op jit(solution)/shard_map/ppermute | solution.py:741
  278.2 25.5 %collective-permute-start.44 = (bf16[128,1664]{1,0:T(8,128)(2,1)S(1)}, bf16[128,1664]{1,0:T(8,128)(2,1)S(1)}, u32[]{:S(2)}, u32[]{:S(2)}) collective-permute-start(bf16[128,1664]{1,0:T(8,128)(2,1)S(1)} %collective-permute-done.43.refs_2_), channel_id=1, source_target_pairs={{0,8},{1,9},{2,10},{3,11},{4,12},{5,13},{6,14},{7,15},{8,0},{9,1},... | collective-permute-start | bytes 1277960 | tf_op jit(solution)/shard_map/ppermute | solution.py:741
  280.5 23.3 %collective-permute-start.46 = (bf16[128,1664]{1,0:T(8,128)(2,1)S(1)}, bf16[128,1664]{1,0:T(8,128)(2,1)S(1)}, u32[]{:S(2)}, u32[]{:S(2)}) collective-permute-start(bf16[128,1664]{1,0:T(8,128)(2,1)S(1)} %collective-permute-done.45.refs_4_), channel_id=1, source_target_pairs={{0,8},{1,9},{2,10},{3,11},{4,12},{5,13},{6,14},{7,15},{8,0},{9,1},... | collective-permute-start | bytes 1277960 | tf_op jit(solution)/shard_map/ppermute | solution.py:741
  288.6 15.2 %collective-permute-start.48 = (bf16[128,1664]{1,0:T(8,128)(2,1)}, bf16[128,1664]{1,0:T(8,128)(2,1)S(1)}, u32[]{:S(2)}, u32[]{:S(2)}) collective-permute-start(bf16[128,1664]{1,0:T(8,128)(2,1)} %collective-permute-done.47.refs_6_), channel_id=1, source_target_pairs={{0,8},{1,9},{2,10},{3,11},{4,12},{5,13},{6,14},{7,15},{8,0},{9,1},... | collective-permute-start | bytes 1277960 | tf_op jit(solution)/shard_map/ppermute | solution.py:741
  298.2 92.9 %collective-permute-start.71 = (bf16[1536,768]{1,0:T(8,128)(2,1)}, bf16[1536,768]{1,0:T(8,128)(2,1)S(1)}, u32[]{:S(2)}, u32[]{:S(2)}) collective-permute-start(bf16[1536,768]{1,0:T(8,128)(2,1)} %weight_products.3), channel_id=1, source_target_pairs={{4,0},{5,1},{6,2},{7,3},{8,12},{9,13},{10,14},{11,15},{20,16},{21,... | collective-permute-start | bytes 7077896 | tf_op jit(solution)/shard_map/ppermute | solution.py:741
  324.4 32.3 %collective-permute-start.50 = (bf16[384,1280]{1,0:T(8,128)(2,1)}, bf16[384,1280]{1,0:T(8,128)(2,1)S(1)}, u32[]{:S(2)}, u32[]{:S(2)}) collective-permute-start(bf16[384,1280]{1,0:T(8,128)(2,1)} %get-tuple-element.174), channel_id=1, source_target_pairs={{0,32},{1,33},{2,34},{3,35},{4,36},{5,37},{6,38},{7,39},{8,40},{9,... | collective-permute-start | bytes 2949128 | tf_op jit(solution)/shard_map/ppermute | solution.py:741
  325.6 43.3 %collective-permute-start.51 = (bf16[384,1280]{1,0:T(8,128)(2,1)}, bf16[384,1280]{1,0:T(8,128)(2,1)S(1)}, u32[]{:S(2)}, u32[]{:S(2)}) collective-permute-start(bf16[384,1280]{1,0:T(8,128)(2,1)} %get-tuple-element.175), channel_id=1, source_target_pairs={{0,64},{1,65},{2,66},{3,67},{4,68},{5,69},{6,70},{7,71},{8,72},{9,... | collective-permute-start | bytes 2949128 | tf_op jit(solution)/shard_map/ppermute | solution.py:741
  328.1 40.9 %collective-permute-start.52 = (bf16[384,1280]{1,0:T(8,128)(2,1)}, bf16[384,1280]{1,0:T(8,128)(2,1)S(1)}, u32[]{:S(2)}, u32[]{:S(2)}) collective-permute-start(bf16[384,1280]{1,0:T(8,128)(2,1)} %get-tuple-element.176), channel_id=1, source_target_pairs={{0,96},{1,97},{2,98},{3,99},{4,100},{5,101},{6,102},{7,103},{8,104... | collective-permute-start | bytes 2949128 | tf_op jit(solution)/shard_map/ppermute | solution.py:741
  356.4 16.5 %collective-permute-start.49 = (bf16[544,256]{1,0:T(8,128)(2,1)S(1)}, bf16[544,256]{1,0:T(8,128)(2,1)S(1)}, u32[]{:S(2)}, u32[]{:S(2)}) collective-permute-start(bf16[544,256]{1,0:T(8,128)(2,1)S(1)} %pad_maximum_fusion.11), channel_id=1, source_target_pairs={{0,8},{1,9},{2,10},{3,11},{4,12},{5,13},{6,14},{7,15},{8,0},{9,1},... | collective-permute-start | bytes 835592 | tf_op jit(solution)/shard_map/ppermute | solution.py:741
  369.5 21.6 %collective-permute-start.56 = (bf16[384,1280]{1,0:T(8,128)(2,1)S(1)}, bf16[384,1280]{1,0:T(8,128)(2,1)}, u32[]{:S(2)}, u32[]{:S(2)}) collective-permute-start(bf16[384,1280]{1,0:T(8,128)(2,1)S(1)} %add_convert_fusion.2), channel_id=1, source_target_pairs={{4,0},{5,1},{6,2},{7,3},{8,12},{9,13},{10,14},{11,15},{20,16},{21,... | collective-permute-start | bytes 2949128 | tf_op jit(solution)/shard_map/ppermute | solution.py:741
  406.4 16.0 %collective-permute-start.74 = (bf16[192,768]{1,0:T(8,128)(2,1)S(1)}, bf16[192,768]{1,0:T(8,128)(2,1)S(1)}, u32[]{:S(2)}, u32[]{:S(2)}) collective-permute-start(bf16[192,768]{1,0:T(8,128)(2,1)S(1)} %get-tuple-element.262), channel_id=1, source_target_pairs={{0,64},{1,65},{2,66},{3,67},{4,68},{5,69},{6,70},{7,71},{8,72},{9,... | collective-permute-start | bytes 884744 | tf_op jit(solution)/shard_map/ppermute | solution.py:741
  409.3 14.4 %collective-permute-start.75 = (bf16[192,768]{1,0:T(8,128)(2,1)S(1)}, bf16[192,768]{1,0:T(8,128)(2,1)S(1)}, u32[]{:S(2)}, u32[]{:S(2)}) collective-permute-start(bf16[192,768]{1,0:T(8,128)(2,1)S(1)} %get-tuple-element.261), channel_id=1, source_target_pairs={{0,96},{1,97},{2,98},{3,99},{4,100},{5,101},{6,102},{7,103},{8,104... | collective-permute-start | bytes 884744 | tf_op jit(solution)/shard_map/ppermute | solution.py:741
  410.6 14.4 %collective-permute-start.59 = (bf16[128,1536]{1,0:T(8,128)(2,1)S(1)}, bf16[128,1536]{1,0:T(8,128)(2,1)S(1)}, u32[]{:S(2)}, u32[]{:S(2)}) collective-permute-start(bf16[128,1536]{1,0:T(8,128)(2,1)S(1)} %get-tuple-element.243), channel_id=1, source_target_pairs={{0,1},{1,2},{2,3},{3,0},{4,5},{5,6},{6,7},{7,4},{8,9},{9,10},{10,1... | collective-permute-start | bytes 1179656 | tf_op jit(solution)/shard_map/ppermute | solution.py:741
  417.1 29.4 %collective-permute-start.77 = (bf16[192,1280]{1,0:T(8,128)(2,1)S(1)}, bf16[192,1280]{1,0:T(8,128)(2,1)S(1)}, u32[]{:S(2)}, u32[]{:S(2)}) collective-permute-start(bf16[192,1280]{1,0:T(8,128)(2,1)S(1)} %add_convert_fusion.3), channel_id=1, source_target_pairs={{0,32},{1,33},{2,34},{3,35},{4,36},{5,37},{6,38},{7,39},{8,40},{9,... | collective-permute-start | bytes 1474568 | tf_op jit(solution)/shard_map/ppermute | solution.py:741
  418.8 29.8 %collective-permute-start.78 = (bf16[192,1280]{1,0:T(8,128)(2,1)S(1)}, bf16[192,1280]{1,0:T(8,128)(2,1)S(1)}, u32[]{:S(2)}, u32[]{:S(2)}) collective-permute-start(bf16[192,1280]{1,0:T(8,128)(2,1)S(1)} %add_convert_fusion.3), channel_id=1, source_target_pairs={{0,64},{1,65},{2,66},{3,67},{4,68},{5,69},{6,70},{7,71},{8,72},{9,... | collective-permute-start | bytes 1474568 | tf_op jit(solution)/shard_map/ppermute | solution.py:741
  423.8 22.5 %collective-permute-start.76 = (bf16[192,768]{1,0:T(8,128)(2,1)S(1)}, bf16[192,768]{1,0:T(8,128)(2,1)S(1)}, u32[]{:S(2)}, u32[]{:S(2)}) collective-permute-start(bf16[192,768]{1,0:T(8,128)(2,1)S(1)} %add_convert_fusion.16), channel_id=1, source_target_pairs={{0,16},{1,17},{2,18},{3,19},{4,20},{5,21},{6,22},{7,23},{8,24},{9,... | collective-permute-start | bytes 884744 | tf_op jit(solution)/shard_map/ppermute | solution.py:741
  425.0 17.2 %collective-permute-start.61 = (bf16[128,1536]{1,0:T(8,128)(2,1)S(1)}, bf16[128,1536]{1,0:T(8,128)(2,1)S(1)}, u32[]{:S(2)}, u32[]{:S(2)}) collective-permute-start(bf16[128,1536]{1,0:T(8,128)(2,1)S(1)} %get-tuple-element.241), channel_id=1, source_target_pairs={{0,3},{1,0},{2,1},{3,2},{4,7},{5,4},{6,5},{7,6},{8,11},{9,8},{10,9... | collective-permute-start | bytes 1179656 | tf_op jit(solution)/shard_map/ppermute | solution.py:741
  433.3 22.3 %collective-permute-start.79 = (bf16[192,1280]{1,0:T(8,128)(2,1)S(1)}, bf16[192,1280]{1,0:T(8,128)(2,1)S(1)}, u32[]{:S(2)}, u32[]{:S(2)}) collective-permute-start(bf16[192,1280]{1,0:T(8,128)(2,1)S(1)} %add_convert_fusion.3), channel_id=1, source_target_pairs={{0,96},{1,97},{2,98},{3,99},{4,100},{5,101},{6,102},{7,103},{8,104... | collective-permute-start | bytes 1474568 | tf_op jit(solution)/shard_map/ppermute | solution.py:741
  446.5 20.4 %collective-permute-start.66 = (bf16[384,512]{1,0:T(8,128)(2,1)S(1)}, bf16[384,512]{1,0:T(8,128)(2,1)S(1)}, u32[]{:S(2)}, u32[]{:S(2)}) collective-permute-start(bf16[384,512]{1,0:T(8,128)(2,1)S(1)} %get-tuple-element.256), channel_id=1, source_target_pairs={{0,96},{1,97},{2,98},{3,99},{4,100},{5,101},{6,102},{7,103},{8,104... | collective-permute-start | bytes 1179656 | tf_op jit(solution)/shard_map/ppermute | solution.py:741
  448.6 22.5 %collective-permute-start.62 = (bf16[128,3072]{1,0:T(8,128)(2,1)}, bf16[128,3072]{1,0:T(8,128)(2,1)S(1)}, u32[]{:S(2)}, u32[]{:S(2)}) collective-permute-start(bf16[128,3072]{1,0:T(8,128)(2,1)} %outputs.1), channel_id=1, source_target_pairs={{4,8},{5,9},{6,10},{7,11},{8,4},{9,5},{10,6},{11,7},{20,24},{21,25... | collective-permute-start | bytes 2359304 | tf_op jit(solution)/shard_map/ppermute | solution.py:741
  455.8 40.9 %collective-permute-start.84 = (bf16[4,192,1280]{2,1,0:T(8,128)(2,1)S(1)}, bf16[4,192,1280]{2,1,0:T(8,128)(2,1)S(1)}, u32[]{:S(2)}, u32[]{:S(2)}) collective-permute-start(bf16[4,192,1280]{2,1,0:T(8,128)(2,1)S(1)} %pad_maximum_fusion.2.here_ref), channel_id=1, source_target_pairs={{0,8},{1,9},{2,10},{3,11},{4,12},{5,13},{6,14},{7,15},{8,0},{9,1},... | collective-permute-start | bytes 5898248 | tf_op jit(solution)/shard_map/ppermute | solution.py:741
  456.0 20.6 %collective-permute-start.80 = (bf16[192,768]{1,0:T(8,128)(2,1)S(1)}, bf16[192,768]{1,0:T(8,128)(2,1)S(1)}, u32[]{:S(2)}, u32[]{:S(2)}) collective-permute-start(bf16[192,768]{1,0:T(8,128)(2,1)S(1)} %add_convert_fusion.15), channel_id=1, source_target_pairs={{0,32},{1,33},{2,34},{3,35},{4,36},{5,37},{6,38},{7,39},{8,40},{9,... | collective-permute-start | bytes 884744 | tf_op jit(solution)/shard_map/ppermute | solution.py:741
  459.6 16.9 %collective-permute-start.81 = (bf16[192,768]{1,0:T(8,128)(2,1)S(1)}, bf16[192,768]{1,0:T(8,128)(2,1)S(1)}, u32[]{:S(2)}, u32[]{:S(2)}) collective-permute-start(bf16[192,768]{1,0:T(8,128)(2,1)S(1)} %add_convert_fusion.15), channel_id=1, source_target_pairs={{0,64},{1,65},{2,66},{3,67},{4,68},{5,69},{6,70},{7,71},{8,72},{9,... | collective-permute-start | bytes 884744 | tf_op jit(solution)/shard_map/ppermute | solution.py:741
  479.5 24.9 %collective-permute-start.83 = (bf16[4,192,768]{2,1,0:T(8,128)(2,1)S(1)}, bf16[4,192,768]{2,1,0:T(8,128)(2,1)S(1)}, u32[]{:S(2)}, u32[]{:S(2)}) collective-permute-start(bf16[4,192,768]{2,1,0:T(8,128)(2,1)S(1)} %pad_maximum_fusion.3.here_ref), channel_id=1, source_target_pairs={{0,8},{1,9},{2,10},{3,11},{4,12},{5,13},{6,14},{7,15},{8,0},{9,1},... | collective-permute-start | bytes 3538952 | tf_op jit(solution)/shard_map/ppermute | solution.py:741
  492.4 17.6 %collective-permute-start.70 = (bf16[192,512]{1,0:T(8,128)(2,1)S(1)}, bf16[192,512]{1,0:T(8,128)(2,1)S(1)}, u32[]{:S(2)}, u32[]{:S(2)}) collective-permute-start(bf16[192,512]{1,0:T(8,128)(2,1)S(1)} %add_convert_fusion.17), channel_id=1, source_target_pairs={{0,32},{1,33},{2,34},{3,35},{4,36},{5,37},{6,38},{7,39},{8,40},{9,... | collective-permute-start | bytes 589832 | tf_op jit(solution)/shard_map/ppermute | solution.py:741
  492.7 17.4 %collective-permute-start.85 = (bf16[192,512]{1,0:T(8,128)(2,1)S(1)}, bf16[192,512]{1,0:T(8,128)(2,1)S(1)}, u32[]{:S(2)}, u32[]{:S(2)}) collective-permute-start(bf16[192,512]{1,0:T(8,128)(2,1)S(1)} %add_convert_fusion.17), channel_id=1, source_target_pairs={{0,64},{1,65},{2,66},{3,67},{4,68},{5,69},{6,70},{7,71},{8,72},{9,... | collective-permute-start | bytes 589832 | tf_op jit(solution)/shard_map/ppermute | solution.py:741
  (118 other events, 1110.3 us)
